TPU v7x, 128 devices: a whole 4x4x4 slice. The times are simulated.
128 devices in a mesh: seq: 32 (over y, x, core), mp: 4 (over z).
Axes of the slice: x: 4, y: 4, z: 4, core: 2. Of those that a mesh axis runs over, the one named last changes fastest.
Arguments:
- tokens: bfloat16 [32768, 1024], P('seq', 'mp'), may hold values from -400 to 400
- w_query: bfloat16 [1024, 1024], P(None, 'mp'), may hold values from -0.125 to 0.125
- w_key: bfloat16 [1024, 1024], P(None, 'mp'), may hold values from -3.875 to 3.875
- w_value: bfloat16 [1024, 1024], P(None, 'mp'), may hold values from -0.1875 to 0.1875
- w_out: bfloat16 [1024, 1024], P('mp'), may hold values from -1.5 to 1.5
- grad_out: bfloat16 [32768, 1024], P('seq', 'mp'), may hold values from -6 to 6
Outputs:
- attn_out: bfloat16 [32768, 1024], P('seq', 'mp')
- grad_tokens: float32 [32768, 1024], P('seq', 'mp')
- grad_w_query: float32 [1024, 1024], P('seq', 'mp')
- grad_w_key: float32 [1024, 1024], P('seq', 'mp')
- grad_w_value: float32 [1024, 1024], P('seq', 'mp')
- grad_w_out: float32 [1024, 1024], P('mp', 'seq')
All inputs are finite; a program needn't handle non-finite values.
Results may differ from a plain program's by a relative error of at most 0.02.
The roundings to bfloat16 on the way count: a program that leaves them out, or rounds other values in their place, can miss the bound.
Values may be sent and summed in bfloat16 or wider, within the bound.
No kernel may reach another device: no remote copies, remote signals or barrier semaphores. Data moves between devices by JAX's collectives and lax.ppermute only.
A program may use at most 192 MiB of HBM per device.

v0:
```python
import jax
import jax.numpy as jnp
from jax import lax
from jax.sharding import PartitionSpec as P

HD = 64
BLOCK = 256
LEVELS = 3


EPSILON = 1e-06
NEGATIVE = -1e30


def with_halo(cells, sides, width):
    for axis, dim in sides:
        count = lax.axis_size(axis)
        ends = count - 1
        head = lax.slice_in_dim(cells, 0, width, axis=dim)
        tail = lax.slice_in_dim(cells, cells.shape[dim] - width, cells.shape[dim], axis=dim)
        cells = jnp.concatenate(
            [
                lax.ppermute(tail, axis, [(i, (i + 1) % count) for i in range(ends)]),
                cells,
                lax.ppermute(head, axis, [((i + 1) % count, i) for i in range(ends)]),
            ],
            axis=dim,
        )
    return cells


def product(form, left_side, right_side):
    return jnp.einsum(form, left_side, right_side, preferred_element_type=jnp.float32)


def pool_rows(source, factor):
    if factor == 1:
        return source
    row_count, channels = source.shape
    grouped = source.reshape(row_count // factor, factor, channels)
    return jnp.mean(grouped, axis=1, dtype=jnp.float32).astype(jnp.bfloat16)


def pool_sums(source, factor):
    if factor == 1:
        return source
    row_count, channels = source.shape
    grouped = source.reshape(row_count // factor, factor, channels)
    return jnp.sum(grouped, axis=1, dtype=jnp.float32).astype(jnp.bfloat16)


def usable_keys(first_block, block_total, block_count, offsets):
    neighbour = (
        first_block
        + jnp.arange(block_count, dtype=jnp.int32)[:, None]
        + jnp.array(offsets, dtype=jnp.int32)[None, :]
        - 1
    )
    return jnp.repeat((neighbour >= 0) & (neighbour < block_total), BLOCK, axis=1)


def level_forward(queries, extended, first_block, block_total, with_own):
    row_count, channels = queries.shape
    head_count = channels // HD
    block_count = row_count // BLOCK
    offsets = (0, 1, 2) if with_own else (0, 2)
    blocks_ext = extended.reshape(block_count + 2, BLOCK, 2, head_count, HD)
    picked = jnp.concatenate(
        [blocks_ext[offset : offset + block_count] for offset in offsets], axis=1
    )
    key_rows = picked[:, :, 0]
    value_rows = picked[:, :, 1]
    query_blocks = queries.reshape(block_count, BLOCK, head_count, HD)
    scores = product("jqhd,jkhd->jhqk", query_blocks, key_rows) * HD ** (-0.5)
    usable = usable_keys(first_block, block_total, block_count, offsets)
    scores = jnp.where(usable[:, None, None, :], scores, NEGATIVE)
    row_max = jnp.max(scores, axis=-1, keepdims=True)
    exponent = jnp.exp(scores - row_max)
    probabilities = exponent / jnp.sum(exponent, axis=-1, keepdims=True)
    weights = probabilities.astype(jnp.bfloat16)
    level_out = product("jhqk,jkhd->jqhd", weights, value_rows)
    kept = (query_blocks, key_rows, value_rows, probabilities, weights, offsets)
    return (level_out.reshape(queries.shape), kept)


def level_backward(kept, d_level):
    query_blocks, key_rows, value_rows, probabilities, weights, offsets = kept
    block_count, block_rows, head_count, head_size = query_blocks.shape
    channels = head_count * head_size
    row_count = block_count * block_rows
    grad_blocks = d_level.reshape(block_count, BLOCK, head_count, HD)
    d_weights = product("jqhd,jkhd->jhqk", grad_blocks, value_rows)
    d_value_rows = product("jhqk,jqhd->jkhd", weights, grad_blocks)
    row_dot = jnp.sum(probabilities * d_weights, axis=-1, keepdims=True)
    d_scores = (probabilities * (d_weights - row_dot) * HD ** (-0.5)).astype(jnp.bfloat16)
    d_query_blocks = product("jhqk,jkhd->jqhd", d_scores, key_rows)
    d_key_rows = product("jhqk,jqhd->jkhd", d_scores, query_blocks)
    d_picked = jnp.stack([d_key_rows, d_value_rows], axis=2).reshape(
        block_count, len(offsets), BLOCK, 2 * channels
    )
    d_ext = jnp.zeros((block_count + 2, BLOCK, 2 * channels), jnp.float32)
    for position, offset in enumerate(offsets):
        d_ext = d_ext.at[offset : offset + block_count].add(d_picked[:, position])
    return (
        d_query_blocks.reshape(row_count, channels),
        d_ext.reshape((block_count + 2) * BLOCK, 2 * channels),
    )


def gather_rims(pooled_kv):
    return [with_halo(pooled, (("seq", 0),), BLOCK) for pooled in pooled_kv]


def return_rims(level_grads):
    interior = [level_grad[BLOCK:-BLOCK] for level_grad in level_grads]
    coarse = []
    for level_grad, middle in zip(level_grads, interior):
        padded = with_halo(level_grad.astype(jnp.bfloat16), (("seq", 0),), BLOCK).astype(
            level_grad.dtype
        )
        coarse.append(middle.at[:BLOCK].add(padded[:BLOCK]).at[-BLOCK:].add(padded[-BLOCK:]))
    return coarse


def per_device(tokens, w_query, w_key, w_value, w_out, grad_out):
    token_full, grad_full = (
        lax.all_gather(tokens, "mp", axis=1, tiled=True),
        lax.all_gather(grad_out, "mp", axis=1, tiled=True),
    )
    row_count, model_width = token_full.shape
    channels = w_query.shape[1]
    share_width = tokens.shape[1]
    seq_count = lax.axis_size("seq")
    seq_index = lax.axis_index("seq")
    as_float = token_full.astype(jnp.float32)
    inverse = lax.rsqrt(jnp.mean(as_float * as_float, axis=1, keepdims=True) + EPSILON)
    normed_f = as_float * inverse
    normed = normed_f.astype(jnp.bfloat16)
    stacked_w = jnp.concatenate([w_query, w_key, w_value], axis=1)
    projected = jnp.dot(normed, stacked_w, preferred_element_type=jnp.float32).astype(jnp.bfloat16)
    queries = projected[:, :channels]
    key_value = projected[:, channels:]
    factors = [2**level_index for level_index in range(LEVELS)]
    pooled_q = [pool_rows(queries, factor) for factor in factors]
    pooled_kv = [pool_rows(key_value, factor) for factor in factors]
    extended = gather_rims(pooled_kv)
    firsts = [seq_index * (row_count // (BLOCK * factor)) for factor in factors]
    totals = [row_count * seq_count // (BLOCK * factor) for factor in factors]
    attended_f = jnp.zeros((row_count, channels), jnp.float32)
    kept_levels = []
    for level_index in range(LEVELS):
        level_out, kept = level_forward(
            pooled_q[level_index],
            extended[level_index],
            firsts[level_index],
            totals[level_index],
            level_index == 0,
        )
        kept_levels.append(kept)
        attended_f = attended_f + jnp.repeat(level_out, factors[level_index], axis=0)
    attended = attended_f.astype(jnp.bfloat16)
    partial_out = jnp.dot(attended, w_out, preferred_element_type=jnp.float32)
    attn_out = lax.psum_scatter(
        partial_out.astype(jnp.bfloat16), "mp", scatter_dimension=1, tiled=True
    )
    d_attended = jnp.einsum(
        "nd,cd->nc", grad_full, w_out, preferred_element_type=jnp.float32
    ).astype(jnp.bfloat16)
    d_queries_f = jnp.zeros((row_count, channels), jnp.float32)
    level_grads = []
    for level_index in range(LEVELS):
        factor = factors[level_index]
        d_level = pool_sums(d_attended, factor)
        d_pooled_q, d_ext = level_backward(kept_levels[level_index], d_level)
        d_queries_f = d_queries_f + jnp.repeat(d_pooled_q, factor, axis=0) / factor
        level_grads.append(d_ext)
    coarse = return_rims(level_grads)
    d_kv_f = jnp.zeros((row_count, 2 * channels), jnp.float32)
    for level_index in range(LEVELS):
        d_kv_f = (
            d_kv_f
            + jnp.repeat(coarse[level_index], factors[level_index], axis=0) / factors[level_index]
        )
    d_proj = jnp.concatenate([d_queries_f, d_kv_f], axis=1).astype(jnp.bfloat16)
    d_normed_part = jnp.einsum("nc,dc->nd", d_proj, stacked_w, preferred_element_type=jnp.float32)
    inner_terms = jnp.einsum("nd,nc->dc", normed, d_proj, preferred_element_type=jnp.float32)
    outer_terms = jnp.einsum("nd,nc->dc", grad_full, attended, preferred_element_type=jnp.float32)
    shares = lax.psum_scatter(
        jnp.concatenate([inner_terms, outer_terms], axis=1).astype(jnp.bfloat16),
        "seq",
        scatter_dimension=0,
        tiled=True,
    ).astype(jnp.float32)
    grad_w_query = shares[:, :channels]
    grad_w_key = shares[:, channels : 2 * channels]
    grad_w_value = shares[:, 2 * channels : 3 * channels]
    grad_w_out = shares[:, 3 * channels :].T
    mp_index = lax.axis_index("mp")
    summed_all = lax.psum(d_normed_part.astype(jnp.bfloat16), "mp").astype(jnp.float32)
    row_dot = jnp.mean(summed_all * normed_f, axis=1, keepdims=True)
    grad_whole = inverse * (summed_all - normed_f * row_dot)
    grad_tokens = lax.dynamic_slice_in_dim(grad_whole, mp_index * share_width, share_width, 1)
    return (attn_out, grad_tokens, grad_w_query, grad_w_key, grad_w_value, grad_w_out)


def solution(mesh):
    return jax.shard_map(
        per_device,
        mesh=mesh,
        in_specs=(
            P("seq", "mp"),
            P(None, "mp"),
            P(None, "mp"),
            P(None, "mp"),
            P("mp", None),
            P("seq", "mp"),
        ),
        out_specs=(
            P("seq", "mp"),
            P("seq", "mp"),
            P("seq", "mp"),
            P("seq", "mp"),
            P("seq", "mp"),
            P("mp", "seq"),
        ),
        check_vma=False,
    )
```

profile of v0, /device:TPU:0, one launch (start us, length us, event | category | flops | bytes accessed | tf_op | source)
XLA Modules:
  0.0 669.7 jit_solution(13298587339152242031)
XLA Ops:
  10.7 36.2 %all-gather.3.cloned.1.call-done = bf16[1024,1024]{1,0:T(8,128)(2,1)} async-done(((bf16[1024,256]{1,0:T(8,128)(2,1)}), bf16[1024,1024]{1,0:T(8,128)(2,1)}) %all-gather.3.cloned.1.call-update) | async-done | bytes 2097168 | tf_op jit(solution)/shard_map/all_gather | solution.py:127
  57.4 4.2 reduce_sum.134
  76.6 7.5 %all-gather.5.cloned.1.call-done = bf16[1024,1024]{1,0:T(8,128)(2,1)} async-done(((bf16[1024,256]{1,0:T(8,128)(2,1)}), bf16[1024,1024]{1,0:T(8,128)(2,1)}) %all-gather.5.cloned.1.call-update) | async-done | bytes 2097168 | tf_op jit(solution)/shard_map/all_gather | solution.py:128
  91.7 13.4 %collective-permute-start.5 = (bf16[256,512]{1,0:T(8,128)(2,1)}, bf16[256,512]{1,0:T(8,128)(2,1)}, u32[]{:S(2)}, u32[]{:S(2)}) collective-permute-start(bf16[256,512]{1,0:T(8,128)(2,1)} %multiply_convert_fusion.4), channel_id=1, source_target_pairs={{4,0},{8,4},{12,8},{16,12},{20,16},{24,20},{28,24},{32,28},{36,32}... | collective-permute-start | bytes 786440 | tf_op jit(solution)/shard_map/ppermute | solution.py:25
  112.1 4.7 collective-permute-start
  146.1 4.4 fusion.174
  154.3 18.8 %fusion.63 = f32[2,512,1,4,64]{1,4,3,0,2:T(8,128)} fusion(bf16[2,256,4,64]{1,3,2,0:T(8,128)(2,1)} %copy.198, f32[2,4,256,512]{3,2,1,0:T(8,128)} %fusion.142, f32[2,4,256,512]{3,2,1,0:T(8,128)} %get-tuple-element.243, f32[2,4,256]{2,1,0:T(4,128)S(1)} %get-tuple-element.242), kind=kOutput, calls=%fused_computation.77 | convolution fusion | flops 141560320 | bytes 9707520 | tf_op jit(solution)/shard_map/jhqk,jqhd->jkhd/dot_general | solution.py:33
  173.0 18.3 %fusion.81 = f32[2,256,4,64]{1,3,2,0:T(8,128)} fusion(f32[2,4,256,512]{3,2,1,0:T(8,128)} %fusion.142, bf16[2,256,2,4,64]{1,4,3,0,2:T(8,128)(2,1)S(1)} %copy-done.26, bf16[2,256,2,4,64]{1,4,3,0,2:T(8,128)(2,1)S(1)} %copy-done.24, f32[2,4,256,512]{3,2,1,0:T(8,128)} %get-tuple-element.243, f32[2,4,256]{2,1,0:T(4,128)S(1)} %get-tuple-element.242), kind=kOutput, calls=%fused_computation.89 | convolution fusion | flops 142739968 | bytes 9969664 | tf_op jit(solution)/shard_map/jhqk,jkhd->jqhd/dot_general | solution.py:33
  210.5 6.4 fusion.61
  216.9 6.6 fusion.173
  223.6 39.8 %fusion.69 = f32[4,256,4,64]{1,3,2,0:T(8,128)} fusion(f32[4,4,256,768]{3,2,1,0:T(8,128)} %fusion.61, bf16[4,768,2,4,64]{1,4,3,0,2:T(8,128)(2,1)} %copy-done.2, f32[4,4,256,768]{3,2,1,0:T(8,128)} %get-tuple-element.241, f32[4,4,256]{2,1,0:T(4,128)S(1)} %get-tuple-element.240), kind=kOutput, calls=%fused_computation.80 | convolution fusion | flops 424678144 | bytes 52985856 | tf_op jit(solution)/shard_map/jhqk,jkhd->jqhd/dot_general | solution.py:33
  263.3 40.1 %fusion.48 = f32[4,768,1,4,64]{1,4,3,0,2:T(8,128)} fusion(bf16[4,256,4,64]{1,3,2,0:T(8,128)(2,1)S(1)} %copy-done.19, f32[4,4,256,768]{3,2,1,0:T(8,128)} %fusion.61, f32[4,4,256,768]{3,2,1,0:T(8,128)} %get-tuple-element.241, f32[4,4,256]{2,1,0:T(4,128)S(1)} %get-tuple-element.240), kind=kOutput, calls=%fused_computation.63 | convolution fusion | flops 424678144 | bytes 28852224 | tf_op jit(solution)/shard_map/jhqk,jqhd->jkhd/dot_general | solution.py:33
  303.5 7.2 %fusion.51 = f32[4,768,1,4,64]{1,4,3,0,2:T(8,128)} fusion(bf16[4,256,4,64]{1,3,2,0:T(8,128)(2,1)S(1)} %copy.208, f32[4,4,256,768]{3,2,1,0:T(8,128)} %get-tuple-element.241, f32[4,4,256]{2,1,0:T(4,128)S(1)} %get-tuple-element.240), kind=kOutput, calls=%fused_computation.64 | convolution fusion | flops 408944640 | bytes 16269312 | tf_op jit(solution)/shard_map/jhqk,jqhd->jkhd/dot_general | solution.py:33
  329.9 10.7 %reshape.595 = f32[4,3,256,512]{2,1,3,0:T(4,128)} reshape(f32[4,768,2,4,64]{1,4,3,2,0:T(8,128)} %copy.220) | data formatting | bytes 12582912 | tf_op jit(solution)/shard_map/reshape | solution.py:98
  340.6 14.1 %fusion.162 = (f32[4,1,256,512]{2,1,3,0:T(1,128)S(1)}, f32[4,1,256,512]{2,1,3,0:T(1,128)S(1)}, f32[4,1,256,512]{2,1,3,0:T(1,128)S(1)}) fusion(f32[4,3,256,512]{2,1,3,0:T(4,128)} %reshape.595), kind=kLoop, calls=%fused_computation.200 | loop fusion | bytes 12582912 | tf_op jit(solution)/shard_map/slice | solution.py:103
  370.5 9.6 %fusion.84 = f32[4,64,256]{2,1,0:T(8,128)} fusion(f32[4,256,512]{2,1,0:T(8,128)} %fusion.139, bf16[1,256,2,4,64]{1,4,3,2,0:T(8,128)(2,1)S(1)} %bitcast.219, bf16[1,256,2,4,64]{1,4,3,2,0:T(8,128)(2,1)S(1)} %bitcast.214, f32[4,256,512]{2,1,0:T(8,128)} %get-tuple-element.239, f32[4,256]{1,0:T(4,128)S(1)} %get-tuple-element.238), kind=kOutput, calls=%fused_computation.90 | convolution fusion | flops 71370240 | bytes 4984832 | tf_op jit(solution)/shard_map/jhqk,jkhd->jqhd/dot_general | solution.py:33
  380.1 9.8 %fusion.75 = f32[1,512,1,4,64]{1,4,3,2,0:T(8,128)} fusion(bf16[256,4,64]{0,2,1:T(8,128)(2,1)S(1)} %bitcast.227, f32[4,256,512]{2,1,0:T(8,128)} %fusion.139, f32[4,256,512]{2,1,0:T(8,128)} %get-tuple-element.239, f32[4,256]{1,0:T(4,128)S(1)} %get-tuple-element.238), kind=kOutput, calls=%fused_computation.85 | convolution fusion | flops 70780416 | bytes 4853760 | tf_op jit(solution)/shard_map/jhqk,jqhd->jkhd/dot_general | solution.py:33
  404.4 4.3 collective-permute-start.8
  440.7 5.1 collective-permute-start.10
  479.3 8.3 %fusion.66 = f32[4,256,4,64]{1,3,2,0:T(8,128)} fusion(bf16[4,768,2,4,64]{1,4,3,0,2:T(8,128)(2,1)} %copy-done.2, f32[4,4,256,768]{3,2,1,0:T(8,128)} %get-tuple-element.241, f32[4,4,256]{2,1,0:T(4,128)S(1)} %copy-done.56), kind=kOutput, calls=%fused_computation.79 | convolution fusion | flops 408944640 | bytes 15220736 | tf_op jit(solution)/shard_map/jhqk,jkhd->jqhd/dot_general | solution.py:33
  508.0 3.9 copy.252
  514.1 34.4 %all-reduce.4.cloned.1.call-done = bf16[1024,1024]{1,0:T(8,128)(2,1)} async-done(((bf16[1024,1024]{1,0:T(8,128)(2,1)}), bf16[1024,1024]{1,0:T(8,128)(2,1)}) %all-reduce.4.cloned.1.call-update) | async-done | bytes 2097168 | tf_op jit(solution)/shard_map/psum | solution.py:199
  552.9 77.8 %reduce-scatter.7.cloned.1.call-done = bf16[32,1024]{1,0:T(8,128)(2,1)} async-done(((bf16[1024,1024]{1,0:T(8,128)(2,1)}), bf16[32,1024]{1,0:T(8,128)(2,1)}) %reduce-scatter.7.cloned.1.call-update) | async-done | bytes 65552
  634.6 28.4 %reduce-scatter.5.cloned.1.call-done = bf16[1024,256]{1,0:T(8,128)(2,1)} async-done(((bf16[1024,1024]{1,0:T(8,128)(2,1)}), bf16[1024,256]{1,0:T(8,128)(2,1)}) %reduce-scatter.5.cloned.1.call-update) | async-done | bytes 524304 | tf_op jit(solution)/shard_map/reduce_scatter | solution.py:163
  (303 shorter events, 240.7 us)
Async XLA Ops:
  7.2 77.0 %copy-start = (bf16[256,1024]{1,0:T(8,128)(2,1)S(1)}, bf16[256,1024]{1,0:T(8,128)(2,1)}, u32[]{:S(2)}) copy-start(bf16[256,1024]{1,0:T(8,128)(2,1)} %param.43) | copy-start | bytes 1572868
  7.2 39.7 %all-gather.3.cloned.1.call-start = ((), (), s32[]{:S(2)}) async-start(), calls=%async_computation.2 | async-start | bytes 2621440 | tf_op jit(solution)/shard_map/all_gather | solution.py:127
  7.9 76.2 %all-gather.5.cloned.1.call-start = ((), (), s32[]{:S(2)}) async-start(), calls=%async_computation.4 | async-start | bytes 2621440 | tf_op jit(solution)/shard_map/all_gather | solution.py:128
  8.7 539.8 %all-reduce.4.cloned.1.call-start = ((), (), s32[]{:S(2)}) async-start(), calls=%async_computation.5 | async-start | bytes 4194304 | tf_op jit(solution)/shard_map/psum | solution.py:199
  10.7 38.4 %copy-start.46 = (bf16[1024,768]{1,0:T(8,128)(2,1)}, bf16[1024,768]{1,0:T(8,128)(2,1)S(1)}, u32[]{:S(2)}) copy-start(bf16[1024,768]{1,0:T(8,128)(2,1)S(1)} %constant_dynamic-update-slice_fusion) | copy-start | bytes 4718596
  62.6 68.8 %collective-permute-start.2 = (bf16[256,512]{1,0:T(8,128)(2,1)}, bf16[256,512]{1,0:T(8,128)(2,1)}, u32[]{:S(2)}, u32[]{:S(2)}) collective-permute-start(bf16[256,512]{1,0:T(8,128)(2,1)} %get-tuple-element.234), channel_id=1, source_target_pairs={{0,4},{4,8},{8,12},{12,16},{16,20},{20,24},{24,28},{28,32},{32,36}... | collective-permute-start | bytes 786440 | tf_op jit(solution)/shard_map/ppermute | solution.py:23
  64.5 68.1 %collective-permute-start.3 = (bf16[256,512]{1,0:T(8,128)(2,1)}, bf16[256,512]{1,0:T(8,128)(2,1)}, u32[]{:S(2)}, u32[]{:S(2)}) collective-permute-start(bf16[256,512]{1,0:T(8,128)(2,1)} %get-tuple-element.233), channel_id=1, source_target_pairs={{4,0},{8,4},{12,8},{16,12},{20,16},{24,20},{28,24},{32,28},{36,32}... | collective-permute-start | bytes 786440 | tf_op jit(solution)/shard_map/ppermute | solution.py:25
  89.7 273.8 %collective-permute-start.4 = (bf16[256,512]{1,0:T(8,128)(2,1)}, bf16[256,512]{1,0:T(8,128)(2,1)}, u32[]{:S(2)}, u32[]{:S(2)}) collective-permute-start(bf16[256,512]{1,0:T(8,128)(2,1)} %multiply_convert_fusion.4), channel_id=1, source_target_pairs={{0,4},{4,8},{8,12},{12,16},{16,20},{20,24},{24,28},{28,32},{32,36}... | collective-permute-start | bytes 786440 | tf_op jit(solution)/shard_map/ppermute | solution.py:23
  91.7 273.8 %collective-permute-start.5 = (bf16[256,512]{1,0:T(8,128)(2,1)}, bf16[256,512]{1,0:T(8,128)(2,1)}, u32[]{:S(2)}, u32[]{:S(2)}) collective-permute-start(bf16[256,512]{1,0:T(8,128)(2,1)} %multiply_convert_fusion.4), channel_id=1, source_target_pairs={{4,0},{8,4},{12,8},{16,12},{20,16},{24,20},{28,24},{32,28},{36,32}... | collective-permute-start | bytes 786440 | tf_op jit(solution)/shard_map/ppermute | solution.py:25
  112.1 79.2 %collective-permute-start = (bf16[256,512]{1,0:T(8,128)(2,1)}, bf16[256,512]{1,0:T(8,128)(2,1)}, u32[]{:S(2)}, u32[]{:S(2)}) collective-permute-start(bf16[256,512]{1,0:T(8,128)(2,1)} %get-tuple-element.219), channel_id=1, source_target_pairs={{0,4},{4,8},{8,12},{12,16},{16,20},{20,24},{24,28},{28,32},{32,36}... | collective-permute-start | bytes 786440 | tf_op jit(solution)/shard_map/ppermute | solution.py:23
  131.3 60.0 %collective-permute-start.1 = (bf16[256,512]{1,0:T(8,128)(2,1)}, bf16[256,512]{1,0:T(8,128)(2,1)}, u32[]{:S(2)}, u32[]{:S(2)}) collective-permute-start(bf16[256,512]{1,0:T(8,128)(2,1)} %get-tuple-element.220), channel_id=1, source_target_pairs={{4,0},{8,4},{12,8},{16,12},{20,16},{24,20},{28,24},{32,28},{36,32}... | collective-permute-start | bytes 786440 | tf_op jit(solution)/shard_map/ppermute | solution.py:25
  150.5 22.5 %copy-start.57 = (f32[2,4,256]{2,1,0:T(4,128)}, f32[2,4,256]{2,1,0:T(4,128)S(1)}, u32[]{:S(2)}) copy-start(f32[2,4,256]{2,1,0:T(4,128)S(1)} %get-tuple-element.242) | copy-start | bytes 24580
  223.6 79.9 %copy-start.55 = (f32[4,4,256]{2,1,0:T(4,128)}, f32[4,4,256]{2,1,0:T(4,128)S(1)}, u32[]{:S(2)}) copy-start(f32[4,4,256]{2,1,0:T(4,128)S(1)} %get-tuple-element.240) | copy-start | bytes 49156
  364.6 25.4 %copy-start.33 = (bf16[256,512]{0,1:T(8,128)(2,1)}, bf16[256,512]{0,1:T(8,128)(2,1)S(1)}, u32[]{:S(2)}) copy-start(bf16[256,512]{0,1:T(8,128)(2,1)S(1)} %copy.202) | copy-start | bytes 786436
  366.6 23.4 %copy-start.35 = (bf16[256,512]{0,1:T(8,128)(2,1)}, bf16[256,512]{0,1:T(8,128)(2,1)S(1)}, u32[]{:S(2)}) copy-start(bf16[256,512]{0,1:T(8,128)(2,1)S(1)} %copy.203) | copy-start | bytes 786436
  404.4 42.4 %collective-permute-start.8 = (bf16[256,512]{1,0:T(8,128)(2,1)}, bf16[256,512]{1,0:T(8,128)(2,1)}, u32[]{:S(2)}, u32[]{:S(2)}) collective-permute-start(bf16[256,512]{1,0:T(8,128)(2,1)} %get-tuple-element.223), channel_id=1, source_target_pairs={{0,4},{4,8},{8,12},{12,16},{16,20},{20,24},{24,28},{28,32},{32,36}... | collective-permute-start | bytes 786440 | tf_op jit(solution)/shard_map/ppermute | solution.py:23
  408.7 39.4 %collective-permute-start.9 = (bf16[256,512]{1,0:T(8,128)(2,1)}, bf16[256,512]{1,0:T(8,128)(2,1)}, u32[]{:S(2)}, u32[]{:S(2)}) collective-permute-start(bf16[256,512]{1,0:T(8,128)(2,1)} %get-tuple-element.224), channel_id=1, source_target_pairs={{4,0},{8,4},{12,8},{16,12},{20,16},{24,20},{28,24},{32,28},{36,32}... | collective-permute-start | bytes 786440 | tf_op jit(solution)/shard_map/ppermute | solution.py:25
  416.4 51.5 %collective-permute-start.6 = (bf16[256,512]{0,1:T(8,128)(2,1)}, bf16[256,512]{0,1:T(8,128)(2,1)S(1)}, u32[]{:S(2)}, u32[]{:S(2)}) collective-permute-start(bf16[256,512]{0,1:T(8,128)(2,1)} %get-tuple-element.215), channel_id=1, source_target_pairs={{0,4},{4,8},{8,12},{12,16},{16,20},{20,24},{24,28},{28,32},{32,36}... | collective-permute-start | bytes 786440 | tf_op jit(solution)/shard_map/ppermute | solution.py:23
  420.0 47.9 %collective-permute-start.7 = (bf16[256,512]{0,1:T(8,128)(2,1)}, bf16[256,512]{0,1:T(8,128)(2,1)}, u32[]{:S(2)}, u32[]{:S(2)}) collective-permute-start(bf16[256,512]{0,1:T(8,128)(2,1)} %get-tuple-element.216), channel_id=1, source_target_pairs={{4,0},{8,4},{12,8},{16,12},{20,16},{24,20},{28,24},{32,28},{36,32}... | collective-permute-start | bytes 786440 | tf_op jit(solution)/shard_map/ppermute | solution.py:25
  435.4 10.4 %copy-start.16 = (f32[1024,256]{0,1:T(8,128)S(1)}, f32[1024,256]{0,1:T(8,128)}, u32[]{:S(2)}) copy-start(f32[1024,256]{0,1:T(8,128)} %copy.217) | copy-start | bytes 3145732
  440.7 18.3 %collective-permute-start.10 = (bf16[256,512]{1,0:T(8,128)(2,1)}, bf16[256,512]{1,0:T(8,128)(2,1)}, u32[]{:S(2)}, u32[]{:S(2)}) collective-permute-start(bf16[256,512]{1,0:T(8,128)(2,1)} %get-tuple-element.229), channel_id=1, source_target_pairs={{0,4},{4,8},{8,12},{12,16},{16,20},{20,24},{24,28},{28,32},{32,36}... | collective-permute-start | bytes 786440 | tf_op jit(solution)/shard_map/ppermute | solution.py:23
  446.8 12.2 %collective-permute-start.11 = (bf16[256,512]{1,0:T(8,128)(2,1)}, bf16[256,512]{1,0:T(8,128)(2,1)}, u32[]{:S(2)}, u32[]{:S(2)}) collective-permute-start(bf16[256,512]{1,0:T(8,128)(2,1)} %get-tuple-element.230), channel_id=1, source_target_pairs={{4,0},{8,4},{12,8},{16,12},{20,16},{24,20},{28,24},{32,28},{36,32}... | collective-permute-start | bytes 786440 | tf_op jit(solution)/shard_map/ppermute | solution.py:25
  478.6 152.1 %reduce-scatter.7.cloned.1.call-start = ((), (), s32[]{:S(2)}) async-start(), calls=%async_computation.6 | async-start | bytes 2162688
  511.9 151.1 %reduce-scatter.5.cloned.1.call-start = ((), (), s32[]{:S(2)}) async-start(), calls=%async_computation.3 | async-start | bytes 2621440 | tf_op jit(solution)/shard_map/reduce_scatter | solution.py:163
  (52 other events, 220.1 us)
Sparse Core Ops, SparseCore 0:
  9.7 37.1 all-gather.2
  48.6 35.5 all-gather.4
  478.7 69.7 all-reduce.3
  552.3 78.3 reduce-scatter.6
  633.7 29.3 reduce-scatter.4
where the time goes:
time: 681 us; the launch traced here: 670 us
  matrix products  192 us (28%)
  waiting for transfers between devices  186 us (27%)
  local copies, waits for them, and re-layouts  173 us (25%)
  other arithmetic  61.3 us (9%)
  starting transfers between devices  42.3 us (6%)
  between operations  15 us (2%)
    dot_general x16, matrix products, product(): jnp.einsum(form, left_side, right_side, preferred_element_type=jnp.float32)  173 us
    unnamed x6, waiting for transfers between devices  79.2 us
    all_gather x1, waiting for transfers between devices, per_device(): lax.all_gather(tokens, 'mp', axis=1, tiled=True)  36.2 us
    psum x1, waiting for transfers between devices, per_device(): lax.psum(d_normed_part.astype(jnp.bfloat16), 'mp').astype(jnp.float32)  34.4 us
    reduce_scatter x1, waiting for transfers between devices, per_device(): lax.psum_scatter(partial_out.astype(jnp.bfloat16), 'mp', scatter_dimensio...  28.4 us
    unnamed x137, local copies, waits for them, and re-layouts  27.9 us
    slice x10, local copies, waits for them, and re-layouts, level_forward(): blocks_ext[offset:offset + block_count]  26.1 us
    ppermute x6, starting transfers between devices, with_halo(): lax.ppermute(tail, axis, [(i, (i + 1) % count) for i in range(ends)])  21.7 us
  transfers between devices with their start and end apart: 17, of which 5 were waited for; matrix products, arithmetic and copies ran while one was open for 56% of the time, Pallas kernels for 0%

commit v1 on v0

v1 whole, which is shorter than its diff:
```python
import jax
import jax.numpy as jnp
from jax import lax
from jax.experimental import pallas as pl
from jax.experimental.pallas import tpu as pltpu
from jax.sharding import PartitionSpec as P

HD = 64
BLOCK = 256
LEVELS = 3
PAIR = 2 * HD
MP = 4
LANES = 128
DOT_ROWS = 16

EPSILON = 1e-06
NEGATIVE = -1e30

F32 = jnp.float32
BF16 = jnp.bfloat16

FIRST_EXT = (0, 6, 10)
EXT_BLOCKS = (6, 4, 3)
EXT_TOTAL = 13


def nn(left, right):
    return lax.dot_general(left, right, (((1,), (0,)), ((), ())), preferred_element_type=F32)


def nt(left, right):
    return lax.dot_general(left, right, (((1,), (1,)), ((), ())), preferred_element_type=F32)


def tn(left, right):
    return lax.dot_general(left, right, (((0,), (0,)), ((), ())), preferred_element_type=F32)


def pool_matrix(coarse, factor, value):
    shape = (coarse, coarse * factor)
    row = lax.broadcasted_iota(jnp.int32, shape, 0)
    low = row * factor
    col = lax.broadcasted_iota(jnp.int32, shape, 1)
    return jnp.where((col >= low) & (col < low + factor), value, 0.0).astype(BF16)


def spread_matrix(coarse, factor, value):
    shape = (coarse * factor, coarse)
    low = lax.broadcasted_iota(jnp.int32, shape, 1) * factor
    row = lax.broadcasted_iota(jnp.int32, shape, 0)
    return jnp.where((row >= low) & (row < low + factor), value, 0.0).astype(BF16)


def share_rows(me, step, width):
    return pl.ds(pl.multiple_of(((me + step) & (MP - 1)) * width, width), width)


def params(limit_mib):
    return pltpu.CompilerParams(vmem_limit_bytes=limit_mib * 2**20)


SMALL = pl.CostEstimate(flops=10**6, bytes_accessed=10**4, transcendentals=0)


def in_hbm(*values):
    return [pltpu.with_memory_space_constraint(value, pltpu.HBM) for value in values]


def hbm_shape(shape, dtype):
    return pltpu.HBM(shape, dtype)


def whole(shape):
    return pl.BlockSpec(shape, lambda i: (0,) * len(shape))


def rows_spec(rows, width):
    return pl.BlockSpec((rows, width), lambda i: (i, 0))


SCALAR = pl.BlockSpec(memory_space=pltpu.SMEM)


def low_spec(width):
    return pl.BlockSpec((BLOCK, width), lambda i: (jnp.minimum(i, 1), 0))


def high_spec(width):
    return pl.BlockSpec((BLOCK, width), lambda i: (jnp.maximum(i - 2, 0), 0))


def share_specs(width):
    return [rows_spec(BLOCK, width)] + [low_spec(width), high_spec(width)] * 3


def read_shares(step, refs):
    own, *halves = refs
    shares = [own[...]]
    for low, high in zip(halves[0::2], halves[1::2]):
        shares.append(jnp.where(step < 2, low[...], high[...]))
    return shares


def project_kernel(
    me_ref, t0, t1a, t1b, t2a, t2b, t3a, t3b, wq, wk, wv,
    normed, inverse, q0, kv0, q1, kv1, q2, kv2, to_left, to_right,
):
    step = pl.program_id(0)
    me = me_ref[0]
    width = t0.shape[1]
    read = read_shares(step, (t0, t1a, t1b, t2a, t2b, t3a, t3b))
    shares = [share.astype(F32) for share in read]
    total = jnp.sum(shares[0] * shares[0], axis=1, keepdims=True)
    for share in shares[1:]:
        total = total + jnp.sum(share * share, axis=1, keepdims=True)
    inv = lax.rsqrt(total / (MP * width) + EPSILON)
    inverse[...] = jnp.broadcast_to(inv, inverse.shape)
    sums = [None, None, None]
    for r, share in enumerate(shares):
        part = (share * inv).astype(BF16)
        normed[:, r * width : (r + 1) * width] = part
        rows = share_rows(me, r, width)
        for n, w in enumerate((wq, wk, wv)):
            term = nn(part, w[rows, :])
            sums[n] = term if sums[n] is None else sums[n] + term
    fine = [s.astype(BF16) for s in sums]
    half = pool_matrix(BLOCK // 2, 2, 0.5)
    quarter = pool_matrix(BLOCK // 4, 4, 0.25)
    mid = [nn(half, x).astype(BF16) for x in fine]
    low = [nn(quarter, x).astype(BF16) for x in fine]
    q0[...] = fine[0]
    q1[...] = mid[0]
    q2[...] = low[0]
    half_rows = pl.ds(pl.multiple_of(256 + (step & 1) * 128, 128), 128)
    low_rows = pl.ds(pl.multiple_of(512 + step * 64, 64), 64)
    for n in range(2):
        kv0[n] = fine[1 + n]
        kv1[n] = mid[1 + n]
        kv2[n] = low[1 + n]
        to_left[n, low_rows, :] = low[1 + n]
        to_right[n, low_rows, :] = low[1 + n]

    @pl.when(step == 0)
    def _():
        for n in range(2):
            to_left[n, 0:BLOCK, :] = fine[1 + n]

    @pl.when(step < 2)
    def _():
        for n in range(2):
            to_left[n, half_rows, :] = mid[1 + n]

    @pl.when(step >= 2)
    def _():
        for n in range(2):
            to_right[n, half_rows, :] = mid[1 + n]

    @pl.when(step == 3)
    def _():
        for n in range(2):
            to_right[n, 0:BLOCK, :] = fine[1 + n]


def project(me, shares, wq, wk, wv):
    rows, width = shares[0].shape
    out = jax.ShapeDtypeStruct
    edge = out((2, 3 * BLOCK, width), BF16)
    pair_spec = lambda n: pl.BlockSpec((2, n, width), lambda i: (0, i, 0))
    return pl.pallas_call(
        project_kernel,
        grid=(rows // BLOCK,),
        in_specs=[SCALAR] + share_specs(width) + [whole(wq.shape)] * 3,
        out_specs=[
            rows_spec(BLOCK, MP * width),
            rows_spec(BLOCK, LANES),
            rows_spec(BLOCK, width),
            pair_spec(BLOCK),
            rows_spec(BLOCK // 2, width),
            pair_spec(BLOCK // 2),
            rows_spec(BLOCK // 4, width),
            pair_spec(BLOCK // 4),
            whole(edge.shape),
            whole(edge.shape),
        ],
        out_shape=[
            hbm_shape((rows, MP * width), BF16),
            hbm_shape((rows, LANES), F32),
            hbm_shape((rows, width), BF16),
            hbm_shape((2, rows, width), BF16),
            hbm_shape((rows // 2, width), BF16),
            hbm_shape((2, rows // 2, width), BF16),
            hbm_shape((rows // 4, width), BF16),
            hbm_shape((2, rows // 4, width), BF16),
            edge,
            edge,
        ],
        compiler_params=params(20),
        cost_estimate=SMALL,
        name="project",
    )(me, *in_hbm(shares[0]), *shares[1:], *in_hbm(wq, wk, wv))


def cotangent_kernel(me_ref, g0, g1, g2, g3, w_out, a0, a1, a2):
    me = me_ref[0]
    width = g0.shape[1]
    total = None
    for r, share in enumerate((g0, g1, g2, g3)):
        term = nt(share[...], w_out[:, share_rows(me, r, width)])
        total = term if total is None else total + term
    fine = total.astype(BF16)
    a0[...] = fine
    a1[...] = nn(pool_matrix(BLOCK // 2, 2, 1.0), fine).astype(BF16)
    a2[...] = nn(pool_matrix(BLOCK // 4, 4, 1.0), fine).astype(BF16)


def cotangent(me, shares, w_out):
    rows, width = shares[0].shape
    return pl.pallas_call(
        cotangent_kernel,
        grid=(rows // BLOCK,),
        in_specs=[SCALAR] + [rows_spec(BLOCK, width)] * 4 + [whole(w_out.shape)],
        out_specs=[rows_spec(BLOCK // n, width) for n in (1, 2, 4)],
        out_shape=[hbm_shape((rows // n, width), BF16) for n in (1, 2, 4)],
        compiler_params=params(12),
        cost_estimate=SMALL,
        name="cotangent",
    )(me, *in_hbm(shares[0]), *shares[1:], *in_hbm(w_out))


EDGE_UNITS = ((0, 0), (0, 3), (1, 0), (1, 1), (2, 0))
INNER_UNITS = ((0, 1), (0, 2))


def unit_keys(level, block):
    last = EXT_BLOCKS[level] - 1
    offsets = (0, 1, 2) if level == 0 else (0, 2)
    keys = []
    for offset in offsets:
        at = block + offset
        keys.append((at, 0 if at == 0 else 1 if at == last else None))
    return keys


def block_rows(block):
    return slice(block * BLOCK, (block + 1) * BLOCK)


def ext_rows(own, from_left, from_right, n, level, at):
    if at == 0:
        return from_left[n, block_rows(level), :]
    if at == EXT_BLOCKS[level] - 1:
        return from_right[n, block_rows(level), :]
    return own[level][n, block_rows(at - 1), :]


def head_part(lane, head, rows):
    mine = (lane >= head * HD) & (lane < (head + 1) * HD)
    return jnp.where(mine, rows, 0.0).astype(BF16)


def unit_scores(keys, key_rows, query, bias_ref):
    scores = []
    for (_, bias), rows in zip(keys, key_rows):
        s = nt(rows, query)
        scores.append(s if bias is None else s + bias_ref[bias])
    return scores


def add_spread(target, block, factor, rows):
    if factor == 1:
        target[block_rows(block), :] = target[block_rows(block), :] + rows
        return
    for s in range(factor):
        spread = pl.ds(block * factor * BLOCK + s, BLOCK, factor)
        target[spread, :] = target[spread, :] + rows


def forward_units(units, bias_ref, queries, own, from_left, from_right, stats, vt, out_f):
    lane = lax.broadcasted_iota(jnp.int32, (BLOCK, PAIR), 1)
    turned = set()
    for level, block in units:
        for at, _ in unit_keys(level, block):
            if (level, at) not in turned:
                turned.add((level, at))
                rows = ext_rows(own, from_left, from_right, 1, level, at)
                vt[FIRST_EXT[level] + at] = rows.T
    for u, (level, block) in enumerate(units):
        keys = unit_keys(level, block)
        key_rows = [ext_rows(own, from_left, from_right, 0, level, at) for at, _ in keys]
        q_rows = queries[level][block_rows(block), :] * HD ** (-0.5)
        outs = []
        for head in range(2):
            scores = unit_scores(keys, key_rows, head_part(lane, head, q_rows), bias_ref)
            top = scores[0].max(axis=0, keepdims=True)
            for s in scores[1:]:
                top = jnp.maximum(top, s.max(axis=0, keepdims=True))
            part = slice(head * HD, (head + 1) * HD)
            exps = [jnp.exp(s - top) for s in scores]
            total = exps[0].sum(axis=0, keepdims=True)
            for e in exps[1:]:
                total = total + e.sum(axis=0, keepdims=True)
            scale = 1.0 / total
            row = 4 * u + 2 * head
            stats[0, row : row + 1, :] = top
            stats[0, row + 1 : row + 2, :] = scale
            o_t = None
            for (at, _), e in zip(keys, exps):
                o = nn(vt[FIRST_EXT[level] + at, part, :], (e * scale).astype(BF16))
                o_t = o if o_t is None else o_t + o
            outs.append(o_t)
        add_spread(out_f, block, 2**level, jnp.concatenate(outs, axis=0).T)


def forward_inner_kernel(bias_ref, q0, kv0, out, stats, vt):
    out[...] = jnp.zeros_like(out)
    forward_units(INNER_UNITS, bias_ref, (q0,), (kv0,), None, None, stats, vt, out)


def forward_edge_kernel(
    bias_ref, q0, q1, q2, kv0, kv1, kv2, from_left, from_right, inner, attended, stats, vt, out_f
):
    out_f[...] = inner[...]
    forward_units(
        EDGE_UNITS, bias_ref, (q0, q1, q2), (kv0, kv1, kv2), from_left, from_right, stats, vt, out_f
    )
    stats[0, 20:24, :] = jnp.zeros((4, BLOCK), F32)
    attended[...] = out_f[...].astype(BF16)


def backward_units(
    units, bias_ref, queries, own, from_left, from_right, grads, stats, kt, dq_f, keep_key, keep_value
):
    lane = lax.broadcasted_iota(jnp.int32, (BLOCK, PAIR), 1)
    turned = set()
    for level, block in units:
        for at, _ in unit_keys(level, block):
            if (level, at) not in turned:
                turned.add((level, at))
                rows = ext_rows(own, from_left, from_right, 0, level, at)
                kt[FIRST_EXT[level] + at] = rows.T
    for u, (level, block) in enumerate(units):
        keys = unit_keys(level, block)
        key_rows = [ext_rows(own, from_left, from_right, 0, level, at) for at, _ in keys]
        value_rows = [ext_rows(own, from_left, from_right, 1, level, at) for at, _ in keys]
        q_rows = queries[level][block_rows(block), :] * HD ** (-0.5)
        a_rows = grads[level][block_rows(block), :]
        d_queries = []
        d_keys, d_values = [None] * len(keys), [None] * len(keys)
        for head in range(2):
            qm = head_part(lane, head, q_rows)
            am = head_part(lane, head, a_rows)
            row = 4 * u + 2 * head
            top, scale = stats[0, row : row + 1, :], stats[0, row + 1 : row + 2, :]
            scores = unit_scores(keys, key_rows, qm, bias_ref)
            probs = [jnp.exp(s - top) * scale for s in scores]
            d_weights = [nt(rows, am) for rows in value_rows]
            dots = None
            for p, dw in zip(probs, d_weights):
                d = (p * dw).sum(axis=0, keepdims=True)
                dots = d if dots is None else dots + d
            part = slice(head * HD, (head + 1) * HD)
            dq_t = None
            for n, (at, _) in enumerate(keys):
                gv = nn(probs[n].astype(BF16), am)
                d_scores = (probs[n] * (d_weights[n] - dots)).astype(BF16)
                gk = nn(d_scores, qm)
                g = nn(kt[FIRST_EXT[level] + at, part, :], d_scores)
                dq_t = g if dq_t is None else dq_t + g
                d_keys[n] = gk if head == 0 else d_keys[n] + gk
                d_values[n] = gv if head == 0 else d_values[n] + gv
            d_queries.append(dq_t)
        for n, (at, _) in enumerate(keys):
            keep_key(level, at, d_keys[n])
            keep_value(level, at, d_values[n])
        dq = jnp.concatenate(d_queries, axis=0).T * (HD ** (-0.5) / 2**level)
        add_spread(dq_f, block, 2**level, dq)


def edge_kernel(
    bias_ref, stats, q0, q1, q2, kv0, kv1, kv2, from_left, from_right, a0, a1, a2,
    dq_f, d_kv, to_left, to_right, kt, held, dq_s, sums,
):
    dq_s[...] = jnp.zeros_like(dq_s)
    seen = set()

    def keeper(n):
        def keep(level, at, rows):
            slot = FIRST_EXT[level] + at
            if (n, slot) in seen:
                held[n, slot] = held[n, slot] + rows
            else:
                seen.add((n, slot))
                held[n, slot] = rows

        return keep

    backward_units(
        EDGE_UNITS, bias_ref, (q0, q1, q2), (kv0, kv1, kv2), from_left, from_right,
        (a0, a1, a2), stats, kt, dq_s, keeper(0), keeper(1),
    )
    dq_f[...] = dq_s[...]
    for n in range(2):
        for level in range(LEVELS):
            first, last = FIRST_EXT[level], FIRST_EXT[level] + EXT_BLOCKS[level] - 1
            to_left[n, block_rows(level), :] = held[n, first].astype(BF16)
            to_right[n, block_rows(level), :] = held[n, last].astype(BF16)
        for b in range(4):
            sums[block_rows(b), :] = held[n, 1 + b]
        for b in range(2):
            add_spread(sums, b, 2, held[n, FIRST_EXT[1] + 1 + b] * 0.5)
        d_kv[n] = sums[...]


def inner_units_kernel(
    bias_ref, stats, q0, kv0, a0, dq_in, d_kv_in, d_query, d_kv, kt, dq_s
):
    dq_s[...] = dq_in[...]
    d_kv[...] = d_kv_in[...]

    def keeper(n):
        def keep(level, at, rows):
            d_kv[n, block_rows(at - 1), :] = d_kv[n, block_rows(at - 1), :] + rows

        return keep

    backward_units(
        INNER_UNITS, bias_ref, (q0,), (kv0,), None, None, (a0,), stats, kt, dq_s,
        keeper(0), keeper(1),
    )
    d_query[...] = dq_s[...].astype(BF16)


def lanes(n):
    return pl.BlockSpec((n, PAIR), lambda i: (0, i))


def lanes2(n):
    return pl.BlockSpec((2, n, PAIR), lambda i: (0, 0, i))


EDGE_STATS = pl.BlockSpec((1, 24, BLOCK), lambda i: (i, 0, 0))
INNER_STATS = pl.BlockSpec((1, 8, BLOCK), lambda i: (i, 0, 0))


def forward_inner(bias, q, kv):
    rows, width = q.shape
    out = jax.ShapeDtypeStruct
    return pl.pallas_call(
        forward_inner_kernel,
        grid=(width // PAIR,),
        in_specs=[SCALAR, lanes(rows), lanes2(rows)],
        out_specs=[lanes(rows), INNER_STATS],
        out_shape=[hbm_shape((rows, width), F32), hbm_shape((width // PAIR, 8, BLOCK), F32)],
        scratch_shapes=[pltpu.VMEM((EXT_BLOCKS[0], PAIR, BLOCK), BF16)],
        compiler_params=params(20),
        cost_estimate=SMALL,
        name="forward_inner",
    )(bias, *in_hbm(q, kv))


def forward_edge(bias, q, kv, from_left, from_right, inner):
    rows, width = q[0].shape
    out = jax.ShapeDtypeStruct
    return pl.pallas_call(
        forward_edge_kernel,
        grid=(width // PAIR,),
        in_specs=[SCALAR]
        + [lanes(rows // n) for n in (1, 2, 4)]
        + [lanes2(rows // n) for n in (1, 2, 4)]
        + [lanes2(3 * BLOCK)] * 2
        + [lanes(rows)],
        out_specs=[lanes(rows), EDGE_STATS],
        out_shape=[hbm_shape((rows, width), BF16), hbm_shape((width // PAIR, 24, BLOCK), F32)],
        scratch_shapes=[
            pltpu.VMEM((EXT_TOTAL, PAIR, BLOCK), BF16),
            pltpu.VMEM((rows, PAIR), F32),
        ],
        compiler_params=params(24),
        cost_estimate=SMALL,
        name="forward_edge",
    )(bias, *in_hbm(*q, *kv), from_left, from_right, inner)


def edge_backward(bias, stats, q, kv, from_left, from_right, d_level):
    rows, width = q[0].shape
    out = jax.ShapeDtypeStruct
    edge = out((2, 3 * BLOCK, width), BF16)
    return pl.pallas_call(
        edge_kernel,
        grid=(width // PAIR,),
        in_specs=[SCALAR, EDGE_STATS]
        + [lanes(rows // n) for n in (1, 2, 4)]
        + [lanes2(rows // n) for n in (1, 2, 4)]
        + [lanes2(3 * BLOCK)] * 2
        + [lanes(rows // n) for n in (1, 2, 4)],
        out_specs=[lanes(rows), lanes2(rows), lanes2(3 * BLOCK), lanes2(3 * BLOCK)],
        out_shape=[hbm_shape((rows, width), F32), hbm_shape((2, rows, width), F32), edge, edge],
        scratch_shapes=[
            pltpu.VMEM((EXT_TOTAL, PAIR, BLOCK), BF16),
            pltpu.VMEM((2, EXT_TOTAL, BLOCK, PAIR), F32),
            pltpu.VMEM((rows, PAIR), F32),
            pltpu.VMEM((rows, PAIR), F32),
        ],
        compiler_params=params(32),
        cost_estimate=SMALL,
        name="edge_backward",
    )(bias, *in_hbm(stats, *q, *kv), from_left, from_right, *d_level)


def inner_backward(bias, stats, q, kv, d_level, dq_f, d_kv):
    rows, width = q.shape
    out = jax.ShapeDtypeStruct
    return pl.pallas_call(
        inner_units_kernel,
        grid=(width // PAIR,),
        in_specs=[SCALAR, INNER_STATS, lanes(rows), lanes2(rows), lanes(rows), lanes(rows), lanes2(rows)],
        out_specs=[lanes(rows), lanes2(rows)],
        out_shape=[hbm_shape((rows, width), BF16), hbm_shape((2, rows, width), F32)],
        scratch_shapes=[
            pltpu.VMEM((EXT_BLOCKS[0], PAIR, BLOCK), BF16),
            pltpu.VMEM((rows, PAIR), F32),
        ],
        compiler_params=params(24),
        cost_estimate=SMALL,
        name="inner_backward",
    )(bias, *in_hbm(stats, q, kv), d_level, dq_f, d_kv)


def store_terms(step, terms, own, keep_right, keep_left, right, left):
    own[...] = terms[0]
    low = pl.ds(pl.multiple_of((step & 1) * BLOCK, BLOCK), BLOCK)
    high = pl.ds(pl.multiple_of(2 * BLOCK + (step & 1) * BLOCK, BLOCK), BLOCK)

    @pl.when(step < 2)
    def _():
        keep_right[low, :] = terms[1]
        right[high, :] = terms[2]
        left[low, :] = terms[3]

    @pl.when(step >= 2)
    def _():
        right[low, :] = terms[1]
        left[high, :] = terms[2]
        keep_left[low, :] = terms[3]


def term_outputs(rows, width, extra=0):
    out = jax.ShapeDtypeStruct
    shapes = [rows, rows // 2, rows // 2, rows + extra, rows + extra]
    return (
        [rows_spec(BLOCK, width)] + [whole((n, width)) for n in shapes[1:]],
        [hbm_shape((rows, width), BF16)] + [out((n, width), BF16) for n in shapes[1:]],
    )


def send_out_kernel(me_ref, attended, w_out, *outs):
    me = me_ref[0]
    width = attended.shape[1]
    rows = attended[...]
    terms = [nn(rows, w_out[:, share_rows(me, r, width)]).astype(BF16) for r in range(MP)]
    store_terms(pl.program_id(0), terms, *outs)


def out_terms(me, attended, w_out):
    rows, width = attended.shape
    specs, shapes = term_outputs(rows, width)
    return pl.pallas_call(
        send_out_kernel,
        grid=(rows // BLOCK,),
        in_specs=[SCALAR, rows_spec(BLOCK, width), whole(w_out.shape)],
        out_specs=specs,
        out_shape=shapes,
        compiler_params=params(12),
        cost_estimate=SMALL,
        name="out_terms",
    )(me, *in_hbm(attended, w_out))


def input_terms_kernel(
    me_ref, d_query, d_kv, from_left, from_right, t0, t1a, t1b, t2a, t2b, t3a, t3b, inverse,
    wq, wk, wv, d_proj, dots, own, keep_right, keep_left, right, left, dot_rows,
):
    step = pl.program_id(0)
    me = me_ref[0]
    width = d_query.shape[1]
    grads = [d_query[...]]
    half = spread_matrix(BLOCK // 2, 2, 0.5)
    quarter = spread_matrix(BLOCK // 4, 4, 0.25)
    half_rows = pl.ds(pl.multiple_of(256 + (step & 1) * 128, 128), 128)
    low_rows = pl.ds(pl.multiple_of(512 + step * 64, 64), 64)
    for n in range(2):
        total = d_kv[n]
        total = total + jnp.where(step == 0, from_left[n, 0:BLOCK, :].astype(F32), 0.0)
        total = total + jnp.where(step == 3, from_right[n, 0:BLOCK, :].astype(F32), 0.0)
        mid = jnp.where(step < 2, from_left[n, half_rows, :], from_right[n, half_rows, :])
        total = total + nn(half, mid)
        total = total + nn(quarter, from_left[n, low_rows, :])
        total = total + nn(quarter, from_right[n, low_rows, :])
        grads.append(total.astype(BF16))
    for n, grad in enumerate(grads):
        d_proj[:, n * width : (n + 1) * width] = grad
    shares = read_shares(step, (t0, t1a, t1b, t2a, t2b, t3a, t3b))
    terms, dot = [], None
    for r in range(MP):
        rows = share_rows(me, r, width)
        term = nt(grads[0], wq[rows, :]) + nt(grads[1], wk[rows, :]) + nt(grads[2], wv[rows, :])
        term = term.astype(BF16)
        terms.append(term)
        part = jnp.sum(term.astype(F32) * shares[r].astype(F32), axis=1, keepdims=True)
        dot = part if dot is None else dot + part
    dot = jnp.broadcast_to(dot * inverse[:, 0:1], (BLOCK, LANES)).T[0:1, :]
    high = dot.astype(BF16).astype(F32)
    middle = (dot - high).astype(BF16).astype(F32)
    for n, piece in enumerate((high, middle, dot - high - middle)):
        dot_rows[pl.ds(4 * n + step, 1), :] = piece
    store_terms(step, terms, own, keep_right, keep_left, right, left)

    @pl.when(step == 3)
    def _():
        dot_rows[12:16, :] = jnp.zeros((4, BLOCK), F32)
        pieces = dot_rows[...].astype(BF16)
        dots[...] = pieces
        right[4 * BLOCK :, :] = pieces
        left[4 * BLOCK :, :] = pieces


def input_terms(me, d_query, d_kv, from_left, from_right, shares, inverse, wq, wk, wv):
    rows, width = d_query.shape
    specs, shapes = term_outputs(rows, width, DOT_ROWS)
    out = jax.ShapeDtypeStruct
    return pl.pallas_call(
        input_terms_kernel,
        grid=(rows // BLOCK,),
        in_specs=[
            SCALAR,
            rows_spec(BLOCK, width),
            pl.BlockSpec((2, BLOCK, width), lambda i: (0, i, 0)),
            whole(from_left.shape),
            whole(from_right.shape),
        ]
        + share_specs(width)
        + [rows_spec(BLOCK, LANES)]
        + [whole(wq.shape)] * 3,
        out_specs=[rows_spec(BLOCK, 3 * width), whole((DOT_ROWS, width))] + specs,
        out_shape=[hbm_shape((rows, 3 * width), BF16), hbm_shape((DOT_ROWS, width), BF16)] + shapes,
        scratch_shapes=[pltpu.VMEM((DOT_ROWS, width), F32)],
        compiler_params=params(24),
        cost_estimate=SMALL,
        name="input_terms",
    )(
        me, d_query, d_kv, from_left, from_right, *in_hbm(shares[0]), *shares[1:],
        *in_hbm(inverse, wq, wk, wv)
    )


def relay_kernel(keep_right, keep_left, l1, r1, onward_right, onward_left):
    half = keep_right.shape[0]
    passed = l1[half : 2 * half, :].astype(F32)
    onward_right[0:half, :] = (keep_right[...].astype(F32) + passed).astype(BF16)
    passed = r1[half : 2 * half, :].astype(F32)
    onward_left[...] = (keep_left[...].astype(F32) + passed).astype(BF16)
    if onward_right.shape[0] > half:
        onward_right[half:, :] = l1[2 * half :, :]


def relay(keep_right, keep_left, l1, r1):
    half, width = keep_right.shape
    extra = l1.shape[0] - 2 * half
    out = jax.ShapeDtypeStruct
    return pl.pallas_call(
        relay_kernel,
        out_shape=[out((half + extra, width), BF16), out((half, width), BF16)],
        compiler_params=params(8),
        cost_estimate=SMALL,
        name="relay",
    )(keep_right, keep_left, l1, r1)


def summed(own, l1, r1, l2, r2):
    half = r2.shape[0]
    low = r1[0:half, :].astype(F32) + l2[0:half, :].astype(F32)
    high = l1[0:half, :].astype(F32) + r2[...].astype(F32)
    return own[0:half, :].astype(F32) + low, own[half:, :].astype(F32) + high


def finish_out_kernel(own, l1, r1, l2, r2, result):
    half = r2.shape[0]
    low, high = summed(own, l1, r1, l2, r2)
    result[0:half, :] = low.astype(BF16)
    result[half:, :] = high.astype(BF16)


def finish_out(own, l1, r1, l2, r2):
    rows, width = own.shape
    return pl.pallas_call(
        finish_out_kernel,
        out_shape=jax.ShapeDtypeStruct((rows, width), BF16),
        compiler_params=params(10),
        cost_estimate=SMALL,
        name="finish_out",
    )(*in_hbm(own, l1, r1, l2, r2))


def finish_grad_kernel(own, l1, r1, l2, r2, tokens, inverse, dots, result):
    rows, width = own.shape
    half = r2.shape[0]
    pieces = dots[...].astype(F32)
    for message, first in ((l1, rows), (r1, rows), (l2, half)):
        pieces = pieces + message[first : first + DOT_ROWS, :].astype(F32)
    means = (pieces[0:4] + pieces[4:8] + pieces[8:12]) / (MP * width)
    halves = summed(own, l1, r1, l2, r2)
    for b in range(rows // BLOCK):
        mean = jnp.broadcast_to(means[b : b + 1, :], (LANES, BLOCK)).T[:, 0:1]
        at = block_rows(b)
        inv = inverse[at, 0:1]
        total = halves[b // 2][block_rows(b % 2), :]
        result[at, :] = inv * (total - tokens[at, :].astype(F32) * inv * mean)


def finish_grad(own, l1, r1, l2, r2, tokens, inverse, dots):
    rows, width = own.shape
    return pl.pallas_call(
        finish_grad_kernel,
        out_shape=jax.ShapeDtypeStruct((rows, width), F32),
        compiler_params=params(16),
        cost_estimate=SMALL,
        name="finish_grad",
    )(*in_hbm(own), l1, r1, l2, r2, *in_hbm(tokens, inverse, dots))


def outer_kernel(g0, g1, g2, g3, attended, result):
    width = g0.shape[1]
    rows = attended[...]
    for r, share in enumerate((g0, g1, g2, g3)):
        result[r * width : (r + 1) * width, :] = tn(share[...], rows).astype(BF16)


def outer_terms(shares, attended):
    rows, width = attended.shape
    return pl.pallas_call(
        outer_kernel,
        out_shape=hbm_shape((MP * width, width), BF16),
        compiler_params=params(12),
        cost_estimate=SMALL,
        name="outer_terms",
    )(*in_hbm(shares[0]), *shares[1:], attended)


def inner_kernel(place, normed, d_proj, outer, mine, other, held):
    core = place[1]
    width = outer.shape[1]
    held[:, 0 : 3 * width] = tn(normed[...], d_proj[...]).astype(BF16)
    held[:, 3 * width :] = outer[...]
    for n in range(width // 64):
        rows = slice(n * 32, (n + 1) * 32)
        mine[rows, :] = held[pl.ds(pl.multiple_of(n * 64 + core * 32, 32), 32), :]
        other[rows, :] = held[pl.ds(pl.multiple_of(n * 64 + 32 - core * 32, 32), 32), :]


def inner_terms(place, normed, d_proj, outer):
    rows, total = normed.shape
    width = outer.shape[1]
    half = jax.ShapeDtypeStruct((total // 2, 4 * width), BF16)
    return pl.pallas_call(
        inner_kernel,
        grid=(total // width,),
        in_specs=[
            SCALAR,
            pl.BlockSpec((rows, width), lambda i: (0, i)),
            whole(d_proj.shape),
            rows_spec(width, width),
        ],
        out_specs=[rows_spec(width // 2, 4 * width)] * 2,
        out_shape=[half, half],
        scratch_shapes=[pltpu.VMEM((width, 4 * width), BF16)],
        compiler_params=params(16),
        cost_estimate=SMALL,
        name="inner_terms",
    )(place, *in_hbm(normed), d_proj, *in_hbm(outer))


def pair_sum_kernel(place, mine, got, *outs):
    x = place[2]
    for d, out in enumerate(outs):
        for y in range(4):
            rows = pl.ds(pl.multiple_of((4 * y + ((x + d) & 3)) * 32, 32), 32)
            total = mine[rows, :].astype(F32) + got[rows, :].astype(F32)
            out[32 * y : 32 * (y + 1), :] = total.astype(BF16)


def row_sum_kernel(place, a, b, c, d, *refs):
    *outs, total = refs
    first = place[3] - place[0] + 4
    total[...] = (
        a[...].astype(F32) + b[...].astype(F32) + c[...].astype(F32) + d[...].astype(F32)
    ).astype(BF16)
    for n, out in enumerate(outs):
        out[...] = total[pl.ds(pl.multiple_of(((first + n) & 3) * 32, 32), 32), :]


def last_sum_kernel(a, b, c, d, gq, gk, gv, go):
    width = gq.shape[1]
    total = a[...].astype(F32) + b[...].astype(F32) + c[...].astype(F32) + d[...].astype(F32)
    gq[...] = total[:, 0:width]
    gk[...] = total[:, width : 2 * width]
    gv[...] = total[:, 2 * width : 3 * width]
    go[...] = total[:, 3 * width :]


def sum_over_seq(place, mine, other):
    cols = mine.shape[1]
    out = jax.ShapeDtypeStruct
    vmem = pl.BlockSpec(memory_space=pltpu.VMEM)

    def sent(value, dy, dx, dc):
        pairs = []
        for i in range(32):
            c, a, b = i % 2, (i // 2) % 4, i // 8
            pairs.append((i, (((b + dy) % 4) * 4 + (a + dx) % 4) * 2 + (c + dc) % 2))
        return lax.ppermute(value, "seq", pairs)

    parts = pl.pallas_call(
        pair_sum_kernel,
        in_specs=[SCALAR, vmem, vmem],
        out_shape=[out((128, cols), BF16)] * 4,
        compiler_params=params(8),
        cost_estimate=SMALL,
        name="pair_sum",
    )(place, mine, sent(other, 0, 0, 1))
    parts = [parts[0]] + [sent(parts[d], 0, d, 0) for d in (1, 3, 2)]
    rows = pl.pallas_call(
        row_sum_kernel,
        in_specs=[SCALAR] + [vmem] * 4,
        out_shape=[out((32, cols), BF16)] * 4,
        scratch_shapes=[pltpu.VMEM((128, cols), BF16)],
        compiler_params=params(8),
        cost_estimate=SMALL,
        name="row_sum",
    )(place, *parts)
    rows = [rows[0]] + [sent(rows[d], d, 0, 0) for d in (1, 3, 2)]
    width = cols // 4
    return pl.pallas_call(
        last_sum_kernel,
        out_shape=[out((32, width), F32)] * 4,
        compiler_params=params(8),
        cost_estimate=SMALL,
        name="last_sum",
    )(*rows)


def to_next(value):
    return lax.ppermute(value, "mp", [(i, (i + 1) % MP) for i in range(MP)])


def to_previous(value):
    return lax.ppermute(value, "mp", [((i + 1) % MP, i) for i in range(MP)])


def gather_shares(share):
    half = share.shape[0] // 2
    low, high = share[:half], share[half:]
    after_low, before_high = to_previous(low), to_next(high)
    after_high, before_low = to_previous(high), to_next(low)
    far_low, far_high = to_previous(after_low), to_next(before_high)
    return [share, after_low, after_high, far_low, far_high, before_low, before_high]


def gather_direct(share):
    far = lax.ppermute(share, "mp", [(i, (i + 2) % MP) for i in range(MP)])
    return [share, to_previous(share), far, to_next(share)]


def exchange(to_left, to_right):
    count = lax.axis_size("seq")
    ends = count - 1
    from_left = lax.ppermute(to_right, "seq", [(i, i + 1) for i in range(ends)])
    from_right = lax.ppermute(to_left, "seq", [(i + 1, i) for i in range(ends)])
    return from_left, from_right


def tied(values, *others):
    flat, tree = jax.tree.flatten(values)
    flat = lax.optimization_barrier((*flat, *others))[: len(flat)]
    return jax.tree.unflatten(tree, flat)


def per_device(tokens, w_query, w_key, w_value, w_out, grad_out):
    count = lax.axis_size("seq")
    index = lax.axis_index("seq")
    me = jnp.stack([lax.axis_index("mp"), index & 1, (index >> 1) & 3, index >> 3])
    me = me.astype(jnp.int32)
    bias = jnp.stack(
        [
            jnp.where(index == 0, NEGATIVE, 0.0).astype(F32),
            jnp.where(index == count - 1, NEGATIVE, 0.0).astype(F32),
        ]
    )
    token_shares = gather_shares(tokens)
    *token_shares, grad_out = lax.optimization_barrier((*token_shares, grad_out))
    grad_shares = gather_direct(grad_out)
    normed, inverse, q0, kv0, q1, kv1, q2, kv2, to_left, to_right = project(
        me, token_shares, w_query, w_key, w_value
    )
    from_left, from_right = exchange(to_left, to_right)
    q, kv = (q0, q1, q2), (kv0, kv1, kv2)
    inner_out, inner_stats = forward_inner(bias, q0, kv0)
    attended, stats = forward_edge(bias, q, kv, from_left, from_right, inner_out)
    grad_shares = tied(grad_shares, attended)
    out_own, keep_right, keep_left, right, left = out_terms(me, attended, w_out)
    l1, r1 = to_next(right), to_previous(left)
    d_level = cotangent(me, grad_shares, w_out)
    dq_f, d_kv, to_left, to_right = edge_backward(
        bias, stats, q, kv, from_left, from_right, d_level
    )
    onward_right, onward_left = relay(keep_right, keep_left, l1, r1)
    l2, r2 = to_next(onward_right), to_previous(onward_left)
    from_left, from_right = exchange(to_left, to_right)
    dq_f = tied(dq_f, onward_right, onward_left)
    d_query, d_kv = inner_backward(bias, inner_stats, q0, kv0, d_level[0], dq_f, d_kv)
    d_query = tied(d_query, l2, r2)
    d_proj, dots, own, keep_right, keep_left, right, left = input_terms(
        me, d_query, d_kv, from_left, from_right, token_shares, inverse, w_query, w_key, w_value
    )
    attn_out = finish_out(out_own, l1, r1, l2, r2)
    l1, r1 = to_next(right), to_previous(left)
    outer = outer_terms(grad_shares, attended)
    mine, other = inner_terms(me, normed, d_proj, outer)
    onward_right, onward_left = relay(keep_right, keep_left, l1, r1)
    l2, r2 = to_next(onward_right), to_previous(onward_left)
    grad_tokens = finish_grad(own, l1, r1, l2, r2, tokens, inverse, dots)
    *weight_grads, grad_w_out = sum_over_seq(me, mine, other)
    return (attn_out, grad_tokens, *weight_grads, grad_w_out.T)


def solution(mesh):
    return jax.shard_map(
        per_device,
        mesh=mesh,
        in_specs=(
            P("seq", "mp"),
            P(None, "mp"),
            P(None, "mp"),
            P(None, "mp"),
            P("mp", None),
            P("seq", "mp"),
        ),
        out_specs=(
            P("seq", "mp"),
            P("seq", "mp"),
            P("seq", "mp"),
            P("seq", "mp"),
            P("seq", "mp"),
            P("mp", "seq"),
        ),
        check_vma=False,
    )
```

time: 681 us -> 163 us (0.24); the launches traced: 670 us -> 162 us
  matrix products: 192 us -> 0 us
  local copies, waits for them, and re-layouts: 173 us -> 9.38 us
  waiting for transfers between devices: 186 us -> 22.9 us
  Pallas kernels: 0 us -> 77.9 us
  other arithmetic: 61.3 us -> 0.15 us
  between operations: 15 us -> 1.02 us
  starting transfers between devices: 42.3 us -> 51.1 us
    dot_general x22 -> x0, matrix products: 185 us -> none  [the longest x16 173 us: product(): jnp.einsum(form, left_side, right_side, preferred_element_type=jnp.float32)]
    unnamed x6 -> x0, waiting for transfers between devices: 79.2 us -> none
    pallas_call x0 -> x17, Pallas kernels: none -> 77.9 us  [the longest x1 14.2 us: edge_backward(): pl.pallas_call(edge_kernel, grid=(width // PAIR,), in_specs=[SCALAR, EDGE...]
    slice x20 -> x1, local copies, waits for them, and re-layouts: 55.1 us -> 1.07 us  [gather_shares(): low, high = (share[:half], share[half:])]
    all_gather x2 -> x0, waiting for transfers between devices: 43.7 us -> none  [the longest x1 36.2 us: per_device(): lax.all_gather(tokens, 'mp', axis=1, tiled=True)]
    psum x1 -> x0, waiting for transfers between devices: 34.4 us -> none  [per_device(): lax.psum(d_normed_part.astype(jnp.bfloat16), 'mp').astype(jnp.float32)]
    reshape x18 -> x0, local copies, waits for them, and re-layouts: 33 us -> none  [the longest x3 16.1 us: level_backward(): jnp.stack([d_key_rows, d_value_rows], axis=2)]
    reduce_scatter x1 -> x0, waiting for transfers between devices: 28.4 us -> none  [per_device(): lax.psum_scatter(partial_out.astype(jnp.bfloat16), 'mp', scatter_dimensio...]
  transfers between devices with their start and end apart: 17 -> 28, of which waited for: 5 -> 7; matrix products, arithmetic and copies ran while one was open for 56% -> 0% of each run, Pallas kernels for 0% -> 33%
where the time goes in v1:
time: 163 us; the launch traced here: 162 us
  Pallas kernels  77.9 us (48%)
  starting transfers between devices  51.1 us (31%)
  waiting for transfers between devices  22.9 us (14%)
  local copies, waits for them, and re-layouts  9.38 us (6%)
    ppermute x8, starting transfers between devices, to_previous(): return lax.ppermute(value, 'mp', [((i + 1) % MP, i) for i in range(MP)])  18.6 us
    ppermute x7, starting transfers between devices, sent(): return lax.ppermute(value, 'seq', pairs)  16.4 us
    ppermute x8, waiting for transfers between devices, to_next(): return lax.ppermute(value, 'mp', [(i, (i + 1) % MP) for i in range(MP)])  15.5 us
    pallas_call x1, Pallas kernels, edge_backward(): pl.pallas_call(edge_kernel, grid=(width // PAIR,), in_specs=[SCALAR, EDGE...  14.2 us
    pallas_call x1, Pallas kernels, forward_edge(): pl.pallas_call(forward_edge_kernel, grid=(width // PAIR,), in_specs=[SCAL...  11 us
    unnamed x48, local copies, waits for them, and re-layouts  8.31 us
    pallas_call x1, Pallas kernels, inner_backward(): pl.pallas_call(inner_units_kernel, grid=(width // PAIR,), in_specs=[SCALA...  8.05 us
    pallas_call x1, Pallas kernels, project(): pl.pallas_call(project_kernel, grid=(rows // BLOCK,), in_specs=[SCALAR] +...  7.95 us
  transfers between devices with their start and end apart: 28, of which 7 were waited for; matrix products, arithmetic and copies ran while one was open for 0% of the time, Pallas kernels for 33%

profile of v1, /device:TPU:0, one launch (start us, length us, event | category | flops | bytes accessed | tf_op | source)
XLA Modules:
  0.0 162.4 jit_solution(2744911332526881918)
XLA Ops:
  8.0 5.0 %collective-permute-done.3.t3b = bf16[512,256]{1,0:T(8,128)(2,1)S(1)} collective-permute-done((bf16[512,256]{1,0:T(8,128)(2,1)S(1)}, bf16[512,256]{1,0:T(8,128)(2,1)S(1)}, u32[]{:S(2)}, u32[]{:S(2)}) %collective-permute-start.3) | collective-permute-done | bytes 262176 | tf_op jit(solution)/shard_map/ppermute | solution.py:852
  13.0 3.3 %collective-permute-start.2 = (bf16[512,256]{1,0:T(8,128)(2,1)S(1)}, bf16[512,256]{1,0:T(8,128)(2,1)S(1)}, u32[]{:S(2)}, u32[]{:S(2)}) collective-permute-start(bf16[512,256]{1,0:T(8,128)(2,1)S(1)} %collective-permute-done.t1a), channel_id=1, source_target_pairs={{1,0},{2,1},{3,2},{0,3},{5,4},{6,5},{7,6},{4,7},{9,8},{10,9},{11,1... | collective-permute-start | bytes 786440 | tf_op jit(solution)/shard_map/ppermute | solution.py:856
  18.6 4.8 %collective-permute-done.4.t2b = bf16[512,256]{1,0:T(8,128)(2,1)S(1)} collective-permute-done((bf16[512,256]{1,0:T(8,128)(2,1)S(1)}, bf16[512,256]{1,0:T(8,128)(2,1)S(1)}, u32[]{:S(2)}, u32[]{:S(2)}) %collective-permute-start.4) | collective-permute-done | bytes 262176 | tf_op jit(solution)/shard_map/ppermute | solution.py:852
  23.4 7.9 %project.1 = (bf16[1024,1024]{1,0:T(8,128)(2,1)}, f32[1024,128]{1,0:T(8,128)}, bf16[1024,256]{1,0:T(8,128)(2,1)}, bf16[2,1024,256]{2,1,0:T(8,128)(2,1)}, bf16[51...) custom-call(s32[4]{0:T(128)S(1)} %pad_add_fusion.me_ref.place, ...), custom_call_target="tpu_custom_call" | custom-call | flops 1000000 | bytes 10000 | tf_op jit(solution)/shard_map/project/pallas_call | solution.py:169
  35.3 3.2 %collective-permute-start.13 = (bf16[1024,256]{1,0:T(8,128)(2,1)}, bf16[1024,256]{1,0:T(8,128)(2,1)S(1)}, u32[]{:S(2)}, u32[]{:S(2)}) collective-permute-start(bf16[1024,256]{1,0:T(8,128)(2,1)} %g0.1), channel_id=1, source_target_pairs={{0,2},{1,3},{2,0},{3,1},{4,6},{5,7},{6,4},{7,5},{8,10},{9,11},{10,... | collective-permute-start | bytes 1572872 | tf_op jit(solution)/shard_map/ppermute | solution.py:869
  39.7 6.3 %forward_inner.1 = (f32[1024,256]{1,0:T(8,128)}, f32[2,8,256]{2,1,0:T(8,128)}) custom-call(f32[2]{0:T(128)S(1)} %pad_maximum_fusion.bias_ref, bf16[1024,256]{1,0:T(8,128)(2,1)} %get-tuple-element.80.q0, bf16[2,1024,256]{2,1,0:T(8,128)(2,1)} %get-tuple-element.83.kv0), custom_call_target="tpu_custom_call" | custom-call | flops 1000000 | bytes 10000 | tf_op jit(solution)/shard_map/forward_inner/pallas_call | solution.py:448
  47.3 11.0 %forward_edge.1 = (bf16[1024,256]{1,0:T(8,128)(2,1)}, f32[2,24,256]{2,1,0:T(8,128)}) custom-call(f32[2]{0:T(128)S(1)} %pad_maximum_fusion.bias_ref, bf16[1024,256]{1,0:T(8,128)(2,1)} %get-tuple-element.80.q0, bf16[512,256]{1,0:T(8,128)(2,1)} %get-tuple-element.81.q1, bf16[256,256]{1,0:T(8,128)(2,1)} %get-tuple-element.82.q2, ...), custom_call_target="tpu_custom_call" | custom-call | flops 1000000 | bytes 10000 | tf_op jit(solution)/shard_map/forward_edge/pallas_call | solution.py:464
  58.3 2.6 %collective-permute-done.13.g2 = bf16[1024,256]{1,0:T(8,128)(2,1)S(1)} collective-permute-done((bf16[1024,256]{1,0:T(8,128)(2,1)}, bf16[1024,256]{1,0:T(8,128)(2,1)S(1)}, u32[]{:S(2)}, u32[]{:S(2)}) %collective-permute-start.13) | collective-permute-done | bytes 524320 | tf_op jit(solution)/shard_map/ppermute | solution.py:869
  61.5 4.1 %out_terms.1 = (bf16[1024,256]{1,0:T(8,128)(2,1)}, bf16[512,256]{1,0:T(8,128)(2,1)S(1)}, bf16[512,256]{1,0:T(8,128)(2,1)S(1)}, bf16[1024,256]{1,0:T(8,128)(2,1)S(1)}, bf16[1024,256]{1,0:T(8,128)(2,1)S(1)}) custom-call(s32[4]{0:T(128)S(1)} %pad_add_fusion.me_ref.place, bf16[1024,256]{1,0:T(8,128)(2,1)} %get-tuple-element.89.attended, bf16[256,1024]{1,0:T(8,128)(2,1)} %w_out.3), custom_call_target="tpu_custom_call" | custom-call | flops 1000000 | bytes 10000 | tf_op jit(solution)/shard_map/out_terms/pallas_call | solution.py:567
  65.5 2.7 %collective-permute-start.8 = (bf16[1024,256]{1,0:T(8,128)(2,1)S(1)}, bf16[1024,256]{1,0:T(8,128)(2,1)S(1)}, u32[]{:S(2)}, u32[]{:S(2)}) collective-permute-start(bf16[1024,256]{1,0:T(8,128)(2,1)S(1)} %get-tuple-element.91), channel_id=1, source_target_pairs={{0,1},{1,2},{2,3},{3,0},{4,5},{5,6},{6,7},{7,4},{8,9},{9,10},{10,1... | collective-permute-start | bytes 1572872 | tf_op jit(solution)/shard_map/ppermute | solution.py:852
  69.1 4.4 %cotangent.1 = (bf16[1024,256]{1,0:T(8,128)(2,1)}, bf16[512,256]{1,0:T(8,128)(2,1)}, bf16[256,256]{1,0:T(8,128)(2,1)}) custom-call(s32[4]{0:T(128)S(1)} %pad_add_fusion.me_ref.place, bf16[1024,256]{1,0:T(8,128)(2,1)} %g0.1, bf16[1024,256]{1,0:T(8,128)(2,1)S(1)} %collective-permute-done.12.g1, bf16[1024,256]{1,0:T(8,128)(2,1)S(1)} %collective-permute-done.13.g2, ...), custom_call_target="tpu_custom_call" | custom-call | flops 1000000 | bytes 10000 | tf_op jit(solution)/shard_map/cotangent/pallas_call | solution.py:218
  76.4 14.2 %edge_backward.1 = (f32[1024,256]{1,0:T(8,128)}, f32[2,1024,256]{2,1,0:T(8,128)}, bf16[2,768,256]{2,1,0:T(8,128)(2,1)S(1)}, bf16[2,768,256]{2,1,0:T(8,128)(2,1)S(1)}) custom-call(f32[2]{0:T(128)S(1)} %pad_maximum_fusion.bias_ref, f32[2,24,256]{2,1,0:T(8,128)} %get-tuple-element.104.stats, bf16[1024,256]{1,0:T(8,128)(2,1)} %get-tuple-element.80.q0, ...), custom_call_target="tpu_custom_call" | custom-call | flops 1000000 | bytes 10000 | tf_op jit(solution)/shard_map/edge_backward/pallas_call | solution.py:488
  94.9 2.7 %collective-permute-start.11 = (bf16[512,256]{1,0:T(8,128)(2,1)S(1)}, bf16[512,256]{1,0:T(8,128)(2,1)S(1)}, u32[]{:S(2)}, u32[]{:S(2)}) collective-permute-start(bf16[512,256]{1,0:T(8,128)(2,1)S(1)} %get-tuple-element.96), channel_id=1, source_target_pairs={{1,0},{2,1},{3,2},{0,3},{5,4},{6,5},{7,6},{4,7},{9,8},{10,9},{11,1... | collective-permute-start | bytes 786440 | tf_op jit(solution)/shard_map/ppermute | solution.py:856
  97.7 2.6 %outer_terms.1.outer = bf16[1024,256]{1,0:T(8,128)(2,1)} custom-call(bf16[1024,256]{1,0:T(8,128)(2,1)} %g0.1, bf16[1024,256]{1,0:T(8,128)(2,1)S(1)} %collective-permute-done.12.g1, bf16[1024,256]{1,0:T(8,128)(2,1)S(1)} %collective-permute-done.13.g2, bf16[1024,256]{1,0:T(8,128)(2,1)S(1)} %collective-permute-done.14.g3, bf16[1024,256]{1,0:T(8,128)(2,1)S(1)} %copy-done.4), custom_call_target="tpu_custom_call" | custom-call | flops 1000000 | bytes 10000 | tf_op jit(solution)/shard_map/outer_terms/pallas_call | solution.py:740
  100.4 8.1 %inner_backward.1 = (bf16[1024,256]{1,0:T(8,128)(2,1)}, f32[2,1024,256]{2,1,0:T(8,128)}) custom-call(f32[2]{0:T(128)S(1)} %pad_maximum_fusion.bias_ref, f32[2,8,256]{2,1,0:T(8,128)} %get-tuple-element.97.stats, bf16[1024,256]{1,0:T(8,128)(2,1)} %get-tuple-element.80.q0, bf16[2,1024,256]{2,1,0:T(8,128)(2,1)} %get-tuple-element.83.kv0, ...), custom_call_target="tpu_custom_call" | custom-call | flops 1000000 | bytes 10000 | tf_op jit(solution)/shard_map/inner_backward/pallas_call | solution.py:513
  111.2 7.1 %input_terms.1 = (bf16[1024,768]{1,0:T(8,128)(2,1)}, bf16[16,256]{1,0:T(8,128)(2,1)}, bf16[1024,256]{1,0:T(8,128)(2,1)}, bf16[512,256]{1,0:T(8,128)(2,1)S(1)}, b...) custom-call(s32[4]{0:T(128)S(1)} %pad_add_fusion.me_ref.place, ...), custom_call_target="tpu_custom_call" | custom-call | flops 1000000 | bytes 10000 | tf_op jit(solution)/shard_map/input_terms/pallas_call | solution.py:631
  119.7 4.2 %inner_terms.1 = (bf16[512,1024]{1,0:T(8,128)(2,1)S(1)}, bf16[512,1024]{1,0:T(8,128)(2,1)S(1)}) custom-call(s32[4]{0:T(128)S(1)} %pad_add_fusion.me_ref.place, bf16[1024,1024]{1,0:T(8,128)(2,1)} %get-tuple-element.124.normed, bf16[1024,768]{1,0:T(8,128)(2,1)S(1)} %copy-done.6, bf16[1024,256]{1,0:T(8,128)(2,1)} %outer_terms.1.outer), custom_call_target="tpu_custom_call" | custom-call | flops 1000000 | bytes 10000 | tf_op jit(solution)/shard_map/inner_terms/pallas_call | solution.py:764
  124.0 4.3 %collective-permute-start.21 = (bf16[512,1024]{1,0:T(8,128)(2,1)S(1)}, bf16[512,1024]{1,0:T(8,128)(2,1)S(1)}, u32[]{:S(2)}, u32[]{:S(2)}) collective-permute-start(bf16[512,1024]{1,0:T(8,128)(2,1)S(1)} %get-tuple-element.127), channel_id=1, source_target_pairs={{0,4},{4,0},{8,12},{12,8},{16,20},{20,16},{24,28},{28,24},{32,36},... | collective-permute-start | bytes 3145736 | tf_op jit(solution)/shard_map/ppermute | solution.py:820
  128.3 3.2 %collective-permute-start.18 = (bf16[1040,256]{1,0:T(8,128)(2,1)S(1)}, bf16[1040,256]{1,0:T(8,128)(2,1)S(1)}, u32[]{:S(2)}, u32[]{:S(2)}) collective-permute-start(bf16[1040,256]{1,0:T(8,128)(2,1)S(1)} %get-tuple-element.118), channel_id=1, source_target_pairs={{1,0},{2,1},{3,2},{0,3},{5,4},{6,5},{7,6},{4,7},{9,8},{10,9},{11,1... | collective-permute-start | bytes 1597448 | tf_op jit(solution)/shard_map/ppermute | solution.py:856
  137.9 5.7 %collective-permute-done.17.l1 = bf16[1040,256]{1,0:T(8,128)(2,1)S(1)} collective-permute-done((bf16[1040,256]{1,0:T(8,128)(2,1)S(1)}, bf16[1040,256]{1,0:T(8,128)(2,1)S(1)}, u32[]{:S(2)}, u32[]{:S(2)}) %collective-permute-start.17) | collective-permute-done | bytes 532512 | tf_op jit(solution)/shard_map/ppermute | solution.py:852
  143.8 3.2 %collective-permute-start.20 = (bf16[512,256]{1,0:T(8,128)(2,1)S(1)}, bf16[512,256]{1,0:T(8,128)(2,1)S(1)}, u32[]{:S(2)}, u32[]{:S(2)}) collective-permute-start(bf16[512,256]{1,0:T(8,128)(2,1)S(1)} %get-tuple-element.122), channel_id=1, source_target_pairs={{1,0},{2,1},{3,2},{0,3},{5,4},{6,5},{7,6},{4,7},{9,8},{10,9},{11,1... | collective-permute-start | bytes 786440 | tf_op jit(solution)/shard_map/ppermute | solution.py:856
  149.8 2.9 %collective-permute-start.25 = (bf16[32,1024]{1,0:T(8,128)(2,1)S(1)}, bf16[32,1024]{1,0:T(8,128)(2,1)S(1)}, u32[]{:S(2)}, u32[]{:S(2)}) collective-permute-start(bf16[32,1024]{1,0:T(8,128)(2,1)S(1)} %get-tuple-element.133), channel_id=1, source_target_pairs={{0,32},{4,36},{8,40},{12,44},{16,48},{20,52},{24,56},{28,60},{32,6... | collective-permute-start | bytes 196616 | tf_op jit(solution)/shard_map/ppermute | solution.py:820
  156.3 2.5 %finish_out.1 = bf16[1024,256]{1,0:T(8,128)(2,1)} custom-call(bf16[1024,256]{1,0:T(8,128)(2,1)} %get-tuple-element.90.own, bf16[1024,256]{1,0:T(8,128)(2,1)} %copy-done, bf16[1024,256]{1,0:T(8,128)(2,1)} %copy-done.1, bf16[512,256]{1,0:T(8,128)(2,1)} %copy-done.22, bf16[512,256]{1,0:T(8,128)(2,1)} %copy-done.23), custom_call_target="tpu_custom_call" | custom-call | flops 1000000 | bytes 10000 | tf_op jit(solution)/shard_map/finish_out/pallas_call | solution.py:695
  158.8 2.9 %finish_grad.1 = f32[1024,256]{1,0:T(8,128)} custom-call(bf16[1024,256]{1,0:T(8,128)(2,1)} %get-tuple-element.116.own, bf16[1040,256]{1,0:T(8,128)(2,1)S(1)} %collective-permute-done.17.l1, bf16[1040,256]{1,0:T(8,128)(2,1)S(1)} %collective-permute-done.18.r1, bf16[528,256]{1,0:T(8,128)(2,1)S(1)} %collective-permute-done.19.l2, ...), custom_call_target="tpu_custom_call" | custom-call | flops 1000000 | bytes 10000 | tf_op jit(solution)/shard_map/finish_grad/pallas_call | solution.py:722
  (100 shorter events, 42.3 us)
Async XLA Ops:
  1.7 11.3 %collective-permute-start.3 = (bf16[512,256]{1,0:T(8,128)(2,1)S(1)}, bf16[512,256]{1,0:T(8,128)(2,1)S(1)}, u32[]{:S(2)}, u32[]{:S(2)}) collective-permute-start(bf16[512,256]{1,0:T(8,128)(2,1)S(1)} %get-tuple-element.140), channel_id=1, source_target_pairs={{0,1},{1,2},{2,3},{3,0},{4,5},{5,6},{6,7},{7,4},{8,9},{9,10},{10,1... | collective-permute-start | bytes 786440 | tf_op jit(solution)/shard_map/ppermute | solution.py:852
  6.0 12.6 %collective-permute-start.1 = (bf16[512,256]{1,0:T(8,128)(2,1)S(1)}, bf16[512,256]{1,0:T(8,128)(2,1)S(1)}, u32[]{:S(2)}, u32[]{:S(2)}) collective-permute-start(bf16[512,256]{1,0:T(8,128)(2,1)S(1)} %get-tuple-element.140), channel_id=1, source_target_pairs={{1,0},{2,1},{3,2},{0,3},{5,4},{6,5},{7,6},{4,7},{9,8},{10,9},{11,1... | collective-permute-start | bytes 786440 | tf_op jit(solution)/shard_map/ppermute | solution.py:856
  7.9 10.7 %collective-permute-start.5 = (bf16[512,256]{1,0:T(8,128)(2,1)S(1)}, bf16[512,256]{1,0:T(8,128)(2,1)S(1)}, u32[]{:S(2)}, u32[]{:S(2)}) collective-permute-start(bf16[512,256]{1,0:T(8,128)(2,1)S(1)} %get-tuple-element.141), channel_id=1, source_target_pairs={{0,1},{1,2},{2,3},{3,0},{4,5},{5,6},{6,7},{7,4},{8,9},{9,10},{10,1... | collective-permute-start | bytes 786440 | tf_op jit(solution)/shard_map/ppermute | solution.py:852
  13.0 10.4 %collective-permute-start.4 = (bf16[512,256]{1,0:T(8,128)(2,1)S(1)}, bf16[512,256]{1,0:T(8,128)(2,1)S(1)}, u32[]{:S(2)}, u32[]{:S(2)}) collective-permute-start(bf16[512,256]{1,0:T(8,128)(2,1)S(1)} %collective-permute-done.3.t3b), channel_id=1, source_target_pairs={{0,1},{1,2},{2,3},{3,0},{4,5},{5,6},{6,7},{7,4},{8,9},{9,10},{10,1... | collective-permute-start | bytes 786440 | tf_op jit(solution)/shard_map/ppermute | solution.py:852
  13.0 10.4 %collective-permute-start.2 = (bf16[512,256]{1,0:T(8,128)(2,1)S(1)}, bf16[512,256]{1,0:T(8,128)(2,1)S(1)}, u32[]{:S(2)}, u32[]{:S(2)}) collective-permute-start(bf16[512,256]{1,0:T(8,128)(2,1)S(1)} %collective-permute-done.t1a), channel_id=1, source_target_pairs={{1,0},{2,1},{3,2},{0,3},{5,4},{6,5},{7,6},{4,7},{9,8},{10,9},{11,1... | collective-permute-start | bytes 786440 | tf_op jit(solution)/shard_map/ppermute | solution.py:856
  31.4 14.6 %collective-permute-start.6 = (bf16[2,768,256]{2,1,0:T(8,128)(2,1)}, bf16[2,768,256]{2,1,0:T(8,128)(2,1)S(1)}, u32[]{:S(2)}, u32[]{:S(2)}) collective-permute-start(bf16[2,768,256]{2,1,0:T(8,128)(2,1)} %get-tuple-element.86), channel_id=1, source_target_pairs={{0,4},{4,8},{8,12},{12,16},{16,20},{20,24},{24,28},{28,32},{32,36}... | collective-permute-start | bytes 2359304 | tf_op jit(solution)/shard_map/ppermute | solution.py:876
  32.8 13.3 %collective-permute-start.7 = (bf16[2,768,256]{2,1,0:T(8,128)(2,1)}, bf16[2,768,256]{2,1,0:T(8,128)(2,1)S(1)}, u32[]{:S(2)}, u32[]{:S(2)}) collective-permute-start(bf16[2,768,256]{2,1,0:T(8,128)(2,1)} %get-tuple-element.87), channel_id=1, source_target_pairs={{4,0},{8,4},{12,8},{16,12},{20,16},{24,20},{28,24},{32,28},{36,32}... | collective-permute-start | bytes 2359304 | tf_op jit(solution)/shard_map/ppermute | solution.py:877
  34.1 24.2 %collective-permute-start.14 = (bf16[1024,256]{1,0:T(8,128)(2,1)}, bf16[1024,256]{1,0:T(8,128)(2,1)S(1)}, u32[]{:S(2)}, u32[]{:S(2)}) collective-permute-start(bf16[1024,256]{1,0:T(8,128)(2,1)} %g0.1), channel_id=1, source_target_pairs={{0,1},{1,2},{2,3},{3,0},{4,5},{5,6},{6,7},{7,4},{8,9},{9,10},{10,1... | collective-permute-start | bytes 1572872 | tf_op jit(solution)/shard_map/ppermute | solution.py:852
  35.3 25.6 %collective-permute-start.13 = (bf16[1024,256]{1,0:T(8,128)(2,1)}, bf16[1024,256]{1,0:T(8,128)(2,1)S(1)}, u32[]{:S(2)}, u32[]{:S(2)}) collective-permute-start(bf16[1024,256]{1,0:T(8,128)(2,1)} %g0.1), channel_id=1, source_target_pairs={{0,2},{1,3},{2,0},{3,1},{4,6},{5,7},{6,4},{7,5},{8,10},{9,11},{10,... | collective-permute-start | bytes 1572872 | tf_op jit(solution)/shard_map/ppermute | solution.py:869
  38.6 22.9 %collective-permute-start.12 = (bf16[1024,256]{1,0:T(8,128)(2,1)}, bf16[1024,256]{1,0:T(8,128)(2,1)S(1)}, u32[]{:S(2)}, u32[]{:S(2)}) collective-permute-start(bf16[1024,256]{1,0:T(8,128)(2,1)} %g0.1), channel_id=1, source_target_pairs={{1,0},{2,1},{3,2},{0,3},{5,4},{6,5},{7,6},{4,7},{9,8},{10,9},{11,1... | collective-permute-start | bytes 1572872 | tf_op jit(solution)/shard_map/ppermute | solution.py:856
  65.5 28.7 %collective-permute-start.8 = (bf16[1024,256]{1,0:T(8,128)(2,1)S(1)}, bf16[1024,256]{1,0:T(8,128)(2,1)S(1)}, u32[]{:S(2)}, u32[]{:S(2)}) collective-permute-start(bf16[1024,256]{1,0:T(8,128)(2,1)S(1)} %get-tuple-element.91), channel_id=1, source_target_pairs={{0,1},{1,2},{2,3},{3,0},{4,5},{5,6},{6,7},{7,4},{8,9},{9,10},{10,1... | collective-permute-start | bytes 1572872 | tf_op jit(solution)/shard_map/ppermute | solution.py:852
  68.3 25.9 %collective-permute-start.9 = (bf16[1024,256]{1,0:T(8,128)(2,1)S(1)}, bf16[1024,256]{1,0:T(8,128)(2,1)S(1)}, u32[]{:S(2)}, u32[]{:S(2)}) collective-permute-start(bf16[1024,256]{1,0:T(8,128)(2,1)S(1)} %get-tuple-element.92), channel_id=1, source_target_pairs={{1,0},{2,1},{3,2},{0,3},{5,4},{6,5},{7,6},{4,7},{9,8},{10,9},{11,1... | collective-permute-start | bytes 1572872 | tf_op jit(solution)/shard_map/ppermute | solution.py:856
  90.7 17.8 %collective-permute-start.15 = (bf16[2,768,256]{2,1,0:T(8,128)(2,1)S(1)}, bf16[2,768,256]{2,1,0:T(8,128)(2,1)S(1)}, u32[]{:S(2)}, u32[]{:S(2)}) collective-permute-start(bf16[2,768,256]{2,1,0:T(8,128)(2,1)S(1)} %get-tuple-element.113), channel_id=1, source_target_pairs={{0,4},{4,8},{8,12},{12,16},{16,20},{20,24},{24,28},{28,32},{32,36}... | collective-permute-start | bytes 2359304 | tf_op jit(solution)/shard_map/ppermute | solution.py:876
  92.9 15.6 %collective-permute-start.16 = (bf16[2,768,256]{2,1,0:T(8,128)(2,1)S(1)}, bf16[2,768,256]{2,1,0:T(8,128)(2,1)S(1)}, u32[]{:S(2)}, u32[]{:S(2)}) collective-permute-start(bf16[2,768,256]{2,1,0:T(8,128)(2,1)S(1)} %get-tuple-element.114), channel_id=1, source_target_pairs={{4,0},{8,4},{12,8},{16,12},{20,16},{24,20},{28,24},{32,28},{36,32}... | collective-permute-start | bytes 2359304 | tf_op jit(solution)/shard_map/ppermute | solution.py:877
  94.4 14.0 %collective-permute-start.10 = (bf16[512,256]{1,0:T(8,128)(2,1)S(1)}, bf16[512,256]{1,0:T(8,128)(2,1)S(1)}, u32[]{:S(2)}, u32[]{:S(2)}) collective-permute-start(bf16[512,256]{1,0:T(8,128)(2,1)S(1)} %get-tuple-element.95), channel_id=1, source_target_pairs={{0,1},{1,2},{2,3},{3,0},{4,5},{5,6},{6,7},{7,4},{8,9},{9,10},{10,1... | collective-permute-start | bytes 786440 | tf_op jit(solution)/shard_map/ppermute | solution.py:852
  94.9 13.5 %collective-permute-start.11 = (bf16[512,256]{1,0:T(8,128)(2,1)S(1)}, bf16[512,256]{1,0:T(8,128)(2,1)S(1)}, u32[]{:S(2)}, u32[]{:S(2)}) collective-permute-start(bf16[512,256]{1,0:T(8,128)(2,1)S(1)} %get-tuple-element.96), channel_id=1, source_target_pairs={{1,0},{2,1},{3,2},{0,3},{5,4},{6,5},{7,6},{4,7},{9,8},{10,9},{11,1... | collective-permute-start | bytes 786440 | tf_op jit(solution)/shard_map/ppermute | solution.py:856
  128.3 15.3 %collective-permute-start.17 = (bf16[1040,256]{1,0:T(8,128)(2,1)S(1)}, bf16[1040,256]{1,0:T(8,128)(2,1)S(1)}, u32[]{:S(2)}, u32[]{:S(2)}) collective-permute-start(bf16[1040,256]{1,0:T(8,128)(2,1)S(1)} %get-tuple-element.117), channel_id=1, source_target_pairs={{0,1},{1,2},{2,3},{3,0},{4,5},{5,6},{6,7},{7,4},{8,9},{9,10},{10,1... | collective-permute-start | bytes 1597448 | tf_op jit(solution)/shard_map/ppermute | solution.py:852
  128.3 15.3 %collective-permute-start.18 = (bf16[1040,256]{1,0:T(8,128)(2,1)S(1)}, bf16[1040,256]{1,0:T(8,128)(2,1)S(1)}, u32[]{:S(2)}, u32[]{:S(2)}) collective-permute-start(bf16[1040,256]{1,0:T(8,128)(2,1)S(1)} %get-tuple-element.118), channel_id=1, source_target_pairs={{1,0},{2,1},{3,2},{0,3},{5,4},{6,5},{7,6},{4,7},{9,8},{10,9},{11,1... | collective-permute-start | bytes 1597448 | tf_op jit(solution)/shard_map/ppermute | solution.py:856
  132.3 14.7 %collective-permute-start.22 = (bf16[128,1024]{1,0:T(8,128)(2,1)S(1)}, bf16[128,1024]{1,0:T(8,128)(2,1)S(1)}, u32[]{:S(2)}, u32[]{:S(2)}) collective-permute-start(bf16[128,1024]{1,0:T(8,128)(2,1)S(1)} %get-tuple-element.129), channel_id=1, source_target_pairs={{0,8},{4,12},{8,16},{12,20},{16,24},{20,28},{24,0},{28,4},{32,40},... | collective-permute-start | bytes 786440 | tf_op jit(solution)/shard_map/ppermute | solution.py:820
  134.6 12.4 %collective-permute-start.23 = (bf16[128,1024]{1,0:T(8,128)(2,1)S(1)}, bf16[128,1024]{1,0:T(8,128)(2,1)S(1)}, u32[]{:S(2)}, u32[]{:S(2)}) collective-permute-start(bf16[128,1024]{1,0:T(8,128)(2,1)S(1)} %get-tuple-element.130), channel_id=1, source_target_pairs={{0,24},{4,28},{8,0},{12,4},{16,8},{20,12},{24,16},{28,20},{32,56},... | collective-permute-start | bytes 786440 | tf_op jit(solution)/shard_map/ppermute | solution.py:820
  136.0 13.1 %collective-permute-start.24 = (bf16[128,1024]{1,0:T(8,128)(2,1)S(1)}, bf16[128,1024]{1,0:T(8,128)(2,1)S(1)}, u32[]{:S(2)}, u32[]{:S(2)}) collective-permute-start(bf16[128,1024]{1,0:T(8,128)(2,1)S(1)} %get-tuple-element.131), channel_id=1, source_target_pairs={{0,16},{4,20},{8,24},{12,28},{16,0},{20,4},{24,8},{28,12},{32,48},... | collective-permute-start | bytes 786440 | tf_op jit(solution)/shard_map/ppermute | solution.py:820
  143.7 15.1 %collective-permute-start.19 = (bf16[528,256]{1,0:T(8,128)(2,1)S(1)}, bf16[528,256]{1,0:T(8,128)(2,1)S(1)}, u32[]{:S(2)}, u32[]{:S(2)}) collective-permute-start(bf16[528,256]{1,0:T(8,128)(2,1)S(1)} %get-tuple-element.121), channel_id=1, source_target_pairs={{0,1},{1,2},{2,3},{3,0},{4,5},{5,6},{6,7},{7,4},{8,9},{9,10},{10,1... | collective-permute-start | bytes 811016 | tf_op jit(solution)/shard_map/ppermute | solution.py:852
  143.8 15.0 %collective-permute-start.20 = (bf16[512,256]{1,0:T(8,128)(2,1)S(1)}, bf16[512,256]{1,0:T(8,128)(2,1)S(1)}, u32[]{:S(2)}, u32[]{:S(2)}) collective-permute-start(bf16[512,256]{1,0:T(8,128)(2,1)S(1)} %get-tuple-element.122), channel_id=1, source_target_pairs={{1,0},{2,1},{3,2},{0,3},{5,4},{6,5},{7,6},{4,7},{9,8},{10,9},{11,1... | collective-permute-start | bytes 786440 | tf_op jit(solution)/shard_map/ppermute | solution.py:856
  149.8 11.9 %collective-permute-start.25 = (bf16[32,1024]{1,0:T(8,128)(2,1)S(1)}, bf16[32,1024]{1,0:T(8,128)(2,1)S(1)}, u32[]{:S(2)}, u32[]{:S(2)}) collective-permute-start(bf16[32,1024]{1,0:T(8,128)(2,1)S(1)} %get-tuple-element.133), channel_id=1, source_target_pairs={{0,32},{4,36},{8,40},{12,44},{16,48},{20,52},{24,56},{28,60},{32,6... | collective-permute-start | bytes 196616 | tf_op jit(solution)/shard_map/ppermute | solution.py:820
  (28 other events, 210.4 us)

commit v2 on v0

v2 whole, which is shorter than its diff:
```python
import jax
import jax.numpy as jnp
from jax import lax
from jax.experimental import pallas as pl
from jax.experimental.pallas import tpu as pltpu
from jax.sharding import PartitionSpec as P

HD = 64
BLOCK = 256
LEVELS = 3
PAIR = 2 * HD
MP = 4
LANES = 128
DOT_ROWS = 16

EPSILON = 1e-06
NEGATIVE = -1e30

F32 = jnp.float32
BF16 = jnp.bfloat16

FIRST_EXT = (0, 6, 10)
EXT_BLOCKS = (6, 4, 3)
EXT_TOTAL = 13


def nn(left, right):
    return lax.dot_general(left, right, (((1,), (0,)), ((), ())), preferred_element_type=F32)


def nt(left, right):
    return lax.dot_general(left, right, (((1,), (1,)), ((), ())), preferred_element_type=F32)


def tn(left, right):
    return lax.dot_general(left, right, (((0,), (0,)), ((), ())), preferred_element_type=F32)


def pool_matrix(coarse, factor, value):
    shape = (coarse, coarse * factor)
    row = lax.broadcasted_iota(jnp.int32, shape, 0)
    low = row * factor
    col = lax.broadcasted_iota(jnp.int32, shape, 1)
    return jnp.where((col >= low) & (col < low + factor), value, 0.0).astype(BF16)


def spread_matrix(coarse, factor, value):
    shape = (coarse * factor, coarse)
    low = lax.broadcasted_iota(jnp.int32, shape, 1) * factor
    row = lax.broadcasted_iota(jnp.int32, shape, 0)
    return jnp.where((row >= low) & (row < low + factor), value, 0.0).astype(BF16)


def share_rows(me, step, width):
    return pl.ds(pl.multiple_of(((me + step) & (MP - 1)) * width, width), width)


SMALL = pl.CostEstimate(flops=10**6, bytes_accessed=10**4, transcendentals=0)
SCALAR = pl.BlockSpec(memory_space=pltpu.SMEM)
RESIDENT = pl.BlockSpec(memory_space=pltpu.VMEM)


def held(shape, dtype):
    return jax.ShapeDtypeStruct(shape, dtype)


def run(kernel, name, limit_mib, scalars, inputs, outputs, scratch=()):
    return pl.pallas_call(
        kernel,
        in_specs=[SCALAR] * len(scalars) + [RESIDENT] * len(inputs),
        out_specs=[RESIDENT] * len(outputs),
        out_shape=outputs,
        scratch_shapes=list(scratch),
        compiler_params=pltpu.CompilerParams(vmem_limit_bytes=limit_mib * 2**20),
        cost_estimate=SMALL,
        name=name,
    )(*scalars, *inputs)


def block_rows(block):
    return slice(block * BLOCK, (block + 1) * BLOCK)


def read_shares(step, refs):
    own, *halves = refs
    at = block_rows(step % 2)
    return [own[block_rows(step), :]] + [ref[at, :] for ref in halves[step // 2 :: 2]]


def level_rows(level, rows=4 * BLOCK):
    first = sum(rows // 2**n for n in range(level))
    return slice(first, first + rows // 2**level)


ALL_ROWS = 7 * BLOCK
LEVEL_BLOCK = (0, 4, 6)


def as_row(column):
    return jnp.broadcast_to(column, (column.shape[0], LANES)).T[0:1, :]


def as_column(row):
    return jnp.broadcast_to(row, (LANES, row.shape[1])).T[:, 0:1]


def project_kernel(
    place, t1a, t1b, t2a, t2b, t3a, t3b, t0_hbm, wq_hbm, wk_hbm, wv_hbm,
    inverse, q, kv, to_left, to_right, normed_hbm,
    t0, wq, wk, wv, normed, in_sems, out_sems,
):
    me = place[0]
    width = t0.shape[1]
    sources = (t0_hbm, wq_hbm, wk_hbm, wv_hbm)
    loads = [
        pltpu.make_async_copy(source, target, in_sems.at[n])
        for n, (source, target) in enumerate(zip(sources, (t0, wq, wk, wv)))
    ]
    for load in loads:
        load.start()
    half = pool_matrix(BLOCK // 2, 2, 0.5)
    quarter = pool_matrix(BLOCK // 4, 4, 0.25)
    inverse[4:8, :] = jnp.zeros((4, BLOCK), F32)
    stores = []
    for step in range(4):
        rows = block_rows(step)
        if step == 0:
            loads[0].wait()
        read = read_shares(step, (t0, t1a, t1b, t2a, t2b, t3a, t3b))
        shares = [share.astype(F32) for share in read]
        squares = shares[0] * shares[0]
        for share in shares[1:]:
            squares = squares + share * share
        total = jnp.sum(squares, axis=1, keepdims=True)
        inv = lax.rsqrt(total / (MP * width) + EPSILON)
        inverse[step : step + 1, :] = as_row(inv)
        parts = [(share * inv).astype(BF16) for share in shares]
        for r, part in enumerate(parts):
            normed[rows, r * width : (r + 1) * width] = part
        store = pltpu.make_async_copy(normed.at[rows], normed_hbm.at[rows], out_sems.at[step])
        store.start()
        stores.append(store)
        if step == 0:
            for load in loads[1:]:
                load.wait()
        sums = [None, None, None]
        for r, part in enumerate(parts):
            w_rows = share_rows(me, r, width)
            for n, w in enumerate((wq, wk, wv)):
                term = nn(part, w[w_rows, :])
                sums[n] = term if sums[n] is None else sums[n] + term
        fine = [x.astype(BF16) for x in sums]
        mid = [nn(half, x).astype(BF16) for x in fine]
        low = [nn(quarter, x).astype(BF16) for x in fine]
        mid_rows = slice(1024 + step * 128, 1024 + (step + 1) * 128)
        low_rows = slice(1536 + step * 64, 1536 + (step + 1) * 64)
        q[rows, :] = fine[0]
        q[mid_rows, :] = mid[0]
        q[low_rows, :] = low[0]
        edge_mid = slice(256 + (step % 2) * 128, 384 + (step % 2) * 128)
        edge_low = slice(512 + step * 64, 576 + step * 64)
        for n in range(2):
            kv[n, rows, :] = fine[1 + n]
            kv[n, mid_rows, :] = mid[1 + n]
            kv[n, low_rows, :] = low[1 + n]
            to_left[n, edge_low, :] = low[1 + n]
            to_right[n, edge_low, :] = low[1 + n]
            edge = to_left if step < 2 else to_right
            edge[n, edge_mid, :] = mid[1 + n]
            if step in (0, 3):
                edge[n, 0:BLOCK, :] = fine[1 + n]
    for store in stores:
        store.wait()


def project(place, shares, wq, wk, wv):
    rows, width = shares[0].shape
    out = jax.ShapeDtypeStruct
    edge = out((2, 3 * BLOCK, width), BF16)
    anywhere = pl.BlockSpec(memory_space=pl.ANY)
    share = pltpu.VMEM((rows, width), BF16)
    fixed = [
        pltpu.with_memory_space_constraint(value, pltpu.HBM)
        for value in (shares[0], wq, wk, wv)
    ]
    return pl.pallas_call(
        project_kernel,
        in_specs=[SCALAR] + [RESIDENT] * 6 + [anywhere] * 4,
        out_specs=[RESIDENT] * 5 + [anywhere],
        out_shape=[
            out((8, width), F32),
            out((ALL_ROWS, width), BF16),
            out((2, ALL_ROWS, width), BF16),
            edge,
            edge,
            pltpu.HBM((rows, MP * width), BF16),
        ],
        scratch_shapes=[share] * 4
        + [
            pltpu.VMEM((rows, MP * width), BF16),
            pltpu.SemaphoreType.DMA((4,)),
            pltpu.SemaphoreType.DMA((4,)),
        ],
        compiler_params=pltpu.CompilerParams(vmem_limit_bytes=20 * 2**20),
        cost_estimate=SMALL,
        name="project",
    )(place, *shares[1:], *fixed)


def cotangent_kernel(place, g0, g1, g2, g3, w_out, d_att):
    me = place[0]
    width = g0.shape[1]
    half = pool_matrix(BLOCK // 2, 2, 1.0)
    quarter = pool_matrix(BLOCK // 4, 4, 1.0)
    for step in range(4):
        rows = block_rows(step)
        total = None
        for r, share in enumerate((g0, g1, g2, g3)):
            term = nt(share[rows, :], w_out[:, share_rows(me, r, width)])
            total = term if total is None else total + term
        fine = total.astype(BF16)
        d_att[rows, :] = fine
        d_att[1024 + step * 128 : 1024 + (step + 1) * 128, :] = nn(half, fine).astype(BF16)
        d_att[1536 + step * 64 : 1536 + (step + 1) * 64, :] = nn(quarter, fine).astype(BF16)


def cotangent(place, shares, w_out):
    rows, width = shares[0].shape
    outputs = [held((ALL_ROWS, width), BF16)]
    return run(cotangent_kernel, "cotangent", 8, [place], [*shares, w_out], outputs)[0]


EDGE_UNITS = ((0, 0), (0, 3), (1, 0), (1, 1), (2, 0))
INNER_UNITS = ((0, 1), (0, 2))


def unit_keys(level, block):
    last = EXT_BLOCKS[level] - 1
    offsets = (0, 1, 2) if level == 0 else (0, 2)
    keys = []
    for offset in offsets:
        at = block + offset
        keys.append((at, 0 if at == 0 else 1 if at == last else None))
    return keys


def ext_rows(kv, from_left, from_right, n, level, at, lanes):
    if at == 0:
        return from_left[n, block_rows(level), lanes]
    if at == EXT_BLOCKS[level] - 1:
        return from_right[n, block_rows(level), lanes]
    return kv[n, block_rows(LEVEL_BLOCK[level] + at - 1), lanes]


def head_part(lane, head, rows):
    mine = (lane >= head * HD) & (lane < (head + 1) * HD)
    return jnp.where(mine, rows, 0.0).astype(BF16)


def unit_scores(keys, key_rows, query, bias_ref):
    scores = []
    for (_, bias), rows in zip(keys, key_rows):
        s = nt(rows, query)
        scores.append(s if bias is None else s + bias_ref[bias])
    return scores


def add_spread(target, block, factor, rows):
    if factor == 1:
        target[block_rows(block), :] = target[block_rows(block), :] + rows
        return
    for s in range(factor):
        spread = pl.ds(block * factor * BLOCK + s, BLOCK, factor)
        target[spread, :] = target[spread, :] + rows


def each_pair(width, body):
    def step(pair, _):
        body(pair, pl.ds(pl.multiple_of(pair * PAIR, PAIR), PAIR))
        return 0

    lax.fori_loop(0, width // PAIR, step, 0)


def head_part(lane, head, rows):
    mine = (lane >= head * HD) & (lane < (head + 1) * HD)
    return jnp.where(mine, rows, 0.0).astype(BF16)


def unit_scores(keys, key_rows, query, bias_ref):
    scores = []
    for (_, bias), rows in zip(keys, key_rows):
        s = nt(rows, query)
        scores.append(s if bias is None else s + bias_ref[bias])
    return scores


def add_spread(target, block, factor, rows):
    if factor == 1:
        target[block_rows(block), :] = target[block_rows(block), :] + rows
        return
    for s in range(factor):
        spread = pl.ds(block * factor * BLOCK + s, BLOCK, factor)
        target[spread, :] = target[spread, :] + rows


def forward_units(pair, lanes, units, bias_ref, q, kv, from_left, from_right, stats, vt, out_f):
    lane = lax.broadcasted_iota(jnp.int32, (BLOCK, PAIR), 1)
    done = set()
    for level, block in units:
        for at, _ in unit_keys(level, block):
            if (level, at) not in done:
                done.add((level, at))
                rows = ext_rows(kv, from_left, from_right, 1, level, at, lanes)
                vt[FIRST_EXT[level] + at] = rows.T

    def begin(u, head):
        level, block = units[u]
        keys = unit_keys(level, block)
        key_rows = [ext_rows(kv, from_left, from_right, 0, level, at, lanes) for at, _ in keys]
        q_rows = q[block_rows(LEVEL_BLOCK[level] + block), lanes] * HD ** (-0.5)
        return unit_scores(keys, key_rows, head_part(lane, head, q_rows), bias_ref)

    def finish(u, head, scores):
        level, block = units[u]
        top = scores[0].max(axis=0, keepdims=True)
        for s in scores[1:]:
            top = jnp.maximum(top, s.max(axis=0, keepdims=True))
        exps = [jnp.exp(s - top) for s in scores]
        total = exps[0].sum(axis=0, keepdims=True)
        for e in exps[1:]:
            total = total + e.sum(axis=0, keepdims=True)
        scale = 1.0 / total
        row = 4 * u + 2 * head
        stats[pair, row : row + 1, :] = top
        stats[pair, row + 1 : row + 2, :] = scale
        part = slice(head * HD, (head + 1) * HD)
        o_t = None
        for (at, _), e in zip(unit_keys(level, block), exps):
            o = nn(vt[FIRST_EXT[level] + at, part, :], (e * scale).astype(BF16))
            o_t = o if o_t is None else o_t + o
        return o_t

    items = [(u, head) for u in range(len(units)) for head in range(2)]
    scores, outs = begin(*items[0]), []
    for n, (u, head) in enumerate(items):
        following = begin(*items[n + 1]) if n + 1 < len(items) else None
        outs.append(finish(u, head, scores))
        scores = following
        if head == 1:
            level, block = units[u]
            add_spread(out_f, block, 2**level, jnp.concatenate(outs, axis=0).T)
            outs = []


def forward_inner_kernel(bias_ref, q, kv, out, stats, vt, out_f):
    def one(pair, lanes):
        out_f[...] = jnp.zeros_like(out_f)
        forward_units(pair, lanes, INNER_UNITS, bias_ref, q, kv, None, None, stats, vt, out_f)
        out[:, lanes] = out_f[BLOCK : 3 * BLOCK, :]

    each_pair(q.shape[1], one)


def forward_edge_kernel(
    bias_ref, q, kv, from_left, from_right, inner, attended, stats, vt, out_f
):
    def one(pair, lanes):
        out_f[0:BLOCK, :] = jnp.zeros((BLOCK, PAIR), F32)
        out_f[BLOCK : 3 * BLOCK, :] = inner[:, lanes]
        out_f[3 * BLOCK :, :] = jnp.zeros((BLOCK, PAIR), F32)
        forward_units(
            pair, lanes, EDGE_UNITS, bias_ref, q, kv, from_left, from_right, stats, vt, out_f
        )
        attended[:, lanes] = out_f[...].astype(BF16)

    each_pair(q.shape[1], one)


def backward_units(
    pair, lanes, units, bias_ref, q, kv, from_left, from_right, grads, stats, kt, dq_f, keep
):
    lane = lax.broadcasted_iota(jnp.int32, (BLOCK, PAIR), 1)
    done = set()
    for level, block in units:
        for at, _ in unit_keys(level, block):
            if (level, at) not in done:
                done.add((level, at))
                rows = ext_rows(kv, from_left, from_right, 0, level, at, lanes)
                kt[FIRST_EXT[level] + at] = rows.T

    def begin(u, head):
        level, block = units[u]
        keys = unit_keys(level, block)
        key_rows = [ext_rows(kv, from_left, from_right, 0, level, at, lanes) for at, _ in keys]
        value_rows = [ext_rows(kv, from_left, from_right, 1, level, at, lanes) for at, _ in keys]
        at = block_rows(LEVEL_BLOCK[level] + block)
        qm = head_part(lane, head, q[at, lanes] * HD ** (-0.5))
        am = head_part(lane, head, grads[at, lanes])
        scores = unit_scores(keys, key_rows, qm, bias_ref)
        return qm, am, scores, [nt(rows, am) for rows in value_rows]

    def finish(u, head, qm, am, scores, d_weights):
        level, block = units[u]
        row = 4 * u + 2 * head
        top, scale = stats[pair, row : row + 1, :], stats[pair, row + 1 : row + 2, :]
        probs = [jnp.exp(s - top) * scale for s in scores]
        dots = None
        for p, dw in zip(probs, d_weights):
            d = (p * dw).sum(axis=0, keepdims=True)
            dots = d if dots is None else dots + d
        part = slice(head * HD, (head + 1) * HD)
        dq_t, d_keys, d_values = None, [], []
        for (at, _), p, dw in zip(unit_keys(level, block), probs, d_weights):
            d_values.append(nn(p.astype(BF16), am))
            d_scores = (p * (dw - dots)).astype(BF16)
            d_keys.append(nn(d_scores, qm))
            g = nn(kt[FIRST_EXT[level] + at, part, :], d_scores)
            dq_t = g if dq_t is None else dq_t + g
        return dq_t, d_keys, d_values

    items = [(u, head) for u in range(len(units)) for head in range(2)]
    ready, first = begin(*items[0]), None
    for n, (u, head) in enumerate(items):
        following = begin(*items[n + 1]) if n + 1 < len(items) else None
        got = finish(u, head, *ready)
        ready = following
        if head == 0:
            first = got
            continue
        level, block = units[u]
        for m, (at, _) in enumerate(unit_keys(level, block)):
            keep(0, level, at, first[1][m] + got[1][m])
            keep(1, level, at, first[2][m] + got[2][m])
        dq = jnp.concatenate([first[0], got[0]], axis=0).T * (HD ** (-0.5) / 2**level)
        add_spread(dq_f, block, 2**level, dq)


def edge_kernel(
    bias_ref, stats, q, kv, from_left, from_right, grads,
    dq_f, d_kv, to_left, to_right, kt, ext, dq_s, sums,
):
    def one(pair, lanes):
        dq_s[...] = jnp.zeros_like(dq_s)
        seen = set()

        def keep(n, level, at, rows):
            slot = FIRST_EXT[level] + at
            if (n, slot) in seen:
                ext[n, slot] = ext[n, slot] + rows
            else:
                seen.add((n, slot))
                ext[n, slot] = rows

        backward_units(
            pair, lanes, EDGE_UNITS, bias_ref, q, kv, from_left, from_right, grads, stats, kt,
            dq_s, keep,
        )
        dq_f[:, lanes] = dq_s[...]
        for n in range(2):
            for level in range(LEVELS):
                first, last = FIRST_EXT[level], FIRST_EXT[level] + EXT_BLOCKS[level] - 1
                to_left[n, block_rows(level), lanes] = ext[n, first].astype(BF16)
                to_right[n, block_rows(level), lanes] = ext[n, last].astype(BF16)
            for b in range(4):
                sums[block_rows(b), :] = ext[n, 1 + b]
            for b in range(2):
                add_spread(sums, b, 2, ext[n, FIRST_EXT[1] + 1 + b] * 0.5)
            d_kv[n, :, lanes] = sums[...]

    each_pair(q.shape[1], one)


def inner_units_kernel(bias_ref, stats, q, kv, grads, dq_in, d_kv_in, d_query, d_kv, kt, dq_s):
    def one(pair, lanes):
        dq_s[...] = dq_in[:, lanes]
        d_kv[:, :, lanes] = d_kv_in[:, :, lanes]

        def keep(n, level, at, rows):
            where = block_rows(at - 1)
            d_kv[n, where, lanes] = d_kv[n, where, lanes] + rows

        backward_units(
            pair, lanes, INNER_UNITS, bias_ref, q, kv, None, None, grads, stats, kt, dq_s, keep
        )
        d_query[:, lanes] = dq_s[...].astype(BF16)

    each_pair(q.shape[1], one)


def turned(count):
    return pltpu.VMEM((count, PAIR, BLOCK), BF16)


def forward_inner(bias, q, kv):
    width = q.shape[1]
    outputs = [held((2 * BLOCK, width), F32), held((width // PAIR, 8, BLOCK), F32)]
    scratch = [turned(EXT_BLOCKS[0]), pltpu.VMEM((4 * BLOCK, PAIR), F32)]
    return run(forward_inner_kernel, "forward_inner", 12, [bias], [q, kv], outputs, scratch)


def forward_edge(bias, q, kv, from_left, from_right, inner):
    width = q.shape[1]
    inputs = [q, kv, from_left, from_right, inner]
    outputs = [held((4 * BLOCK, width), BF16), held((width // PAIR, 24, BLOCK), F32)]
    scratch = [turned(EXT_TOTAL), pltpu.VMEM((4 * BLOCK, PAIR), F32)]
    return run(forward_edge_kernel, "forward_edge", 12, [bias], inputs, outputs, scratch)


def edge_backward(bias, stats, q, kv, from_left, from_right, d_att):
    rows, width = 4 * BLOCK, q.shape[1]
    edge = held((2, 3 * BLOCK, width), BF16)
    inputs = [stats, q, kv, from_left, from_right, d_att]
    outputs = [held((rows, width), F32), held((2, rows, width), F32), edge, edge]
    scratch = [
        turned(EXT_TOTAL),
        pltpu.VMEM((2, EXT_TOTAL, BLOCK, PAIR), F32),
        pltpu.VMEM((rows, PAIR), F32),
        pltpu.VMEM((rows, PAIR), F32),
    ]
    return run(edge_kernel, "edge_backward", 20, [bias], inputs, outputs, scratch)


def inner_backward(bias, stats, q, kv, d_att, dq_f, d_kv):
    rows, width = 4 * BLOCK, q.shape[1]
    inputs = [stats, q, kv, d_att, dq_f, d_kv]
    outputs = [held((rows, width), BF16), held((2, rows, width), F32)]
    scratch = [turned(EXT_BLOCKS[0]), pltpu.VMEM((rows, PAIR), F32)]
    return run(inner_units_kernel, "inner_backward", 12, [bias], inputs, outputs, scratch)


def store_terms(step, terms, own, keep_right, keep_left, right, left):
    own[block_rows(step), :] = terms[0]
    low, high = block_rows(step % 2), block_rows(2 + step % 2)
    if step < 2:
        keep_right[low, :] = terms[1]
        right[high, :] = terms[2]
        left[low, :] = terms[3]
    else:
        right[low, :] = terms[1]
        left[high, :] = terms[2]
        keep_left[low, :] = terms[3]


def term_outputs(rows, width, extra=0):
    lengths = [rows, rows // 2, rows // 2, rows + extra, rows + extra]
    return [held((n, width), BF16) for n in lengths]


def out_terms_kernel(place, attended, w_out, *outs):
    me = place[0]
    width = attended.shape[1]
    for step in range(4):
        rows = attended[block_rows(step), :]
        terms = [nn(rows, w_out[:, share_rows(me, r, width)]).astype(BF16) for r in range(MP)]
        store_terms(step, terms, *outs)


def out_terms(place, attended, w_out):
    outputs = term_outputs(*attended.shape)
    return run(out_terms_kernel, "out_terms", 8, [place], [attended, w_out], outputs)


def input_terms_kernel(
    place, d_query, d_kv, from_left, from_right, normed, wq, wk, wv, d_proj,
    dots, own, keep_right, keep_left, right, left, dot_rows,
):
    me = place[0]
    width = d_query.shape[1]
    half = spread_matrix(BLOCK // 2, 2, 0.5)
    quarter = spread_matrix(BLOCK // 4, 4, 0.25)
    dot_rows[12:16, :] = jnp.zeros((4, BLOCK), F32)
    for step in range(4):
        rows = block_rows(step)
        grads = [d_query[rows, :]]
        mid_rows = slice(256 + (step % 2) * 128, 384 + (step % 2) * 128)
        low_rows = slice(512 + step * 64, 576 + step * 64)
        near = from_left if step < 2 else from_right
        for n in range(2):
            total = d_kv[n, rows, :]
            if step in (0, 3):
                total = total + near[n, 0:BLOCK, :].astype(F32)
            total = total + nn(half, near[n, mid_rows, :])
            total = total + nn(quarter, from_left[n, low_rows, :])
            total = total + nn(quarter, from_right[n, low_rows, :])
            grads.append(total.astype(BF16))
        for n, grad in enumerate(grads):
            d_proj[rows, n * width : (n + 1) * width] = grad
        terms, dot = [], None
        for r in range(MP):
            at = share_rows(me, r, width)
            term = nt(grads[0], wq[at, :]) + nt(grads[1], wk[at, :]) + nt(grads[2], wv[at, :])
            term = term.astype(BF16)
            terms.append(term)
            part = term.astype(F32) * normed[rows, r * width : (r + 1) * width].astype(F32)
            dot = part if dot is None else dot + part
        dot = as_row(jnp.sum(dot, axis=1, keepdims=True))
        first = dot.astype(BF16).astype(F32)
        second = (dot - first).astype(BF16).astype(F32)
        for n, piece in enumerate((first, second, dot - first - second)):
            dot_rows[4 * n + step : 4 * n + step + 1, :] = piece
        store_terms(step, terms, own, keep_right, keep_left, right, left)
    pieces = dot_rows[...].astype(BF16)
    dots[...] = pieces
    right[4 * BLOCK :, :] = pieces
    left[4 * BLOCK :, :] = pieces


def input_terms(place, d_query, d_kv, from_left, from_right, normed, wq, wk, wv):
    rows, width = d_query.shape
    inputs = [d_query, d_kv, from_left, from_right, normed, wq, wk, wv]
    outputs = [held((rows, 3 * width), BF16), held((DOT_ROWS, width), BF16)]
    outputs += term_outputs(rows, width, DOT_ROWS)
    scratch = [pltpu.VMEM((DOT_ROWS, width), F32)]
    return run(input_terms_kernel, "input_terms", 16, [place], inputs, outputs, scratch)


def relay_kernel(keep_right, keep_left, l1, r1, onward_right, onward_left):
    half = keep_right.shape[0]
    passed = l1[half : 2 * half, :].astype(F32)
    onward_right[0:half, :] = (keep_right[...].astype(F32) + passed).astype(BF16)
    passed = r1[half : 2 * half, :].astype(F32)
    onward_left[...] = (keep_left[...].astype(F32) + passed).astype(BF16)
    if onward_right.shape[0] > half:
        onward_right[half:, :] = l1[2 * half :, :]


def relay(keep_right, keep_left, l1, r1):
    half, width = keep_right.shape
    extra = l1.shape[0] - 2 * half
    outputs = [held((half + extra, width), BF16), held((half, width), BF16)]
    return run(relay_kernel, "relay", 4, [], [keep_right, keep_left, l1, r1], outputs)


def summed(own, l1, r1, l2, r2):
    half = r2.shape[0]
    low = r1[0:half, :].astype(F32) + l2[0:half, :].astype(F32)
    high = l1[0:half, :].astype(F32) + r2[...].astype(F32)
    return own[0:half, :].astype(F32) + low, own[half:, :].astype(F32) + high


def finish_out_kernel(own, l1, r1, l2, r2, result):
    half = r2.shape[0]
    low, high = summed(own, l1, r1, l2, r2)
    result[0:half, :] = low.astype(BF16)
    result[half:, :] = high.astype(BF16)


def finish_out(own, l1, r1, l2, r2):
    outputs = [jax.ShapeDtypeStruct(own.shape, BF16)]
    return run(finish_out_kernel, "finish_out", 8, [], [own, l1, r1, l2, r2], outputs)[0]


def finish_grad_kernel(own, l1, r1, l2, r2, tokens, inverse, dots, result):
    rows, width = own.shape
    half = r2.shape[0]
    pieces = dots[...].astype(F32)
    for message, first in ((l1, rows), (r1, rows), (l2, half)):
        pieces = pieces + message[first : first + DOT_ROWS, :].astype(F32)
    means = (pieces[0:4] + pieces[4:8] + pieces[8:12]) / (MP * width)
    halves = summed(own, l1, r1, l2, r2)
    for b in range(rows // BLOCK):
        mean = as_column(means[b : b + 1, :])
        inv = as_column(inverse[b : b + 1, :])
        at = block_rows(b)
        total = halves[b // 2][block_rows(b % 2), :]
        result[at, :] = inv * (total - tokens[at, :].astype(F32) * inv * mean)


def finish_grad(own, l1, r1, l2, r2, tokens, inverse, dots):
    inputs = [own, l1, r1, l2, r2, tokens, inverse, dots]
    outputs = [jax.ShapeDtypeStruct(own.shape, F32)]
    return run(finish_grad_kernel, "finish_grad", 8, [], inputs, outputs)[0]


def outer_kernel(g0, g1, g2, g3, attended, result):
    width = g0.shape[1]
    rows = attended[...]
    for r, share in enumerate((g0, g1, g2, g3)):
        result[r * width : (r + 1) * width, :] = tn(share[...], rows).astype(BF16)


def outer_terms(shares, attended):
    rows, width = attended.shape
    outputs = [held((MP * width, width), BF16)]
    return run(outer_kernel, "outer_terms", 10, [], [*shares, attended], outputs)[0]


def inner_kernel(place, normed, d_proj, outer, mine, other, rows_held):
    core = place[1]
    width = outer.shape[1]
    for block in range(MP):
        at = block_rows(block)
        rows_held[at, 0 : 3 * width] = tn(normed[:, at], d_proj[...]).astype(BF16)
        rows_held[at, 3 * width :] = outer[at, :]
        for n in range(width // 64):
            out = slice((4 * block + n) * 32, (4 * block + n + 1) * 32)
            first = block * width + n * 64
            mine[out, :] = rows_held[pl.ds(pl.multiple_of(first + core * 32, 32), 32), :]
            other[out, :] = rows_held[pl.ds(pl.multiple_of(first + 32 - core * 32, 32), 32), :]


def inner_terms(place, normed, d_proj, outer):
    total = normed.shape[1]
    width = outer.shape[1]
    outputs = [held((total // 2, 4 * width), BF16)] * 2
    scratch = [pltpu.VMEM((total, 4 * width), BF16)]
    return run(inner_kernel, "inner_terms", 16, [place], [normed, d_proj, outer], outputs, scratch)


def pair_sum_kernel(place, mine, got, *outs):
    x = place[2]
    for d, out in enumerate(outs):
        for y in range(4):
            rows = pl.ds(pl.multiple_of((4 * y + ((x + d) & 3)) * 32, 32), 32)
            total = mine[rows, :].astype(F32) + got[rows, :].astype(F32)
            out[32 * y : 32 * (y + 1), :] = total.astype(BF16)


def row_sum_kernel(place, a, b, c, d, *refs):
    *outs, total = refs
    first = place[3] - place[0] + 4
    total[...] = (
        a[...].astype(F32) + b[...].astype(F32) + c[...].astype(F32) + d[...].astype(F32)
    ).astype(BF16)
    for n, out in enumerate(outs):
        out[...] = total[pl.ds(pl.multiple_of(((first + n) & 3) * 32, 32), 32), :]


def last_sum_kernel(a, b, c, d, gq, gk, gv, go):
    width = gq.shape[1]
    total = a[...].astype(F32) + b[...].astype(F32) + c[...].astype(F32) + d[...].astype(F32)
    gq[...] = total[:, 0:width]
    gk[...] = total[:, width : 2 * width]
    gv[...] = total[:, 2 * width : 3 * width]
    go[...] = total[:, 3 * width :]


def sum_over_seq(place, mine, other):
    cols = mine.shape[1]

    def sent(value, dy, dx, dc):
        pairs = []
        for i in range(32):
            c, a, b = i % 2, (i // 2) % 4, i // 8
            pairs.append((i, (((b + dy) % 4) * 4 + (a + dx) % 4) * 2 + (c + dc) % 2))
        return lax.ppermute(value, "seq", pairs)

    parts = [held((128, cols), BF16)] * 4
    parts = run(pair_sum_kernel, "pair_sum", 6, [place], [mine, sent(other, 0, 0, 1)], parts)
    parts = [parts[0]] + [sent(parts[d], 0, d, 0) for d in (1, 3, 2)]
    rows = [held((32, cols), BF16)] * 4
    scratch = [pltpu.VMEM((128, cols), BF16)]
    rows = run(row_sum_kernel, "row_sum", 4, [place], parts, rows, scratch)
    rows = [rows[0]] + [sent(rows[d], d, 0, 0) for d in (1, 3, 2)]
    outputs = [held((32, cols // 4), F32)] * 4
    return run(last_sum_kernel, "last_sum", 4, [], rows, outputs)


def to_next(value):
    return lax.ppermute(value, "mp", [(i, (i + 1) % MP) for i in range(MP)])


def to_previous(value):
    return lax.ppermute(value, "mp", [((i + 1) % MP, i) for i in range(MP)])


def gather_shares(share):
    half = share.shape[0] // 2
    low, high = share[:half], share[half:]
    after_low, before_high = to_previous(low), to_next(high)
    after_high, before_low = to_previous(high), to_next(low)
    far_low, far_high = to_previous(after_low), to_next(before_high)
    return [share, after_low, after_high, far_low, far_high, before_low, before_high]


def gather_direct(share):
    far = lax.ppermute(share, "mp", [(i, (i + 2) % MP) for i in range(MP)])
    return [share, to_previous(share), far, to_next(share)]


def exchange(to_left, to_right):
    count = lax.axis_size("seq")
    ends = count - 1
    from_left = lax.ppermute(to_right, "seq", [(i, i + 1) for i in range(ends)])
    from_right = lax.ppermute(to_left, "seq", [(i + 1, i) for i in range(ends)])
    return from_left, from_right


def tied(values, *others):
    flat, tree = jax.tree.flatten(values)
    flat = lax.optimization_barrier((*flat, *others))[: len(flat)]
    return jax.tree.unflatten(tree, flat)


def per_device(tokens, w_query, w_key, w_value, w_out, grad_out):
    count = lax.axis_size("seq")
    index = lax.axis_index("seq")
    me = jnp.stack([lax.axis_index("mp"), index & 1, (index >> 1) & 3, index >> 3])
    me = me.astype(jnp.int32)
    bias = jnp.stack(
        [
            jnp.where(index == 0, NEGATIVE, 0.0).astype(F32),
            jnp.where(index == count - 1, NEGATIVE, 0.0).astype(F32),
        ]
    )
    token_shares = gather_shares(tokens)
    sent_grad = tied(grad_out, *token_shares)
    grad_shares = gather_direct(sent_grad)
    grad_shares[0] = grad_out
    inverse, q, kv, to_left, to_right, normed = project(
        me, token_shares, w_query, w_key, w_value
    )
    from_left, from_right = exchange(to_left, to_right)
    inner_out, inner_stats = forward_inner(bias, q, kv)
    attended, stats = forward_edge(bias, q, kv, from_left, from_right, inner_out)
    grad_shares = tied(grad_shares, attended)
    out_own, keep_right, keep_left, right, left = out_terms(me, attended, w_out)
    l1, r1 = to_next(right), to_previous(left)
    d_att = cotangent(me, grad_shares, w_out)
    dq_f, d_kv, to_left, to_right = edge_backward(
        bias, stats, q, kv, from_left, from_right, d_att
    )
    onward_right, onward_left = relay(keep_right, keep_left, l1, r1)
    l2, r2 = to_next(onward_right), to_previous(onward_left)
    from_left, from_right = exchange(to_left, to_right)
    dq_f = tied(dq_f, onward_right, onward_left)
    d_query, d_kv = inner_backward(bias, inner_stats, q, kv, d_att, dq_f, d_kv)
    d_query = tied(d_query, l2, r2)
    d_proj, dots, own, keep_right, keep_left, right, left = input_terms(
        me, d_query, d_kv, from_left, from_right, normed, w_query, w_key, w_value
    )
    attn_out = finish_out(out_own, l1, r1, l2, r2)
    l1, r1 = to_next(right), to_previous(left)
    outer = outer_terms(grad_shares, attended)
    mine, other = inner_terms(me, normed, d_proj, outer)
    onward_right, onward_left = relay(keep_right, keep_left, l1, r1)
    l2, r2 = to_next(onward_right), to_previous(onward_left)
    grad_tokens = finish_grad(own, l1, r1, l2, r2, tokens, inverse, dots)
    *weight_grads, grad_w_out = sum_over_seq(me, mine, other)
    return (attn_out, grad_tokens, *weight_grads, grad_w_out.T)


def solution(mesh):
    return jax.shard_map(
        per_device,
        mesh=mesh,
        in_specs=(
            P("seq", "mp"),
            P(None, "mp"),
            P(None, "mp"),
            P(None, "mp"),
            P("mp", None),
            P("seq", "mp"),
        ),
        out_specs=(
            P("seq", "mp"),
            P("seq", "mp"),
            P("seq", "mp"),
            P("seq", "mp"),
            P("seq", "mp"),
            P("mp", "seq"),
        ),
        check_vma=False,
    )
```

time: 681 us -> 141 us (0.21); the launches traced: 670 us -> 140 us
  matrix products: 192 us -> 0 us
  local copies, waits for them, and re-layouts: 173 us -> 6.06 us
  waiting for transfers between devices: 186 us -> 27.2 us
  other arithmetic: 61.3 us -> 0.15 us
  Pallas kernels: 0 us -> 52.1 us
  between operations: 15 us -> 0.94 us
  starting transfers between devices: 42.3 us -> 53.7 us
    dot_general x22 -> x0, matrix products: 185 us -> none  [the longest x16 173 us: product(): jnp.einsum(form, left_side, right_side, preferred_element_type=jnp.float32)]
    unnamed x6 -> x0, waiting for transfers between devices: 79.2 us -> none
    slice x20 -> x1, local copies, waits for them, and re-layouts: 55.1 us -> 1.07 us  [gather_shares(): low, high = (share[:half], share[half:])]
    pallas_call x0 -> x17, Pallas kernels: none -> 52.1 us  [the longest x16 45.3 us: run(): pl.pallas_call(kernel, in_specs=[SCALAR] * len(scalars) + [RESIDENT] * le...]
    all_gather x2 -> x0, waiting for transfers between devices: 43.7 us -> none  [the longest x1 36.2 us: per_device(): lax.all_gather(tokens, 'mp', axis=1, tiled=True)]
    psum x1 -> x0, waiting for transfers between devices: 34.4 us -> none  [per_device(): lax.psum(d_normed_part.astype(jnp.bfloat16), 'mp').astype(jnp.float32)]
    reshape x18 -> x0, local copies, waits for them, and re-layouts: 33 us -> none  [the longest x3 16.1 us: level_backward(): jnp.stack([d_key_rows, d_value_rows], axis=2)]
    reduce_scatter x1 -> x0, waiting for transfers between devices: 28.4 us -> none  [per_device(): lax.psum_scatter(partial_out.astype(jnp.bfloat16), 'mp', scatter_dimensio...]
  transfers between devices with their start and end apart: 17 -> 28, of which waited for: 5 -> 9; matrix products, arithmetic and copies ran while one was open for 56% -> 0% of each run, Pallas kernels for 0% -> 27%
where the time goes in v2:
time: 141 us; the launch traced here: 140 us
  starting transfers between devices  53.7 us (38%)
  Pallas kernels  52.1 us (37%)
  waiting for transfers between devices  27.2 us (19%)
  local copies, waits for them, and re-layouts  6.06 us (4%)
    pallas_call x16, Pallas kernels, run(): pl.pallas_call(kernel, in_specs=[SCALAR] * len(scalars) + [RESIDENT] * le...  45.3 us
    ppermute x8, starting transfers between devices, to_previous(): return lax.ppermute(value, 'mp', [((i + 1) % MP, i) for i in range(MP)])  19.6 us
    ppermute x7, starting transfers between devices, sent(): return lax.ppermute(value, 'seq', pairs)  17.3 us
    ppermute x8, waiting for transfers between devices, to_next(): return lax.ppermute(value, 'mp', [(i, (i + 1) % MP) for i in range(MP)])  11.9 us
    pallas_call x1, Pallas kernels, project(): pl.pallas_call(project_kernel, in_specs=[SCALAR] + [RESIDENT] * 6 + [anyw...  6.82 us
    ppermute x7, waiting for transfers between devices, sent(): return lax.ppermute(value, 'seq', pairs)  6.49 us
    ppermute x2, starting transfers between devices, exchange(): from_left = lax.ppermute(to_right, 'seq', [(i, i + 1) for i in range(ends)])  6.09 us
    ppermute x1, waiting for transfers between devices, gather_direct(): far = lax.ppermute(share, 'mp', [(i, (i + 2) % MP) for i in range(MP)])  5.59 us
  transfers between devices with their start and end apart: 28, of which 9 were waited for; matrix products, arithmetic and copies ran while one was open for 0% of the time, Pallas kernels for 27%

profile of v2, /device:TPU:0, one launch (start us, length us, event | category | flops | bytes accessed | tf_op | source)
XLA Modules:
  0.0 140.2 jit_solution(421206512275393216)
XLA Ops:
  3.8 2.2 %collective-permute-start = (bf16[512,256]{1,0:T(8,128)(2,1)S(1)}, bf16[512,256]{1,0:T(8,128)(2,1)S(1)}, u32[]{:S(2)}, u32[]{:S(2)}) collective-permute-start(bf16[512,256]{1,0:T(8,128)(2,1)S(1)} %get-tuple-element.113), channel_id=1, source_target_pairs={{1,0},{2,1},{3,2},{0,3},{5,4},{6,5},{7,6},{4,7},{9,8},{10,9},{11,1... | collective-permute-start | bytes 786440 | tf_op jit(solution)/shard_map/ppermute | solution.py:765
  8.0 5.0 %collective-permute-done.3.t3b = bf16[512,256]{1,0:T(8,128)(2,1)S(1)} collective-permute-done((bf16[512,256]{1,0:T(8,128)(2,1)S(1)}, bf16[512,256]{1,0:T(8,128)(2,1)S(1)}, u32[]{:S(2)}, u32[]{:S(2)}) %collective-permute-start.3) | collective-permute-done | bytes 262176 | tf_op jit(solution)/shard_map/ppermute | solution.py:761
  13.0 3.3 %collective-permute-start.2 = (bf16[512,256]{1,0:T(8,128)(2,1)S(1)}, bf16[512,256]{1,0:T(8,128)(2,1)S(1)}, u32[]{:S(2)}, u32[]{:S(2)}) collective-permute-start(bf16[512,256]{1,0:T(8,128)(2,1)S(1)} %collective-permute-done.t1a), channel_id=1, source_target_pairs={{1,0},{2,1},{3,2},{0,3},{5,4},{6,5},{7,6},{4,7},{9,8},{10,9},{11,1... | collective-permute-start | bytes 786440 | tf_op jit(solution)/shard_map/ppermute | solution.py:765
  16.5 2.1 %collective-permute-done.1.t1b = bf16[512,256]{1,0:T(8,128)(2,1)S(1)} collective-permute-done((bf16[512,256]{1,0:T(8,128)(2,1)S(1)}, bf16[512,256]{1,0:T(8,128)(2,1)S(1)}, u32[]{:S(2)}, u32[]{:S(2)}) %collective-permute-start.1) | collective-permute-done | bytes 262176 | tf_op jit(solution)/shard_map/ppermute | solution.py:765
  19.3 4.1 %collective-permute-done.4.t2b = bf16[512,256]{1,0:T(8,128)(2,1)S(1)} collective-permute-done((bf16[512,256]{1,0:T(8,128)(2,1)S(1)}, bf16[512,256]{1,0:T(8,128)(2,1)S(1)}, u32[]{:S(2)}, u32[]{:S(2)}) %collective-permute-start.4) | collective-permute-done | bytes 262176 | tf_op jit(solution)/shard_map/ppermute | solution.py:761
  27.7 6.8 %project.1 = (f32[8,256]{1,0:T(8,128)S(1)}, bf16[1792,256]{1,0:T(8,128)(2,1)S(1)}, bf16[2,1792,256]{2,1,0:T(8,128)(2,1)S(1)}, bf16[2,768,256]{2,1,0:T(8,128)(2,1...) custom-call(s32[4]{0:T(128)S(1)} %pad_add_fusion.place, bf16[512,256]{1,0:T(8,128)(2,1)S(1)} %collective-permute-done.t1a, ...), custom_call_target="tpu_custom_call" | custom-call | flops 1000000 | bytes 10000 | tf_op jit(solution)/shard_map/project/pallas_call | solution.py:186
  37.8 3.2 %collective-permute-start.13 = (bf16[1024,256]{1,0:T(8,128)(2,1)}, bf16[1024,256]{1,0:T(8,128)(2,1)}, u32[]{:S(2)}, u32[]{:S(2)}) collective-permute-start(bf16[1024,256]{1,0:T(8,128)(2,1)} %g0.1), channel_id=1, source_target_pairs={{0,2},{1,3},{2,0},{3,1},{4,6},{5,7},{6,4},{7,5},{8,10},{9,11},{10,... | collective-permute-start | bytes 1572872 | tf_op jit(solution)/shard_map/ppermute | solution.py:778
  42.2 3.8 %forward_inner.1 = (f32[512,256]{1,0:T(8,128)S(1)}, f32[2,8,256]{2,1,0:T(8,128)S(1)}) custom-call(f32[2]{0:T(128)S(1)} %pad_maximum_fusion.bias_ref, bf16[1792,256]{1,0:T(8,128)(2,1)S(1)} %get-tuple-element.59.q, bf16[2,1792,256]{2,1,0:T(8,128)(2,1)S(1)} %get-tuple-element.60.kv), custom_call_target="tpu_custom_call" | custom-call | flops 1000000 | bytes 10000 | tf_op jit(solution)/shard_map/forward_inner/pallas_call | solution.py:68
  46.0 7.4 %forward_edge.1 = (bf16[1024,256]{1,0:T(8,128)(2,1)S(1)}, f32[2,24,256]{2,1,0:T(8,128)S(1)}) custom-call(f32[2]{0:T(128)S(1)} %pad_maximum_fusion.bias_ref, bf16[1792,256]{1,0:T(8,128)(2,1)S(1)} %get-tuple-element.59.q, bf16[2,1792,256]{2,1,0:T(8,128)(2,1)S(1)} %get-tuple-element.60.kv, bf16[2,768,256]{2,1,0:T(8,128)(2,1)S(1)} %collective-permute-done.6.from_left, ...), custom_call_target="tpu_custom_call" | custom-call | flops 1000000 | bytes 10000 | tf_op jit(solution)/shard_map/forward_edge/pallas_call | solution.py:68
  55.7 2.3 %collective-permute-start.9 = (bf16[1024,256]{1,0:T(8,128)(2,1)S(1)}, bf16[1024,256]{1,0:T(8,128)(2,1)S(1)}, u32[]{:S(2)}, u32[]{:S(2)}) collective-permute-start(bf16[1024,256]{1,0:T(8,128)(2,1)S(1)} %get-tuple-element.67), channel_id=1, source_target_pairs={{1,0},{2,1},{3,2},{0,3},{5,4},{6,5},{7,6},{4,7},{9,8},{10,9},{11,1... | collective-permute-start | bytes 1572872 | tf_op jit(solution)/shard_map/ppermute | solution.py:765
  57.9 5.6 %collective-permute-done.13.g2 = bf16[1024,256]{1,0:T(8,128)(2,1)} collective-permute-done((bf16[1024,256]{1,0:T(8,128)(2,1)}, bf16[1024,256]{1,0:T(8,128)(2,1)}, u32[]{:S(2)}, u32[]{:S(2)}) %collective-permute-start.13) | collective-permute-done | bytes 524320 | tf_op jit(solution)/shard_map/ppermute | solution.py:778
  64.5 3.2 %cotangent.1.grads = bf16[1792,256]{1,0:T(8,128)(2,1)S(1)} custom-call(s32[4]{0:T(128)S(1)} %pad_add_fusion.place, bf16[1024,256]{1,0:T(8,128)(2,1)S(1)} %copy-done.6, bf16[1024,256]{1,0:T(8,128)(2,1)} %collective-permute-done.12.g1, bf16[1024,256]{1,0:T(8,128)(2,1)} %collective-permute-done.13.g2, bf16[1024,256]{1,0:T(8,128)(2,1)} %collective-permute-done.14.g3, ...), custom_call_target="tpu_custom_call" | custom-call | flops 1000000 | bytes 10000 | tf_op jit(solution)/shard_map/cotangent/pallas_call | solution.py:68
  67.8 10.5 %edge_backward.1 = (f32[1024,256]{1,0:T(8,128)S(1)}, f32[2,1024,256]{2,1,0:T(8,128)S(1)}, bf16[2,768,256]{2,1,0:T(8,128)(2,1)S(1)}, bf16[2,768,256]{2,1,0:T(8,128)(2,1)S(1)}) custom-call(f32[2]{0:T(128)S(1)} %pad_maximum_fusion.bias_ref, f32[2,24,256]{2,1,0:T(8,128)S(1)} %get-tuple-element.78.stats, bf16[1792,256]{1,0:T(8,128)(2,1)S(1)} %get-tuple-element.59.q, ...), custom_call_target="tpu_custom_call" | custom-call | flops 1000000 | bytes 10000 | tf_op jit(solution)/shard_map/edge_backward/pallas_call | solution.py:68
  78.3 4.8 %collective-permute-start.15 = (bf16[2,768,256]{2,1,0:T(8,128)(2,1)S(1)}, bf16[2,768,256]{2,1,0:T(8,128)(2,1)S(1)}, u32[]{:S(2)}, u32[]{:S(2)}) collective-permute-start(bf16[2,768,256]{2,1,0:T(8,128)(2,1)S(1)} %get-tuple-element.85), channel_id=1, source_target_pairs={{0,4},{4,8},{8,12},{12,16},{16,20},{20,24},{24,28},{28,32},{32,36}... | collective-permute-start | bytes 2359304 | tf_op jit(solution)/shard_map/ppermute | solution.py:785
  84.7 3.2 %collective-permute-start.11 = (bf16[512,256]{1,0:T(8,128)(2,1)S(1)}, bf16[512,256]{1,0:T(8,128)(2,1)S(1)}, u32[]{:S(2)}, u32[]{:S(2)}) collective-permute-start(bf16[512,256]{1,0:T(8,128)(2,1)S(1)} %get-tuple-element.71), channel_id=1, source_target_pairs={{1,0},{2,1},{3,2},{0,3},{5,4},{6,5},{7,6},{4,7},{9,8},{10,9},{11,1... | collective-permute-start | bytes 786440 | tf_op jit(solution)/shard_map/ppermute | solution.py:765
  90.0 5.4 %inner_backward.1 = (bf16[1024,256]{1,0:T(8,128)(2,1)S(1)}, f32[2,1024,256]{2,1,0:T(8,128)S(1)}) custom-call(f32[2]{0:T(128)S(1)} %pad_maximum_fusion.bias_ref, f32[2,8,256]{2,1,0:T(8,128)S(1)} %get-tuple-element.72.stats, bf16[1792,256]{1,0:T(8,128)(2,1)S(1)} %get-tuple-element.59.q, bf16[2,1792,256]{2,1,0:T(8,128)(2,1)S(1)} %get-tuple-element.60.kv, ...), custom_call_target="tpu_custom_call" | custom-call | flops 1000000 | bytes 10000 | tf_op jit(solution)/shard_map/inner_backward/pallas_call | solution.py:68
  95.5 3.7 %input_terms.1 = (bf16[1024,768]{1,0:T(8,128)(2,1)S(1)}, bf16[16,256]{1,0:T(8,128)(2,1)S(1)}, bf16[1024,256]{1,0:T(8,128)(2,1)S(1)}, bf16[512,256]{1,0:T(8,128)(...) custom-call(s32[4]{0:T(128)S(1)} %pad_add_fusion.place, ...), custom_call_target="tpu_custom_call" | custom-call | flops 1000000 | bytes 10000 | tf_op jit(solution)/shard_map/input_terms/pallas_call | solution.py:68
  99.3 2.7 %inner_terms.1 = (bf16[512,1024]{1,0:T(8,128)(2,1)S(1)}, bf16[512,1024]{1,0:T(8,128)(2,1)S(1)}) custom-call(s32[4]{0:T(128)S(1)} %pad_add_fusion.place, bf16[1024,1024]{1,0:T(8,128)(2,1)S(1)} %copy-done, bf16[1024,768]{1,0:T(8,128)(2,1)S(1)} %get-tuple-element.97.d_proj, bf16[1024,256]{1,0:T(8,128)(2,1)S(1)} %outer_terms.1.outer), custom_call_target="tpu_custom_call" | custom-call | flops 1000000 | bytes 10000 | tf_op jit(solution)/shard_map/inner_terms/pallas_call | solution.py:68
  102.0 3.9 %collective-permute-start.21 = (bf16[512,1024]{1,0:T(8,128)(2,1)S(1)}, bf16[512,1024]{1,0:T(8,128)(2,1)S(1)}, u32[]{:S(2)}, u32[]{:S(2)}) collective-permute-start(bf16[512,1024]{1,0:T(8,128)(2,1)S(1)} %get-tuple-element.99), channel_id=1, source_target_pairs={{0,4},{4,0},{8,12},{12,8},{16,20},{20,16},{24,28},{28,24},{32,36},... | collective-permute-start | bytes 3145736 | tf_op jit(solution)/shard_map/ppermute | solution.py:747
  106.1 3.0 %collective-permute-start.18 = (bf16[1040,256]{1,0:T(8,128)(2,1)S(1)}, bf16[1040,256]{1,0:T(8,128)(2,1)S(1)}, u32[]{:S(2)}, u32[]{:S(2)}) collective-permute-start(bf16[1040,256]{1,0:T(8,128)(2,1)S(1)} %get-tuple-element.90), channel_id=1, source_target_pairs={{1,0},{2,1},{3,2},{0,3},{5,4},{6,5},{7,6},{4,7},{9,8},{10,9},{11,1... | collective-permute-start | bytes 1597448 | tf_op jit(solution)/shard_map/ppermute | solution.py:765
  111.5 5.5 %collective-permute-start.23 = (bf16[128,1024]{1,0:T(8,128)(2,1)S(1)}, bf16[128,1024]{1,0:T(8,128)(2,1)S(1)}, u32[]{:S(2)}, u32[]{:S(2)}) collective-permute-start(bf16[128,1024]{1,0:T(8,128)(2,1)S(1)} %get-tuple-element.102), channel_id=1, source_target_pairs={{0,24},{4,28},{8,0},{12,4},{16,8},{20,12},{24,16},{28,20},{32,56},... | collective-permute-start | bytes 786440 | tf_op jit(solution)/shard_map/ppermute | solution.py:747
  118.3 2.8 %collective-permute-done.17.l1 = bf16[1040,256]{1,0:T(8,128)(2,1)S(1)} collective-permute-done((bf16[1040,256]{1,0:T(8,128)(2,1)S(1)}, bf16[1040,256]{1,0:T(8,128)(2,1)S(1)}, u32[]{:S(2)}, u32[]{:S(2)}) %collective-permute-start.17) | collective-permute-done | bytes 532512 | tf_op jit(solution)/shard_map/ppermute | solution.py:761
  122.0 2.6 %collective-permute-start.20 = (bf16[512,256]{1,0:T(8,128)(2,1)S(1)}, bf16[512,256]{1,0:T(8,128)(2,1)S(1)}, u32[]{:S(2)}, u32[]{:S(2)}) collective-permute-start(bf16[512,256]{1,0:T(8,128)(2,1)S(1)} %get-tuple-element.94), channel_id=1, source_target_pairs={{1,0},{2,1},{3,2},{0,3},{5,4},{6,5},{7,6},{4,7},{9,8},{10,9},{11,1... | collective-permute-start | bytes 786440 | tf_op jit(solution)/shard_map/ppermute | solution.py:765
  124.6 3.3 %collective-permute-done.23.c = bf16[128,1024]{1,0:T(8,128)(2,1)S(1)} collective-permute-done((bf16[128,1024]{1,0:T(8,128)(2,1)S(1)}, bf16[128,1024]{1,0:T(8,128)(2,1)S(1)}, u32[]{:S(2)}, u32[]{:S(2)}) %collective-permute-start.23) | collective-permute-done | bytes 262176 | tf_op jit(solution)/shard_map/ppermute | solution.py:747
  (78 shorter events, 38.9 us)
Async XLA Ops:
  1.7 11.3 %collective-permute-start.3 = (bf16[512,256]{1,0:T(8,128)(2,1)S(1)}, bf16[512,256]{1,0:T(8,128)(2,1)S(1)}, u32[]{:S(2)}, u32[]{:S(2)}) collective-permute-start(bf16[512,256]{1,0:T(8,128)(2,1)S(1)} %get-tuple-element.112), channel_id=1, source_target_pairs={{0,1},{1,2},{2,3},{3,0},{4,5},{5,6},{6,7},{7,4},{8,9},{9,10},{10,1... | collective-permute-start | bytes 786440 | tf_op jit(solution)/shard_map/ppermute | solution.py:761
  3.8 9.3 %collective-permute-start = (bf16[512,256]{1,0:T(8,128)(2,1)S(1)}, bf16[512,256]{1,0:T(8,128)(2,1)S(1)}, u32[]{:S(2)}, u32[]{:S(2)}) collective-permute-start(bf16[512,256]{1,0:T(8,128)(2,1)S(1)} %get-tuple-element.113), channel_id=1, source_target_pairs={{1,0},{2,1},{3,2},{0,3},{5,4},{6,5},{7,6},{4,7},{9,8},{10,9},{11,1... | collective-permute-start | bytes 786440 | tf_op jit(solution)/shard_map/ppermute | solution.py:765
  6.0 12.6 %collective-permute-start.1 = (bf16[512,256]{1,0:T(8,128)(2,1)S(1)}, bf16[512,256]{1,0:T(8,128)(2,1)S(1)}, u32[]{:S(2)}, u32[]{:S(2)}) collective-permute-start(bf16[512,256]{1,0:T(8,128)(2,1)S(1)} %get-tuple-element.112), channel_id=1, source_target_pairs={{1,0},{2,1},{3,2},{0,3},{5,4},{6,5},{7,6},{4,7},{9,8},{10,9},{11,1... | collective-permute-start | bytes 786440 | tf_op jit(solution)/shard_map/ppermute | solution.py:765
  7.9 10.7 %collective-permute-start.5 = (bf16[512,256]{1,0:T(8,128)(2,1)S(1)}, bf16[512,256]{1,0:T(8,128)(2,1)S(1)}, u32[]{:S(2)}, u32[]{:S(2)}) collective-permute-start(bf16[512,256]{1,0:T(8,128)(2,1)S(1)} %get-tuple-element.113), channel_id=1, source_target_pairs={{0,1},{1,2},{2,3},{3,0},{4,5},{5,6},{6,7},{7,4},{8,9},{9,10},{10,1... | collective-permute-start | bytes 786440 | tf_op jit(solution)/shard_map/ppermute | solution.py:761
  13.0 10.4 %collective-permute-start.4 = (bf16[512,256]{1,0:T(8,128)(2,1)S(1)}, bf16[512,256]{1,0:T(8,128)(2,1)S(1)}, u32[]{:S(2)}, u32[]{:S(2)}) collective-permute-start(bf16[512,256]{1,0:T(8,128)(2,1)S(1)} %collective-permute-done.3.t3b), channel_id=1, source_target_pairs={{0,1},{1,2},{2,3},{3,0},{4,5},{5,6},{6,7},{7,4},{8,9},{9,10},{10,1... | collective-permute-start | bytes 786440 | tf_op jit(solution)/shard_map/ppermute | solution.py:761
  13.0 11.1 %collective-permute-start.2 = (bf16[512,256]{1,0:T(8,128)(2,1)S(1)}, bf16[512,256]{1,0:T(8,128)(2,1)S(1)}, u32[]{:S(2)}, u32[]{:S(2)}) collective-permute-start(bf16[512,256]{1,0:T(8,128)(2,1)S(1)} %collective-permute-done.t1a), channel_id=1, source_target_pairs={{1,0},{2,1},{3,2},{0,3},{5,4},{6,5},{7,6},{4,7},{9,8},{10,9},{11,1... | collective-permute-start | bytes 786440 | tf_op jit(solution)/shard_map/ppermute | solution.py:765
  34.5 11.4 %collective-permute-start.6 = (bf16[2,768,256]{2,1,0:T(8,128)(2,1)}, bf16[2,768,256]{2,1,0:T(8,128)(2,1)S(1)}, u32[]{:S(2)}, u32[]{:S(2)}) collective-permute-start(bf16[2,768,256]{2,1,0:T(8,128)(2,1)} %get-tuple-element.61), channel_id=1, source_target_pairs={{0,4},{4,8},{8,12},{12,16},{16,20},{20,24},{24,28},{28,32},{32,36}... | collective-permute-start | bytes 2359304 | tf_op jit(solution)/shard_map/ppermute | solution.py:785
  35.9 10.1 %collective-permute-start.7 = (bf16[2,768,256]{2,1,0:T(8,128)(2,1)}, bf16[2,768,256]{2,1,0:T(8,128)(2,1)}, u32[]{:S(2)}, u32[]{:S(2)}) collective-permute-start(bf16[2,768,256]{2,1,0:T(8,128)(2,1)} %get-tuple-element.62), channel_id=1, source_target_pairs={{4,0},{8,4},{12,8},{16,12},{20,16},{24,20},{28,24},{32,28},{36,32}... | collective-permute-start | bytes 2359304 | tf_op jit(solution)/shard_map/ppermute | solution.py:786
  37.2 20.8 %collective-permute-start.14 = (bf16[1024,256]{1,0:T(8,128)(2,1)}, bf16[1024,256]{1,0:T(8,128)(2,1)}, u32[]{:S(2)}, u32[]{:S(2)}) collective-permute-start(bf16[1024,256]{1,0:T(8,128)(2,1)} %g0.1), channel_id=1, source_target_pairs={{0,1},{1,2},{2,3},{3,0},{4,5},{5,6},{6,7},{7,4},{8,9},{9,10},{10,1... | collective-permute-start | bytes 1572872 | tf_op jit(solution)/shard_map/ppermute | solution.py:761
  37.8 25.7 %collective-permute-start.13 = (bf16[1024,256]{1,0:T(8,128)(2,1)}, bf16[1024,256]{1,0:T(8,128)(2,1)}, u32[]{:S(2)}, u32[]{:S(2)}) collective-permute-start(bf16[1024,256]{1,0:T(8,128)(2,1)} %g0.1), channel_id=1, source_target_pairs={{0,2},{1,3},{2,0},{3,1},{4,6},{5,7},{6,4},{7,5},{8,10},{9,11},{10,... | collective-permute-start | bytes 1572872 | tf_op jit(solution)/shard_map/ppermute | solution.py:778
  41.0 23.5 %collective-permute-start.12 = (bf16[1024,256]{1,0:T(8,128)(2,1)}, bf16[1024,256]{1,0:T(8,128)(2,1)}, u32[]{:S(2)}, u32[]{:S(2)}) collective-permute-start(bf16[1024,256]{1,0:T(8,128)(2,1)} %g0.1), channel_id=1, source_target_pairs={{1,0},{2,1},{3,2},{0,3},{5,4},{6,5},{7,6},{4,7},{9,8},{10,9},{11,1... | collective-permute-start | bytes 1572872 | tf_op jit(solution)/shard_map/ppermute | solution.py:765
  54.6 29.8 %collective-permute-start.8 = (bf16[1024,256]{1,0:T(8,128)(2,1)S(1)}, bf16[1024,256]{1,0:T(8,128)(2,1)S(1)}, u32[]{:S(2)}, u32[]{:S(2)}) collective-permute-start(bf16[1024,256]{1,0:T(8,128)(2,1)S(1)} %get-tuple-element.66), channel_id=1, source_target_pairs={{0,1},{1,2},{2,3},{3,0},{4,5},{5,6},{6,7},{7,4},{8,9},{9,10},{10,1... | collective-permute-start | bytes 1572872 | tf_op jit(solution)/shard_map/ppermute | solution.py:761
  55.7 28.7 %collective-permute-start.9 = (bf16[1024,256]{1,0:T(8,128)(2,1)S(1)}, bf16[1024,256]{1,0:T(8,128)(2,1)S(1)}, u32[]{:S(2)}, u32[]{:S(2)}) collective-permute-start(bf16[1024,256]{1,0:T(8,128)(2,1)S(1)} %get-tuple-element.67), channel_id=1, source_target_pairs={{1,0},{2,1},{3,2},{0,3},{5,4},{6,5},{7,6},{4,7},{9,8},{10,9},{11,1... | collective-permute-start | bytes 1572872 | tf_op jit(solution)/shard_map/ppermute | solution.py:765
  78.3 17.2 %collective-permute-start.15 = (bf16[2,768,256]{2,1,0:T(8,128)(2,1)S(1)}, bf16[2,768,256]{2,1,0:T(8,128)(2,1)S(1)}, u32[]{:S(2)}, u32[]{:S(2)}) collective-permute-start(bf16[2,768,256]{2,1,0:T(8,128)(2,1)S(1)} %get-tuple-element.85), channel_id=1, source_target_pairs={{0,4},{4,8},{8,12},{12,16},{16,20},{20,24},{24,28},{28,32},{32,36}... | collective-permute-start | bytes 2359304 | tf_op jit(solution)/shard_map/ppermute | solution.py:785
  83.1 12.4 %collective-permute-start.16 = (bf16[2,768,256]{2,1,0:T(8,128)(2,1)S(1)}, bf16[2,768,256]{2,1,0:T(8,128)(2,1)S(1)}, u32[]{:S(2)}, u32[]{:S(2)}) collective-permute-start(bf16[2,768,256]{2,1,0:T(8,128)(2,1)S(1)} %get-tuple-element.86), channel_id=1, source_target_pairs={{4,0},{8,4},{12,8},{16,12},{20,16},{24,20},{28,24},{32,28},{36,32}... | collective-permute-start | bytes 2359304 | tf_op jit(solution)/shard_map/ppermute | solution.py:786
  84.5 10.9 %collective-permute-start.10 = (bf16[512,256]{1,0:T(8,128)(2,1)S(1)}, bf16[512,256]{1,0:T(8,128)(2,1)S(1)}, u32[]{:S(2)}, u32[]{:S(2)}) collective-permute-start(bf16[512,256]{1,0:T(8,128)(2,1)S(1)} %get-tuple-element.70), channel_id=1, source_target_pairs={{0,1},{1,2},{2,3},{3,0},{4,5},{5,6},{6,7},{7,4},{8,9},{9,10},{10,1... | collective-permute-start | bytes 786440 | tf_op jit(solution)/shard_map/ppermute | solution.py:761
  84.7 10.8 %collective-permute-start.11 = (bf16[512,256]{1,0:T(8,128)(2,1)S(1)}, bf16[512,256]{1,0:T(8,128)(2,1)S(1)}, u32[]{:S(2)}, u32[]{:S(2)}) collective-permute-start(bf16[512,256]{1,0:T(8,128)(2,1)S(1)} %get-tuple-element.71), channel_id=1, source_target_pairs={{1,0},{2,1},{3,2},{0,3},{5,4},{6,5},{7,6},{4,7},{9,8},{10,9},{11,1... | collective-permute-start | bytes 786440 | tf_op jit(solution)/shard_map/ppermute | solution.py:765
  105.8 15.3 %collective-permute-start.17 = (bf16[1040,256]{1,0:T(8,128)(2,1)S(1)}, bf16[1040,256]{1,0:T(8,128)(2,1)S(1)}, u32[]{:S(2)}, u32[]{:S(2)}) collective-permute-start(bf16[1040,256]{1,0:T(8,128)(2,1)S(1)} %get-tuple-element.89), channel_id=1, source_target_pairs={{0,1},{1,2},{2,3},{3,0},{4,5},{5,6},{6,7},{7,4},{8,9},{9,10},{10,1... | collective-permute-start | bytes 1597448 | tf_op jit(solution)/shard_map/ppermute | solution.py:761
  106.1 15.1 %collective-permute-start.18 = (bf16[1040,256]{1,0:T(8,128)(2,1)S(1)}, bf16[1040,256]{1,0:T(8,128)(2,1)S(1)}, u32[]{:S(2)}, u32[]{:S(2)}) collective-permute-start(bf16[1040,256]{1,0:T(8,128)(2,1)S(1)} %get-tuple-element.90), channel_id=1, source_target_pairs={{1,0},{2,1},{3,2},{0,3},{5,4},{6,5},{7,6},{4,7},{9,8},{10,9},{11,1... | collective-permute-start | bytes 1597448 | tf_op jit(solution)/shard_map/ppermute | solution.py:765
  109.9 14.7 %collective-permute-start.22 = (bf16[128,1024]{1,0:T(8,128)(2,1)S(1)}, bf16[128,1024]{1,0:T(8,128)(2,1)S(1)}, u32[]{:S(2)}, u32[]{:S(2)}) collective-permute-start(bf16[128,1024]{1,0:T(8,128)(2,1)S(1)} %get-tuple-element.101), channel_id=1, source_target_pairs={{0,8},{4,12},{8,16},{12,20},{16,24},{20,28},{24,0},{28,4},{32,40},... | collective-permute-start | bytes 786440 | tf_op jit(solution)/shard_map/ppermute | solution.py:747
  111.5 16.4 %collective-permute-start.23 = (bf16[128,1024]{1,0:T(8,128)(2,1)S(1)}, bf16[128,1024]{1,0:T(8,128)(2,1)S(1)}, u32[]{:S(2)}, u32[]{:S(2)}) collective-permute-start(bf16[128,1024]{1,0:T(8,128)(2,1)S(1)} %get-tuple-element.102), channel_id=1, source_target_pairs={{0,24},{4,28},{8,0},{12,4},{16,8},{20,12},{24,16},{28,20},{32,56},... | collective-permute-start | bytes 786440 | tf_op jit(solution)/shard_map/ppermute | solution.py:747
  117.0 12.7 %collective-permute-start.24 = (bf16[128,1024]{1,0:T(8,128)(2,1)S(1)}, bf16[128,1024]{1,0:T(8,128)(2,1)S(1)}, u32[]{:S(2)}, u32[]{:S(2)}) collective-permute-start(bf16[128,1024]{1,0:T(8,128)(2,1)S(1)} %get-tuple-element.103), channel_id=1, source_target_pairs={{0,16},{4,20},{8,24},{12,28},{16,0},{20,4},{24,8},{28,12},{32,48},... | collective-permute-start | bytes 786440 | tf_op jit(solution)/shard_map/ppermute | solution.py:747
  121.3 15.2 %collective-permute-start.19 = (bf16[528,256]{1,0:T(8,128)(2,1)S(1)}, bf16[528,256]{1,0:T(8,128)(2,1)S(1)}, u32[]{:S(2)}, u32[]{:S(2)}) collective-permute-start(bf16[528,256]{1,0:T(8,128)(2,1)S(1)} %get-tuple-element.93), channel_id=1, source_target_pairs={{0,1},{1,2},{2,3},{3,0},{4,5},{5,6},{6,7},{7,4},{8,9},{9,10},{10,1... | collective-permute-start | bytes 811016 | tf_op jit(solution)/shard_map/ppermute | solution.py:761
  122.0 14.4 %collective-permute-start.20 = (bf16[512,256]{1,0:T(8,128)(2,1)S(1)}, bf16[512,256]{1,0:T(8,128)(2,1)S(1)}, u32[]{:S(2)}, u32[]{:S(2)}) collective-permute-start(bf16[512,256]{1,0:T(8,128)(2,1)S(1)} %get-tuple-element.94), channel_id=1, source_target_pairs={{1,0},{2,1},{3,2},{0,3},{5,4},{6,5},{7,6},{4,7},{9,8},{10,9},{11,1... | collective-permute-start | bytes 786440 | tf_op jit(solution)/shard_map/ppermute | solution.py:765
  (17 other events, 94.8 us)

commit v3 on v2

--- a/solution.py
+++ b/solution.py
@@ -56,6 +56,8 @@
 
 
 SMALL = pl.CostEstimate(flops=10**6, bytes_accessed=10**4, transcendentals=0)
+LARGE = pl.CostEstimate(flops=4 * 10**9, bytes_accessed=10**4, transcendentals=0)
+LAST = pl.CostEstimate(flops=1 * 10**9, bytes_accessed=10**4, transcendentals=0)
 SCALAR = pl.BlockSpec(memory_space=pltpu.SMEM)
 RESIDENT = pl.BlockSpec(memory_space=pltpu.VMEM)
 
@@ -64,7 +66,7 @@
     return jax.ShapeDtypeStruct(shape, dtype)
 
 
-def run(kernel, name, limit_mib, scalars, inputs, outputs, scratch=()):
+def run(kernel, name, limit_mib, scalars, inputs, outputs, scratch=(), cost=SMALL):
     return pl.pallas_call(
         kernel,
         in_specs=[SCALAR] * len(scalars) + [RESIDENT] * len(inputs),
@@ -72,7 +74,7 @@
         out_shape=outputs,
         scratch_shapes=list(scratch),
         compiler_params=pltpu.CompilerParams(vmem_limit_bytes=limit_mib * 2**20),
-        cost_estimate=SMALL,
+        cost_estimate=cost,
         name=name,
     )(*scalars, *inputs)
 
@@ -81,17 +83,6 @@
     return slice(block * BLOCK, (block + 1) * BLOCK)
 
 
-def read_shares(step, refs):
-    own, *halves = refs
-    at = block_rows(step % 2)
-    return [own[block_rows(step), :]] + [ref[at, :] for ref in halves[step // 2 :: 2]]
-
-
-def level_rows(level, rows=4 * BLOCK):
-    first = sum(rows // 2**n for n in range(level))
-    return slice(first, first + rows // 2**level)
-
-
 ALL_ROWS = 7 * BLOCK
 LEVEL_BLOCK = (0, 4, 6)
 
@@ -105,16 +96,29 @@
 
 
 def project_kernel(
-    place, t1a, t1b, t2a, t2b, t3a, t3b, t0_hbm, wq_hbm, wk_hbm, wv_hbm,
+    place, t1a_any, t1b_any, t2a_any, t2b_any, t3a_any, t3b_any,
+    t0_hbm, wq_hbm, wk_hbm, wv_hbm,
     inverse, q, kv, to_left, to_right, normed_hbm,
-    t0, wq, wk, wv, normed, in_sems, out_sems,
+    t0, t1, t2, t3, wq, wk, wv, normed, in_sems, out_sems,
 ):
     me = place[0]
     width = t0.shape[1]
-    sources = (t0_hbm, wq_hbm, wk_hbm, wv_hbm)
+    low, high = pl.ds(0, 2 * BLOCK), pl.ds(2 * BLOCK, 2 * BLOCK)
+    moves = [
+        (t0_hbm, t0),
+        (t1a_any, t1.at[low]),
+        (t2a_any, t2.at[low]),
+        (t3a_any, t3.at[low]),
+        (t1b_any, t1.at[high]),
+        (t2b_any, t2.at[high]),
+        (t3b_any, t3.at[high]),
+        (wq_hbm, wq),
+        (wk_hbm, wk),
+        (wv_hbm, wv),
+    ]
     loads = [
         pltpu.make_async_copy(source, target, in_sems.at[n])
-        for n, (source, target) in enumerate(zip(sources, (t0, wq, wk, wv)))
+        for n, (source, target) in enumerate(moves)
     ]
     for load in loads:
         load.start()
@@ -122,12 +126,13 @@
     quarter = pool_matrix(BLOCK // 4, 4, 0.25)
     inverse[4:8, :] = jnp.zeros((4, BLOCK), F32)
     stores = []
-    for step in range(4):
+
+    def normalise(step):
+        if step in (0, 2):
+            for load in loads[0:4] if step == 0 else loads[4:7]:
+                load.wait()
         rows = block_rows(step)
-        if step == 0:
-            loads[0].wait()
-        read = read_shares(step, (t0, t1a, t1b, t2a, t2b, t3a, t3b))
-        shares = [share.astype(F32) for share in read]
+        shares = [share[rows, :].astype(F32) for share in (t0, t1, t2, t3)]
         squares = shares[0] * shares[0]
         for share in shares[1:]:
             squares = squares + share * share
@@ -140,9 +145,13 @@
         store = pltpu.make_async_copy(normed.at[rows], normed_hbm.at[rows], out_sems.at[step])
         store.start()
         stores.append(store)
+        return parts
+
+    def spread(step, parts):
         if step == 0:
-            for load in loads[1:]:
+            for load in loads[7:]:
                 load.wait()
+        rows = block_rows(step)
         sums = [None, None, None]
         for r, part in enumerate(parts):
             w_rows = share_rows(me, r, width)
@@ -169,6 +178,12 @@
             edge[n, edge_mid, :] = mid[1 + n]
             if step in (0, 3):
                 edge[n, 0:BLOCK, :] = fine[1 + n]
+
+    parts = normalise(0)
+    for step in range(4):
+        following = normalise(step + 1) if step < 3 else None
+        spread(step, parts)
+        parts = following
     for store in stores:
         store.wait()
 
@@ -185,7 +200,7 @@
     ]
     return pl.pallas_call(
         project_kernel,
-        in_specs=[SCALAR] + [RESIDENT] * 6 + [anywhere] * 4,
+        in_specs=[SCALAR] + [anywhere] * 10,
         out_specs=[RESIDENT] * 5 + [anywhere],
         out_shape=[
             out((8, width), F32),
@@ -195,10 +210,10 @@
             edge,
             pltpu.HBM((rows, MP * width), BF16),
         ],
-        scratch_shapes=[share] * 4
+        scratch_shapes=[share] * 7
         + [
             pltpu.VMEM((rows, MP * width), BF16),
-            pltpu.SemaphoreType.DMA((4,)),
+            pltpu.SemaphoreType.DMA((10,)),
             pltpu.SemaphoreType.DMA((4,)),
         ],
         compiler_params=pltpu.CompilerParams(vmem_limit_bytes=20 * 2**20),
@@ -496,7 +511,7 @@
     width = q.shape[1]
     outputs = [held((2 * BLOCK, width), F32), held((width // PAIR, 8, BLOCK), F32)]
     scratch = [turned(EXT_BLOCKS[0]), pltpu.VMEM((4 * BLOCK, PAIR), F32)]
-    return run(forward_inner_kernel, "forward_inner", 12, [bias], [q, kv], outputs, scratch)
+    return run(forward_inner_kernel, "forward_inner", 12, [bias], [q, kv], outputs, scratch, LARGE)
 
 
 def forward_edge(bias, q, kv, from_left, from_right, inner):
@@ -526,25 +541,11 @@
     inputs = [stats, q, kv, d_att, dq_f, d_kv]
     outputs = [held((rows, width), BF16), held((2, rows, width), F32)]
     scratch = [turned(EXT_BLOCKS[0]), pltpu.VMEM((rows, PAIR), F32)]
-    return run(inner_units_kernel, "inner_backward", 12, [bias], inputs, outputs, scratch)
-
-
-def store_terms(step, terms, own, keep_right, keep_left, right, left):
-    own[block_rows(step), :] = terms[0]
-    low, high = block_rows(step % 2), block_rows(2 + step % 2)
-    if step < 2:
-        keep_right[low, :] = terms[1]
-        right[high, :] = terms[2]
-        left[low, :] = terms[3]
-    else:
-        right[low, :] = terms[1]
-        left[high, :] = terms[2]
-        keep_left[low, :] = terms[3]
+    return run(inner_units_kernel, "inner_backward", 12, [bias], inputs, outputs, scratch, LARGE)
 
 
 def term_outputs(rows, width, extra=0):
-    lengths = [rows, rows // 2, rows // 2, rows + extra, rows + extra]
-    return [held((n, width), BF16) for n in lengths]
+    return [held((rows, width), BF16)] + [held((rows + extra, width), BF16)] * (MP - 1)
 
 
 def out_terms_kernel(place, attended, w_out, *outs):
@@ -552,8 +553,9 @@
     width = attended.shape[1]
     for step in range(4):
         rows = attended[block_rows(step), :]
-        terms = [nn(rows, w_out[:, share_rows(me, r, width)]).astype(BF16) for r in range(MP)]
-        store_terms(step, terms, *outs)
+        for r, out in enumerate(outs):
+            term = nn(rows, w_out[:, share_rows(me, r, width)])
+            out[block_rows(step), :] = term.astype(BF16)
 
 
 def out_terms(place, attended, w_out):
@@ -563,7 +565,7 @@
 
 def input_terms_kernel(
     place, d_query, d_kv, from_left, from_right, normed, wq, wk, wv, d_proj,
-    dots, own, keep_right, keep_left, right, left, dot_rows,
+    dots, own, one, two, three, dot_rows,
 ):
     me = place[0]
     width = d_query.shape[1]
@@ -586,12 +588,12 @@
             grads.append(total.astype(BF16))
         for n, grad in enumerate(grads):
             d_proj[rows, n * width : (n + 1) * width] = grad
-        terms, dot = [], None
-        for r in range(MP):
+        dot = None
+        for r, out in enumerate((own, one, two, three)):
             at = share_rows(me, r, width)
             term = nt(grads[0], wq[at, :]) + nt(grads[1], wk[at, :]) + nt(grads[2], wv[at, :])
             term = term.astype(BF16)
-            terms.append(term)
+            out[rows, :] = term
             part = term.astype(F32) * normed[rows, r * width : (r + 1) * width].astype(F32)
             dot = part if dot is None else dot + part
         dot = as_row(jnp.sum(dot, axis=1, keepdims=True))
@@ -599,11 +601,10 @@
         second = (dot - first).astype(BF16).astype(F32)
         for n, piece in enumerate((first, second, dot - first - second)):
             dot_rows[4 * n + step : 4 * n + step + 1, :] = piece
-        store_terms(step, terms, own, keep_right, keep_left, right, left)
     pieces = dot_rows[...].astype(BF16)
     dots[...] = pieces
-    right[4 * BLOCK :, :] = pieces
-    left[4 * BLOCK :, :] = pieces
+    for out in (one, two, three):
+        out[4 * BLOCK :, :] = pieces
 
 
 def input_terms(place, d_query, d_kv, from_left, from_right, normed, wq, wk, wv):
@@ -615,62 +616,42 @@
     return run(input_terms_kernel, "input_terms", 16, [place], inputs, outputs, scratch)
 
 
-def relay_kernel(keep_right, keep_left, l1, r1, onward_right, onward_left):
-    half = keep_right.shape[0]
-    passed = l1[half : 2 * half, :].astype(F32)
-    onward_right[0:half, :] = (keep_right[...].astype(F32) + passed).astype(BF16)
-    passed = r1[half : 2 * half, :].astype(F32)
-    onward_left[...] = (keep_left[...].astype(F32) + passed).astype(BF16)
-    if onward_right.shape[0] > half:
-        onward_right[half:, :] = l1[2 * half :, :]
-
-
-def relay(keep_right, keep_left, l1, r1):
-    half, width = keep_right.shape
-    extra = l1.shape[0] - 2 * half
-    outputs = [held((half + extra, width), BF16), held((half, width), BF16)]
-    return run(relay_kernel, "relay", 4, [], [keep_right, keep_left, l1, r1], outputs)
-
-
-def summed(own, l1, r1, l2, r2):
-    half = r2.shape[0]
-    low = r1[0:half, :].astype(F32) + l2[0:half, :].astype(F32)
-    high = l1[0:half, :].astype(F32) + r2[...].astype(F32)
-    return own[0:half, :].astype(F32) + low, own[half:, :].astype(F32) + high
-
-
-def finish_out_kernel(own, l1, r1, l2, r2, result):
-    half = r2.shape[0]
-    low, high = summed(own, l1, r1, l2, r2)
-    result[0:half, :] = low.astype(BF16)
-    result[half:, :] = high.astype(BF16)
-
-
-def finish_out(own, l1, r1, l2, r2):
-    outputs = [jax.ShapeDtypeStruct(own.shape, BF16)]
-    return run(finish_out_kernel, "finish_out", 8, [], [own, l1, r1, l2, r2], outputs)[0]
-
-
-def finish_grad_kernel(own, l1, r1, l2, r2, tokens, inverse, dots, result):
+def sum_terms(own, received, at):
+    total = own[at, :].astype(F32)
+    for term in received:
+        total = total + term[at, :].astype(F32)
+    return total
+
+
+def finish_out_kernel(own, one, two, three, result):
+    for b in range(4):
+        at = block_rows(b)
+        result[at, :] = sum_terms(own, (one, two, three), at).astype(BF16)
+
+
+def finish_out(own, received):
+    outputs = [held(own.shape, BF16)]
+    return run(finish_out_kernel, "finish_out", 8, [], [own, *received], outputs)[0]
+
+
+def finish_grad_kernel(own, one, two, three, tokens, inverse, dots, result):
     rows, width = own.shape
-    half = r2.shape[0]
     pieces = dots[...].astype(F32)
-    for message, first in ((l1, rows), (r1, rows), (l2, half)):
-        pieces = pieces + message[first : first + DOT_ROWS, :].astype(F32)
+    for term in (one, two, three):
+        pieces = pieces + term[rows:, :].astype(F32)
     means = (pieces[0:4] + pieces[4:8] + pieces[8:12]) / (MP * width)
-    halves = summed(own, l1, r1, l2, r2)
     for b in range(rows // BLOCK):
+        at = block_rows(b)
         mean = as_column(means[b : b + 1, :])
         inv = as_column(inverse[b : b + 1, :])
-        at = block_rows(b)
-        total = halves[b // 2][block_rows(b % 2), :]
+        total = sum_terms(own, (one, two, three), at)
         result[at, :] = inv * (total - tokens[at, :].astype(F32) * inv * mean)
 
 
-def finish_grad(own, l1, r1, l2, r2, tokens, inverse, dots):
-    inputs = [own, l1, r1, l2, r2, tokens, inverse, dots]
-    outputs = [jax.ShapeDtypeStruct(own.shape, F32)]
-    return run(finish_grad_kernel, "finish_grad", 8, [], inputs, outputs)[0]
+def finish_grad(own, received, tokens, inverse, dots):
+    inputs = [own, *received, tokens, inverse, dots]
+    outputs = [held(own.shape, F32)]
+    return run(finish_grad_kernel, "finish_grad", 8, [], inputs, outputs, (), LAST)[0]
 
 
 def outer_kernel(g0, g1, g2, g3, attended, result):
@@ -709,17 +690,19 @@
 
 
 def pair_sum_kernel(place, mine, got, *outs):
-    x = place[2]
+    z, core, x, y = place[0], place[1], place[2], place[3]
     for d, out in enumerate(outs):
-        for y in range(4):
-            rows = pl.ds(pl.multiple_of((4 * y + ((x + d) & 3)) * 32, 32), 32)
+        for n in range(4):
+            chunk = jnp.where(core == 0, 4 * n + ((x + d) & 3), 4 * ((y + d - z + 4) & 3) + n)
+            rows = pl.ds(pl.multiple_of(chunk * 32, 32), 32)
             total = mine[rows, :].astype(F32) + got[rows, :].astype(F32)
-            out[32 * y : 32 * (y + 1), :] = total.astype(BF16)
+            out[32 * n : 32 * (n + 1), :] = total.astype(BF16)
 
 
 def row_sum_kernel(place, a, b, c, d, *refs):
     *outs, total = refs
-    first = place[3] - place[0] + 4
+    z, core, x, y = place[0], place[1], place[2], place[3]
+    first = jnp.where(core == 0, y - z + 4, x)
     total[...] = (
         a[...].astype(F32) + b[...].astype(F32) + c[...].astype(F32) + d[...].astype(F32)
     ).astype(BF16)
@@ -739,20 +722,25 @@
 def sum_over_seq(place, mine, other):
     cols = mine.shape[1]
 
-    def sent(value, dy, dx, dc):
+    def sent(value, stage, d):
         pairs = []
         for i in range(32):
-            c, a, b = i % 2, (i // 2) % 4, i // 8
-            pairs.append((i, (((b + dy) % 4) * 4 + (a + dx) % 4) * 2 + (c + dc) % 2))
+            core, x, y = i % 2, (i // 2) % 4, i // 8
+            if stage == core:
+                x = (x + d) % 4
+            else:
+                y = (y + d) % 4
+            pairs.append((i, (y * 4 + x) * 2 + core))
         return lax.ppermute(value, "seq", pairs)
 
+    got = lax.ppermute(other, "seq", [(i, i ^ 1) for i in range(32)])
     parts = [held((128, cols), BF16)] * 4
-    parts = run(pair_sum_kernel, "pair_sum", 6, [place], [mine, sent(other, 0, 0, 1)], parts)
-    parts = [parts[0]] + [sent(parts[d], 0, d, 0) for d in (1, 3, 2)]
+    parts = run(pair_sum_kernel, "pair_sum", 6, [place], [mine, got], parts)
+    parts = [parts[0]] + [sent(parts[d], 0, d) for d in (1, 2, 3)]
     rows = [held((32, cols), BF16)] * 4
     scratch = [pltpu.VMEM((128, cols), BF16)]
     rows = run(row_sum_kernel, "row_sum", 4, [place], parts, rows, scratch)
-    rows = [rows[0]] + [sent(rows[d], d, 0, 0) for d in (1, 3, 2)]
+    rows = [rows[0]] + [sent(rows[d], 1, d) for d in (1, 2, 3)]
     outputs = [held((32, cols // 4), F32)] * 4
     return run(last_sum_kernel, "last_sum", 4, [], rows, outputs)
 
@@ -774,9 +762,12 @@
     return [share, after_low, after_high, far_low, far_high, before_low, before_high]
 
 
-def gather_direct(share):
-    far = lax.ppermute(share, "mp", [(i, (i + 2) % MP) for i in range(MP)])
-    return [share, to_previous(share), far, to_next(share)]
+def turned_by(value, step):
+    return lax.ppermute(value, "mp", [(i, (i + step) % MP) for i in range(MP)])
+
+
+def sum_over_mp(terms):
+    return [turned_by(term, step) for step, term in zip((1, 2, 3), terms)]
 
 
 def exchange(to_left, to_right):
@@ -805,38 +796,35 @@
         ]
     )
     token_shares = gather_shares(tokens)
-    sent_grad = tied(grad_out, *token_shares)
-    grad_shares = gather_direct(sent_grad)
-    grad_shares[0] = grad_out
+    near_grad = tied(grad_out, *(token_shares[n] for n in (1, 2, 5, 6)))
+    far_grad = tied(grad_out, *token_shares)
+    far = turned_by(far_grad, 2)
+    grad_shares = [grad_out, to_previous(near_grad), far, to_next(near_grad)]
     inverse, q, kv, to_left, to_right, normed = project(
         me, token_shares, w_query, w_key, w_value
     )
     from_left, from_right = exchange(to_left, to_right)
-    inner_out, inner_stats = forward_inner(bias, q, kv)
+    near_q = tied(q, grad_shares[1], grad_shares[3])
+    inner_out, inner_stats = forward_inner(bias, near_q, kv)
     attended, stats = forward_edge(bias, q, kv, from_left, from_right, inner_out)
-    grad_shares = tied(grad_shares, attended)
-    out_own, keep_right, keep_left, right, left = out_terms(me, attended, w_out)
-    l1, r1 = to_next(right), to_previous(left)
+    out_own, *terms = out_terms(me, attended, w_out)
+    out_received = sum_over_mp(terms)
+    grad_shares = tied(grad_shares, out_own)
     d_att = cotangent(me, grad_shares, w_out)
     dq_f, d_kv, to_left, to_right = edge_backward(
         bias, stats, q, kv, from_left, from_right, d_att
     )
-    onward_right, onward_left = relay(keep_right, keep_left, l1, r1)
-    l2, r2 = to_next(onward_right), to_previous(onward_left)
     from_left, from_right = exchange(to_left, to_right)
-    dq_f = tied(dq_f, onward_right, onward_left)
+    dq_f = tied(dq_f, *out_received)
     d_query, d_kv = inner_backward(bias, inner_stats, q, kv, d_att, dq_f, d_kv)
-    d_query = tied(d_query, l2, r2)
-    d_proj, dots, own, keep_right, keep_left, right, left = input_terms(
+    d_proj, dots, own, *terms = input_terms(
         me, d_query, d_kv, from_left, from_right, normed, w_query, w_key, w_value
     )
-    attn_out = finish_out(out_own, l1, r1, l2, r2)
-    l1, r1 = to_next(right), to_previous(left)
+    received = sum_over_mp(terms)
+    attn_out = finish_out(out_own, out_received)
     outer = outer_terms(grad_shares, attended)
     mine, other = inner_terms(me, normed, d_proj, outer)
-    onward_right, onward_left = relay(keep_right, keep_left, l1, r1)
-    l2, r2 = to_next(onward_right), to_previous(onward_left)
-    grad_tokens = finish_grad(own, l1, r1, l2, r2, tokens, inverse, dots)
+    grad_tokens = finish_grad(own, received, tokens, inverse, dots)
     *weight_grads, grad_w_out = sum_over_seq(me, mine, other)
     return (attn_out, grad_tokens, *weight_grads, grad_w_out.T)
 

time: 141 us -> 139 us (0.986)
  waiting for transfers between devices: 27.2 us -> 15.2 us
  starting transfers between devices: 53.7 us -> 63.3 us
    ppermute x1 -> x8, starting transfers between devices: 3.23 us -> 14.8 us  [the longest x7 10.1 us: turned_by(): return lax.ppermute(value, 'mp', [(i, (i + step) % MP) for i in range(MP)])]
    ppermute x8 -> x4, starting transfers between devices: 19.6 us -> 8.95 us  [to_previous(): return lax.ppermute(value, 'mp', [((i + 1) % MP, i) for i in range(MP)])]
    ppermute x2, starting transfers between devices: 6.09 us -> 12.3 us  [exchange(): from_left = lax.ppermute(to_right, 'seq', [(i, i + 1) for i in range(ends)])]
    ppermute x1 -> x8, waiting for transfers between devices: 5.59 us -> 0.02 us  [the longest x7 0.02 us: turned_by(): return lax.ppermute(value, 'mp', [(i, (i + step) % MP) for i in range(MP)])]
    ppermute x8 -> x4, waiting for transfers between devices: 11.9 us -> 6.55 us  [to_next(): return lax.ppermute(value, 'mp', [(i, (i + 1) % MP) for i in range(MP)])]
    ppermute x7 -> x6, starting transfers between devices: 17.3 us -> 20.4 us  [sent(): return lax.ppermute(value, 'seq', pairs)]
    ppermute x8 -> x4, waiting for transfers between devices: 3.16 us -> 2.23 us  [to_previous(): return lax.ppermute(value, 'mp', [((i + 1) % MP, i) for i in range(MP)])]
    ppermute x8 -> x4, starting transfers between devices: 4.91 us -> 4.05 us  [to_next(): return lax.ppermute(value, 'mp', [(i, (i + 1) % MP) for i in range(MP)])]
  transfers between devices with their start and end apart: 28 -> 26, of which waited for: 9 -> 7; matrix products, arithmetic and copies ran while one was open for 0% -> 0% of each run, Pallas kernels for 27% -> 33%
where the time goes in v3:
time: 139 us; the launch traced here: 137 us
  starting transfers between devices  63.3 us (46%)
  Pallas kernels  51.7 us (37%)
  waiting for transfers between devices  15.2 us (11%)
  local copies, waits for them, and re-layouts  6.06 us (4%)
    pallas_call x14, Pallas kernels, run(): pl.pallas_call(kernel, in_specs=[SCALAR] * len(scalars) + [RESIDENT] * le...  44.8 us
    ppermute x6, starting transfers between devices, sent(): return lax.ppermute(value, 'seq', pairs)  20.4 us
    ppermute x2, starting transfers between devices, exchange(): from_left = lax.ppermute(to_right, 'seq', [(i, i + 1) for i in range(ends)])  12.3 us
    ppermute x7, starting transfers between devices, turned_by(): return lax.ppermute(value, 'mp', [(i, (i + step) % MP) for i in range(MP)])  10.1 us
    ppermute x4, starting transfers between devices, to_previous(): return lax.ppermute(value, 'mp', [((i + 1) % MP, i) for i in range(MP)])  8.95 us
    pallas_call x1, Pallas kernels, project(): pl.pallas_call(project_kernel, in_specs=[SCALAR] + [anywhere] * 10, out_s...  6.96 us
    ppermute x4, waiting for transfers between devices, to_next(): return lax.ppermute(value, 'mp', [(i, (i + 1) % MP) for i in range(MP)])  6.55 us
    ppermute x6, waiting for transfers between devices, sent(): return lax.ppermute(value, 'seq', pairs)  6.36 us
  transfers between devices with their start and end apart: 26, of which 7 were waited for; matrix products, arithmetic and copies ran while one was open for 0% of the time, Pallas kernels for 33%

profile of v3, /device:TPU:0, one launch (start us, length us, event | category | flops | bytes accessed | tf_op | source)
XLA Modules:
  0.0 137.3 jit_solution(1962477561554007461)
XLA Ops:
  1.7 2.1 %collective-permute-start.3 = (bf16[512,256]{1,0:T(8,128)(2,1)S(1)}, bf16[512,256]{1,0:T(8,128)(2,1)S(1)}, u32[]{:S(2)}, u32[]{:S(2)}) collective-permute-start(bf16[512,256]{1,0:T(8,128)(2,1)S(1)} %get-tuple-element.102), channel_id=1, source_target_pairs={{0,1},{1,2},{2,3},{3,0},{4,5},{5,6},{6,7},{7,4},{8,9},{9,10},{10,1... | collective-permute-start | bytes 786440 | tf_op jit(solution)/shard_map/ppermute | solution.py:749
  3.8 2.2 %collective-permute-start = (bf16[512,256]{1,0:T(8,128)(2,1)S(1)}, bf16[512,256]{1,0:T(8,128)(2,1)S(1)}, u32[]{:S(2)}, u32[]{:S(2)}) collective-permute-start(bf16[512,256]{1,0:T(8,128)(2,1)S(1)} %get-tuple-element.103), channel_id=1, source_target_pairs={{1,0},{2,1},{3,2},{0,3},{5,4},{6,5},{7,6},{4,7},{9,8},{10,9},{11,1... | collective-permute-start | bytes 786440 | tf_op jit(solution)/shard_map/ppermute | solution.py:753
  6.0 1.9 %collective-permute-start.1 = (bf16[512,256]{1,0:T(8,128)(2,1)S(1)}, bf16[512,256]{1,0:T(8,128)(2,1)S(1)}, u32[]{:S(2)}, u32[]{:S(2)}) collective-permute-start(bf16[512,256]{1,0:T(8,128)(2,1)S(1)} %get-tuple-element.102), channel_id=1, source_target_pairs={{1,0},{2,1},{3,2},{0,3},{5,4},{6,5},{7,6},{4,7},{9,8},{10,9},{11,1... | collective-permute-start | bytes 786440 | tf_op jit(solution)/shard_map/ppermute | solution.py:753
  8.0 5.0 %collective-permute-done.3.t3b_any = bf16[512,256]{1,0:T(8,128)(2,1)S(1)} collective-permute-done((bf16[512,256]{1,0:T(8,128)(2,1)S(1)}, bf16[512,256]{1,0:T(8,128)(2,1)S(1)}, u32[]{:S(2)}, u32[]{:S(2)}) %collective-permute-start.3) | collective-permute-done | bytes 262176 | tf_op jit(solution)/shard_map/ppermute | solution.py:749
  13.0 3.3 %collective-permute-start.2 = (bf16[512,256]{1,0:T(8,128)(2,1)S(1)}, bf16[512,256]{1,0:T(8,128)(2,1)S(1)}, u32[]{:S(2)}, u32[]{:S(2)}) collective-permute-start(bf16[512,256]{1,0:T(8,128)(2,1)S(1)} %collective-permute-done.t1a_any), channel_id=1, source_target_pairs={{1,0},{2,1},{3,2},{0,3},{5,4},{6,5},{7,6},{4,7},{9,8},{10,9},{11,1... | collective-permute-start | bytes 786440 | tf_op jit(solution)/shard_map/ppermute | solution.py:753
  16.4 2.2 %collective-permute-done.1.t1b_any = bf16[512,256]{1,0:T(8,128)(2,1)S(1)} collective-permute-done((bf16[512,256]{1,0:T(8,128)(2,1)S(1)}, bf16[512,256]{1,0:T(8,128)(2,1)S(1)}, u32[]{:S(2)}, u32[]{:S(2)}) %collective-permute-start.1) | collective-permute-done | bytes 262176 | tf_op jit(solution)/shard_map/ppermute | solution.py:753
  28.5 7.0 %project.1 = (f32[8,256]{1,0:T(8,128)S(1)}, bf16[1792,256]{1,0:T(8,128)(2,1)S(1)}, bf16[2,1792,256]{2,1,0:T(8,128)(2,1)S(1)}, bf16[2,768,256]{2,1,0:T(8,128)(2,1...) custom-call(s32[4]{0:T(128)S(1)} %pad_add_fusion.place, bf16[512,256]{1,0:T(8,128)(2,1)S(1)} %collective-permute-done.t1a_any, ...), custom_call_target="tpu_custom_call" | custom-call | flops 1000000 | bytes 10000 | tf_op jit(solution)/shard_map/project/pallas_call | solution.py:201
  38.1 2.9 %collective-permute-start.13 = (bf16[1024,256]{1,0:T(8,128)(2,1)}, bf16[1024,256]{1,0:T(8,128)(2,1)S(1)}, u32[]{:S(2)}, u32[]{:S(2)}) collective-permute-start(bf16[1024,256]{1,0:T(8,128)(2,1)} %g0.1), channel_id=1, source_target_pairs={{0,2},{1,3},{2,0},{3,1},{4,6},{5,7},{6,4},{7,5},{8,10},{9,11},{10,... | collective-permute-start | bytes 1572872 | tf_op jit(solution)/shard_map/ppermute | solution.py:766
  41.1 3.8 %forward_inner.1 = (f32[512,256]{1,0:T(8,128)S(1)}, f32[2,8,256]{2,1,0:T(8,128)S(1)}) custom-call(f32[2]{0:T(128)S(1)} %pad_maximum_fusion.bias_ref, bf16[1792,256]{1,0:T(8,128)(2,1)S(1)} %get-tuple-element.59.q, bf16[2,1792,256]{2,1,0:T(8,128)(2,1)S(1)} %get-tuple-element.55.kv), custom_call_target="tpu_custom_call" | custom-call | flops 4000000000 | bytes 10000 | tf_op jit(solution)/shard_map/forward_inner/pallas_call | solution.py:70
  45.0 7.4 %forward_edge.1 = (bf16[1024,256]{1,0:T(8,128)(2,1)S(1)}, f32[2,24,256]{2,1,0:T(8,128)S(1)}) custom-call(f32[2]{0:T(128)S(1)} %pad_maximum_fusion.bias_ref, bf16[1792,256]{1,0:T(8,128)(2,1)S(1)} %get-tuple-element.59.q, bf16[2,1792,256]{2,1,0:T(8,128)(2,1)S(1)} %get-tuple-element.55.kv, bf16[2,768,256]{2,1,0:T(8,128)(2,1)S(1)} %collective-permute-done.6.from_left, ...), custom_call_target="tpu_custom_call" | custom-call | flops 1000000 | bytes 10000 | tf_op jit(solution)/shard_map/forward_edge/pallas_call | solution.py:70
  57.5 3.1 %cotangent.1.grads = bf16[1792,256]{1,0:T(8,128)(2,1)S(1)} custom-call(s32[4]{0:T(128)S(1)} %pad_add_fusion.place, bf16[1024,256]{1,0:T(8,128)(2,1)S(1)} %copy-done.6, bf16[1024,256]{1,0:T(8,128)(2,1)} %collective-permute-done.8.g1, bf16[1024,256]{1,0:T(8,128)(2,1)S(1)} %collective-permute-done.13.g2, bf16[1024,256]{1,0:T(8,128)(2,1)} %collective-permute-done.9.g3, ...), custom_call_target="tpu_custom_call" | custom-call | flops 1000000 | bytes 10000 | tf_op jit(solution)/shard_map/cotangent/pallas_call | solution.py:70
  60.5 10.5 %edge_backward.1 = (f32[1024,256]{1,0:T(8,128)S(1)}, f32[2,1024,256]{2,1,0:T(8,128)S(1)}, bf16[2,768,256]{2,1,0:T(8,128)(2,1)S(1)}, bf16[2,768,256]{2,1,0:T(8,128)(2,1)S(1)}) custom-call(f32[2]{0:T(128)S(1)} %pad_maximum_fusion.bias_ref, f32[2,24,256]{2,1,0:T(8,128)S(1)} %get-tuple-element.72.stats, bf16[1792,256]{1,0:T(8,128)(2,1)S(1)} %get-tuple-element.59.q, ...), custom_call_target="tpu_custom_call" | custom-call | flops 1000000 | bytes 10000 | tf_op jit(solution)/shard_map/edge_backward/pallas_call | solution.py:70
  71.1 10.9 %collective-permute-start.14 = (bf16[2,768,256]{2,1,0:T(8,128)(2,1)S(1)}, bf16[2,768,256]{2,1,0:T(8,128)(2,1)S(1)}, u32[]{:S(2)}, u32[]{:S(2)}) collective-permute-start(bf16[2,768,256]{2,1,0:T(8,128)(2,1)S(1)} %get-tuple-element.78), channel_id=1, source_target_pairs={{0,4},{4,8},{8,12},{12,16},{16,20},{20,24},{24,28},{28,32},{32,36}... | collective-permute-start | bytes 2359304 | tf_op jit(solution)/shard_map/ppermute | solution.py:776
  83.5 2.0 %outer_terms.1.outer = bf16[1024,256]{1,0:T(8,128)(2,1)S(1)} custom-call(bf16[1024,256]{1,0:T(8,128)(2,1)S(1)} %copy-done.6, bf16[1024,256]{1,0:T(8,128)(2,1)} %collective-permute-done.8.g1, bf16[1024,256]{1,0:T(8,128)(2,1)S(1)} %collective-permute-done.13.g2, bf16[1024,256]{1,0:T(8,128)(2,1)} %collective-permute-done.9.g3, ...), custom_call_target="tpu_custom_call" | custom-call | flops 1000000 | bytes 10000 | tf_op jit(solution)/shard_map/outer_terms/pallas_call | solution.py:70
  85.6 5.5 %inner_backward.1 = (bf16[1024,256]{1,0:T(8,128)(2,1)S(1)}, f32[2,1024,256]{2,1,0:T(8,128)S(1)}) custom-call(f32[2]{0:T(128)S(1)} %pad_maximum_fusion.bias_ref, f32[2,8,256]{2,1,0:T(8,128)S(1)} %get-tuple-element.66.stats, bf16[1792,256]{1,0:T(8,128)(2,1)S(1)} %get-tuple-element.59.q, bf16[2,1792,256]{2,1,0:T(8,128)(2,1)S(1)} %get-tuple-element.55.kv, ...), custom_call_target="tpu_custom_call" | custom-call | flops 4000000000 | bytes 10000 | tf_op jit(solution)/shard_map/inner_backward/pallas_call | solution.py:70
  91.1 3.7 %input_terms.1 = (bf16[1024,768]{1,0:T(8,128)(2,1)S(1)}, bf16[16,256]{1,0:T(8,128)(2,1)S(1)}, bf16[1024,256]{1,0:T(8,128)(2,1)S(1)}, bf16[1040,256]{1,0:T(8,128)...) custom-call(s32[4]{0:T(128)S(1)} %pad_add_fusion.place, ...), custom_call_target="tpu_custom_call" | custom-call | flops 1000000 | bytes 10000 | tf_op jit(solution)/shard_map/input_terms/pallas_call | solution.py:70
  94.8 2.6 %inner_terms.1 = (bf16[512,1024]{1,0:T(8,128)(2,1)S(1)}, bf16[512,1024]{1,0:T(8,128)(2,1)S(1)}) custom-call(s32[4]{0:T(128)S(1)} %pad_add_fusion.place, bf16[1024,1024]{1,0:T(8,128)(2,1)S(1)} %copy-done, bf16[1024,768]{1,0:T(8,128)(2,1)S(1)} %get-tuple-element.87.d_proj, bf16[1024,256]{1,0:T(8,128)(2,1)S(1)} %outer_terms.1.outer), custom_call_target="tpu_custom_call" | custom-call | flops 1000000 | bytes 10000 | tf_op jit(solution)/shard_map/inner_terms/pallas_call | solution.py:70
  97.4 4.7 %collective-permute-start.19 = (bf16[512,1024]{1,0:T(8,128)(2,1)S(1)}, bf16[512,1024]{1,0:T(8,128)(2,1)S(1)}, u32[]{:S(2)}, u32[]{:S(2)}) collective-permute-start(bf16[512,1024]{1,0:T(8,128)(2,1)S(1)} %get-tuple-element.89), channel_id=1, source_target_pairs={{0,4},{4,0},{8,12},{12,8},{16,20},{20,16},{24,28},{28,24},{32,36},... | collective-permute-start | bytes 3145736 | tf_op jit(solution)/shard_map/ppermute | solution.py:736
  107.9 7.0 %collective-permute-start.21 = (bf16[128,1024]{1,0:T(8,128)(2,1)S(1)}, bf16[128,1024]{1,0:T(8,128)(2,1)S(1)}, u32[]{:S(2)}, u32[]{:S(2)}) collective-permute-start(bf16[128,1024]{1,0:T(8,128)(2,1)S(1)} %get-tuple-element.92), channel_id=1, source_target_pairs={{0,16},{4,68},{8,24},{12,76},{16,0},{20,84},{24,8},{28,92},{32,48}... | collective-permute-start | bytes 786440 | tf_op jit(solution)/shard_map/ppermute | solution.py:734
  114.8 2.9 %collective-permute-done.20.b = bf16[128,1024]{1,0:T(8,128)(2,1)S(1)} collective-permute-done((bf16[128,1024]{1,0:T(8,128)(2,1)S(1)}, bf16[128,1024]{1,0:T(8,128)(2,1)S(1)}, u32[]{:S(2)}, u32[]{:S(2)}) %collective-permute-start.20) | collective-permute-done | bytes 262176 | tf_op jit(solution)/shard_map/ppermute | solution.py:734
  117.7 2.0 %collective-permute-start.22 = (bf16[128,1024]{1,0:T(8,128)(2,1)S(1)}, bf16[128,1024]{1,0:T(8,128)(2,1)S(1)}, u32[]{:S(2)}, u32[]{:S(2)}) collective-permute-start(bf16[128,1024]{1,0:T(8,128)(2,1)S(1)} %get-tuple-element.93), channel_id=1, source_target_pairs={{0,24},{4,100},{8,0},{12,108},{16,8},{20,116},{24,16},{28,124},{32... | collective-permute-start | bytes 786440 | tf_op jit(solution)/shard_map/ppermute | solution.py:734
  122.0 2.1 %collective-permute-done.22.d = bf16[128,1024]{1,0:T(8,128)(2,1)S(1)} collective-permute-done((bf16[128,1024]{1,0:T(8,128)(2,1)S(1)}, bf16[128,1024]{1,0:T(8,128)(2,1)S(1)}, u32[]{:S(2)}, u32[]{:S(2)}) %collective-permute-start.22) | collective-permute-done | bytes 262176 | tf_op jit(solution)/shard_map/ppermute | solution.py:734
  126.5 4.6 %collective-permute-start.24 = (bf16[32,1024]{1,0:T(8,128)(2,1)S(1)}, bf16[32,1024]{1,0:T(8,128)(2,1)S(1)}, u32[]{:S(2)}, u32[]{:S(2)}) collective-permute-start(bf16[32,1024]{1,0:T(8,128)(2,1)S(1)} %get-tuple-element.96), channel_id=1, source_target_pairs={{0,64},{4,20},{8,72},{12,28},{16,80},{20,4},{24,88},{28,12},{32,96... | collective-permute-start | bytes 196616 | tf_op jit(solution)/shard_map/ppermute | solution.py:734
  131.1 3.7 %collective-permute-start.25 = (bf16[32,1024]{1,0:T(8,128)(2,1)S(1)}, bf16[32,1024]{1,0:T(8,128)(2,1)S(1)}, u32[]{:S(2)}, u32[]{:S(2)}) collective-permute-start(bf16[32,1024]{1,0:T(8,128)(2,1)S(1)} %get-tuple-element.97), channel_id=1, source_target_pairs={{0,96},{4,28},{8,104},{12,4},{16,112},{20,12},{24,120},{28,20},{32... | collective-permute-start | bytes 196616 | tf_op jit(solution)/shard_map/ppermute | solution.py:734
  (72 shorter events, 33.4 us)
Async XLA Ops:
  1.7 11.3 %collective-permute-start.3 = (bf16[512,256]{1,0:T(8,128)(2,1)S(1)}, bf16[512,256]{1,0:T(8,128)(2,1)S(1)}, u32[]{:S(2)}, u32[]{:S(2)}) collective-permute-start(bf16[512,256]{1,0:T(8,128)(2,1)S(1)} %get-tuple-element.102), channel_id=1, source_target_pairs={{0,1},{1,2},{2,3},{3,0},{4,5},{5,6},{6,7},{7,4},{8,9},{9,10},{10,1... | collective-permute-start | bytes 786440 | tf_op jit(solution)/shard_map/ppermute | solution.py:749
  3.8 9.3 %collective-permute-start = (bf16[512,256]{1,0:T(8,128)(2,1)S(1)}, bf16[512,256]{1,0:T(8,128)(2,1)S(1)}, u32[]{:S(2)}, u32[]{:S(2)}) collective-permute-start(bf16[512,256]{1,0:T(8,128)(2,1)S(1)} %get-tuple-element.103), channel_id=1, source_target_pairs={{1,0},{2,1},{3,2},{0,3},{5,4},{6,5},{7,6},{4,7},{9,8},{10,9},{11,1... | collective-permute-start | bytes 786440 | tf_op jit(solution)/shard_map/ppermute | solution.py:753
  6.0 12.6 %collective-permute-start.1 = (bf16[512,256]{1,0:T(8,128)(2,1)S(1)}, bf16[512,256]{1,0:T(8,128)(2,1)S(1)}, u32[]{:S(2)}, u32[]{:S(2)}) collective-permute-start(bf16[512,256]{1,0:T(8,128)(2,1)S(1)} %get-tuple-element.102), channel_id=1, source_target_pairs={{1,0},{2,1},{3,2},{0,3},{5,4},{6,5},{7,6},{4,7},{9,8},{10,9},{11,1... | collective-permute-start | bytes 786440 | tf_op jit(solution)/shard_map/ppermute | solution.py:753
  7.9 10.7 %collective-permute-start.5 = (bf16[512,256]{1,0:T(8,128)(2,1)S(1)}, bf16[512,256]{1,0:T(8,128)(2,1)S(1)}, u32[]{:S(2)}, u32[]{:S(2)}) collective-permute-start(bf16[512,256]{1,0:T(8,128)(2,1)S(1)} %get-tuple-element.103), channel_id=1, source_target_pairs={{0,1},{1,2},{2,3},{3,0},{4,5},{5,6},{6,7},{7,4},{8,9},{9,10},{10,1... | collective-permute-start | bytes 786440 | tf_op jit(solution)/shard_map/ppermute | solution.py:749
  13.0 11.2 %collective-permute-start.4 = (bf16[512,256]{1,0:T(8,128)(2,1)S(1)}, bf16[512,256]{1,0:T(8,128)(2,1)S(1)}, u32[]{:S(2)}, u32[]{:S(2)}) collective-permute-start(bf16[512,256]{1,0:T(8,128)(2,1)S(1)} %collective-permute-done.3.t3b_any), channel_id=1, source_target_pairs={{0,1},{1,2},{2,3},{3,0},{4,5},{5,6},{6,7},{7,4},{8,9},{9,10},{10,1... | collective-permute-start | bytes 786440 | tf_op jit(solution)/shard_map/ppermute | solution.py:749
  13.0 11.9 %collective-permute-start.2 = (bf16[512,256]{1,0:T(8,128)(2,1)S(1)}, bf16[512,256]{1,0:T(8,128)(2,1)S(1)}, u32[]{:S(2)}, u32[]{:S(2)}) collective-permute-start(bf16[512,256]{1,0:T(8,128)(2,1)S(1)} %collective-permute-done.t1a_any), channel_id=1, source_target_pairs={{1,0},{2,1},{3,2},{0,3},{5,4},{6,5},{7,6},{4,7},{9,8},{10,9},{11,1... | collective-permute-start | bytes 786440 | tf_op jit(solution)/shard_map/ppermute | solution.py:753
  19.3 21.8 %collective-permute-start.9 = (bf16[1024,256]{1,0:T(8,128)(2,1)}, bf16[1024,256]{1,0:T(8,128)(2,1)}, u32[]{:S(2)}, u32[]{:S(2)}) collective-permute-start(bf16[1024,256]{1,0:T(8,128)(2,1)} %g0.1), channel_id=1, source_target_pairs={{0,1},{1,2},{2,3},{3,0},{4,5},{5,6},{6,7},{7,4},{8,9},{9,10},{10,1... | collective-permute-start | bytes 1572872 | tf_op jit(solution)/shard_map/ppermute | solution.py:749
  21.2 19.9 %collective-permute-start.8 = (bf16[1024,256]{1,0:T(8,128)(2,1)}, bf16[1024,256]{1,0:T(8,128)(2,1)}, u32[]{:S(2)}, u32[]{:S(2)}) collective-permute-start(bf16[1024,256]{1,0:T(8,128)(2,1)} %g0.1), channel_id=1, source_target_pairs={{1,0},{2,1},{3,2},{0,3},{5,4},{6,5},{7,6},{4,7},{9,8},{10,9},{11,1... | collective-permute-start | bytes 1572872 | tf_op jit(solution)/shard_map/ppermute | solution.py:753
  35.5 9.4 %collective-permute-start.6 = (bf16[2,768,256]{2,1,0:T(8,128)(2,1)}, bf16[2,768,256]{2,1,0:T(8,128)(2,1)S(1)}, u32[]{:S(2)}, u32[]{:S(2)}) collective-permute-start(bf16[2,768,256]{2,1,0:T(8,128)(2,1)} %get-tuple-element.56), channel_id=1, source_target_pairs={{0,4},{4,8},{8,12},{12,16},{16,20},{20,24},{24,28},{28,32},{32,36}... | collective-permute-start | bytes 2359304 | tf_op jit(solution)/shard_map/ppermute | solution.py:776
  36.8 8.1 %collective-permute-start.7 = (bf16[2,768,256]{2,1,0:T(8,128)(2,1)}, bf16[2,768,256]{2,1,0:T(8,128)(2,1)}, u32[]{:S(2)}, u32[]{:S(2)}) collective-permute-start(bf16[2,768,256]{2,1,0:T(8,128)(2,1)} %get-tuple-element.57), channel_id=1, source_target_pairs={{4,0},{8,4},{12,8},{16,12},{20,16},{24,20},{28,24},{32,28},{36,32}... | collective-permute-start | bytes 2359304 | tf_op jit(solution)/shard_map/ppermute | solution.py:777
  38.1 19.3 %collective-permute-start.13 = (bf16[1024,256]{1,0:T(8,128)(2,1)}, bf16[1024,256]{1,0:T(8,128)(2,1)S(1)}, u32[]{:S(2)}, u32[]{:S(2)}) collective-permute-start(bf16[1024,256]{1,0:T(8,128)(2,1)} %g0.1), channel_id=1, source_target_pairs={{0,2},{1,3},{2,0},{3,1},{4,6},{5,7},{6,4},{7,5},{8,10},{9,11},{10,... | collective-permute-start | bytes 1572872 | tf_op jit(solution)/shard_map/ppermute | solution.py:766
  53.6 31.9 %collective-permute-start.10 = (bf16[1024,256]{1,0:T(8,128)(2,1)S(1)}, bf16[1024,256]{1,0:T(8,128)(2,1)S(1)}, u32[]{:S(2)}, u32[]{:S(2)}) collective-permute-start(bf16[1024,256]{1,0:T(8,128)(2,1)S(1)} %get-tuple-element.63), channel_id=1, source_target_pairs={{0,1},{1,2},{2,3},{3,0},{4,5},{5,6},{6,7},{7,4},{8,9},{9,10},{10,1... | collective-permute-start | bytes 1572872 | tf_op jit(solution)/shard_map/ppermute | solution.py:766
  54.5 31.0 %collective-permute-start.11 = (bf16[1024,256]{1,0:T(8,128)(2,1)S(1)}, bf16[1024,256]{1,0:T(8,128)(2,1)S(1)}, u32[]{:S(2)}, u32[]{:S(2)}) collective-permute-start(bf16[1024,256]{1,0:T(8,128)(2,1)S(1)} %get-tuple-element.64), channel_id=1, source_target_pairs={{0,2},{1,3},{2,0},{3,1},{4,6},{5,7},{6,4},{7,5},{8,10},{9,11},{10,... | collective-permute-start | bytes 1572872 | tf_op jit(solution)/shard_map/ppermute | solution.py:766
  56.4 29.1 %collective-permute-start.12 = (bf16[1024,256]{1,0:T(8,128)(2,1)S(1)}, bf16[1024,256]{1,0:T(8,128)(2,1)S(1)}, u32[]{:S(2)}, u32[]{:S(2)}) collective-permute-start(bf16[1024,256]{1,0:T(8,128)(2,1)S(1)} %get-tuple-element.65), channel_id=1, source_target_pairs={{0,3},{1,0},{2,1},{3,2},{4,7},{5,4},{6,5},{7,6},{8,11},{9,8},{10,9... | collective-permute-start | bytes 1572872 | tf_op jit(solution)/shard_map/ppermute | solution.py:766
  71.1 20.0 %collective-permute-start.14 = (bf16[2,768,256]{2,1,0:T(8,128)(2,1)S(1)}, bf16[2,768,256]{2,1,0:T(8,128)(2,1)S(1)}, u32[]{:S(2)}, u32[]{:S(2)}) collective-permute-start(bf16[2,768,256]{2,1,0:T(8,128)(2,1)S(1)} %get-tuple-element.78), channel_id=1, source_target_pairs={{0,4},{4,8},{8,12},{12,16},{16,20},{20,24},{24,28},{28,32},{32,36}... | collective-permute-start | bytes 2359304 | tf_op jit(solution)/shard_map/ppermute | solution.py:776
  82.0 9.1 %collective-permute-start.15 = (bf16[2,768,256]{2,1,0:T(8,128)(2,1)S(1)}, bf16[2,768,256]{2,1,0:T(8,128)(2,1)S(1)}, u32[]{:S(2)}, u32[]{:S(2)}) collective-permute-start(bf16[2,768,256]{2,1,0:T(8,128)(2,1)S(1)} %get-tuple-element.79), channel_id=1, source_target_pairs={{4,0},{8,4},{12,8},{16,12},{20,16},{24,20},{28,24},{32,28},{36,32}... | collective-permute-start | bytes 2359304 | tf_op jit(solution)/shard_map/ppermute | solution.py:777
  97.4 8.1 %collective-permute-start.19 = (bf16[512,1024]{1,0:T(8,128)(2,1)S(1)}, bf16[512,1024]{1,0:T(8,128)(2,1)S(1)}, u32[]{:S(2)}, u32[]{:S(2)}) collective-permute-start(bf16[512,1024]{1,0:T(8,128)(2,1)S(1)} %get-tuple-element.89), channel_id=1, source_target_pairs={{0,4},{4,0},{8,12},{12,8},{16,20},{20,16},{24,28},{28,24},{32,36},... | collective-permute-start | bytes 3145736 | tf_op jit(solution)/shard_map/ppermute | solution.py:736
  102.1 29.0 %collective-permute-start.16 = (bf16[1040,256]{1,0:T(8,128)(2,1)S(1)}, bf16[1040,256]{1,0:T(8,128)(2,1)S(1)}, u32[]{:S(2)}, u32[]{:S(2)}) collective-permute-start(bf16[1040,256]{1,0:T(8,128)(2,1)S(1)} %get-tuple-element.82), channel_id=1, source_target_pairs={{0,1},{1,2},{2,3},{3,0},{4,5},{5,6},{6,7},{7,4},{8,9},{9,10},{10,1... | collective-permute-start | bytes 1597448 | tf_op jit(solution)/shard_map/ppermute | solution.py:766
  102.8 31.9 %collective-permute-start.17 = (bf16[1040,256]{1,0:T(8,128)(2,1)S(1)}, bf16[1040,256]{1,0:T(8,128)(2,1)S(1)}, u32[]{:S(2)}, u32[]{:S(2)}) collective-permute-start(bf16[1040,256]{1,0:T(8,128)(2,1)S(1)} %get-tuple-element.83), channel_id=1, source_target_pairs={{0,2},{1,3},{2,0},{3,1},{4,6},{5,7},{6,4},{7,5},{8,10},{9,11},{10,... | collective-permute-start | bytes 1597448 | tf_op jit(solution)/shard_map/ppermute | solution.py:766
  103.6 31.1 %collective-permute-start.18 = (bf16[1040,256]{1,0:T(8,128)(2,1)S(1)}, bf16[1040,256]{1,0:T(8,128)(2,1)S(1)}, u32[]{:S(2)}, u32[]{:S(2)}) collective-permute-start(bf16[1040,256]{1,0:T(8,128)(2,1)S(1)} %get-tuple-element.84), channel_id=1, source_target_pairs={{0,3},{1,0},{2,1},{3,2},{4,7},{5,4},{6,5},{7,6},{8,11},{9,8},{10,9... | collective-permute-start | bytes 1597448 | tf_op jit(solution)/shard_map/ppermute | solution.py:766
  106.3 11.4 %collective-permute-start.20 = (bf16[128,1024]{1,0:T(8,128)(2,1)S(1)}, bf16[128,1024]{1,0:T(8,128)(2,1)S(1)}, u32[]{:S(2)}, u32[]{:S(2)}) collective-permute-start(bf16[128,1024]{1,0:T(8,128)(2,1)S(1)} %get-tuple-element.91), channel_id=1, source_target_pairs={{0,8},{4,36},{8,16},{12,44},{16,24},{20,52},{24,0},{28,60},{32,40}... | collective-permute-start | bytes 786440 | tf_op jit(solution)/shard_map/ppermute | solution.py:734
  107.9 14.1 %collective-permute-start.21 = (bf16[128,1024]{1,0:T(8,128)(2,1)S(1)}, bf16[128,1024]{1,0:T(8,128)(2,1)S(1)}, u32[]{:S(2)}, u32[]{:S(2)}) collective-permute-start(bf16[128,1024]{1,0:T(8,128)(2,1)S(1)} %get-tuple-element.92), channel_id=1, source_target_pairs={{0,16},{4,68},{8,24},{12,76},{16,0},{20,84},{24,8},{28,92},{32,48}... | collective-permute-start | bytes 786440 | tf_op jit(solution)/shard_map/ppermute | solution.py:734
  124.8 11.6 %collective-permute-start.23 = (bf16[32,1024]{1,0:T(8,128)(2,1)S(1)}, bf16[32,1024]{1,0:T(8,128)(2,1)S(1)}, u32[]{:S(2)}, u32[]{:S(2)}) collective-permute-start(bf16[32,1024]{1,0:T(8,128)(2,1)S(1)} %get-tuple-element.95), channel_id=1, source_target_pairs={{0,32},{4,12},{8,40},{12,20},{16,48},{20,28},{24,56},{28,4},{32,64... | collective-permute-start | bytes 196616 | tf_op jit(solution)/shard_map/ppermute | solution.py:734
  126.5 10.0 %collective-permute-start.24 = (bf16[32,1024]{1,0:T(8,128)(2,1)S(1)}, bf16[32,1024]{1,0:T(8,128)(2,1)S(1)}, u32[]{:S(2)}, u32[]{:S(2)}) collective-permute-start(bf16[32,1024]{1,0:T(8,128)(2,1)S(1)} %get-tuple-element.96), channel_id=1, source_target_pairs={{0,64},{4,20},{8,72},{12,28},{16,80},{20,4},{24,88},{28,12},{32,96... | collective-permute-start | bytes 196616 | tf_op jit(solution)/shard_map/ppermute | solution.py:734
  (15 other events, 87.5 us)

commit v4 on v3

--- a/solution.py
+++ b/solution.py
@@ -196,7 +196,7 @@
     share = pltpu.VMEM((rows, width), BF16)
     fixed = [
         pltpu.with_memory_space_constraint(value, pltpu.HBM)
-        for value in (shares[0], wq, wk, wv)
+        for value in (*shares[1:], shares[0], wq, wk, wv)
     ]
     return pl.pallas_call(
         project_kernel,
@@ -219,7 +219,7 @@
         compiler_params=pltpu.CompilerParams(vmem_limit_bytes=20 * 2**20),
         cost_estimate=SMALL,
         name="project",
-    )(place, *shares[1:], *fixed)
+    )(place, *fixed)
 
 
 def cotangent_kernel(place, g0, g1, g2, g3, w_out, d_att):
@@ -349,23 +349,31 @@
         row = 4 * u + 2 * head
         stats[pair, row : row + 1, :] = top
         stats[pair, row + 1 : row + 2, :] = scale
+        return [(e * scale).astype(BF16) for e in exps]
+
+    outs = []
+
+    def give(u, head, weights):
+        level, block = units[u]
         part = slice(head * HD, (head + 1) * HD)
         o_t = None
-        for (at, _), e in zip(unit_keys(level, block), exps):
-            o = nn(vt[FIRST_EXT[level] + at, part, :], (e * scale).astype(BF16))
+        for (at, _), w in zip(unit_keys(level, block), weights):
+            o = nn(vt[FIRST_EXT[level] + at, part, :], w)
             o_t = o if o_t is None else o_t + o
-        return o_t
+        outs.append(o_t)
+        if head == 1:
+            add_spread(out_f, block, 2**level, jnp.concatenate(outs, axis=0).T)
+            outs.clear()
 
     items = [(u, head) for u in range(len(units)) for head in range(2)]
-    scores, outs = begin(*items[0]), []
-    for n, (u, head) in enumerate(items):
+    scores, last = begin(*items[0]), None
+    for n, item in enumerate(items):
         following = begin(*items[n + 1]) if n + 1 < len(items) else None
-        outs.append(finish(u, head, scores))
+        if last is not None:
+            give(*items[n - 1], last)
+        last = finish(*item, scores)
         scores = following
-        if head == 1:
-            level, block = units[u]
-            add_spread(out_f, block, 2**level, jnp.concatenate(outs, axis=0).T)
-            outs = []
+    give(*items[-1], last)
 
 
 def forward_inner_kernel(bias_ref, q, kv, out, stats, vt, out_f):
@@ -424,31 +432,41 @@
         for p, dw in zip(probs, d_weights):
             d = (p * dw).sum(axis=0, keepdims=True)
             dots = d if dots is None else dots + d
+        weights = [p.astype(BF16) for p in probs]
+        d_scores = [(p * (dw - dots)).astype(BF16) for p, dw in zip(probs, d_weights)]
+        return qm, am, weights, d_scores
+
+    first = []
+
+    def give(u, head, qm, am, weights, d_scores):
+        level, block = units[u]
+        keys = unit_keys(level, block)
         part = slice(head * HD, (head + 1) * HD)
-        dq_t, d_keys, d_values = None, [], []
-        for (at, _), p, dw in zip(unit_keys(level, block), probs, d_weights):
-            d_values.append(nn(p.astype(BF16), am))
-            d_scores = (p * (dw - dots)).astype(BF16)
-            d_keys.append(nn(d_scores, qm))
-            g = nn(kt[FIRST_EXT[level] + at, part, :], d_scores)
+        d_values = [nn(w, am) for w in weights]
+        d_keys = [nn(ds, qm) for ds in d_scores]
+        dq_t = None
+        for (at, _), ds in zip(keys, d_scores):
+            g = nn(kt[FIRST_EXT[level] + at, part, :], ds)
             dq_t = g if dq_t is None else dq_t + g
-        return dq_t, d_keys, d_values
+        if head == 0:
+            first.append((dq_t, d_keys, d_values))
+            return
+        dq_first, k_first, v_first = first.pop()
+        for n, (at, _) in enumerate(keys):
+            keep(0, level, at, k_first[n] + d_keys[n])
+            keep(1, level, at, v_first[n] + d_values[n])
+        dq = jnp.concatenate([dq_first, dq_t], axis=0).T * (HD ** (-0.5) / 2**level)
+        add_spread(dq_f, block, 2**level, dq)
 
     items = [(u, head) for u in range(len(units)) for head in range(2)]
-    ready, first = begin(*items[0]), None
-    for n, (u, head) in enumerate(items):
+    ready, last = begin(*items[0]), None
+    for n, item in enumerate(items):
         following = begin(*items[n + 1]) if n + 1 < len(items) else None
-        got = finish(u, head, *ready)
+        if last is not None:
+            give(*items[n - 1], *last)
+        last = finish(*item, *ready)
         ready = following
-        if head == 0:
-            first = got
-            continue
-        level, block = units[u]
-        for m, (at, _) in enumerate(unit_keys(level, block)):
-            keep(0, level, at, first[1][m] + got[1][m])
-            keep(1, level, at, first[2][m] + got[2][m])
-        dq = jnp.concatenate([first[0], got[0]], axis=0).T * (HD ** (-0.5) / 2**level)
-        add_spread(dq_f, block, 2**level, dq)
+    give(*items[-1], *last)
 
 
 def edge_kernel(
@@ -541,7 +559,7 @@
     inputs = [stats, q, kv, d_att, dq_f, d_kv]
     outputs = [held((rows, width), BF16), held((2, rows, width), F32)]
     scratch = [turned(EXT_BLOCKS[0]), pltpu.VMEM((rows, PAIR), F32)]
-    return run(inner_units_kernel, "inner_backward", 12, [bias], inputs, outputs, scratch, LARGE)
+    return run(inner_units_kernel, "inner_backward", 12, [bias], inputs, outputs, scratch)
 
 
 def term_outputs(rows, width, extra=0):
@@ -586,7 +604,7 @@
             total = total + nn(quarter, from_left[n, low_rows, :])
             total = total + nn(quarter, from_right[n, low_rows, :])
             grads.append(total.astype(BF16))
-        for n, grad in enumerate(grads):
+        for n, grad in enumerate(grads[1:]):
             d_proj[rows, n * width : (n + 1) * width] = grad
         dot = None
         for r, out in enumerate((own, one, two, three)):
@@ -610,7 +628,7 @@
 def input_terms(place, d_query, d_kv, from_left, from_right, normed, wq, wk, wv):
     rows, width = d_query.shape
     inputs = [d_query, d_kv, from_left, from_right, normed, wq, wk, wv]
-    outputs = [held((rows, 3 * width), BF16), held((DOT_ROWS, width), BF16)]
+    outputs = [held((rows, 2 * width), BF16), held((DOT_ROWS, width), BF16)]
     outputs += term_outputs(rows, width, DOT_ROWS)
     scratch = [pltpu.VMEM((DOT_ROWS, width), F32)]
     return run(input_terms_kernel, "input_terms", 16, [place], inputs, outputs, scratch)
@@ -654,25 +672,29 @@
     return run(finish_grad_kernel, "finish_grad", 8, [], inputs, outputs, (), LAST)[0]
 
 
-def outer_kernel(g0, g1, g2, g3, attended, result):
+def early_kernel(g0, g1, g2, g3, attended, normed, d_query, outer, inner):
     width = g0.shape[1]
     rows = attended[...]
     for r, share in enumerate((g0, g1, g2, g3)):
-        result[r * width : (r + 1) * width, :] = tn(share[...], rows).astype(BF16)
-
-
-def outer_terms(shares, attended):
-    rows, width = attended.shape
-    outputs = [held((MP * width, width), BF16)]
-    return run(outer_kernel, "outer_terms", 10, [], [*shares, attended], outputs)[0]
-
-
-def inner_kernel(place, normed, d_proj, outer, mine, other, rows_held):
+        at = slice(r * width, (r + 1) * width)
+        outer[at, :] = tn(share[...], rows).astype(BF16)
+        inner[at, :] = tn(normed[:, at], d_query[...]).astype(BF16)
+
+
+def early_terms(shares, attended, normed, d_query):
+    width = attended.shape[1]
+    inputs = [*shares, attended, normed, d_query]
+    outputs = [held((MP * width, width), BF16)] * 2
+    return run(early_kernel, "early_terms", 14, [], inputs, outputs, (), LARGE)
+
+
+def inner_kernel(place, normed, d_proj, inner, outer, mine, other, rows_held):
     core = place[1]
     width = outer.shape[1]
     for block in range(MP):
         at = block_rows(block)
-        rows_held[at, 0 : 3 * width] = tn(normed[:, at], d_proj[...]).astype(BF16)
+        rows_held[at, 0:width] = inner[at, :]
+        rows_held[at, width : 3 * width] = tn(normed[:, at], d_proj[...]).astype(BF16)
         rows_held[at, 3 * width :] = outer[at, :]
         for n in range(width // 64):
             out = slice((4 * block + n) * 32, (4 * block + n + 1) * 32)
@@ -681,12 +703,12 @@
             other[out, :] = rows_held[pl.ds(pl.multiple_of(first + 32 - core * 32, 32), 32), :]
 
 
-def inner_terms(place, normed, d_proj, outer):
+def inner_terms(place, normed, d_proj, inner, outer):
     total = normed.shape[1]
     width = outer.shape[1]
     outputs = [held((total // 2, 4 * width), BF16)] * 2
     scratch = [pltpu.VMEM((total, 4 * width), BF16)]
-    return run(inner_kernel, "inner_terms", 16, [place], [normed, d_proj, outer], outputs, scratch)
+    return run(inner_kernel, "inner_terms", 16, [place], [normed, d_proj, inner, outer], outputs, scratch)
 
 
 def pair_sum_kernel(place, mine, got, *outs):
@@ -815,15 +837,16 @@
         bias, stats, q, kv, from_left, from_right, d_att
     )
     from_left, from_right = exchange(to_left, to_right)
-    dq_f = tied(dq_f, *out_received)
     d_query, d_kv = inner_backward(bias, inner_stats, q, kv, d_att, dq_f, d_kv)
+    attended = tied(attended, *out_received)
+    outer, inner = early_terms(grad_shares, attended, normed, d_query)
+    d_query = tied(d_query, outer)
     d_proj, dots, own, *terms = input_terms(
         me, d_query, d_kv, from_left, from_right, normed, w_query, w_key, w_value
     )
     received = sum_over_mp(terms)
     attn_out = finish_out(out_own, out_received)
-    outer = outer_terms(grad_shares, attended)
-    mine, other = inner_terms(me, normed, d_proj, outer)
+    mine, other = inner_terms(me, normed, d_proj, inner, outer)
     grad_tokens = finish_grad(own, received, tokens, inverse, dots)
     *weight_grads, grad_w_out = sum_over_seq(me, mine, other)
     return (attn_out, grad_tokens, *weight_grads, grad_w_out.T)

time: 139 us -> 134 us (0.964)
  local copies, waits for them, and re-layouts: 6.06 us -> 1.84 us
    unnamed x26 -> x24, local copies, waits for them, and re-layouts: 5 us -> 0.77 us
  transfers between devices with their start and end apart: 26 -> 26, of which waited for: 7 -> 7; matrix products, arithmetic and copies ran while one was open for 0% -> 0% of each run, Pallas kernels for 33% -> 34%
where the time goes in v4:
time: 134 us; the launch traced here: 133 us
  starting transfers between devices  62.9 us (47%)
  Pallas kernels  51.4 us (38%)
  waiting for transfers between devices  15.7 us (12%)
  local copies, waits for them, and re-layouts  1.84 us (1%)
    pallas_call x14, Pallas kernels, run(): pl.pallas_call(kernel, in_specs=[SCALAR] * len(scalars) + [RESIDENT] * le...  44 us
    ppermute x6, starting transfers between devices, sent(): return lax.ppermute(value, 'seq', pairs)  20.4 us
    ppermute x2, starting transfers between devices, exchange(): from_left = lax.ppermute(to_right, 'seq', [(i, i + 1) for i in range(ends)])  12.2 us
    ppermute x7, starting transfers between devices, turned_by(): return lax.ppermute(value, 'mp', [(i, (i + step) % MP) for i in range(MP)])  10.2 us
    ppermute x4, starting transfers between devices, to_previous(): return lax.ppermute(value, 'mp', [((i + 1) % MP, i) for i in range(MP)])  9.02 us
    pallas_call x1, Pallas kernels, project(): pl.pallas_call(project_kernel, in_specs=[SCALAR] + [anywhere] * 10, out_s...  7.41 us
    ppermute x4, waiting for transfers between devices, to_next(): return lax.ppermute(value, 'mp', [(i, (i + 1) % MP) for i in range(MP)])  7.1 us
    ppermute x6, waiting for transfers between devices, sent(): return lax.ppermute(value, 'seq', pairs)  6.36 us
  transfers between devices with their start and end apart: 26, of which 7 were waited for; matrix products, arithmetic and copies ran while one was open for 0% of the time, Pallas kernels for 34%

profile of v4, /device:TPU:0, one launch (start us, length us, event | category | flops | bytes accessed | tf_op | source)
XLA Modules:
  0.0 132.9 jit_solution(9799764642395442675)
XLA Ops:
  1.7 2.1 %collective-permute-start.3 = (bf16[512,256]{1,0:T(8,128)(2,1)S(1)}, bf16[512,256]{1,0:T(8,128)(2,1)S(1)}, u32[]{:S(2)}, u32[]{:S(2)}) collective-permute-start(bf16[512,256]{1,0:T(8,128)(2,1)S(1)} %get-tuple-element.108), channel_id=1, source_target_pairs={{0,1},{1,2},{2,3},{3,0},{4,5},{5,6},{6,7},{7,4},{8,9},{9,10},{10,1... | collective-permute-start | bytes 786440 | tf_op jit(solution)/shard_map/ppermute | solution.py:771
  3.8 2.2 %collective-permute-start = (bf16[512,256]{1,0:T(8,128)(2,1)S(1)}, bf16[512,256]{1,0:T(8,128)(2,1)S(1)}, u32[]{:S(2)}, u32[]{:S(2)}) collective-permute-start(bf16[512,256]{1,0:T(8,128)(2,1)S(1)} %get-tuple-element.109), channel_id=1, source_target_pairs={{1,0},{2,1},{3,2},{0,3},{5,4},{6,5},{7,6},{4,7},{9,8},{10,9},{11,1... | collective-permute-start | bytes 786440 | tf_op jit(solution)/shard_map/ppermute | solution.py:775
  8.0 5.0 %collective-permute-done.3.t3b_any = bf16[512,256]{1,0:T(8,128)(2,1)S(1)} collective-permute-done((bf16[512,256]{1,0:T(8,128)(2,1)S(1)}, bf16[512,256]{1,0:T(8,128)(2,1)S(1)}, u32[]{:S(2)}, u32[]{:S(2)}) %collective-permute-start.3) | collective-permute-done | bytes 262176 | tf_op jit(solution)/shard_map/ppermute | solution.py:771
  13.0 3.3 %collective-permute-start.2 = (bf16[512,256]{1,0:T(8,128)(2,1)S(1)}, bf16[512,256]{1,0:T(8,128)(2,1)}, u32[]{:S(2)}, u32[]{:S(2)}) collective-permute-start(bf16[512,256]{1,0:T(8,128)(2,1)S(1)} %collective-permute-done.t1a_any), channel_id=1, source_target_pairs={{1,0},{2,1},{3,2},{0,3},{5,4},{6,5},{7,6},{4,7},{9,8},{10,9},{11,1... | collective-permute-start | bytes 786440 | tf_op jit(solution)/shard_map/ppermute | solution.py:775
  16.4 2.2 %collective-permute-done.1.t1b_any = bf16[512,256]{1,0:T(8,128)(2,1)S(1)} collective-permute-done((bf16[512,256]{1,0:T(8,128)(2,1)S(1)}, bf16[512,256]{1,0:T(8,128)(2,1)S(1)}, u32[]{:S(2)}, u32[]{:S(2)}) %collective-permute-start.1) | collective-permute-done | bytes 262176 | tf_op jit(solution)/shard_map/ppermute | solution.py:775
  22.2 2.0 %collective-permute-done.4.t2b_any = bf16[512,256]{1,0:T(8,128)(2,1)S(1)} collective-permute-done((bf16[512,256]{1,0:T(8,128)(2,1)S(1)}, bf16[512,256]{1,0:T(8,128)(2,1)S(1)}, u32[]{:S(2)}, u32[]{:S(2)}) %collective-permute-start.4) | collective-permute-done | bytes 262176 | tf_op jit(solution)/shard_map/ppermute | solution.py:771
  25.0 7.4 %project.1 = (f32[8,256]{1,0:T(8,128)S(1)}, bf16[1792,256]{1,0:T(8,128)(2,1)S(1)}, bf16[2,1792,256]{2,1,0:T(8,128)(2,1)S(1)}, bf16[2,768,256]{2,1,0:T(8,128)(2,1...) custom-call(s32[4]{0:T(128)S(1)} %pad_add_fusion.place, bf16[512,256]{1,0:T(8,128)(2,1)} %copy-done.8, ...), custom_call_target="tpu_custom_call" | custom-call | flops 1000000 | bytes 10000 | tf_op jit(solution)/shard_map/project/pallas_call | solution.py:201
  35.1 3.0 %collective-permute-start.13 = (bf16[1024,256]{1,0:T(8,128)(2,1)}, bf16[1024,256]{1,0:T(8,128)(2,1)S(1)}, u32[]{:S(2)}, u32[]{:S(2)}) collective-permute-start(bf16[1024,256]{1,0:T(8,128)(2,1)} %g0.1), channel_id=1, source_target_pairs={{0,2},{1,3},{2,0},{3,1},{4,6},{5,7},{6,4},{7,5},{8,10},{9,11},{10,... | collective-permute-start | bytes 1572872 | tf_op jit(solution)/shard_map/ppermute | solution.py:788
  38.2 3.6 %forward_inner.1 = (f32[512,256]{1,0:T(8,128)S(1)}, f32[2,8,256]{2,1,0:T(8,128)S(1)}) custom-call(f32[2]{0:T(128)S(1)} %pad_maximum_fusion.bias_ref, bf16[1792,256]{1,0:T(8,128)(2,1)S(1)} %get-tuple-element.62.q, bf16[2,1792,256]{2,1,0:T(8,128)(2,1)S(1)} %get-tuple-element.58.kv), custom_call_target="tpu_custom_call" | custom-call | flops 4000000000 | bytes 10000 | tf_op jit(solution)/shard_map/forward_inner/pallas_call | solution.py:70
  41.8 6.6 %forward_edge.1 = (bf16[1024,256]{1,0:T(8,128)(2,1)S(1)}, f32[2,24,256]{2,1,0:T(8,128)S(1)}) custom-call(f32[2]{0:T(128)S(1)} %pad_maximum_fusion.bias_ref, bf16[1792,256]{1,0:T(8,128)(2,1)S(1)} %get-tuple-element.62.q, bf16[2,1792,256]{2,1,0:T(8,128)(2,1)S(1)} %get-tuple-element.58.kv, bf16[2,768,256]{2,1,0:T(8,128)(2,1)S(1)} %collective-permute-done.6.from_left, ...), custom_call_target="tpu_custom_call" | custom-call | flops 1000000 | bytes 10000 | tf_op jit(solution)/shard_map/forward_edge/pallas_call | solution.py:70
  53.5 3.1 %cotangent.1.grads = bf16[1792,256]{1,0:T(8,128)(2,1)S(1)} custom-call(s32[4]{0:T(128)S(1)} %pad_add_fusion.place, bf16[1024,256]{1,0:T(8,128)(2,1)S(1)} %copy-done.6, bf16[1024,256]{1,0:T(8,128)(2,1)} %collective-permute-done.8.g1, bf16[1024,256]{1,0:T(8,128)(2,1)S(1)} %collective-permute-done.13.g2, bf16[1024,256]{1,0:T(8,128)(2,1)} %collective-permute-done.9.g3, ...), custom_call_target="tpu_custom_call" | custom-call | flops 1000000 | bytes 10000 | tf_op jit(solution)/shard_map/cotangent/pallas_call | solution.py:70
  56.6 10.6 %edge_backward.1 = (f32[1024,256]{1,0:T(8,128)S(1)}, f32[2,1024,256]{2,1,0:T(8,128)S(1)}, bf16[2,768,256]{2,1,0:T(8,128)(2,1)S(1)}, bf16[2,768,256]{2,1,0:T(8,128)(2,1)S(1)}) custom-call(f32[2]{0:T(128)S(1)} %pad_maximum_fusion.bias_ref, f32[2,24,256]{2,1,0:T(8,128)S(1)} %get-tuple-element.75.stats, bf16[1792,256]{1,0:T(8,128)(2,1)S(1)} %get-tuple-element.62.q, ...), custom_call_target="tpu_custom_call" | custom-call | flops 1000000 | bytes 10000 | tf_op jit(solution)/shard_map/edge_backward/pallas_call | solution.py:70
  67.2 10.9 %collective-permute-start.14 = (bf16[2,768,256]{2,1,0:T(8,128)(2,1)S(1)}, bf16[2,768,256]{2,1,0:T(8,128)(2,1)S(1)}, u32[]{:S(2)}, u32[]{:S(2)}) collective-permute-start(bf16[2,768,256]{2,1,0:T(8,128)(2,1)S(1)} %get-tuple-element.84), channel_id=1, source_target_pairs={{0,4},{4,8},{8,12},{12,16},{16,20},{20,24},{24,28},{28,32},{32,36}... | collective-permute-start | bytes 2359304 | tf_op jit(solution)/shard_map/ppermute | solution.py:798
  79.6 5.5 %inner_backward.1 = (bf16[1024,256]{1,0:T(8,128)(2,1)S(1)}, f32[2,1024,256]{2,1,0:T(8,128)S(1)}) custom-call(f32[2]{0:T(128)S(1)} %pad_maximum_fusion.bias_ref, f32[2,8,256]{2,1,0:T(8,128)S(1)} %get-tuple-element.69.stats, bf16[1792,256]{1,0:T(8,128)(2,1)S(1)} %get-tuple-element.62.q, bf16[2,1792,256]{2,1,0:T(8,128)(2,1)S(1)} %get-tuple-element.58.kv, ...), custom_call_target="tpu_custom_call" | custom-call | flops 1000000 | bytes 10000 | tf_op jit(solution)/shard_map/inner_backward/pallas_call | solution.py:70
  85.2 2.6 %early_terms.1 = (bf16[1024,256]{1,0:T(8,128)(2,1)S(1)}, bf16[1024,256]{1,0:T(8,128)(2,1)S(1)}) custom-call(bf16[1024,256]{1,0:T(8,128)(2,1)S(1)} %copy-done.6, bf16[1024,256]{1,0:T(8,128)(2,1)} %collective-permute-done.8.g1, bf16[1024,256]{1,0:T(8,128)(2,1)S(1)} %collective-permute-done.13.g2, bf16[1024,256]{1,0:T(8,128)(2,1)} %collective-permute-done.9.g3, ...), custom_call_target="tpu_custom_call" | custom-call | flops 4000000000 | bytes 10000 | tf_op jit(solution)/shard_map/early_terms/pallas_call | solution.py:70
  87.9 3.7 %input_terms.1 = (bf16[1024,512]{1,0:T(8,128)(2,1)S(1)}, bf16[16,256]{1,0:T(8,128)(2,1)S(1)}, bf16[1024,256]{1,0:T(8,128)(2,1)S(1)}, bf16[1040,256]{1,0:T(8,128)...) custom-call(s32[4]{0:T(128)S(1)} %pad_add_fusion.place, ...), custom_call_target="tpu_custom_call" | custom-call | flops 1000000 | bytes 10000 | tf_op jit(solution)/shard_map/input_terms/pallas_call | solution.py:70
  91.5 2.1 %inner_terms.1 = (bf16[512,1024]{1,0:T(8,128)(2,1)S(1)}, bf16[512,1024]{1,0:T(8,128)(2,1)S(1)}) custom-call(s32[4]{0:T(128)S(1)} %pad_add_fusion.place, bf16[1024,1024]{1,0:T(8,128)(2,1)S(1)} %copy-done, bf16[1024,512]{1,0:T(8,128)(2,1)S(1)} %get-tuple-element.92.d_proj, bf16[1024,256]{1,0:T(8,128)(2,1)S(1)} %get-tuple-element.93.inner, ...), custom_call_target="tpu_custom_call" | custom-call | flops 1000000 | bytes 10000 | tf_op jit(solution)/shard_map/inner_terms/pallas_call | solution.py:70
  93.6 4.1 %collective-permute-start.19 = (bf16[512,1024]{1,0:T(8,128)(2,1)S(1)}, bf16[512,1024]{1,0:T(8,128)(2,1)S(1)}, u32[]{:S(2)}, u32[]{:S(2)}) collective-permute-start(bf16[512,1024]{1,0:T(8,128)(2,1)S(1)} %get-tuple-element.95), channel_id=1, source_target_pairs={{0,4},{4,0},{8,12},{12,8},{16,20},{20,16},{24,28},{28,24},{32,36},... | collective-permute-start | bytes 3145736 | tf_op jit(solution)/shard_map/ppermute | solution.py:758
  103.4 7.0 %collective-permute-start.21 = (bf16[128,1024]{1,0:T(8,128)(2,1)S(1)}, bf16[128,1024]{1,0:T(8,128)(2,1)S(1)}, u32[]{:S(2)}, u32[]{:S(2)}) collective-permute-start(bf16[128,1024]{1,0:T(8,128)(2,1)S(1)} %get-tuple-element.98), channel_id=1, source_target_pairs={{0,16},{4,68},{8,24},{12,76},{16,0},{20,84},{24,8},{28,92},{32,48}... | collective-permute-start | bytes 786440 | tf_op jit(solution)/shard_map/ppermute | solution.py:756
  110.4 2.9 %collective-permute-done.20.b = bf16[128,1024]{1,0:T(8,128)(2,1)S(1)} collective-permute-done((bf16[128,1024]{1,0:T(8,128)(2,1)S(1)}, bf16[128,1024]{1,0:T(8,128)(2,1)S(1)}, u32[]{:S(2)}, u32[]{:S(2)}) %collective-permute-start.20) | collective-permute-done | bytes 262176 | tf_op jit(solution)/shard_map/ppermute | solution.py:756
  113.3 2.0 %collective-permute-start.22 = (bf16[128,1024]{1,0:T(8,128)(2,1)S(1)}, bf16[128,1024]{1,0:T(8,128)(2,1)S(1)}, u32[]{:S(2)}, u32[]{:S(2)}) collective-permute-start(bf16[128,1024]{1,0:T(8,128)(2,1)S(1)} %get-tuple-element.99), channel_id=1, source_target_pairs={{0,24},{4,100},{8,0},{12,108},{16,8},{20,116},{24,16},{28,124},{32... | collective-permute-start | bytes 786440 | tf_op jit(solution)/shard_map/ppermute | solution.py:756
  117.6 2.1 %collective-permute-done.22.d = bf16[128,1024]{1,0:T(8,128)(2,1)S(1)} collective-permute-done((bf16[128,1024]{1,0:T(8,128)(2,1)S(1)}, bf16[128,1024]{1,0:T(8,128)(2,1)S(1)}, u32[]{:S(2)}, u32[]{:S(2)}) %collective-permute-start.22) | collective-permute-done | bytes 262176 | tf_op jit(solution)/shard_map/ppermute | solution.py:756
  122.1 4.6 %collective-permute-start.24 = (bf16[32,1024]{1,0:T(8,128)(2,1)S(1)}, bf16[32,1024]{1,0:T(8,128)(2,1)S(1)}, u32[]{:S(2)}, u32[]{:S(2)}) collective-permute-start(bf16[32,1024]{1,0:T(8,128)(2,1)S(1)} %get-tuple-element.102), channel_id=1, source_target_pairs={{0,64},{4,20},{8,72},{12,28},{16,80},{20,4},{24,88},{28,12},{32,96... | collective-permute-start | bytes 196616 | tf_op jit(solution)/shard_map/ppermute | solution.py:756
  126.7 3.7 %collective-permute-start.25 = (bf16[32,1024]{1,0:T(8,128)(2,1)S(1)}, bf16[32,1024]{1,0:T(8,128)(2,1)S(1)}, u32[]{:S(2)}, u32[]{:S(2)}) collective-permute-start(bf16[32,1024]{1,0:T(8,128)(2,1)S(1)} %get-tuple-element.103), channel_id=1, source_target_pairs={{0,96},{4,28},{8,104},{12,4},{16,112},{20,12},{24,120},{28,20},{32... | collective-permute-start | bytes 196616 | tf_op jit(solution)/shard_map/ppermute | solution.py:756
  (70 shorter events, 29.7 us)
Async XLA Ops:
  1.7 11.3 %collective-permute-start.3 = (bf16[512,256]{1,0:T(8,128)(2,1)S(1)}, bf16[512,256]{1,0:T(8,128)(2,1)S(1)}, u32[]{:S(2)}, u32[]{:S(2)}) collective-permute-start(bf16[512,256]{1,0:T(8,128)(2,1)S(1)} %get-tuple-element.108), channel_id=1, source_target_pairs={{0,1},{1,2},{2,3},{3,0},{4,5},{5,6},{6,7},{7,4},{8,9},{9,10},{10,1... | collective-permute-start | bytes 786440 | tf_op jit(solution)/shard_map/ppermute | solution.py:771
  3.8 9.3 %collective-permute-start = (bf16[512,256]{1,0:T(8,128)(2,1)S(1)}, bf16[512,256]{1,0:T(8,128)(2,1)S(1)}, u32[]{:S(2)}, u32[]{:S(2)}) collective-permute-start(bf16[512,256]{1,0:T(8,128)(2,1)S(1)} %get-tuple-element.109), channel_id=1, source_target_pairs={{1,0},{2,1},{3,2},{0,3},{5,4},{6,5},{7,6},{4,7},{9,8},{10,9},{11,1... | collective-permute-start | bytes 786440 | tf_op jit(solution)/shard_map/ppermute | solution.py:775
  6.0 12.6 %collective-permute-start.1 = (bf16[512,256]{1,0:T(8,128)(2,1)S(1)}, bf16[512,256]{1,0:T(8,128)(2,1)S(1)}, u32[]{:S(2)}, u32[]{:S(2)}) collective-permute-start(bf16[512,256]{1,0:T(8,128)(2,1)S(1)} %get-tuple-element.108), channel_id=1, source_target_pairs={{1,0},{2,1},{3,2},{0,3},{5,4},{6,5},{7,6},{4,7},{9,8},{10,9},{11,1... | collective-permute-start | bytes 786440 | tf_op jit(solution)/shard_map/ppermute | solution.py:775
  7.9 10.7 %collective-permute-start.5 = (bf16[512,256]{1,0:T(8,128)(2,1)S(1)}, bf16[512,256]{1,0:T(8,128)(2,1)S(1)}, u32[]{:S(2)}, u32[]{:S(2)}) collective-permute-start(bf16[512,256]{1,0:T(8,128)(2,1)S(1)} %get-tuple-element.109), channel_id=1, source_target_pairs={{0,1},{1,2},{2,3},{3,0},{4,5},{5,6},{6,7},{7,4},{8,9},{9,10},{10,1... | collective-permute-start | bytes 786440 | tf_op jit(solution)/shard_map/ppermute | solution.py:771
  13.0 11.2 %collective-permute-start.4 = (bf16[512,256]{1,0:T(8,128)(2,1)S(1)}, bf16[512,256]{1,0:T(8,128)(2,1)S(1)}, u32[]{:S(2)}, u32[]{:S(2)}) collective-permute-start(bf16[512,256]{1,0:T(8,128)(2,1)S(1)} %collective-permute-done.3.t3b_any), channel_id=1, source_target_pairs={{0,1},{1,2},{2,3},{3,0},{4,5},{5,6},{6,7},{7,4},{8,9},{9,10},{10,1... | collective-permute-start | bytes 786440 | tf_op jit(solution)/shard_map/ppermute | solution.py:771
  13.0 11.9 %collective-permute-start.2 = (bf16[512,256]{1,0:T(8,128)(2,1)S(1)}, bf16[512,256]{1,0:T(8,128)(2,1)}, u32[]{:S(2)}, u32[]{:S(2)}) collective-permute-start(bf16[512,256]{1,0:T(8,128)(2,1)S(1)} %collective-permute-done.t1a_any), channel_id=1, source_target_pairs={{1,0},{2,1},{3,2},{0,3},{5,4},{6,5},{7,6},{4,7},{9,8},{10,9},{11,1... | collective-permute-start | bytes 786440 | tf_op jit(solution)/shard_map/ppermute | solution.py:775
  18.6 19.5 %collective-permute-start.9 = (bf16[1024,256]{1,0:T(8,128)(2,1)}, bf16[1024,256]{1,0:T(8,128)(2,1)}, u32[]{:S(2)}, u32[]{:S(2)}) collective-permute-start(bf16[1024,256]{1,0:T(8,128)(2,1)} %g0.1), channel_id=1, source_target_pairs={{0,1},{1,2},{2,3},{3,0},{4,5},{5,6},{6,7},{7,4},{8,9},{9,10},{10,1... | collective-permute-start | bytes 1572872 | tf_op jit(solution)/shard_map/ppermute | solution.py:771
  20.6 17.6 %collective-permute-start.8 = (bf16[1024,256]{1,0:T(8,128)(2,1)}, bf16[1024,256]{1,0:T(8,128)(2,1)}, u32[]{:S(2)}, u32[]{:S(2)}) collective-permute-start(bf16[1024,256]{1,0:T(8,128)(2,1)} %g0.1), channel_id=1, source_target_pairs={{1,0},{2,1},{3,2},{0,3},{5,4},{6,5},{7,6},{4,7},{9,8},{10,9},{11,1... | collective-permute-start | bytes 1572872 | tf_op jit(solution)/shard_map/ppermute | solution.py:775
  32.4 9.4 %collective-permute-start.6 = (bf16[2,768,256]{2,1,0:T(8,128)(2,1)}, bf16[2,768,256]{2,1,0:T(8,128)(2,1)S(1)}, u32[]{:S(2)}, u32[]{:S(2)}) collective-permute-start(bf16[2,768,256]{2,1,0:T(8,128)(2,1)} %get-tuple-element.59), channel_id=1, source_target_pairs={{0,4},{4,8},{8,12},{12,16},{16,20},{20,24},{24,28},{28,32},{32,36}... | collective-permute-start | bytes 2359304 | tf_op jit(solution)/shard_map/ppermute | solution.py:798
  33.8 8.0 %collective-permute-start.7 = (bf16[2,768,256]{2,1,0:T(8,128)(2,1)}, bf16[2,768,256]{2,1,0:T(8,128)(2,1)}, u32[]{:S(2)}, u32[]{:S(2)}) collective-permute-start(bf16[2,768,256]{2,1,0:T(8,128)(2,1)} %get-tuple-element.60), channel_id=1, source_target_pairs={{4,0},{8,4},{12,8},{16,12},{20,16},{24,20},{28,24},{32,28},{36,32}... | collective-permute-start | bytes 2359304 | tf_op jit(solution)/shard_map/ppermute | solution.py:799
  35.1 18.4 %collective-permute-start.13 = (bf16[1024,256]{1,0:T(8,128)(2,1)}, bf16[1024,256]{1,0:T(8,128)(2,1)S(1)}, u32[]{:S(2)}, u32[]{:S(2)}) collective-permute-start(bf16[1024,256]{1,0:T(8,128)(2,1)} %g0.1), channel_id=1, source_target_pairs={{0,2},{1,3},{2,0},{3,1},{4,6},{5,7},{6,4},{7,5},{8,10},{9,11},{10,... | collective-permute-start | bytes 1572872 | tf_op jit(solution)/shard_map/ppermute | solution.py:788
  49.7 35.4 %collective-permute-start.10 = (bf16[1024,256]{1,0:T(8,128)(2,1)S(1)}, bf16[1024,256]{1,0:T(8,128)(2,1)S(1)}, u32[]{:S(2)}, u32[]{:S(2)}) collective-permute-start(bf16[1024,256]{1,0:T(8,128)(2,1)S(1)} %get-tuple-element.66), channel_id=1, source_target_pairs={{0,1},{1,2},{2,3},{3,0},{4,5},{5,6},{6,7},{7,4},{8,9},{9,10},{10,1... | collective-permute-start | bytes 1572872 | tf_op jit(solution)/shard_map/ppermute | solution.py:788
  50.4 34.7 %collective-permute-start.11 = (bf16[1024,256]{1,0:T(8,128)(2,1)S(1)}, bf16[1024,256]{1,0:T(8,128)(2,1)S(1)}, u32[]{:S(2)}, u32[]{:S(2)}) collective-permute-start(bf16[1024,256]{1,0:T(8,128)(2,1)S(1)} %get-tuple-element.67), channel_id=1, source_target_pairs={{0,2},{1,3},{2,0},{3,1},{4,6},{5,7},{6,4},{7,5},{8,10},{9,11},{10,... | collective-permute-start | bytes 1572872 | tf_op jit(solution)/shard_map/ppermute | solution.py:788
  52.3 32.9 %collective-permute-start.12 = (bf16[1024,256]{1,0:T(8,128)(2,1)S(1)}, bf16[1024,256]{1,0:T(8,128)(2,1)S(1)}, u32[]{:S(2)}, u32[]{:S(2)}) collective-permute-start(bf16[1024,256]{1,0:T(8,128)(2,1)S(1)} %get-tuple-element.68), channel_id=1, source_target_pairs={{0,3},{1,0},{2,1},{3,2},{4,7},{5,4},{6,5},{7,6},{8,11},{9,8},{10,9... | collective-permute-start | bytes 1572872 | tf_op jit(solution)/shard_map/ppermute | solution.py:788
  67.2 20.6 %collective-permute-start.14 = (bf16[2,768,256]{2,1,0:T(8,128)(2,1)S(1)}, bf16[2,768,256]{2,1,0:T(8,128)(2,1)S(1)}, u32[]{:S(2)}, u32[]{:S(2)}) collective-permute-start(bf16[2,768,256]{2,1,0:T(8,128)(2,1)S(1)} %get-tuple-element.84), channel_id=1, source_target_pairs={{0,4},{4,8},{8,12},{12,16},{16,20},{20,24},{24,28},{28,32},{32,36}... | collective-permute-start | bytes 2359304 | tf_op jit(solution)/shard_map/ppermute | solution.py:798
  78.1 9.7 %collective-permute-start.15 = (bf16[2,768,256]{2,1,0:T(8,128)(2,1)S(1)}, bf16[2,768,256]{2,1,0:T(8,128)(2,1)S(1)}, u32[]{:S(2)}, u32[]{:S(2)}) collective-permute-start(bf16[2,768,256]{2,1,0:T(8,128)(2,1)S(1)} %get-tuple-element.85), channel_id=1, source_target_pairs={{4,0},{8,4},{12,8},{16,12},{20,16},{24,20},{28,24},{32,28},{36,32}... | collective-permute-start | bytes 2359304 | tf_op jit(solution)/shard_map/ppermute | solution.py:799
  93.6 7.4 %collective-permute-start.19 = (bf16[512,1024]{1,0:T(8,128)(2,1)S(1)}, bf16[512,1024]{1,0:T(8,128)(2,1)S(1)}, u32[]{:S(2)}, u32[]{:S(2)}) collective-permute-start(bf16[512,1024]{1,0:T(8,128)(2,1)S(1)} %get-tuple-element.95), channel_id=1, source_target_pairs={{0,4},{4,0},{8,12},{12,8},{16,20},{20,16},{24,28},{28,24},{32,36},... | collective-permute-start | bytes 3145736 | tf_op jit(solution)/shard_map/ppermute | solution.py:758
  97.7 29.0 %collective-permute-start.16 = (bf16[1040,256]{1,0:T(8,128)(2,1)S(1)}, bf16[1040,256]{1,0:T(8,128)(2,1)S(1)}, u32[]{:S(2)}, u32[]{:S(2)}) collective-permute-start(bf16[1040,256]{1,0:T(8,128)(2,1)S(1)} %get-tuple-element.87), channel_id=1, source_target_pairs={{0,1},{1,2},{2,3},{3,0},{4,5},{5,6},{6,7},{7,4},{8,9},{9,10},{10,1... | collective-permute-start | bytes 1597448 | tf_op jit(solution)/shard_map/ppermute | solution.py:788
  98.4 32.0 %collective-permute-start.17 = (bf16[1040,256]{1,0:T(8,128)(2,1)S(1)}, bf16[1040,256]{1,0:T(8,128)(2,1)S(1)}, u32[]{:S(2)}, u32[]{:S(2)}) collective-permute-start(bf16[1040,256]{1,0:T(8,128)(2,1)S(1)} %get-tuple-element.88), channel_id=1, source_target_pairs={{0,2},{1,3},{2,0},{3,1},{4,6},{5,7},{6,4},{7,5},{8,10},{9,11},{10,... | collective-permute-start | bytes 1597448 | tf_op jit(solution)/shard_map/ppermute | solution.py:788
  99.2 31.2 %collective-permute-start.18 = (bf16[1040,256]{1,0:T(8,128)(2,1)S(1)}, bf16[1040,256]{1,0:T(8,128)(2,1)S(1)}, u32[]{:S(2)}, u32[]{:S(2)}) collective-permute-start(bf16[1040,256]{1,0:T(8,128)(2,1)S(1)} %get-tuple-element.89), channel_id=1, source_target_pairs={{0,3},{1,0},{2,1},{3,2},{4,7},{5,4},{6,5},{7,6},{8,11},{9,8},{10,9... | collective-permute-start | bytes 1597448 | tf_op jit(solution)/shard_map/ppermute | solution.py:788
  101.9 11.4 %collective-permute-start.20 = (bf16[128,1024]{1,0:T(8,128)(2,1)S(1)}, bf16[128,1024]{1,0:T(8,128)(2,1)S(1)}, u32[]{:S(2)}, u32[]{:S(2)}) collective-permute-start(bf16[128,1024]{1,0:T(8,128)(2,1)S(1)} %get-tuple-element.97), channel_id=1, source_target_pairs={{0,8},{4,36},{8,16},{12,44},{16,24},{20,52},{24,0},{28,60},{32,40}... | collective-permute-start | bytes 786440 | tf_op jit(solution)/shard_map/ppermute | solution.py:756
  103.4 14.1 %collective-permute-start.21 = (bf16[128,1024]{1,0:T(8,128)(2,1)S(1)}, bf16[128,1024]{1,0:T(8,128)(2,1)S(1)}, u32[]{:S(2)}, u32[]{:S(2)}) collective-permute-start(bf16[128,1024]{1,0:T(8,128)(2,1)S(1)} %get-tuple-element.98), channel_id=1, source_target_pairs={{0,16},{4,68},{8,24},{12,76},{16,0},{20,84},{24,8},{28,92},{32,48}... | collective-permute-start | bytes 786440 | tf_op jit(solution)/shard_map/ppermute | solution.py:756
  120.5 11.6 %collective-permute-start.23 = (bf16[32,1024]{1,0:T(8,128)(2,1)S(1)}, bf16[32,1024]{1,0:T(8,128)(2,1)S(1)}, u32[]{:S(2)}, u32[]{:S(2)}) collective-permute-start(bf16[32,1024]{1,0:T(8,128)(2,1)S(1)} %get-tuple-element.101), channel_id=1, source_target_pairs={{0,32},{4,12},{8,40},{12,20},{16,48},{20,28},{24,56},{28,4},{32,64... | collective-permute-start | bytes 196616 | tf_op jit(solution)/shard_map/ppermute | solution.py:756
  122.1 10.0 %collective-permute-start.24 = (bf16[32,1024]{1,0:T(8,128)(2,1)S(1)}, bf16[32,1024]{1,0:T(8,128)(2,1)S(1)}, u32[]{:S(2)}, u32[]{:S(2)}) collective-permute-start(bf16[32,1024]{1,0:T(8,128)(2,1)S(1)} %get-tuple-element.102), channel_id=1, source_target_pairs={{0,64},{4,20},{8,72},{12,28},{16,80},{20,4},{24,88},{28,12},{32,96... | collective-permute-start | bytes 196616 | tf_op jit(solution)/shard_map/ppermute | solution.py:756
  (14 other events, 109.0 us)

commit v5 on v4

--- a/solution.py
+++ b/solution.py
@@ -57,7 +57,6 @@
 
 SMALL = pl.CostEstimate(flops=10**6, bytes_accessed=10**4, transcendentals=0)
 LARGE = pl.CostEstimate(flops=4 * 10**9, bytes_accessed=10**4, transcendentals=0)
-LAST = pl.CostEstimate(flops=1 * 10**9, bytes_accessed=10**4, transcendentals=0)
 SCALAR = pl.BlockSpec(memory_space=pltpu.SMEM)
 RESIDENT = pl.BlockSpec(memory_space=pltpu.VMEM)
 
@@ -98,8 +97,8 @@
 def project_kernel(
     place, t1a_any, t1b_any, t2a_any, t2b_any, t3a_any, t3b_any,
     t0_hbm, wq_hbm, wk_hbm, wv_hbm,
-    inverse, q, kv, to_left, to_right, normed_hbm,
-    t0, t1, t2, t3, wq, wk, wv, normed, in_sems, out_sems,
+    inverse, q, kv, to_left, to_right, normed_hbm, w_hbm,
+    t0, t1, t2, t3, w, normed, in_sems, out_sems,
 ):
     me = place[0]
     width = t0.shape[1]
@@ -112,10 +111,11 @@
         (t1b_any, t1.at[high]),
         (t2b_any, t2.at[high]),
         (t3b_any, t3.at[high]),
-        (wq_hbm, wq),
-        (wk_hbm, wk),
-        (wv_hbm, wv),
     ]
+    for n, source in enumerate((wq_hbm, wk_hbm, wv_hbm)):
+        for r in range(MP):
+            target = w.at[pl.ds(r * width, width), pl.ds(n * width, width)]
+            moves.append((source.at[share_rows(me, r, width), :], target))
     loads = [
         pltpu.make_async_copy(source, target, in_sems.at[n])
         for n, (source, target) in enumerate(moves)
@@ -145,20 +145,17 @@
         store = pltpu.make_async_copy(normed.at[rows], normed_hbm.at[rows], out_sems.at[step])
         store.start()
         stores.append(store)
-        return parts
-
-    def spread(step, parts):
+        return jnp.concatenate(parts, axis=1)
+
+    def spread(step, whole):
         if step == 0:
             for load in loads[7:]:
                 load.wait()
+            store = pltpu.make_async_copy(w, w_hbm, out_sems.at[4])
+            store.start()
+            stores.append(store)
         rows = block_rows(step)
-        sums = [None, None, None]
-        for r, part in enumerate(parts):
-            w_rows = share_rows(me, r, width)
-            for n, w in enumerate((wq, wk, wv)):
-                term = nn(part, w[w_rows, :])
-                sums[n] = term if sums[n] is None else sums[n] + term
-        fine = [x.astype(BF16) for x in sums]
+        fine = [nn(whole, w[:, n * width : (n + 1) * width]).astype(BF16) for n in range(3)]
         mid = [nn(half, x).astype(BF16) for x in fine]
         low = [nn(quarter, x).astype(BF16) for x in fine]
         mid_rows = slice(1024 + step * 128, 1024 + (step + 1) * 128)
@@ -201,7 +198,7 @@
     return pl.pallas_call(
         project_kernel,
         in_specs=[SCALAR] + [anywhere] * 10,
-        out_specs=[RESIDENT] * 5 + [anywhere],
+        out_specs=[RESIDENT] * 5 + [anywhere] * 2,
         out_shape=[
             out((8, width), F32),
             out((ALL_ROWS, width), BF16),
@@ -209,12 +206,14 @@
             edge,
             edge,
             pltpu.HBM((rows, MP * width), BF16),
+            pltpu.HBM((MP * width, 3 * width), BF16),
         ],
-        scratch_shapes=[share] * 7
+        scratch_shapes=[share] * 4
         + [
+            pltpu.VMEM((MP * width, 3 * width), BF16),
             pltpu.VMEM((rows, MP * width), BF16),
-            pltpu.SemaphoreType.DMA((10,)),
-            pltpu.SemaphoreType.DMA((4,)),
+            pltpu.SemaphoreType.DMA((19,)),
+            pltpu.SemaphoreType.DMA((5,)),
         ],
         compiler_params=pltpu.CompilerParams(vmem_limit_bytes=20 * 2**20),
         cost_estimate=SMALL,
@@ -227,13 +226,12 @@
     width = g0.shape[1]
     half = pool_matrix(BLOCK // 2, 2, 1.0)
     quarter = pool_matrix(BLOCK // 4, 4, 1.0)
+    columns = [w_out[:, share_rows(me, r, width)] for r in range(MP)]
+    turned_w = jnp.concatenate(columns, axis=1)
     for step in range(4):
         rows = block_rows(step)
-        total = None
-        for r, share in enumerate((g0, g1, g2, g3)):
-            term = nt(share[rows, :], w_out[:, share_rows(me, r, width)])
-            total = term if total is None else total + term
-        fine = total.astype(BF16)
+        shares = jnp.concatenate([share[rows, :] for share in (g0, g1, g2, g3)], axis=1)
+        fine = nt(shares, turned_w).astype(BF16)
         d_att[rows, :] = fine
         d_att[1024 + step * 128 : 1024 + (step + 1) * 128, :] = nn(half, fine).astype(BF16)
         d_att[1536 + step * 64 : 1536 + (step + 1) * 64, :] = nn(quarter, fine).astype(BF16)
@@ -242,7 +240,7 @@
 def cotangent(place, shares, w_out):
     rows, width = shares[0].shape
     outputs = [held((ALL_ROWS, width), BF16)]
-    return run(cotangent_kernel, "cotangent", 8, [place], [*shares, w_out], outputs)[0]
+    return run(cotangent_kernel, "cotangent", 10, [place], [*shares, w_out], outputs, (), LARGE)[0]
 
 
 EDGE_UNITS = ((0, 0), (0, 3), (1, 0), (1, 1), (2, 0))
@@ -529,7 +527,7 @@
     width = q.shape[1]
     outputs = [held((2 * BLOCK, width), F32), held((width // PAIR, 8, BLOCK), F32)]
     scratch = [turned(EXT_BLOCKS[0]), pltpu.VMEM((4 * BLOCK, PAIR), F32)]
-    return run(forward_inner_kernel, "forward_inner", 12, [bias], [q, kv], outputs, scratch, LARGE)
+    return run(forward_inner_kernel, "forward_inner", 12, [bias], [q, kv], outputs, scratch)
 
 
 def forward_edge(bias, q, kv, from_left, from_right, inner):
@@ -582,10 +580,9 @@
 
 
 def input_terms_kernel(
-    place, d_query, d_kv, from_left, from_right, normed, wq, wk, wv, d_proj,
+    d_query, d_kv, from_left, from_right, normed, w, d_proj,
     dots, own, one, two, three, dot_rows,
 ):
-    me = place[0]
     width = d_query.shape[1]
     half = spread_matrix(BLOCK // 2, 2, 0.5)
     quarter = spread_matrix(BLOCK // 4, 4, 0.25)
@@ -607,10 +604,9 @@
         for n, grad in enumerate(grads[1:]):
             d_proj[rows, n * width : (n + 1) * width] = grad
         dot = None
+        every = jnp.concatenate(grads, axis=1)
         for r, out in enumerate((own, one, two, three)):
-            at = share_rows(me, r, width)
-            term = nt(grads[0], wq[at, :]) + nt(grads[1], wk[at, :]) + nt(grads[2], wv[at, :])
-            term = term.astype(BF16)
+            term = nt(every, w[r * width : (r + 1) * width, :]).astype(BF16)
             out[rows, :] = term
             part = term.astype(F32) * normed[rows, r * width : (r + 1) * width].astype(F32)
             dot = part if dot is None else dot + part
@@ -625,13 +621,13 @@
         out[4 * BLOCK :, :] = pieces
 
 
-def input_terms(place, d_query, d_kv, from_left, from_right, normed, wq, wk, wv):
+def input_terms(d_query, d_kv, from_left, from_right, normed, w):
     rows, width = d_query.shape
-    inputs = [d_query, d_kv, from_left, from_right, normed, wq, wk, wv]
+    inputs = [d_query, d_kv, from_left, from_right, normed, w]
     outputs = [held((rows, 2 * width), BF16), held((DOT_ROWS, width), BF16)]
     outputs += term_outputs(rows, width, DOT_ROWS)
     scratch = [pltpu.VMEM((DOT_ROWS, width), F32)]
-    return run(input_terms_kernel, "input_terms", 16, [place], inputs, outputs, scratch)
+    return run(input_terms_kernel, "input_terms", 16, [], inputs, outputs, scratch)
 
 
 def sum_terms(own, received, at):
@@ -652,24 +648,34 @@
     return run(finish_out_kernel, "finish_out", 8, [], [own, *received], outputs)[0]
 
 
-def finish_grad_kernel(own, one, two, three, tokens, inverse, dots, result):
-    rows, width = own.shape
-    pieces = dots[...].astype(F32)
-    for term in (one, two, three):
-        pieces = pieces + term[rows:, :].astype(F32)
-    means = (pieces[0:4] + pieces[4:8] + pieces[8:12]) / (MP * width)
+def near_sum_kernel(own, one, three, dots, total, pieces):
+    rows = own.shape[0]
+    for b in range(rows // BLOCK):
+        at = block_rows(b)
+        total[at, :] = sum_terms(own, (one, three), at)
+    pieces[...] = dots[...].astype(F32) + one[rows:, :].astype(F32) + three[rows:, :].astype(F32)
+
+
+def finish_grad_kernel(near, pieces, far, tokens, inverse, result):
+    rows, width = near.shape
+    every = pieces[...] + far[rows:, :].astype(F32)
+    means = (every[0:4] + every[4:8] + every[8:12]) / (MP * width)
     for b in range(rows // BLOCK):
         at = block_rows(b)
         mean = as_column(means[b : b + 1, :])
         inv = as_column(inverse[b : b + 1, :])
-        total = sum_terms(own, (one, two, three), at)
+        total = near[at, :] + far[at, :].astype(F32)
         result[at, :] = inv * (total - tokens[at, :].astype(F32) * inv * mean)
 
 
 def finish_grad(own, received, tokens, inverse, dots):
-    inputs = [own, *received, tokens, inverse, dots]
+    one, two, three = received
+    outputs = [held(own.shape, F32), held(dots.shape, F32)]
+    inputs = [own, one, three, dots]
+    near, pieces = run(near_sum_kernel, "near_sum", 8, [], inputs, outputs, (), LARGE)
+    inputs = [near, pieces, two, tokens, inverse]
     outputs = [held(own.shape, F32)]
-    return run(finish_grad_kernel, "finish_grad", 8, [], inputs, outputs, (), LAST)[0]
+    return run(finish_grad_kernel, "finish_grad", 8, [], inputs, outputs)[0]
 
 
 def early_kernel(g0, g1, g2, g3, attended, normed, d_query, outer, inner):
@@ -741,8 +747,14 @@
     go[...] = total[:, 3 * width :]
 
 
-def sum_over_seq(place, mine, other):
-    cols = mine.shape[1]
+def sum_over_core(place, mine, other):
+    got = lax.ppermute(other, "seq", [(i, i ^ 1) for i in range(32)])
+    parts = [held((128, mine.shape[1]), BF16)] * 4
+    return run(pair_sum_kernel, "pair_sum", 6, [place], [mine, got], parts)
+
+
+def sum_over_seq(place, parts):
+    cols = parts[0].shape[1]
 
     def sent(value, stage, d):
         pairs = []
@@ -755,9 +767,6 @@
             pairs.append((i, (y * 4 + x) * 2 + core))
         return lax.ppermute(value, "seq", pairs)
 
-    got = lax.ppermute(other, "seq", [(i, i ^ 1) for i in range(32)])
-    parts = [held((128, cols), BF16)] * 4
-    parts = run(pair_sum_kernel, "pair_sum", 6, [place], [mine, got], parts)
     parts = [parts[0]] + [sent(parts[d], 0, d) for d in (1, 2, 3)]
     rows = [held((32, cols), BF16)] * 4
     scratch = [pltpu.VMEM((128, cols), BF16)]
@@ -818,21 +827,22 @@
         ]
     )
     token_shares = gather_shares(tokens)
-    near_grad = tied(grad_out, *(token_shares[n] for n in (1, 2, 5, 6)))
-    far_grad = tied(grad_out, *token_shares)
-    far = turned_by(far_grad, 2)
-    grad_shares = [grad_out, to_previous(near_grad), far, to_next(near_grad)]
-    inverse, q, kv, to_left, to_right, normed = project(
+    sent_grad = tied(grad_out, *(token_shares[n] for n in (1, 2, 5, 6)))
+    grad_shares = [
+        grad_out, to_previous(sent_grad), turned_by(sent_grad, 2), to_next(sent_grad)
+    ]
+    inverse, q, kv, to_left, to_right, normed, w = project(
         me, token_shares, w_query, w_key, w_value
     )
     from_left, from_right = exchange(to_left, to_right)
-    near_q = tied(q, grad_shares[1], grad_shares[3])
-    inner_out, inner_stats = forward_inner(bias, near_q, kv)
+    inner_out, inner_stats = forward_inner(bias, q, kv)
+    grad_shares = tied(grad_shares, inner_out)
+    d_att = cotangent(me, grad_shares, w_out)
+    inner_out = tied(inner_out, d_att)
     attended, stats = forward_edge(bias, q, kv, from_left, from_right, inner_out)
     out_own, *terms = out_terms(me, attended, w_out)
     out_received = sum_over_mp(terms)
-    grad_shares = tied(grad_shares, out_own)
-    d_att = cotangent(me, grad_shares, w_out)
+    stats = tied(stats, out_own)
     dq_f, d_kv, to_left, to_right = edge_backward(
         bias, stats, q, kv, from_left, from_right, d_att
     )
@@ -842,13 +852,15 @@
     outer, inner = early_terms(grad_shares, attended, normed, d_query)
     d_query = tied(d_query, outer)
     d_proj, dots, own, *terms = input_terms(
-        me, d_query, d_kv, from_left, from_right, normed, w_query, w_key, w_value
+        d_query, d_kv, from_left, from_right, normed, w
     )
-    received = sum_over_mp(terms)
     attn_out = finish_out(out_own, out_received)
     mine, other = inner_terms(me, normed, d_proj, inner, outer)
+    core_sums = sum_over_core(me, mine, other)
+    terms[1] = tied(terms[1], core_sums[0])
+    received = sum_over_mp(terms)
     grad_tokens = finish_grad(own, received, tokens, inverse, dots)
-    *weight_grads, grad_w_out = sum_over_seq(me, mine, other)
+    *weight_grads, grad_w_out = sum_over_seq(me, core_sums)
     return (attn_out, grad_tokens, *weight_grads, grad_w_out.T)
 
 

time: 134 us -> 141 us (1.052)
  waiting for transfers between devices: 15.7 us -> 23.2 us
    ppermute x4, waiting for transfers between devices: 2.23 us -> 11.3 us  [to_previous(): return lax.ppermute(value, 'mp', [((i + 1) % MP, i) for i in range(MP)])]
    ppermute x7, starting transfers between devices: 10.2 us -> 12.8 us  [turned_by(): return lax.ppermute(value, 'mp', [(i, (i + step) % MP) for i in range(MP)])]
    ppermute x2, starting transfers between devices: 12.2 us -> 10 us  [exchange(): from_left = lax.ppermute(to_right, 'seq', [(i, i + 1) for i in range(ends)])]
    ppermute x4, waiting for transfers between devices: 7.1 us -> 5.07 us  [to_next(): return lax.ppermute(value, 'mp', [(i, (i + 1) % MP) for i in range(MP)])]
    pallas_call x14 -> x15, Pallas kernels: 44 us -> 43.8 us  [run(): pl.pallas_call(kernel, in_specs=[SCALAR] * len(scalars) + [RESIDENT] * le...]
  transfers between devices with their start and end apart: 26 -> 26, of which waited for: 7 -> 6; matrix products, arithmetic and copies ran while one was open for 0% -> 0% of each run, Pallas kernels for 34% -> 26%
where the time goes in v5:
time: 141 us
  starting transfers between devices  63.2 us (45%)
  Pallas kernels  51.2 us (36%)
  waiting for transfers between devices  23.2 us (16%)
  local copies, waits for them, and re-layouts  1.81 us (1%)
    pallas_call x15, Pallas kernels, run(): pl.pallas_call(kernel, in_specs=[SCALAR] * len(scalars) + [RESIDENT] * le...  43.8 us
    ppermute x6, starting transfers between devices, sent(): return lax.ppermute(value, 'seq', pairs)  20.6 us
    ppermute x7, starting transfers between devices, turned_by(): return lax.ppermute(value, 'mp', [(i, (i + step) % MP) for i in range(MP)])  12.8 us
    ppermute x4, waiting for transfers between devices, to_previous(): return lax.ppermute(value, 'mp', [((i + 1) % MP, i) for i in range(MP)])  11.3 us
    ppermute x2, starting transfers between devices, exchange(): from_left = lax.ppermute(to_right, 'seq', [(i, i + 1) for i in range(ends)])  10 us
    ppermute x4, starting transfers between devices, to_previous(): return lax.ppermute(value, 'mp', [((i + 1) % MP, i) for i in range(MP)])  8.85 us
    pallas_call x1, Pallas kernels, project(): pl.pallas_call(project_kernel, in_specs=[SCALAR] + [anywhere] * 10, out_s...  7.49 us
    ppermute x6, waiting for transfers between devices, sent(): return lax.ppermute(value, 'seq', pairs)  6.87 us
  transfers between devices with their start and end apart: 26, of which 6 were waited for; matrix products, arithmetic and copies ran while one was open for 0% of the time, Pallas kernels for 26%

profile of v5, /device:TPU:0, one launch (start us, length us, event | category | flops | bytes accessed | tf_op | source)
XLA Modules:
  0.0 140.6 jit_solution(2704058596472065106)
XLA Ops:
  1.7 2.1 %collective-permute-start.3 = (bf16[512,256]{1,0:T(8,128)(2,1)S(1)}, bf16[512,256]{1,0:T(8,128)(2,1)S(1)}, u32[]{:S(2)}, u32[]{:S(2)}) collective-permute-start(bf16[512,256]{1,0:T(8,128)(2,1)S(1)} %get-tuple-element.116), channel_id=1, source_target_pairs={{0,1},{1,2},{2,3},{3,0},{4,5},{5,6},{6,7},{7,4},{8,9},{9,10},{10,1... | collective-permute-start | bytes 786440 | tf_op jit(solution)/shard_map/ppermute | solution.py:780
  3.8 2.2 %collective-permute-start = (bf16[512,256]{1,0:T(8,128)(2,1)S(1)}, bf16[512,256]{1,0:T(8,128)(2,1)S(1)}, u32[]{:S(2)}, u32[]{:S(2)}) collective-permute-start(bf16[512,256]{1,0:T(8,128)(2,1)S(1)} %get-tuple-element.117), channel_id=1, source_target_pairs={{1,0},{2,1},{3,2},{0,3},{5,4},{6,5},{7,6},{4,7},{9,8},{10,9},{11,1... | collective-permute-start | bytes 786440 | tf_op jit(solution)/shard_map/ppermute | solution.py:784
  8.0 5.0 %collective-permute-done.3.t3b_any = bf16[512,256]{1,0:T(8,128)(2,1)S(1)} collective-permute-done((bf16[512,256]{1,0:T(8,128)(2,1)S(1)}, bf16[512,256]{1,0:T(8,128)(2,1)S(1)}, u32[]{:S(2)}, u32[]{:S(2)}) %collective-permute-start.3) | collective-permute-done | bytes 262176 | tf_op jit(solution)/shard_map/ppermute | solution.py:780
  13.0 3.3 %collective-permute-start.2 = (bf16[512,256]{1,0:T(8,128)(2,1)S(1)}, bf16[512,256]{1,0:T(8,128)(2,1)}, u32[]{:S(2)}, u32[]{:S(2)}) collective-permute-start(bf16[512,256]{1,0:T(8,128)(2,1)S(1)} %collective-permute-done.t1a_any), channel_id=1, source_target_pairs={{1,0},{2,1},{3,2},{0,3},{5,4},{6,5},{7,6},{4,7},{9,8},{10,9},{11,1... | collective-permute-start | bytes 786440 | tf_op jit(solution)/shard_map/ppermute | solution.py:784
  16.4 2.2 %collective-permute-done.1.t1b_any = bf16[512,256]{1,0:T(8,128)(2,1)S(1)} collective-permute-done((bf16[512,256]{1,0:T(8,128)(2,1)S(1)}, bf16[512,256]{1,0:T(8,128)(2,1)S(1)}, u32[]{:S(2)}, u32[]{:S(2)}) %collective-permute-start.1) | collective-permute-done | bytes 262176 | tf_op jit(solution)/shard_map/ppermute | solution.py:784
  20.6 2.9 %collective-permute-start.9 = (bf16[1024,256]{1,0:T(8,128)(2,1)}, bf16[1024,256]{1,0:T(8,128)(2,1)}, u32[]{:S(2)}, u32[]{:S(2)}) collective-permute-start(bf16[1024,256]{1,0:T(8,128)(2,1)} %g0.1), channel_id=1, source_target_pairs={{0,2},{1,3},{2,0},{3,1},{4,6},{5,7},{6,4},{7,5},{8,10},{9,11},{10,... | collective-permute-start | bytes 1572872 | tf_op jit(solution)/shard_map/ppermute | solution.py:797
  25.7 9.0 %collective-permute-done.2.t2a_any = bf16[512,256]{1,0:T(8,128)(2,1)} collective-permute-done((bf16[512,256]{1,0:T(8,128)(2,1)S(1)}, bf16[512,256]{1,0:T(8,128)(2,1)}, u32[]{:S(2)}, u32[]{:S(2)}) %collective-permute-start.2) | collective-permute-done | bytes 262176 | tf_op jit(solution)/shard_map/ppermute | solution.py:784
  34.7 7.5 %project.1 = (f32[8,256]{1,0:T(8,128)S(1)}, bf16[1792,256]{1,0:T(8,128)(2,1)S(1)}, bf16[2,1792,256]{2,1,0:T(8,128)(2,1)S(1)}, bf16[2,768,256]{2,1,0:T(8,128)(2,1...) custom-call(s32[4]{0:T(128)S(1)} %pad_add_fusion.place, ...), custom_call_target="tpu_custom_call" | custom-call | flops 1000000 | bytes 10000 | tf_op jit(solution)/shard_map/project/pallas_call | solution.py:198
  45.2 3.6 %forward_inner.1 = (f32[512,256]{1,0:T(8,128)S(1)}, f32[2,8,256]{2,1,0:T(8,128)S(1)}) custom-call(f32[2]{0:T(128)S(1)} %pad_maximum_fusion.bias_ref, bf16[1792,256]{1,0:T(8,128)(2,1)S(1)} %get-tuple-element.61.q, bf16[2,1792,256]{2,1,0:T(8,128)(2,1)S(1)} %get-tuple-element.62.kv), custom_call_target="tpu_custom_call" | custom-call | flops 1000000 | bytes 10000 | tf_op jit(solution)/shard_map/forward_inner/pallas_call | solution.py:69
  48.8 3.2 %cotangent.1.grads = bf16[1792,256]{1,0:T(8,128)(2,1)S(1)} custom-call(s32[4]{0:T(128)S(1)} %pad_add_fusion.place, bf16[1024,256]{1,0:T(8,128)(2,1)S(1)} %copy-done.4, bf16[1024,256]{1,0:T(8,128)(2,1)} %collective-permute-done.8.g1, bf16[1024,256]{1,0:T(8,128)(2,1)} %collective-permute-done.9.g2, bf16[1024,256]{1,0:T(8,128)(2,1)} %collective-permute-done.10.g3, ...), custom_call_target="tpu_custom_call" | custom-call | flops 4000000000 | bytes 10000 | tf_op jit(solution)/shard_map/cotangent/pallas_call | solution.py:69
  52.1 6.5 %forward_edge.1 = (bf16[1024,256]{1,0:T(8,128)(2,1)S(1)}, f32[2,24,256]{2,1,0:T(8,128)S(1)}) custom-call(f32[2]{0:T(128)S(1)} %pad_maximum_fusion.bias_ref, bf16[1792,256]{1,0:T(8,128)(2,1)S(1)} %get-tuple-element.61.q, bf16[2,1792,256]{2,1,0:T(8,128)(2,1)S(1)} %get-tuple-element.62.kv, bf16[2,768,256]{2,1,0:T(8,128)(2,1)S(1)} %collective-permute-done.6.from_left, ...), custom_call_target="tpu_custom_call" | custom-call | flops 1000000 | bytes 10000 | tf_op jit(solution)/shard_map/forward_edge/pallas_call | solution.py:69
  60.7 5.0 %collective-permute-start.12 = (bf16[1024,256]{1,0:T(8,128)(2,1)S(1)}, bf16[1024,256]{1,0:T(8,128)(2,1)S(1)}, u32[]{:S(2)}, u32[]{:S(2)}) collective-permute-start(bf16[1024,256]{1,0:T(8,128)(2,1)S(1)} %get-tuple-element.75), channel_id=1, source_target_pairs={{0,2},{1,3},{2,0},{3,1},{4,6},{5,7},{6,4},{7,5},{8,10},{9,11},{10,... | collective-permute-start | bytes 1572872 | tf_op jit(solution)/shard_map/ppermute | solution.py:797
  65.7 10.7 %edge_backward.1 = (f32[1024,256]{1,0:T(8,128)S(1)}, f32[2,1024,256]{2,1,0:T(8,128)S(1)}, bf16[2,768,256]{2,1,0:T(8,128)(2,1)S(1)}, bf16[2,768,256]{2,1,0:T(8,128)(2,1)S(1)}) custom-call(f32[2]{0:T(128)S(1)} %pad_maximum_fusion.bias_ref, f32[2,24,256]{2,1,0:T(8,128)S(1)} %get-tuple-element.79.stats, bf16[1792,256]{1,0:T(8,128)(2,1)S(1)} %get-tuple-element.61.q, ...), custom_call_target="tpu_custom_call" | custom-call | flops 1000000 | bytes 10000 | tf_op jit(solution)/shard_map/edge_backward/pallas_call | solution.py:69
  76.3 8.7 %collective-permute-start.14 = (bf16[2,768,256]{2,1,0:T(8,128)(2,1)S(1)}, bf16[2,768,256]{2,1,0:T(8,128)(2,1)S(1)}, u32[]{:S(2)}, u32[]{:S(2)}) collective-permute-start(bf16[2,768,256]{2,1,0:T(8,128)(2,1)S(1)} %get-tuple-element.88), channel_id=1, source_target_pairs={{0,4},{4,8},{8,12},{12,16},{16,20},{20,24},{24,28},{28,32},{32,36}... | collective-permute-start | bytes 2359304 | tf_op jit(solution)/shard_map/ppermute | solution.py:807
  86.6 5.5 %inner_backward.1 = (bf16[1024,256]{1,0:T(8,128)(2,1)S(1)}, f32[2,1024,256]{2,1,0:T(8,128)S(1)}) custom-call(f32[2]{0:T(128)S(1)} %pad_maximum_fusion.bias_ref, f32[2,8,256]{2,1,0:T(8,128)S(1)} %get-tuple-element.77.stats, bf16[1792,256]{1,0:T(8,128)(2,1)S(1)} %get-tuple-element.61.q, bf16[2,1792,256]{2,1,0:T(8,128)(2,1)S(1)} %get-tuple-element.62.kv, ...), custom_call_target="tpu_custom_call" | custom-call | flops 1000000 | bytes 10000 | tf_op jit(solution)/shard_map/inner_backward/pallas_call | solution.py:69
  92.1 2.8 %early_terms.1 = (bf16[1024,256]{1,0:T(8,128)(2,1)S(1)}, bf16[1024,256]{1,0:T(8,128)(2,1)S(1)}) custom-call(bf16[1024,256]{1,0:T(8,128)(2,1)S(1)} %copy-done.4, bf16[1024,256]{1,0:T(8,128)(2,1)} %collective-permute-done.8.g1, bf16[1024,256]{1,0:T(8,128)(2,1)} %collective-permute-done.9.g2, bf16[1024,256]{1,0:T(8,128)(2,1)} %collective-permute-done.10.g3, ...), custom_call_target="tpu_custom_call" | custom-call | flops 4000000000 | bytes 10000 | tf_op jit(solution)/shard_map/early_terms/pallas_call | solution.py:69
  95.0 2.9 %input_terms.1 = (bf16[1024,512]{1,0:T(8,128)(2,1)S(1)}, bf16[16,256]{1,0:T(8,128)(2,1)S(1)}, bf16[1024,256]{1,0:T(8,128)(2,1)S(1)}, bf16[1040,256]{1,0:T(8,128)...) custom-call(bf16[1024,256]{1,0:T(8,128)(2,1)S(1)} %get-tuple-element.86.d_query, ...), custom_call_target="tpu_custom_call" | custom-call | flops 1000000 | bytes 10000 | tf_op jit(solution)/shard_map/input_terms/pallas_call | solution.py:69
  97.9 2.1 %inner_terms.1 = (bf16[512,1024]{1,0:T(8,128)(2,1)S(1)}, bf16[512,1024]{1,0:T(8,128)(2,1)S(1)}) custom-call(s32[4]{0:T(128)S(1)} %pad_add_fusion.place, bf16[1024,1024]{1,0:T(8,128)(2,1)S(1)} %copy-done, bf16[1024,512]{1,0:T(8,128)(2,1)S(1)} %get-tuple-element.98.d_proj, bf16[1024,256]{1,0:T(8,128)(2,1)S(1)} %get-tuple-element.99.inner, ...), custom_call_target="tpu_custom_call" | custom-call | flops 1000000 | bytes 10000 | tf_op jit(solution)/shard_map/inner_terms/pallas_call | solution.py:69
  100.0 3.8 %collective-permute-start.18 = (bf16[512,1024]{1,0:T(8,128)(2,1)S(1)}, bf16[512,1024]{1,0:T(8,128)(2,1)S(1)}, u32[]{:S(2)}, u32[]{:S(2)}) collective-permute-start(bf16[512,1024]{1,0:T(8,128)(2,1)S(1)} %get-tuple-element.101), channel_id=1, source_target_pairs={{0,4},{4,0},{8,12},{12,8},{16,20},{20,16},{24,28},{28,24},{32,36},... | collective-permute-start | bytes 3145736 | tf_op jit(solution)/shard_map/ppermute | solution.py:751
  109.3 6.9 %collective-permute-start.21 = (bf16[128,1024]{1,0:T(8,128)(2,1)S(1)}, bf16[128,1024]{1,0:T(8,128)(2,1)S(1)}, u32[]{:S(2)}, u32[]{:S(2)}) collective-permute-start(bf16[128,1024]{1,0:T(8,128)(2,1)S(1)} %get-tuple-element.106), channel_id=1, source_target_pairs={{0,16},{4,68},{8,24},{12,76},{16,0},{20,84},{24,8},{28,92},{32,48}... | collective-permute-start | bytes 786440 | tf_op jit(solution)/shard_map/ppermute | solution.py:768
  116.3 2.9 %collective-permute-done.20.b = bf16[128,1024]{1,0:T(8,128)(2,1)S(1)} collective-permute-done((bf16[128,1024]{1,0:T(8,128)(2,1)S(1)}, bf16[128,1024]{1,0:T(8,128)(2,1)S(1)}, u32[]{:S(2)}, u32[]{:S(2)}) %collective-permute-start.20) | collective-permute-done | bytes 262176 | tf_op jit(solution)/shard_map/ppermute | solution.py:768
  121.1 2.3 %collective-permute-done.21.c = bf16[128,1024]{1,0:T(8,128)(2,1)S(1)} collective-permute-done((bf16[128,1024]{1,0:T(8,128)(2,1)S(1)}, bf16[128,1024]{1,0:T(8,128)(2,1)S(1)}, u32[]{:S(2)}, u32[]{:S(2)}) %collective-permute-start.21) | collective-permute-done | bytes 262176 | tf_op jit(solution)/shard_map/ppermute | solution.py:768
  125.9 2.2 %collective-permute-start.24 = (bf16[32,1024]{1,0:T(8,128)(2,1)S(1)}, bf16[32,1024]{1,0:T(8,128)(2,1)S(1)}, u32[]{:S(2)}, u32[]{:S(2)}) collective-permute-start(bf16[32,1024]{1,0:T(8,128)(2,1)S(1)} %get-tuple-element.110), channel_id=1, source_target_pairs={{0,64},{4,20},{8,72},{12,28},{16,80},{20,4},{24,88},{28,12},{32,96... | collective-permute-start | bytes 196616 | tf_op jit(solution)/shard_map/ppermute | solution.py:768
  128.1 8.2 %collective-permute-start.25 = (bf16[32,1024]{1,0:T(8,128)(2,1)S(1)}, bf16[32,1024]{1,0:T(8,128)(2,1)S(1)}, u32[]{:S(2)}, u32[]{:S(2)}) collective-permute-start(bf16[32,1024]{1,0:T(8,128)(2,1)S(1)} %get-tuple-element.111), channel_id=1, source_target_pairs={{0,96},{4,28},{8,104},{12,4},{16,112},{20,12},{24,120},{28,20},{32... | collective-permute-start | bytes 196616 | tf_op jit(solution)/shard_map/ppermute | solution.py:768
  (67 shorter events, 28.0 us)
Async XLA Ops:
  1.7 11.3 %collective-permute-start.3 = (bf16[512,256]{1,0:T(8,128)(2,1)S(1)}, bf16[512,256]{1,0:T(8,128)(2,1)S(1)}, u32[]{:S(2)}, u32[]{:S(2)}) collective-permute-start(bf16[512,256]{1,0:T(8,128)(2,1)S(1)} %get-tuple-element.116), channel_id=1, source_target_pairs={{0,1},{1,2},{2,3},{3,0},{4,5},{5,6},{6,7},{7,4},{8,9},{9,10},{10,1... | collective-permute-start | bytes 786440 | tf_op jit(solution)/shard_map/ppermute | solution.py:780
  3.8 9.3 %collective-permute-start = (bf16[512,256]{1,0:T(8,128)(2,1)S(1)}, bf16[512,256]{1,0:T(8,128)(2,1)S(1)}, u32[]{:S(2)}, u32[]{:S(2)}) collective-permute-start(bf16[512,256]{1,0:T(8,128)(2,1)S(1)} %get-tuple-element.117), channel_id=1, source_target_pairs={{1,0},{2,1},{3,2},{0,3},{5,4},{6,5},{7,6},{4,7},{9,8},{10,9},{11,1... | collective-permute-start | bytes 786440 | tf_op jit(solution)/shard_map/ppermute | solution.py:784
  6.0 12.6 %collective-permute-start.1 = (bf16[512,256]{1,0:T(8,128)(2,1)S(1)}, bf16[512,256]{1,0:T(8,128)(2,1)S(1)}, u32[]{:S(2)}, u32[]{:S(2)}) collective-permute-start(bf16[512,256]{1,0:T(8,128)(2,1)S(1)} %get-tuple-element.116), channel_id=1, source_target_pairs={{1,0},{2,1},{3,2},{0,3},{5,4},{6,5},{7,6},{4,7},{9,8},{10,9},{11,1... | collective-permute-start | bytes 786440 | tf_op jit(solution)/shard_map/ppermute | solution.py:784
  7.9 10.7 %collective-permute-start.5 = (bf16[512,256]{1,0:T(8,128)(2,1)S(1)}, bf16[512,256]{1,0:T(8,128)(2,1)S(1)}, u32[]{:S(2)}, u32[]{:S(2)}) collective-permute-start(bf16[512,256]{1,0:T(8,128)(2,1)S(1)} %get-tuple-element.117), channel_id=1, source_target_pairs={{0,1},{1,2},{2,3},{3,0},{4,5},{5,6},{6,7},{7,4},{8,9},{9,10},{10,1... | collective-permute-start | bytes 786440 | tf_op jit(solution)/shard_map/ppermute | solution.py:780
  13.0 12.0 %collective-permute-start.4 = (bf16[512,256]{1,0:T(8,128)(2,1)S(1)}, bf16[512,256]{1,0:T(8,128)(2,1)S(1)}, u32[]{:S(2)}, u32[]{:S(2)}) collective-permute-start(bf16[512,256]{1,0:T(8,128)(2,1)S(1)} %collective-permute-done.3.t3b_any), channel_id=1, source_target_pairs={{0,1},{1,2},{2,3},{3,0},{4,5},{5,6},{6,7},{7,4},{8,9},{9,10},{10,1... | collective-permute-start | bytes 786440 | tf_op jit(solution)/shard_map/ppermute | solution.py:780
  13.0 21.7 %collective-permute-start.2 = (bf16[512,256]{1,0:T(8,128)(2,1)S(1)}, bf16[512,256]{1,0:T(8,128)(2,1)}, u32[]{:S(2)}, u32[]{:S(2)}) collective-permute-start(bf16[512,256]{1,0:T(8,128)(2,1)S(1)} %collective-permute-done.t1a_any), channel_id=1, source_target_pairs={{1,0},{2,1},{3,2},{0,3},{5,4},{6,5},{7,6},{4,7},{9,8},{10,9},{11,1... | collective-permute-start | bytes 786440 | tf_op jit(solution)/shard_map/ppermute | solution.py:784
  18.6 30.1 %collective-permute-start.10 = (bf16[1024,256]{1,0:T(8,128)(2,1)}, bf16[1024,256]{1,0:T(8,128)(2,1)}, u32[]{:S(2)}, u32[]{:S(2)}) collective-permute-start(bf16[1024,256]{1,0:T(8,128)(2,1)} %g0.1), channel_id=1, source_target_pairs={{0,1},{1,2},{2,3},{3,0},{4,5},{5,6},{6,7},{7,4},{8,9},{9,10},{10,1... | collective-permute-start | bytes 1572872 | tf_op jit(solution)/shard_map/ppermute | solution.py:780
  20.6 28.2 %collective-permute-start.9 = (bf16[1024,256]{1,0:T(8,128)(2,1)}, bf16[1024,256]{1,0:T(8,128)(2,1)}, u32[]{:S(2)}, u32[]{:S(2)}) collective-permute-start(bf16[1024,256]{1,0:T(8,128)(2,1)} %g0.1), channel_id=1, source_target_pairs={{0,2},{1,3},{2,0},{3,1},{4,6},{5,7},{6,4},{7,5},{8,10},{9,11},{10,... | collective-permute-start | bytes 1572872 | tf_op jit(solution)/shard_map/ppermute | solution.py:797
  23.5 25.3 %collective-permute-start.8 = (bf16[1024,256]{1,0:T(8,128)(2,1)}, bf16[1024,256]{1,0:T(8,128)(2,1)}, u32[]{:S(2)}, u32[]{:S(2)}) collective-permute-start(bf16[1024,256]{1,0:T(8,128)(2,1)} %g0.1), channel_id=1, source_target_pairs={{1,0},{2,1},{3,2},{0,3},{5,4},{6,5},{7,6},{4,7},{9,8},{10,9},{11,1... | collective-permute-start | bytes 1572872 | tf_op jit(solution)/shard_map/ppermute | solution.py:784
  42.2 9.8 %collective-permute-start.6 = (bf16[2,768,256]{2,1,0:T(8,128)(2,1)}, bf16[2,768,256]{2,1,0:T(8,128)(2,1)S(1)}, u32[]{:S(2)}, u32[]{:S(2)}) collective-permute-start(bf16[2,768,256]{2,1,0:T(8,128)(2,1)} %get-tuple-element.63), channel_id=1, source_target_pairs={{0,4},{4,8},{8,12},{12,16},{16,20},{20,24},{24,28},{28,32},{32,36}... | collective-permute-start | bytes 2359304 | tf_op jit(solution)/shard_map/ppermute | solution.py:807
  43.6 8.5 %collective-permute-start.7 = (bf16[2,768,256]{2,1,0:T(8,128)(2,1)}, bf16[2,768,256]{2,1,0:T(8,128)(2,1)}, u32[]{:S(2)}, u32[]{:S(2)}) collective-permute-start(bf16[2,768,256]{2,1,0:T(8,128)(2,1)} %get-tuple-element.64), channel_id=1, source_target_pairs={{4,0},{8,4},{12,8},{16,12},{20,16},{24,20},{28,24},{32,28},{36,32}... | collective-permute-start | bytes 2359304 | tf_op jit(solution)/shard_map/ppermute | solution.py:808
  59.9 32.2 %collective-permute-start.11 = (bf16[1024,256]{1,0:T(8,128)(2,1)S(1)}, bf16[1024,256]{1,0:T(8,128)(2,1)S(1)}, u32[]{:S(2)}, u32[]{:S(2)}) collective-permute-start(bf16[1024,256]{1,0:T(8,128)(2,1)S(1)} %get-tuple-element.74), channel_id=1, source_target_pairs={{0,1},{1,2},{2,3},{3,0},{4,5},{5,6},{6,7},{7,4},{8,9},{9,10},{10,1... | collective-permute-start | bytes 1572872 | tf_op jit(solution)/shard_map/ppermute | solution.py:797
  60.7 31.4 %collective-permute-start.12 = (bf16[1024,256]{1,0:T(8,128)(2,1)S(1)}, bf16[1024,256]{1,0:T(8,128)(2,1)S(1)}, u32[]{:S(2)}, u32[]{:S(2)}) collective-permute-start(bf16[1024,256]{1,0:T(8,128)(2,1)S(1)} %get-tuple-element.75), channel_id=1, source_target_pairs={{0,2},{1,3},{2,0},{3,1},{4,6},{5,7},{6,4},{7,5},{8,10},{9,11},{10,... | collective-permute-start | bytes 1572872 | tf_op jit(solution)/shard_map/ppermute | solution.py:797
  65.7 26.4 %collective-permute-start.13 = (bf16[1024,256]{1,0:T(8,128)(2,1)S(1)}, bf16[1024,256]{1,0:T(8,128)(2,1)S(1)}, u32[]{:S(2)}, u32[]{:S(2)}) collective-permute-start(bf16[1024,256]{1,0:T(8,128)(2,1)S(1)} %get-tuple-element.76), channel_id=1, source_target_pairs={{0,3},{1,0},{2,1},{3,2},{4,7},{5,4},{6,5},{7,6},{8,11},{9,8},{10,9... | collective-permute-start | bytes 1572872 | tf_op jit(solution)/shard_map/ppermute | solution.py:797
  76.3 18.6 %collective-permute-start.14 = (bf16[2,768,256]{2,1,0:T(8,128)(2,1)S(1)}, bf16[2,768,256]{2,1,0:T(8,128)(2,1)S(1)}, u32[]{:S(2)}, u32[]{:S(2)}) collective-permute-start(bf16[2,768,256]{2,1,0:T(8,128)(2,1)S(1)} %get-tuple-element.88), channel_id=1, source_target_pairs={{0,4},{4,8},{8,12},{12,16},{16,20},{20,24},{24,28},{28,32},{32,36}... | collective-permute-start | bytes 2359304 | tf_op jit(solution)/shard_map/ppermute | solution.py:807
  85.0 10.0 %collective-permute-start.15 = (bf16[2,768,256]{2,1,0:T(8,128)(2,1)S(1)}, bf16[2,768,256]{2,1,0:T(8,128)(2,1)S(1)}, u32[]{:S(2)}, u32[]{:S(2)}) collective-permute-start(bf16[2,768,256]{2,1,0:T(8,128)(2,1)S(1)} %get-tuple-element.89), channel_id=1, source_target_pairs={{4,0},{8,4},{12,8},{16,12},{20,16},{24,20},{28,24},{32,28},{36,32}... | collective-permute-start | bytes 2359304 | tf_op jit(solution)/shard_map/ppermute | solution.py:808
  103.7 24.4 %collective-permute-start.16 = (bf16[1040,256]{1,0:T(8,128)(2,1)S(1)}, bf16[1040,256]{1,0:T(8,128)(2,1)S(1)}, u32[]{:S(2)}, u32[]{:S(2)}) collective-permute-start(bf16[1040,256]{1,0:T(8,128)(2,1)S(1)} %get-tuple-element.92), channel_id=1, source_target_pairs={{0,1},{1,2},{2,3},{3,0},{4,5},{5,6},{6,7},{7,4},{8,9},{9,10},{10,1... | collective-permute-start | bytes 1597448 | tf_op jit(solution)/shard_map/ppermute | solution.py:797
  105.7 30.6 %collective-permute-start.17 = (bf16[1040,256]{1,0:T(8,128)(2,1)S(1)}, bf16[1040,256]{1,0:T(8,128)(2,1)S(1)}, u32[]{:S(2)}, u32[]{:S(2)}) collective-permute-start(bf16[1040,256]{1,0:T(8,128)(2,1)S(1)} %get-tuple-element.93), channel_id=1, source_target_pairs={{0,3},{1,0},{2,1},{3,2},{4,7},{5,4},{6,5},{7,6},{8,11},{9,8},{10,9... | collective-permute-start | bytes 1597448 | tf_op jit(solution)/shard_map/ppermute | solution.py:797
  107.7 11.4 %collective-permute-start.20 = (bf16[128,1024]{1,0:T(8,128)(2,1)S(1)}, bf16[128,1024]{1,0:T(8,128)(2,1)S(1)}, u32[]{:S(2)}, u32[]{:S(2)}) collective-permute-start(bf16[128,1024]{1,0:T(8,128)(2,1)S(1)} %get-tuple-element.105), channel_id=1, source_target_pairs={{0,8},{4,36},{8,16},{12,44},{16,24},{20,52},{24,0},{28,60},{32,40}... | collective-permute-start | bytes 786440 | tf_op jit(solution)/shard_map/ppermute | solution.py:768
  109.3 14.1 %collective-permute-start.21 = (bf16[128,1024]{1,0:T(8,128)(2,1)S(1)}, bf16[128,1024]{1,0:T(8,128)(2,1)S(1)}, u32[]{:S(2)}, u32[]{:S(2)}) collective-permute-start(bf16[128,1024]{1,0:T(8,128)(2,1)S(1)} %get-tuple-element.106), channel_id=1, source_target_pairs={{0,16},{4,68},{8,24},{12,76},{16,0},{20,84},{24,8},{28,92},{32,48}... | collective-permute-start | bytes 786440 | tf_op jit(solution)/shard_map/ppermute | solution.py:768
  119.2 19.7 %collective-permute-start.19 = (bf16[1040,256]{1,0:T(8,128)(2,1)S(1)}, bf16[1040,256]{1,0:T(8,128)(2,1)S(1)}, u32[]{:S(2)}, u32[]{:S(2)}) collective-permute-start(bf16[1040,256]{1,0:T(8,128)(2,1)S(1)} %get-tuple-element.103), channel_id=1, source_target_pairs={{0,2},{1,3},{2,0},{3,1},{4,6},{5,7},{6,4},{7,5},{8,10},{9,11},{10,... | collective-permute-start | bytes 1597448 | tf_op jit(solution)/shard_map/ppermute | solution.py:797
  124.2 12.4 %collective-permute-start.23 = (bf16[32,1024]{1,0:T(8,128)(2,1)S(1)}, bf16[32,1024]{1,0:T(8,128)(2,1)S(1)}, u32[]{:S(2)}, u32[]{:S(2)}) collective-permute-start(bf16[32,1024]{1,0:T(8,128)(2,1)S(1)} %get-tuple-element.109), channel_id=1, source_target_pairs={{0,32},{4,12},{8,40},{12,20},{16,48},{20,28},{24,56},{28,4},{32,64... | collective-permute-start | bytes 196616 | tf_op jit(solution)/shard_map/ppermute | solution.py:768
  125.9 10.7 %collective-permute-start.24 = (bf16[32,1024]{1,0:T(8,128)(2,1)S(1)}, bf16[32,1024]{1,0:T(8,128)(2,1)S(1)}, u32[]{:S(2)}, u32[]{:S(2)}) collective-permute-start(bf16[32,1024]{1,0:T(8,128)(2,1)S(1)} %get-tuple-element.110), channel_id=1, source_target_pairs={{0,64},{4,20},{8,72},{12,28},{16,80},{20,4},{24,88},{28,12},{32,96... | collective-permute-start | bytes 196616 | tf_op jit(solution)/shard_map/ppermute | solution.py:768
  128.1 10.1 %collective-permute-start.25 = (bf16[32,1024]{1,0:T(8,128)(2,1)S(1)}, bf16[32,1024]{1,0:T(8,128)(2,1)S(1)}, u32[]{:S(2)}, u32[]{:S(2)}) collective-permute-start(bf16[32,1024]{1,0:T(8,128)(2,1)S(1)} %get-tuple-element.111), channel_id=1, source_target_pairs={{0,96},{4,28},{8,104},{12,4},{16,112},{20,12},{24,120},{28,20},{32... | collective-permute-start | bytes 196616 | tf_op jit(solution)/shard_map/ppermute | solution.py:768
  (12 other events, 99.2 us)

commit v6 on v5

--- a/solution.py
+++ b/solution.py
@@ -44,6 +44,11 @@
     return jnp.where((col >= low) & (col < low + factor), value, 0.0).astype(BF16)
 
 
+def pool_both(half, quarter):
+    parts = [pool_matrix(BLOCK // 2, 2, half), pool_matrix(BLOCK // 4, 4, quarter)]
+    return jnp.concatenate(parts, axis=0)
+
+
 def spread_matrix(coarse, factor, value):
     shape = (coarse * factor, coarse)
     low = lax.broadcasted_iota(jnp.int32, shape, 1) * factor
@@ -57,6 +62,7 @@
 
 SMALL = pl.CostEstimate(flops=10**6, bytes_accessed=10**4, transcendentals=0)
 LARGE = pl.CostEstimate(flops=4 * 10**9, bytes_accessed=10**4, transcendentals=0)
+RELAY = pl.CostEstimate(flops=10**9, bytes_accessed=10**4, transcendentals=0)
 SCALAR = pl.BlockSpec(memory_space=pltpu.SMEM)
 RESIDENT = pl.BlockSpec(memory_space=pltpu.VMEM)
 
@@ -122,8 +128,7 @@
     ]
     for load in loads:
         load.start()
-    half = pool_matrix(BLOCK // 2, 2, 0.5)
-    quarter = pool_matrix(BLOCK // 4, 4, 0.25)
+    pools = pool_both(0.5, 0.25)
     inverse[4:8, :] = jnp.zeros((4, BLOCK), F32)
     stores = []
 
@@ -156,8 +161,9 @@
             stores.append(store)
         rows = block_rows(step)
         fine = [nn(whole, w[:, n * width : (n + 1) * width]).astype(BF16) for n in range(3)]
-        mid = [nn(half, x).astype(BF16) for x in fine]
-        low = [nn(quarter, x).astype(BF16) for x in fine]
+        coarse = [nn(pools, x).astype(BF16) for x in fine]
+        mid = [x[0:128] for x in coarse]
+        low = [x[128:192] for x in coarse]
         mid_rows = slice(1024 + step * 128, 1024 + (step + 1) * 128)
         low_rows = slice(1536 + step * 64, 1536 + (step + 1) * 64)
         q[rows, :] = fine[0]
@@ -221,26 +227,27 @@
     )(place, *fixed)
 
 
-def cotangent_kernel(place, g0, g1, g2, g3, w_out, d_att):
+def cotangent_kernel(place, g0, g1, g2, g3, w_out, d_att, w_turned):
     me = place[0]
     width = g0.shape[1]
-    half = pool_matrix(BLOCK // 2, 2, 1.0)
-    quarter = pool_matrix(BLOCK // 4, 4, 1.0)
-    columns = [w_out[:, share_rows(me, r, width)] for r in range(MP)]
-    turned_w = jnp.concatenate(columns, axis=1)
+    pools = pool_both(1.0, 1.0)
+    for r in range(MP):
+        w_turned[block_rows(r), :] = w_out[:, share_rows(me, r, width)].T
     for step in range(4):
         rows = block_rows(step)
         shares = jnp.concatenate([share[rows, :] for share in (g0, g1, g2, g3)], axis=1)
-        fine = nt(shares, turned_w).astype(BF16)
+        fine = nn(shares, w_turned[...]).astype(BF16)
         d_att[rows, :] = fine
-        d_att[1024 + step * 128 : 1024 + (step + 1) * 128, :] = nn(half, fine).astype(BF16)
-        d_att[1536 + step * 64 : 1536 + (step + 1) * 64, :] = nn(quarter, fine).astype(BF16)
+        coarse = nn(pools, fine).astype(BF16)
+        d_att[1024 + step * 128 : 1024 + (step + 1) * 128, :] = coarse[0:128]
+        d_att[1536 + step * 64 : 1536 + (step + 1) * 64, :] = coarse[128:192]
 
 
 def cotangent(place, shares, w_out):
     rows, width = shares[0].shape
     outputs = [held((ALL_ROWS, width), BF16)]
-    return run(cotangent_kernel, "cotangent", 10, [place], [*shares, w_out], outputs, (), LARGE)[0]
+    scratch = [pltpu.VMEM((MP * width, width), BF16)]
+    return run(cotangent_kernel, "cotangent", 10, [place], [*shares, w_out], outputs, scratch)[0]
 
 
 EDGE_UNITS = ((0, 0), (0, 3), (1, 0), (1, 1), (2, 0))
@@ -527,7 +534,7 @@
     width = q.shape[1]
     outputs = [held((2 * BLOCK, width), F32), held((width // PAIR, 8, BLOCK), F32)]
     scratch = [turned(EXT_BLOCKS[0]), pltpu.VMEM((4 * BLOCK, PAIR), F32)]
-    return run(forward_inner_kernel, "forward_inner", 12, [bias], [q, kv], outputs, scratch)
+    return run(forward_inner_kernel, "forward_inner", 12, [bias], [q, kv], outputs, scratch, LARGE)
 
 
 def forward_edge(bias, q, kv, from_left, from_right, inner):
@@ -560,8 +567,21 @@
     return run(inner_units_kernel, "inner_backward", 12, [bias], inputs, outputs, scratch)
 
 
-def term_outputs(rows, width, extra=0):
-    return [held((rows, width), BF16)] + [held((rows + extra, width), BF16)] * (MP - 1)
+def term_outputs(rows, width):
+    return [held((rows, width), BF16)] * MP
+
+
+def store_terms(step, terms, own, keep_right, keep_left, right, left):
+    own[block_rows(step), :] = terms[0]
+    low, high = block_rows(step % 2), block_rows(2 + step % 2)
+    if step < 2:
+        keep_right[low, :] = terms[1]
+        right[high, :] = terms[2]
+        left[low, :] = terms[3]
+    else:
+        right[low, :] = terms[1]
+        left[high, :] = terms[2]
+        keep_left[low, :] = terms[3]
 
 
 def out_terms_kernel(place, attended, w_out, *outs):
@@ -581,12 +601,16 @@
 
 def input_terms_kernel(
     d_query, d_kv, from_left, from_right, normed, w, d_proj,
-    dots, own, one, two, three, dot_rows,
+    dots, own, keep_right, keep_left, right, left, dot_rows, w_turned,
 ):
     width = d_query.shape[1]
     half = spread_matrix(BLOCK // 2, 2, 0.5)
     quarter = spread_matrix(BLOCK // 4, 4, 0.25)
     dot_rows[12:16, :] = jnp.zeros((4, BLOCK), F32)
+    for r in range(MP):
+        for n in range(3):
+            at = slice(r * width, (r + 1) * width)
+            w_turned[block_rows(n), at] = w[at, n * width : (n + 1) * width].T
     for step in range(4):
         rows = block_rows(step)
         grads = [d_query[rows, :]]
@@ -605,11 +629,13 @@
             d_proj[rows, n * width : (n + 1) * width] = grad
         dot = None
         every = jnp.concatenate(grads, axis=1)
-        for r, out in enumerate((own, one, two, three)):
-            term = nt(every, w[r * width : (r + 1) * width, :]).astype(BF16)
-            out[rows, :] = term
+        terms = []
+        for r in range(MP):
+            term = nn(every, w_turned[:, r * width : (r + 1) * width]).astype(BF16)
+            terms.append(term)
             part = term.astype(F32) * normed[rows, r * width : (r + 1) * width].astype(F32)
             dot = part if dot is None else dot + part
+        store_terms(step, terms, own, keep_right, keep_left, right, left)
         dot = as_row(jnp.sum(dot, axis=1, keepdims=True))
         first = dot.astype(BF16).astype(F32)
         second = (dot - first).astype(BF16).astype(F32)
@@ -617,17 +643,18 @@
             dot_rows[4 * n + step : 4 * n + step + 1, :] = piece
     pieces = dot_rows[...].astype(BF16)
     dots[...] = pieces
-    for out in (one, two, three):
-        out[4 * BLOCK :, :] = pieces
+    right[4 * BLOCK :, :] = pieces
+    left[4 * BLOCK :, :] = pieces
 
 
 def input_terms(d_query, d_kv, from_left, from_right, normed, w):
     rows, width = d_query.shape
     inputs = [d_query, d_kv, from_left, from_right, normed, w]
     outputs = [held((rows, 2 * width), BF16), held((DOT_ROWS, width), BF16)]
-    outputs += term_outputs(rows, width, DOT_ROWS)
-    scratch = [pltpu.VMEM((DOT_ROWS, width), F32)]
-    return run(input_terms_kernel, "input_terms", 16, [], inputs, outputs, scratch)
+    lengths = [rows, rows // 2, rows // 2, rows + DOT_ROWS, rows + DOT_ROWS]
+    outputs += [held((n, width), BF16) for n in lengths]
+    scratch = [pltpu.VMEM((DOT_ROWS, width), F32), pltpu.VMEM((3 * width, MP * width), BF16)]
+    return run(input_terms_kernel, "input_terms", 18, [], inputs, outputs, scratch)
 
 
 def sum_terms(own, received, at):
@@ -648,32 +675,41 @@
     return run(finish_out_kernel, "finish_out", 8, [], [own, *received], outputs)[0]
 
 
-def near_sum_kernel(own, one, three, dots, total, pieces):
-    rows = own.shape[0]
+def relay_kernel(keep_right, keep_left, l1, r1, onward_right, onward_left):
+    half = keep_right.shape[0]
+    passed = l1[half : 2 * half, :].astype(F32)
+    onward_right[0:half, :] = (keep_right[...].astype(F32) + passed).astype(BF16)
+    passed = r1[half : 2 * half, :].astype(F32)
+    onward_left[...] = (keep_left[...].astype(F32) + passed).astype(BF16)
+    if onward_right.shape[0] > half:
+        onward_right[half:, :] = l1[2 * half :, :]
+
+
+def relay(keep_right, keep_left, l1, r1):
+    half, width = keep_right.shape
+    outputs = [held((half + DOT_ROWS, width), BF16), held((half, width), BF16)]
+    return run(relay_kernel, "relay", 4, [], [keep_right, keep_left, l1, r1], outputs, (), RELAY)
+
+
+def finish_grad_kernel(own, l1, r1, l2, r2, tokens, inverse, dots, result):
+    rows, width = own.shape
+    half = r2.shape[0]
+    pieces = dots[...].astype(F32)
+    for message, first in ((l1, rows), (r1, rows), (l2, half)):
+        pieces = pieces + message[first : first + DOT_ROWS, :].astype(F32)
+    means = (pieces[0:4] + pieces[4:8] + pieces[8:12]) / (MP * width)
     for b in range(rows // BLOCK):
-        at = block_rows(b)
-        total[at, :] = sum_terms(own, (one, three), at)
-    pieces[...] = dots[...].astype(F32) + one[rows:, :].astype(F32) + three[rows:, :].astype(F32)
-
-
-def finish_grad_kernel(near, pieces, far, tokens, inverse, result):
-    rows, width = near.shape
-    every = pieces[...] + far[rows:, :].astype(F32)
-    means = (every[0:4] + every[4:8] + every[8:12]) / (MP * width)
-    for b in range(rows // BLOCK):
-        at = block_rows(b)
+        at, near = block_rows(b), block_rows(b % 2)
         mean = as_column(means[b : b + 1, :])
         inv = as_column(inverse[b : b + 1, :])
-        total = near[at, :] + far[at, :].astype(F32)
+        total = own[at, :].astype(F32)
+        for part in (r1, l2) if b < 2 else (l1, r2):
+            total = total + part[near, :].astype(F32)
         result[at, :] = inv * (total - tokens[at, :].astype(F32) * inv * mean)
 
 
-def finish_grad(own, received, tokens, inverse, dots):
-    one, two, three = received
-    outputs = [held(own.shape, F32), held(dots.shape, F32)]
-    inputs = [own, one, three, dots]
-    near, pieces = run(near_sum_kernel, "near_sum", 8, [], inputs, outputs, (), LARGE)
-    inputs = [near, pieces, two, tokens, inverse]
+def finish_grad(own, l1, r1, l2, r2, tokens, inverse, dots):
+    inputs = [own, l1, r1, l2, r2, tokens, inverse, dots]
     outputs = [held(own.shape, F32)]
     return run(finish_grad_kernel, "finish_grad", 8, [], inputs, outputs)[0]
 
@@ -694,7 +730,7 @@
     return run(early_kernel, "early_terms", 14, [], inputs, outputs, (), LARGE)
 
 
-def inner_kernel(place, normed, d_proj, inner, outer, mine, other, rows_held):
+def inner_kernel(place, normed, d_proj, inner, outer, mine, other_low, other_high, rows_held):
     core = place[1]
     width = outer.shape[1]
     for block in range(MP):
@@ -706,24 +742,27 @@
             out = slice((4 * block + n) * 32, (4 * block + n + 1) * 32)
             first = block * width + n * 64
             mine[out, :] = rows_held[pl.ds(pl.multiple_of(first + core * 32, 32), 32), :]
-            other[out, :] = rows_held[pl.ds(pl.multiple_of(first + 32 - core * 32, 32), 32), :]
+            other, start = (other_low, 0) if block < 2 else (other_high, 256)
+            other[out.start - start : out.stop - start, :] = rows_held[pl.ds(pl.multiple_of(first + 32 - core * 32, 32), 32), :]
 
 
 def inner_terms(place, normed, d_proj, inner, outer):
     total = normed.shape[1]
     width = outer.shape[1]
-    outputs = [held((total // 2, 4 * width), BF16)] * 2
+    outputs = [held((n, 4 * width), BF16) for n in (total // 2, total // 4, total // 4)]
     scratch = [pltpu.VMEM((total, 4 * width), BF16)]
     return run(inner_kernel, "inner_terms", 16, [place], [normed, d_proj, inner, outer], outputs, scratch)
 
 
-def pair_sum_kernel(place, mine, got, *outs):
+def pair_sum_kernel(place, mine, got_low, got_high, *outs):
     z, core, x, y = place[0], place[1], place[2], place[3]
     for d, out in enumerate(outs):
         for n in range(4):
             chunk = jnp.where(core == 0, 4 * n + ((x + d) & 3), 4 * ((y + d - z + 4) & 3) + n)
             rows = pl.ds(pl.multiple_of(chunk * 32, 32), 32)
-            total = mine[rows, :].astype(F32) + got[rows, :].astype(F32)
+            half = pl.ds(pl.multiple_of((chunk & 7) * 32, 32), 32)
+            got = jnp.where(chunk < 8, got_low[half, :], got_high[half, :])
+            total = mine[rows, :].astype(F32) + got.astype(F32)
             out[32 * n : 32 * (n + 1), :] = total.astype(BF16)
 
 
@@ -747,13 +786,13 @@
     go[...] = total[:, 3 * width :]
 
 
-def sum_over_core(place, mine, other):
-    got = lax.ppermute(other, "seq", [(i, i ^ 1) for i in range(32)])
+def sum_over_core(place, mine, *others):
+    got = [lax.ppermute(other, "seq", [(i, i ^ 1) for i in range(32)]) for other in others]
     parts = [held((128, mine.shape[1]), BF16)] * 4
-    return run(pair_sum_kernel, "pair_sum", 6, [place], [mine, got], parts)
-
-
-def sum_over_seq(place, parts):
+    return run(pair_sum_kernel, "pair_sum", 6, [place], [mine, *got], parts)
+
+
+def sum_over_seq(place, parts, *first):
     cols = parts[0].shape[1]
 
     def sent(value, stage, d):
@@ -768,6 +807,7 @@
         return lax.ppermute(value, "seq", pairs)
 
     parts = [parts[0]] + [sent(parts[d], 0, d) for d in (1, 2, 3)]
+    parts = tied(parts, *first)
     rows = [held((32, cols), BF16)] * 4
     scratch = [pltpu.VMEM((128, cols), BF16)]
     rows = run(row_sum_kernel, "row_sum", 4, [place], parts, rows, scratch)
@@ -827,22 +867,21 @@
         ]
     )
     token_shares = gather_shares(tokens)
-    sent_grad = tied(grad_out, *(token_shares[n] for n in (1, 2, 5, 6)))
-    grad_shares = [
-        grad_out, to_previous(sent_grad), turned_by(sent_grad, 2), to_next(sent_grad)
-    ]
+    near_grad = tied(grad_out, *(token_shares[n] for n in (1, 2, 5, 6)))
+    far_grad = tied(grad_out, *token_shares)
+    far = turned_by(far_grad, 2)
+    grad_shares = [grad_out, to_previous(near_grad), far, to_next(near_grad)]
     inverse, q, kv, to_left, to_right, normed, w = project(
         me, token_shares, w_query, w_key, w_value
     )
     from_left, from_right = exchange(to_left, to_right)
-    inner_out, inner_stats = forward_inner(bias, q, kv)
-    grad_shares = tied(grad_shares, inner_out)
-    d_att = cotangent(me, grad_shares, w_out)
-    inner_out = tied(inner_out, d_att)
+    near_q = tied(q, grad_shares[1], grad_shares[3])
+    inner_out, inner_stats = forward_inner(bias, near_q, kv)
     attended, stats = forward_edge(bias, q, kv, from_left, from_right, inner_out)
     out_own, *terms = out_terms(me, attended, w_out)
     out_received = sum_over_mp(terms)
-    stats = tied(stats, out_own)
+    grad_shares = tied(grad_shares, out_own)
+    d_att = cotangent(me, grad_shares, w_out)
     dq_f, d_kv, to_left, to_right = edge_backward(
         bias, stats, q, kv, from_left, from_right, d_att
     )
@@ -851,16 +890,17 @@
     attended = tied(attended, *out_received)
     outer, inner = early_terms(grad_shares, attended, normed, d_query)
     d_query = tied(d_query, outer)
-    d_proj, dots, own, *terms = input_terms(
+    d_proj, dots, own, keep_right, keep_left, right, left = input_terms(
         d_query, d_kv, from_left, from_right, normed, w
     )
     attn_out = finish_out(out_own, out_received)
-    mine, other = inner_terms(me, normed, d_proj, inner, outer)
-    core_sums = sum_over_core(me, mine, other)
-    terms[1] = tied(terms[1], core_sums[0])
-    received = sum_over_mp(terms)
-    grad_tokens = finish_grad(own, received, tokens, inverse, dots)
-    *weight_grads, grad_w_out = sum_over_seq(me, core_sums)
+    mine, *others = inner_terms(me, normed, d_proj, inner, outer)
+    core_sums = sum_over_core(me, mine, *others)
+    l1, r1 = to_next(right), to_previous(left)
+    onward_right, onward_left = relay(keep_right, keep_left, l1, r1)
+    l2, r2 = to_next(onward_right), to_previous(onward_left)
+    grad_tokens = finish_grad(own, l1, r1, l2, r2, tokens, inverse, dots)
+    *weight_grads, grad_w_out = sum_over_seq(me, core_sums, onward_right)
     return (attn_out, grad_tokens, *weight_grads, grad_w_out.T)
 
 

time: 141 us -> 128 us (0.908)
  waiting for transfers between devices: 23.2 us -> 15.3 us
  starting transfers between devices: 63.2 us -> 59.3 us
    ppermute x4 -> x6, waiting for transfers between devices: 11.3 us -> 2.24 us  [to_previous(): return lax.ppermute(value, 'mp', [((i + 1) % MP, i) for i in range(MP)])]
    ppermute x6, starting transfers between devices: 20.6 us -> 14.1 us  [sent(): return lax.ppermute(value, 'seq', pairs)]
    ppermute x7 -> x4, starting transfers between devices: 12.8 us -> 6.83 us  [turned_by(): return lax.ppermute(value, 'mp', [(i, (i + step) % MP) for i in range(MP)])]
    ppermute x4 -> x6, starting transfers between devices: 8.85 us -> 14.8 us  [to_previous(): return lax.ppermute(value, 'mp', [((i + 1) % MP, i) for i in range(MP)])]
    ppermute x6, waiting for transfers between devices: 6.87 us -> 3.7 us  [sent(): return lax.ppermute(value, 'seq', pairs)]
    ppermute x2, starting transfers between devices: 10 us -> 12.2 us  [exchange(): from_left = lax.ppermute(to_right, 'seq', [(i, i + 1) for i in range(ends)])]
    ppermute x1 -> x2, waiting for transfers between devices: 0.01 us -> 2.19 us  [sum_over_core(): lax.ppermute(other, 'seq', [(i, i ^ 1) for i in range(32)])]
    ppermute x4 -> x6, waiting for transfers between devices: 5.07 us -> 7.1 us  [to_next(): return lax.ppermute(value, 'mp', [(i, (i + 1) % MP) for i in range(MP)])]
  transfers between devices with their start and end apart: 26 -> 28, of which waited for: 6 -> 6; matrix products, arithmetic and copies ran while one was open for 0% -> 0% of each run, Pallas kernels for 26% -> 37%
where the time goes in v6:
time: 128 us
  starting transfers between devices  59.3 us (46%)
  Pallas kernels  50.6 us (40%)
  waiting for transfers between devices  15.3 us (12%)
  local copies, waits for them, and re-layouts  1.8 us (1%)
    pallas_call x15, Pallas kernels, run(): pl.pallas_call(kernel, in_specs=[SCALAR] * len(scalars) + [RESIDENT] * le...  43.5 us
    ppermute x6, starting transfers between devices, to_previous(): return lax.ppermute(value, 'mp', [((i + 1) % MP, i) for i in range(MP)])  14.8 us
    ppermute x6, starting transfers between devices, sent(): return lax.ppermute(value, 'seq', pairs)  14.1 us
    ppermute x2, starting transfers between devices, exchange(): from_left = lax.ppermute(to_right, 'seq', [(i, i + 1) for i in range(ends)])  12.2 us
    pallas_call x1, Pallas kernels, project(): pl.pallas_call(project_kernel, in_specs=[SCALAR] + [anywhere] * 10, out_s...  7.18 us
    ppermute x6, waiting for transfers between devices, to_next(): return lax.ppermute(value, 'mp', [(i, (i + 1) % MP) for i in range(MP)])  7.1 us
    ppermute x4, starting transfers between devices, turned_by(): return lax.ppermute(value, 'mp', [(i, (i + step) % MP) for i in range(MP)])  6.83 us
    ppermute x6, starting transfers between devices, to_next(): return lax.ppermute(value, 'mp', [(i, (i + 1) % MP) for i in range(MP)])  4.9 us
  transfers between devices with their start and end apart: 28, of which 6 were waited for; matrix products, arithmetic and copies ran while one was open for 0% of the time, Pallas kernels for 37%

profile of v6, /device:TPU:0, one launch (start us, length us, event | category | flops | bytes accessed | tf_op | source)
XLA Modules:
  0.0 128.1 jit_solution(7836486254873333473)
XLA Ops:
  1.7 2.1 %collective-permute-start.3 = (bf16[512,256]{1,0:T(8,128)(2,1)S(1)}, bf16[512,256]{1,0:T(8,128)(2,1)S(1)}, u32[]{:S(2)}, u32[]{:S(2)}) collective-permute-start(bf16[512,256]{1,0:T(8,128)(2,1)S(1)} %get-tuple-element.126), channel_id=1, source_target_pairs={{0,1},{1,2},{2,3},{3,0},{4,5},{5,6},{6,7},{7,4},{8,9},{9,10},{10,1... | collective-permute-start | bytes 786440 | tf_op jit(solution)/shard_map/ppermute | solution.py:820
  3.8 2.2 %collective-permute-start = (bf16[512,256]{1,0:T(8,128)(2,1)S(1)}, bf16[512,256]{1,0:T(8,128)(2,1)S(1)}, u32[]{:S(2)}, u32[]{:S(2)}) collective-permute-start(bf16[512,256]{1,0:T(8,128)(2,1)S(1)} %get-tuple-element.127), channel_id=1, source_target_pairs={{1,0},{2,1},{3,2},{0,3},{5,4},{6,5},{7,6},{4,7},{9,8},{10,9},{11,1... | collective-permute-start | bytes 786440 | tf_op jit(solution)/shard_map/ppermute | solution.py:824
  8.0 5.0 %collective-permute-done.3.t3b_any = bf16[512,256]{1,0:T(8,128)(2,1)S(1)} collective-permute-done((bf16[512,256]{1,0:T(8,128)(2,1)S(1)}, bf16[512,256]{1,0:T(8,128)(2,1)S(1)}, u32[]{:S(2)}, u32[]{:S(2)}) %collective-permute-start.3) | collective-permute-done | bytes 262176 | tf_op jit(solution)/shard_map/ppermute | solution.py:820
  13.0 3.3 %collective-permute-start.2 = (bf16[512,256]{1,0:T(8,128)(2,1)S(1)}, bf16[512,256]{1,0:T(8,128)(2,1)}, u32[]{:S(2)}, u32[]{:S(2)}) collective-permute-start(bf16[512,256]{1,0:T(8,128)(2,1)S(1)} %collective-permute-done.t1a_any), channel_id=1, source_target_pairs={{1,0},{2,1},{3,2},{0,3},{5,4},{6,5},{7,6},{4,7},{9,8},{10,9},{11,1... | collective-permute-start | bytes 786440 | tf_op jit(solution)/shard_map/ppermute | solution.py:824
  16.4 2.2 %collective-permute-done.1.t1b_any = bf16[512,256]{1,0:T(8,128)(2,1)S(1)} collective-permute-done((bf16[512,256]{1,0:T(8,128)(2,1)S(1)}, bf16[512,256]{1,0:T(8,128)(2,1)S(1)}, u32[]{:S(2)}, u32[]{:S(2)}) %collective-permute-start.1) | collective-permute-done | bytes 262176 | tf_op jit(solution)/shard_map/ppermute | solution.py:824
  18.6 2.0 %collective-permute-start.9 = (bf16[1024,256]{1,0:T(8,128)(2,1)}, bf16[1024,256]{1,0:T(8,128)(2,1)}, u32[]{:S(2)}, u32[]{:S(2)}) collective-permute-start(bf16[1024,256]{1,0:T(8,128)(2,1)} %g0.1), channel_id=1, source_target_pairs={{0,1},{1,2},{2,3},{3,0},{4,5},{5,6},{6,7},{7,4},{8,9},{9,10},{10,1... | collective-permute-start | bytes 1572872 | tf_op jit(solution)/shard_map/ppermute | solution.py:820
  22.2 2.0 %collective-permute-done.4.t2b_any = bf16[512,256]{1,0:T(8,128)(2,1)S(1)} collective-permute-done((bf16[512,256]{1,0:T(8,128)(2,1)S(1)}, bf16[512,256]{1,0:T(8,128)(2,1)S(1)}, u32[]{:S(2)}, u32[]{:S(2)}) %collective-permute-start.4) | collective-permute-done | bytes 262176 | tf_op jit(solution)/shard_map/ppermute | solution.py:820
  25.0 7.2 %project.1 = (f32[8,256]{1,0:T(8,128)S(1)}, bf16[1792,256]{1,0:T(8,128)(2,1)S(1)}, bf16[2,1792,256]{2,1,0:T(8,128)(2,1)S(1)}, bf16[2,768,256]{2,1,0:T(8,128)(2,1...) custom-call(s32[4]{0:T(128)S(1)} %pad_add_fusion.place, ...), custom_call_target="tpu_custom_call" | custom-call | flops 1000000 | bytes 10000 | tf_op jit(solution)/shard_map/project/pallas_call | solution.py:204
  34.8 3.0 %collective-permute-start.13 = (bf16[1024,256]{1,0:T(8,128)(2,1)}, bf16[1024,256]{1,0:T(8,128)(2,1)S(1)}, u32[]{:S(2)}, u32[]{:S(2)}) collective-permute-start(bf16[1024,256]{1,0:T(8,128)(2,1)} %g0.1), channel_id=1, source_target_pairs={{0,2},{1,3},{2,0},{3,1},{4,6},{5,7},{6,4},{7,5},{8,10},{9,11},{10,... | collective-permute-start | bytes 1572872 | tf_op jit(solution)/shard_map/ppermute | solution.py:837
  37.9 3.6 %forward_inner.1 = (f32[512,256]{1,0:T(8,128)S(1)}, f32[2,8,256]{2,1,0:T(8,128)S(1)}) custom-call(f32[2]{0:T(128)S(1)} %pad_maximum_fusion.bias_ref, bf16[1792,256]{1,0:T(8,128)(2,1)S(1)} %get-tuple-element.71.q, bf16[2,1792,256]{2,1,0:T(8,128)(2,1)S(1)} %get-tuple-element.67.kv), custom_call_target="tpu_custom_call" | custom-call | flops 4000000000 | bytes 10000 | tf_op jit(solution)/shard_map/forward_inner/pallas_call | solution.py:75
  41.6 6.6 %forward_edge.1 = (bf16[1024,256]{1,0:T(8,128)(2,1)S(1)}, f32[2,24,256]{2,1,0:T(8,128)S(1)}) custom-call(f32[2]{0:T(128)S(1)} %pad_maximum_fusion.bias_ref, bf16[1792,256]{1,0:T(8,128)(2,1)S(1)} %get-tuple-element.71.q, bf16[2,1792,256]{2,1,0:T(8,128)(2,1)S(1)} %get-tuple-element.67.kv, bf16[2,768,256]{2,1,0:T(8,128)(2,1)S(1)} %collective-permute-done.6.from_left, ...), custom_call_target="tpu_custom_call" | custom-call | flops 1000000 | bytes 10000 | tf_op jit(solution)/shard_map/forward_edge/pallas_call | solution.py:75
  53.3 3.2 %cotangent.1.grads = bf16[1792,256]{1,0:T(8,128)(2,1)S(1)} custom-call(s32[4]{0:T(128)S(1)} %pad_add_fusion.place, bf16[1024,256]{1,0:T(8,128)(2,1)S(1)} %copy-done.4, bf16[1024,256]{1,0:T(8,128)(2,1)} %collective-permute-done.8.g1, bf16[1024,256]{1,0:T(8,128)(2,1)S(1)} %collective-permute-done.13.g2, bf16[1024,256]{1,0:T(8,128)(2,1)} %collective-permute-done.9.g3, ...), custom_call_target="tpu_custom_call" | custom-call | flops 1000000 | bytes 10000 | tf_op jit(solution)/shard_map/cotangent/pallas_call | solution.py:75
  56.4 10.6 %edge_backward.1 = (f32[1024,256]{1,0:T(8,128)S(1)}, f32[2,1024,256]{2,1,0:T(8,128)S(1)}, bf16[2,768,256]{2,1,0:T(8,128)(2,1)S(1)}, bf16[2,768,256]{2,1,0:T(8,128)(2,1)S(1)}) custom-call(f32[2]{0:T(128)S(1)} %pad_maximum_fusion.bias_ref, f32[2,24,256]{2,1,0:T(8,128)S(1)} %get-tuple-element.84.stats, bf16[1792,256]{1,0:T(8,128)(2,1)S(1)} %get-tuple-element.71.q, ...), custom_call_target="tpu_custom_call" | custom-call | flops 1000000 | bytes 10000 | tf_op jit(solution)/shard_map/edge_backward/pallas_call | solution.py:75
  67.0 10.9 %collective-permute-start.14 = (bf16[2,768,256]{2,1,0:T(8,128)(2,1)S(1)}, bf16[2,768,256]{2,1,0:T(8,128)(2,1)S(1)}, u32[]{:S(2)}, u32[]{:S(2)}) collective-permute-start(bf16[2,768,256]{2,1,0:T(8,128)(2,1)S(1)} %get-tuple-element.93), channel_id=1, source_target_pairs={{0,4},{4,8},{8,12},{12,16},{16,20},{20,24},{24,28},{28,32},{32,36}... | collective-permute-start | bytes 2359304 | tf_op jit(solution)/shard_map/ppermute | solution.py:847
  79.3 5.5 %inner_backward.1 = (bf16[1024,256]{1,0:T(8,128)(2,1)S(1)}, f32[2,1024,256]{2,1,0:T(8,128)S(1)}) custom-call(f32[2]{0:T(128)S(1)} %pad_maximum_fusion.bias_ref, f32[2,8,256]{2,1,0:T(8,128)S(1)} %get-tuple-element.78.stats, bf16[1792,256]{1,0:T(8,128)(2,1)S(1)} %get-tuple-element.71.q, bf16[2,1792,256]{2,1,0:T(8,128)(2,1)S(1)} %get-tuple-element.67.kv, ...), custom_call_target="tpu_custom_call" | custom-call | flops 1000000 | bytes 10000 | tf_op jit(solution)/shard_map/inner_backward/pallas_call | solution.py:75
  84.8 2.7 %early_terms.1 = (bf16[1024,256]{1,0:T(8,128)(2,1)S(1)}, bf16[1024,256]{1,0:T(8,128)(2,1)S(1)}) custom-call(bf16[1024,256]{1,0:T(8,128)(2,1)S(1)} %copy-done.4, bf16[1024,256]{1,0:T(8,128)(2,1)} %collective-permute-done.8.g1, bf16[1024,256]{1,0:T(8,128)(2,1)S(1)} %collective-permute-done.13.g2, bf16[1024,256]{1,0:T(8,128)(2,1)} %collective-permute-done.9.g3, ...), custom_call_target="tpu_custom_call" | custom-call | flops 4000000000 | bytes 10000 | tf_op jit(solution)/shard_map/early_terms/pallas_call | solution.py:75
  87.5 2.9 %input_terms.1 = (bf16[1024,512]{1,0:T(8,128)(2,1)S(1)}, bf16[16,256]{1,0:T(8,128)(2,1)S(1)}, bf16[1024,256]{1,0:T(8,128)(2,1)S(1)}, bf16[512,256]{1,0:T(8,128)(...) custom-call(bf16[1024,256]{1,0:T(8,128)(2,1)S(1)} %get-tuple-element.91.d_query, ...), custom_call_target="tpu_custom_call" | custom-call | flops 1000000 | bytes 10000 | tf_op jit(solution)/shard_map/input_terms/pallas_call | solution.py:75
  91.1 2.6 %collective-permute-start.17 = (bf16[1040,256]{1,0:T(8,128)(2,1)S(1)}, bf16[1040,256]{1,0:T(8,128)(2,1)S(1)}, u32[]{:S(2)}, u32[]{:S(2)}) collective-permute-start(bf16[1040,256]{1,0:T(8,128)(2,1)S(1)} %get-tuple-element.98), channel_id=1, source_target_pairs={{1,0},{2,1},{3,2},{0,3},{5,4},{6,5},{7,6},{4,7},{9,8},{10,9},{11,1... | collective-permute-start | bytes 1597448 | tf_op jit(solution)/shard_map/ppermute | solution.py:824
  93.7 2.1 %inner_terms.1 = (bf16[512,1024]{1,0:T(8,128)(2,1)S(1)}, bf16[256,1024]{1,0:T(8,128)(2,1)S(1)}, bf16[256,1024]{1,0:T(8,128)(2,1)S(1)}) custom-call(s32[4]{0:T(128)S(1)} %pad_add_fusion.place, bf16[1024,1024]{1,0:T(8,128)(2,1)S(1)} %copy-done, bf16[1024,512]{1,0:T(8,128)(2,1)S(1)} %get-tuple-element.105.d_proj, ...), custom_call_target="tpu_custom_call" | custom-call | flops 1000000 | bytes 10000 | tf_op jit(solution)/shard_map/inner_terms/pallas_call | solution.py:75
  95.8 3.7 %collective-permute-start.20 = (bf16[256,1024]{1,0:T(8,128)(2,1)S(1)}, bf16[256,1024]{1,0:T(8,128)(2,1)S(1)}, u32[]{:S(2)}, u32[]{:S(2)}) collective-permute-start(bf16[256,1024]{1,0:T(8,128)(2,1)S(1)} %get-tuple-element.108), channel_id=1, source_target_pairs={{0,4},{4,0},{8,12},{12,8},{16,20},{20,16},{24,28},{28,24},{32,36},... | collective-permute-start | bytes 1572872 | tf_op jit(solution)/shard_map/ppermute | solution.py:790
  104.2 6.9 %collective-permute-start.23 = (bf16[128,1024]{1,0:T(8,128)(2,1)S(1)}, bf16[128,1024]{1,0:T(8,128)(2,1)S(1)}, u32[]{:S(2)}, u32[]{:S(2)}) collective-permute-start(bf16[128,1024]{1,0:T(8,128)(2,1)S(1)} %get-tuple-element.112), channel_id=1, source_target_pairs={{0,16},{4,68},{8,24},{12,76},{16,0},{20,84},{24,8},{28,92},{32,48}... | collective-permute-start | bytes 786440 | tf_op jit(solution)/shard_map/ppermute | solution.py:807
  111.4 3.2 %collective-permute-start.19 = (bf16[512,256]{1,0:T(8,128)(2,1)S(1)}, bf16[512,256]{1,0:T(8,128)(2,1)S(1)}, u32[]{:S(2)}, u32[]{:S(2)}) collective-permute-start(bf16[512,256]{1,0:T(8,128)(2,1)S(1)} %get-tuple-element.102), channel_id=1, source_target_pairs={{1,0},{2,1},{3,2},{0,3},{5,4},{6,5},{7,6},{4,7},{9,8},{10,9},{11,1... | collective-permute-start | bytes 786440 | tf_op jit(solution)/shard_map/ppermute | solution.py:824
  114.6 3.7 %collective-permute-done.23.c = bf16[128,1024]{1,0:T(8,128)(2,1)S(1)} collective-permute-done((bf16[128,1024]{1,0:T(8,128)(2,1)S(1)}, bf16[128,1024]{1,0:T(8,128)(2,1)S(1)}, u32[]{:S(2)}, u32[]{:S(2)}) %collective-permute-start.23) | collective-permute-done | bytes 262176 | tf_op jit(solution)/shard_map/ppermute | solution.py:807
  120.7 2.0 %collective-permute-start.26 = (bf16[32,1024]{1,0:T(8,128)(2,1)S(1)}, bf16[32,1024]{1,0:T(8,128)(2,1)S(1)}, u32[]{:S(2)}, u32[]{:S(2)}) collective-permute-start(bf16[32,1024]{1,0:T(8,128)(2,1)S(1)} %get-tuple-element.120), channel_id=1, source_target_pairs={{0,64},{4,20},{8,72},{12,28},{16,80},{20,4},{24,88},{28,12},{32,96... | collective-permute-start | bytes 196616 | tf_op jit(solution)/shard_map/ppermute | solution.py:807
  (71 shorter events, 28.0 us)
Async XLA Ops:
  1.7 11.3 %collective-permute-start.3 = (bf16[512,256]{1,0:T(8,128)(2,1)S(1)}, bf16[512,256]{1,0:T(8,128)(2,1)S(1)}, u32[]{:S(2)}, u32[]{:S(2)}) collective-permute-start(bf16[512,256]{1,0:T(8,128)(2,1)S(1)} %get-tuple-element.126), channel_id=1, source_target_pairs={{0,1},{1,2},{2,3},{3,0},{4,5},{5,6},{6,7},{7,4},{8,9},{9,10},{10,1... | collective-permute-start | bytes 786440 | tf_op jit(solution)/shard_map/ppermute | solution.py:820
  3.8 9.3 %collective-permute-start = (bf16[512,256]{1,0:T(8,128)(2,1)S(1)}, bf16[512,256]{1,0:T(8,128)(2,1)S(1)}, u32[]{:S(2)}, u32[]{:S(2)}) collective-permute-start(bf16[512,256]{1,0:T(8,128)(2,1)S(1)} %get-tuple-element.127), channel_id=1, source_target_pairs={{1,0},{2,1},{3,2},{0,3},{5,4},{6,5},{7,6},{4,7},{9,8},{10,9},{11,1... | collective-permute-start | bytes 786440 | tf_op jit(solution)/shard_map/ppermute | solution.py:824
  6.0 12.6 %collective-permute-start.1 = (bf16[512,256]{1,0:T(8,128)(2,1)S(1)}, bf16[512,256]{1,0:T(8,128)(2,1)S(1)}, u32[]{:S(2)}, u32[]{:S(2)}) collective-permute-start(bf16[512,256]{1,0:T(8,128)(2,1)S(1)} %get-tuple-element.126), channel_id=1, source_target_pairs={{1,0},{2,1},{3,2},{0,3},{5,4},{6,5},{7,6},{4,7},{9,8},{10,9},{11,1... | collective-permute-start | bytes 786440 | tf_op jit(solution)/shard_map/ppermute | solution.py:824
  7.9 10.7 %collective-permute-start.5 = (bf16[512,256]{1,0:T(8,128)(2,1)S(1)}, bf16[512,256]{1,0:T(8,128)(2,1)S(1)}, u32[]{:S(2)}, u32[]{:S(2)}) collective-permute-start(bf16[512,256]{1,0:T(8,128)(2,1)S(1)} %get-tuple-element.127), channel_id=1, source_target_pairs={{0,1},{1,2},{2,3},{3,0},{4,5},{5,6},{6,7},{7,4},{8,9},{9,10},{10,1... | collective-permute-start | bytes 786440 | tf_op jit(solution)/shard_map/ppermute | solution.py:820
  13.0 11.2 %collective-permute-start.4 = (bf16[512,256]{1,0:T(8,128)(2,1)S(1)}, bf16[512,256]{1,0:T(8,128)(2,1)S(1)}, u32[]{:S(2)}, u32[]{:S(2)}) collective-permute-start(bf16[512,256]{1,0:T(8,128)(2,1)S(1)} %collective-permute-done.3.t3b_any), channel_id=1, source_target_pairs={{0,1},{1,2},{2,3},{3,0},{4,5},{5,6},{6,7},{7,4},{8,9},{9,10},{10,1... | collective-permute-start | bytes 786440 | tf_op jit(solution)/shard_map/ppermute | solution.py:820
  13.0 11.9 %collective-permute-start.2 = (bf16[512,256]{1,0:T(8,128)(2,1)S(1)}, bf16[512,256]{1,0:T(8,128)(2,1)}, u32[]{:S(2)}, u32[]{:S(2)}) collective-permute-start(bf16[512,256]{1,0:T(8,128)(2,1)S(1)} %collective-permute-done.t1a_any), channel_id=1, source_target_pairs={{1,0},{2,1},{3,2},{0,3},{5,4},{6,5},{7,6},{4,7},{9,8},{10,9},{11,1... | collective-permute-start | bytes 786440 | tf_op jit(solution)/shard_map/ppermute | solution.py:824
  18.6 19.3 %collective-permute-start.9 = (bf16[1024,256]{1,0:T(8,128)(2,1)}, bf16[1024,256]{1,0:T(8,128)(2,1)}, u32[]{:S(2)}, u32[]{:S(2)}) collective-permute-start(bf16[1024,256]{1,0:T(8,128)(2,1)} %g0.1), channel_id=1, source_target_pairs={{0,1},{1,2},{2,3},{3,0},{4,5},{5,6},{6,7},{7,4},{8,9},{9,10},{10,1... | collective-permute-start | bytes 1572872 | tf_op jit(solution)/shard_map/ppermute | solution.py:820
  20.6 17.3 %collective-permute-start.8 = (bf16[1024,256]{1,0:T(8,128)(2,1)}, bf16[1024,256]{1,0:T(8,128)(2,1)}, u32[]{:S(2)}, u32[]{:S(2)}) collective-permute-start(bf16[1024,256]{1,0:T(8,128)(2,1)} %g0.1), channel_id=1, source_target_pairs={{1,0},{2,1},{3,2},{0,3},{5,4},{6,5},{7,6},{4,7},{9,8},{10,9},{11,1... | collective-permute-start | bytes 1572872 | tf_op jit(solution)/shard_map/ppermute | solution.py:824
  32.2 9.4 %collective-permute-start.6 = (bf16[2,768,256]{2,1,0:T(8,128)(2,1)}, bf16[2,768,256]{2,1,0:T(8,128)(2,1)S(1)}, u32[]{:S(2)}, u32[]{:S(2)}) collective-permute-start(bf16[2,768,256]{2,1,0:T(8,128)(2,1)} %get-tuple-element.68), channel_id=1, source_target_pairs={{0,4},{4,8},{8,12},{12,16},{16,20},{20,24},{24,28},{28,32},{32,36}... | collective-permute-start | bytes 2359304 | tf_op jit(solution)/shard_map/ppermute | solution.py:847
  33.5 8.1 %collective-permute-start.7 = (bf16[2,768,256]{2,1,0:T(8,128)(2,1)}, bf16[2,768,256]{2,1,0:T(8,128)(2,1)}, u32[]{:S(2)}, u32[]{:S(2)}) collective-permute-start(bf16[2,768,256]{2,1,0:T(8,128)(2,1)} %get-tuple-element.69), channel_id=1, source_target_pairs={{4,0},{8,4},{12,8},{16,12},{20,16},{24,20},{28,24},{32,28},{36,32}... | collective-permute-start | bytes 2359304 | tf_op jit(solution)/shard_map/ppermute | solution.py:848
  34.8 18.5 %collective-permute-start.13 = (bf16[1024,256]{1,0:T(8,128)(2,1)}, bf16[1024,256]{1,0:T(8,128)(2,1)S(1)}, u32[]{:S(2)}, u32[]{:S(2)}) collective-permute-start(bf16[1024,256]{1,0:T(8,128)(2,1)} %g0.1), channel_id=1, source_target_pairs={{0,2},{1,3},{2,0},{3,1},{4,6},{5,7},{6,4},{7,5},{8,10},{9,11},{10,... | collective-permute-start | bytes 1572872 | tf_op jit(solution)/shard_map/ppermute | solution.py:837
  49.5 35.3 %collective-permute-start.10 = (bf16[1024,256]{1,0:T(8,128)(2,1)S(1)}, bf16[1024,256]{1,0:T(8,128)(2,1)S(1)}, u32[]{:S(2)}, u32[]{:S(2)}) collective-permute-start(bf16[1024,256]{1,0:T(8,128)(2,1)S(1)} %get-tuple-element.75), channel_id=1, source_target_pairs={{0,1},{1,2},{2,3},{3,0},{4,5},{5,6},{6,7},{7,4},{8,9},{9,10},{10,1... | collective-permute-start | bytes 1572872 | tf_op jit(solution)/shard_map/ppermute | solution.py:837
  50.2 34.6 %collective-permute-start.11 = (bf16[1024,256]{1,0:T(8,128)(2,1)S(1)}, bf16[1024,256]{1,0:T(8,128)(2,1)S(1)}, u32[]{:S(2)}, u32[]{:S(2)}) collective-permute-start(bf16[1024,256]{1,0:T(8,128)(2,1)S(1)} %get-tuple-element.76), channel_id=1, source_target_pairs={{0,2},{1,3},{2,0},{3,1},{4,6},{5,7},{6,4},{7,5},{8,10},{9,11},{10,... | collective-permute-start | bytes 1572872 | tf_op jit(solution)/shard_map/ppermute | solution.py:837
  52.0 32.7 %collective-permute-start.12 = (bf16[1024,256]{1,0:T(8,128)(2,1)S(1)}, bf16[1024,256]{1,0:T(8,128)(2,1)S(1)}, u32[]{:S(2)}, u32[]{:S(2)}) collective-permute-start(bf16[1024,256]{1,0:T(8,128)(2,1)S(1)} %get-tuple-element.77), channel_id=1, source_target_pairs={{0,3},{1,0},{2,1},{3,2},{4,7},{5,4},{6,5},{7,6},{8,11},{9,8},{10,9... | collective-permute-start | bytes 1572872 | tf_op jit(solution)/shard_map/ppermute | solution.py:837
  67.0 20.4 %collective-permute-start.14 = (bf16[2,768,256]{2,1,0:T(8,128)(2,1)S(1)}, bf16[2,768,256]{2,1,0:T(8,128)(2,1)S(1)}, u32[]{:S(2)}, u32[]{:S(2)}) collective-permute-start(bf16[2,768,256]{2,1,0:T(8,128)(2,1)S(1)} %get-tuple-element.93), channel_id=1, source_target_pairs={{0,4},{4,8},{8,12},{12,16},{16,20},{20,24},{24,28},{28,32},{32,36}... | collective-permute-start | bytes 2359304 | tf_op jit(solution)/shard_map/ppermute | solution.py:847
  78.0 9.5 %collective-permute-start.15 = (bf16[2,768,256]{2,1,0:T(8,128)(2,1)S(1)}, bf16[2,768,256]{2,1,0:T(8,128)(2,1)S(1)}, u32[]{:S(2)}, u32[]{:S(2)}) collective-permute-start(bf16[2,768,256]{2,1,0:T(8,128)(2,1)S(1)} %get-tuple-element.94), channel_id=1, source_target_pairs={{4,0},{8,4},{12,8},{16,12},{20,16},{24,20},{28,24},{32,28},{36,32}... | collective-permute-start | bytes 2359304 | tf_op jit(solution)/shard_map/ppermute | solution.py:848
  90.4 20.8 %collective-permute-start.16 = (bf16[1040,256]{1,0:T(8,128)(2,1)S(1)}, bf16[1040,256]{1,0:T(8,128)(2,1)S(1)}, u32[]{:S(2)}, u32[]{:S(2)}) collective-permute-start(bf16[1040,256]{1,0:T(8,128)(2,1)S(1)} %get-tuple-element.97), channel_id=1, source_target_pairs={{0,1},{1,2},{2,3},{3,0},{4,5},{5,6},{6,7},{7,4},{8,9},{9,10},{10,1... | collective-permute-start | bytes 1597448 | tf_op jit(solution)/shard_map/ppermute | solution.py:820
  91.1 20.0 %collective-permute-start.17 = (bf16[1040,256]{1,0:T(8,128)(2,1)S(1)}, bf16[1040,256]{1,0:T(8,128)(2,1)S(1)}, u32[]{:S(2)}, u32[]{:S(2)}) collective-permute-start(bf16[1040,256]{1,0:T(8,128)(2,1)S(1)} %get-tuple-element.98), channel_id=1, source_target_pairs={{1,0},{2,1},{3,2},{0,3},{5,4},{6,5},{7,6},{4,7},{9,8},{10,9},{11,1... | collective-permute-start | bytes 1597448 | tf_op jit(solution)/shard_map/ppermute | solution.py:824
  102.6 12.0 %collective-permute-start.22 = (bf16[128,1024]{1,0:T(8,128)(2,1)S(1)}, bf16[128,1024]{1,0:T(8,128)(2,1)S(1)}, u32[]{:S(2)}, u32[]{:S(2)}) collective-permute-start(bf16[128,1024]{1,0:T(8,128)(2,1)S(1)} %get-tuple-element.111), channel_id=1, source_target_pairs={{0,8},{4,36},{8,16},{12,44},{16,24},{20,52},{24,0},{28,60},{32,40}... | collective-permute-start | bytes 786440 | tf_op jit(solution)/shard_map/ppermute | solution.py:807
  104.2 14.1 %collective-permute-start.23 = (bf16[128,1024]{1,0:T(8,128)(2,1)S(1)}, bf16[128,1024]{1,0:T(8,128)(2,1)S(1)}, u32[]{:S(2)}, u32[]{:S(2)}) collective-permute-start(bf16[128,1024]{1,0:T(8,128)(2,1)S(1)} %get-tuple-element.112), channel_id=1, source_target_pairs={{0,16},{4,68},{8,24},{12,76},{16,0},{20,84},{24,8},{28,92},{32,48}... | collective-permute-start | bytes 786440 | tf_op jit(solution)/shard_map/ppermute | solution.py:807
  111.1 7.2 %collective-permute-start.24 = (bf16[128,1024]{1,0:T(8,128)(2,1)S(1)}, bf16[128,1024]{1,0:T(8,128)(2,1)S(1)}, u32[]{:S(2)}, u32[]{:S(2)}) collective-permute-start(bf16[128,1024]{1,0:T(8,128)(2,1)S(1)} %get-tuple-element.113), channel_id=1, source_target_pairs={{0,24},{4,100},{8,0},{12,108},{16,8},{20,116},{24,16},{28,124},{32... | collective-permute-start | bytes 786440 | tf_op jit(solution)/shard_map/ppermute | solution.py:807
  111.3 14.4 %collective-permute-start.18 = (bf16[528,256]{1,0:T(8,128)(2,1)S(1)}, bf16[528,256]{1,0:T(8,128)(2,1)S(1)}, u32[]{:S(2)}, u32[]{:S(2)}) collective-permute-start(bf16[528,256]{1,0:T(8,128)(2,1)S(1)} %get-tuple-element.101), channel_id=1, source_target_pairs={{0,1},{1,2},{2,3},{3,0},{4,5},{5,6},{6,7},{7,4},{8,9},{9,10},{10,1... | collective-permute-start | bytes 811016 | tf_op jit(solution)/shard_map/ppermute | solution.py:820
  111.4 14.3 %collective-permute-start.19 = (bf16[512,256]{1,0:T(8,128)(2,1)S(1)}, bf16[512,256]{1,0:T(8,128)(2,1)S(1)}, u32[]{:S(2)}, u32[]{:S(2)}) collective-permute-start(bf16[512,256]{1,0:T(8,128)(2,1)S(1)} %get-tuple-element.102), channel_id=1, source_target_pairs={{1,0},{2,1},{3,2},{0,3},{5,4},{6,5},{7,6},{4,7},{9,8},{10,9},{11,1... | collective-permute-start | bytes 786440 | tf_op jit(solution)/shard_map/ppermute | solution.py:824
  119.1 8.3 %collective-permute-start.25 = (bf16[32,1024]{1,0:T(8,128)(2,1)S(1)}, bf16[32,1024]{1,0:T(8,128)(2,1)S(1)}, u32[]{:S(2)}, u32[]{:S(2)}) collective-permute-start(bf16[32,1024]{1,0:T(8,128)(2,1)S(1)} %get-tuple-element.119), channel_id=1, source_target_pairs={{0,32},{4,12},{8,40},{12,20},{16,48},{20,28},{24,56},{28,4},{32,64... | collective-permute-start | bytes 196616 | tf_op jit(solution)/shard_map/ppermute | solution.py:807
  (14 other events, 96.5 us)

commit v7 on v6

--- a/solution.py
+++ b/solution.py
@@ -92,6 +92,18 @@
 LEVEL_BLOCK = (0, 4, 6)
 
 
+def share_edges(place, edges, to_core, to_other):
+    core = place[1]
+    to_core[...] = edges[1 - core]
+    to_other[...] = edges[core]
+
+
+def halo_rows(halo, left, index):
+    place, from_core, from_other = halo
+    near, away = from_core[index], from_other[index]
+    return jnp.where(place[1] == 0, away if left else near, near if left else away)
+
+
 def as_row(column):
     return jnp.broadcast_to(column, (column.shape[0], LANES)).T[0:1, :]
 
@@ -103,8 +115,8 @@
 def project_kernel(
     place, t1a_any, t1b_any, t2a_any, t2b_any, t3a_any, t3b_any,
     t0_hbm, wq_hbm, wk_hbm, wv_hbm,
-    inverse, q, kv, to_left, to_right, normed_hbm, w_hbm,
-    t0, t1, t2, t3, w, normed, in_sems, out_sems,
+    inverse, q, kv, to_core, to_other, normed_hbm, w_hbm,
+    t0, t1, t2, t3, w, normed, edges, in_sems, out_sems,
 ):
     me = place[0]
     width = t0.shape[1]
@@ -175,18 +187,19 @@
             kv[n, rows, :] = fine[1 + n]
             kv[n, mid_rows, :] = mid[1 + n]
             kv[n, low_rows, :] = low[1 + n]
-            to_left[n, edge_low, :] = low[1 + n]
-            to_right[n, edge_low, :] = low[1 + n]
-            edge = to_left if step < 2 else to_right
-            edge[n, edge_mid, :] = mid[1 + n]
+            edges[0, n, edge_low, :] = low[1 + n]
+            edges[1, n, edge_low, :] = low[1 + n]
+            side = 0 if step < 2 else 1
+            edges[side, n, edge_mid, :] = mid[1 + n]
             if step in (0, 3):
-                edge[n, 0:BLOCK, :] = fine[1 + n]
+                edges[side, n, 0:BLOCK, :] = fine[1 + n]
 
     parts = normalise(0)
     for step in range(4):
         following = normalise(step + 1) if step < 3 else None
         spread(step, parts)
         parts = following
+    share_edges(place, edges, to_core, to_other)
     for store in stores:
         store.wait()
 
@@ -218,6 +231,7 @@
         + [
             pltpu.VMEM((MP * width, 3 * width), BF16),
             pltpu.VMEM((rows, MP * width), BF16),
+            pltpu.VMEM((2, *edge.shape), BF16),
             pltpu.SemaphoreType.DMA((19,)),
             pltpu.SemaphoreType.DMA((5,)),
         ],
@@ -264,11 +278,9 @@
     return keys
 
 
-def ext_rows(kv, from_left, from_right, n, level, at, lanes):
-    if at == 0:
-        return from_left[n, block_rows(level), lanes]
-    if at == EXT_BLOCKS[level] - 1:
-        return from_right[n, block_rows(level), lanes]
+def ext_rows(kv, halo, n, level, at, lanes):
+    if at in (0, EXT_BLOCKS[level] - 1):
+        return halo_rows(halo, at == 0, (n, block_rows(level), lanes))
     return kv[n, block_rows(LEVEL_BLOCK[level] + at - 1), lanes]
 
 
@@ -324,20 +336,20 @@
         target[spread, :] = target[spread, :] + rows
 
 
-def forward_units(pair, lanes, units, bias_ref, q, kv, from_left, from_right, stats, vt, out_f):
+def forward_units(pair, lanes, units, bias_ref, q, kv, halo, stats, vt, out_f):
     lane = lax.broadcasted_iota(jnp.int32, (BLOCK, PAIR), 1)
     done = set()
     for level, block in units:
         for at, _ in unit_keys(level, block):
             if (level, at) not in done:
                 done.add((level, at))
-                rows = ext_rows(kv, from_left, from_right, 1, level, at, lanes)
+                rows = ext_rows(kv, halo, 1, level, at, lanes)
                 vt[FIRST_EXT[level] + at] = rows.T
 
     def begin(u, head):
         level, block = units[u]
         keys = unit_keys(level, block)
-        key_rows = [ext_rows(kv, from_left, from_right, 0, level, at, lanes) for at, _ in keys]
+        key_rows = [ext_rows(kv, halo, 0, level, at, lanes) for at, _ in keys]
         q_rows = q[block_rows(LEVEL_BLOCK[level] + block), lanes] * HD ** (-0.5)
         return unit_scores(keys, key_rows, head_part(lane, head, q_rows), bias_ref)
 
@@ -384,21 +396,23 @@
 def forward_inner_kernel(bias_ref, q, kv, out, stats, vt, out_f):
     def one(pair, lanes):
         out_f[...] = jnp.zeros_like(out_f)
-        forward_units(pair, lanes, INNER_UNITS, bias_ref, q, kv, None, None, stats, vt, out_f)
+        forward_units(pair, lanes, INNER_UNITS, bias_ref, q, kv, None, stats, vt, out_f)
         out[:, lanes] = out_f[BLOCK : 3 * BLOCK, :]
 
     each_pair(q.shape[1], one)
 
 
 def forward_edge_kernel(
-    bias_ref, q, kv, from_left, from_right, inner, attended, stats, vt, out_f
+    place, bias_ref, q, kv, from_other, from_core, inner, attended, stats, vt, out_f
 ):
+    halo = (place, from_core, from_other)
+
     def one(pair, lanes):
         out_f[0:BLOCK, :] = jnp.zeros((BLOCK, PAIR), F32)
         out_f[BLOCK : 3 * BLOCK, :] = inner[:, lanes]
         out_f[3 * BLOCK :, :] = jnp.zeros((BLOCK, PAIR), F32)
         forward_units(
-            pair, lanes, EDGE_UNITS, bias_ref, q, kv, from_left, from_right, stats, vt, out_f
+            pair, lanes, EDGE_UNITS, bias_ref, q, kv, halo, stats, vt, out_f
         )
         attended[:, lanes] = out_f[...].astype(BF16)
 
@@ -406,7 +420,7 @@
 
 
 def backward_units(
-    pair, lanes, units, bias_ref, q, kv, from_left, from_right, grads, stats, kt, dq_f, keep
+    pair, lanes, units, bias_ref, q, kv, halo, grads, stats, kt, dq_f, keep
 ):
     lane = lax.broadcasted_iota(jnp.int32, (BLOCK, PAIR), 1)
     done = set()
@@ -414,14 +428,14 @@
         for at, _ in unit_keys(level, block):
             if (level, at) not in done:
                 done.add((level, at))
-                rows = ext_rows(kv, from_left, from_right, 0, level, at, lanes)
+                rows = ext_rows(kv, halo, 0, level, at, lanes)
                 kt[FIRST_EXT[level] + at] = rows.T
 
     def begin(u, head):
         level, block = units[u]
         keys = unit_keys(level, block)
-        key_rows = [ext_rows(kv, from_left, from_right, 0, level, at, lanes) for at, _ in keys]
-        value_rows = [ext_rows(kv, from_left, from_right, 1, level, at, lanes) for at, _ in keys]
+        key_rows = [ext_rows(kv, halo, 0, level, at, lanes) for at, _ in keys]
+        value_rows = [ext_rows(kv, halo, 1, level, at, lanes) for at, _ in keys]
         at = block_rows(LEVEL_BLOCK[level] + block)
         qm = head_part(lane, head, q[at, lanes] * HD ** (-0.5))
         am = head_part(lane, head, grads[at, lanes])
@@ -475,9 +489,11 @@
 
 
 def edge_kernel(
-    bias_ref, stats, q, kv, from_left, from_right, grads,
-    dq_f, d_kv, to_left, to_right, kt, ext, dq_s, sums,
+    place, bias_ref, stats, q, kv, from_other, from_core, grads,
+    dq_f, d_kv, to_core, to_other, kt, ext, dq_s, sums, edges,
 ):
+    halo = (place, from_core, from_other)
+
     def one(pair, lanes):
         dq_s[...] = jnp.zeros_like(dq_s)
         seen = set()
@@ -491,15 +507,14 @@
                 ext[n, slot] = rows
 
         backward_units(
-            pair, lanes, EDGE_UNITS, bias_ref, q, kv, from_left, from_right, grads, stats, kt,
-            dq_s, keep,
+            pair, lanes, EDGE_UNITS, bias_ref, q, kv, halo, grads, stats, kt, dq_s, keep,
         )
         dq_f[:, lanes] = dq_s[...]
         for n in range(2):
             for level in range(LEVELS):
                 first, last = FIRST_EXT[level], FIRST_EXT[level] + EXT_BLOCKS[level] - 1
-                to_left[n, block_rows(level), lanes] = ext[n, first].astype(BF16)
-                to_right[n, block_rows(level), lanes] = ext[n, last].astype(BF16)
+                edges[0, n, block_rows(level), lanes] = ext[n, first].astype(BF16)
+                edges[1, n, block_rows(level), lanes] = ext[n, last].astype(BF16)
             for b in range(4):
                 sums[block_rows(b), :] = ext[n, 1 + b]
             for b in range(2):
@@ -507,6 +522,7 @@
             d_kv[n, :, lanes] = sums[...]
 
     each_pair(q.shape[1], one)
+    share_edges(place, edges, to_core, to_other)
 
 
 def inner_units_kernel(bias_ref, stats, q, kv, grads, dq_in, d_kv_in, d_query, d_kv, kt, dq_s):
@@ -519,7 +535,7 @@
             d_kv[n, where, lanes] = d_kv[n, where, lanes] + rows
 
         backward_units(
-            pair, lanes, INNER_UNITS, bias_ref, q, kv, None, None, grads, stats, kt, dq_s, keep
+            pair, lanes, INNER_UNITS, bias_ref, q, kv, None, grads, stats, kt, dq_s, keep
         )
         d_query[:, lanes] = dq_s[...].astype(BF16)
 
@@ -537,26 +553,27 @@
     return run(forward_inner_kernel, "forward_inner", 12, [bias], [q, kv], outputs, scratch, LARGE)
 
 
-def forward_edge(bias, q, kv, from_left, from_right, inner):
+def forward_edge(place, bias, q, kv, halo, inner):
     width = q.shape[1]
-    inputs = [q, kv, from_left, from_right, inner]
+    inputs = [q, kv, *halo[::-1], inner]
     outputs = [held((4 * BLOCK, width), BF16), held((width // PAIR, 24, BLOCK), F32)]
     scratch = [turned(EXT_TOTAL), pltpu.VMEM((4 * BLOCK, PAIR), F32)]
-    return run(forward_edge_kernel, "forward_edge", 12, [bias], inputs, outputs, scratch)
-
-
-def edge_backward(bias, stats, q, kv, from_left, from_right, d_att):
+    return run(forward_edge_kernel, "forward_edge", 12, [place, bias], inputs, outputs, scratch)
+
+
+def edge_backward(place, bias, stats, q, kv, halo, d_att):
     rows, width = 4 * BLOCK, q.shape[1]
     edge = held((2, 3 * BLOCK, width), BF16)
-    inputs = [stats, q, kv, from_left, from_right, d_att]
+    inputs = [stats, q, kv, *halo[::-1], d_att]
     outputs = [held((rows, width), F32), held((2, rows, width), F32), edge, edge]
     scratch = [
         turned(EXT_TOTAL),
         pltpu.VMEM((2, EXT_TOTAL, BLOCK, PAIR), F32),
         pltpu.VMEM((rows, PAIR), F32),
         pltpu.VMEM((rows, PAIR), F32),
+        pltpu.VMEM((2, *edge.shape), BF16),
     ]
-    return run(edge_kernel, "edge_backward", 20, [bias], inputs, outputs, scratch)
+    return run(edge_kernel, "edge_backward", 20, [place, bias], inputs, outputs, scratch)
 
 
 def inner_backward(bias, stats, q, kv, d_att, dq_f, d_kv):
@@ -600,9 +617,10 @@
 
 
 def input_terms_kernel(
-    d_query, d_kv, from_left, from_right, normed, w, d_proj,
+    place, d_query, d_kv, from_other, from_core, normed, w, d_proj,
     dots, own, keep_right, keep_left, right, left, dot_rows, w_turned,
 ):
+    halo = (place, from_core, from_other)
     width = d_query.shape[1]
     half = spread_matrix(BLOCK // 2, 2, 0.5)
     quarter = spread_matrix(BLOCK // 4, 4, 0.25)
@@ -616,14 +634,15 @@
         grads = [d_query[rows, :]]
         mid_rows = slice(256 + (step % 2) * 128, 384 + (step % 2) * 128)
         low_rows = slice(512 + step * 64, 576 + step * 64)
-        near = from_left if step < 2 else from_right
+        first = step < 2
         for n in range(2):
             total = d_kv[n, rows, :]
             if step in (0, 3):
-                total = total + near[n, 0:BLOCK, :].astype(F32)
-            total = total + nn(half, near[n, mid_rows, :])
-            total = total + nn(quarter, from_left[n, low_rows, :])
-            total = total + nn(quarter, from_right[n, low_rows, :])
+                fine = halo_rows(halo, first, (n, slice(0, BLOCK), slice(None)))
+                total = total + fine.astype(F32)
+            total = total + nn(half, halo_rows(halo, first, (n, mid_rows, slice(None))))
+            total = total + nn(quarter, from_core[n, low_rows, :])
+            total = total + nn(quarter, from_other[n, low_rows, :])
             grads.append(total.astype(BF16))
         for n, grad in enumerate(grads[1:]):
             d_proj[rows, n * width : (n + 1) * width] = grad
@@ -647,14 +666,14 @@
     left[4 * BLOCK :, :] = pieces
 
 
-def input_terms(d_query, d_kv, from_left, from_right, normed, w):
+def input_terms(place, d_query, d_kv, halo, normed, w):
     rows, width = d_query.shape
-    inputs = [d_query, d_kv, from_left, from_right, normed, w]
+    inputs = [d_query, d_kv, *halo[::-1], normed, w]
     outputs = [held((rows, 2 * width), BF16), held((DOT_ROWS, width), BF16)]
     lengths = [rows, rows // 2, rows // 2, rows + DOT_ROWS, rows + DOT_ROWS]
     outputs += [held((n, width), BF16) for n in lengths]
     scratch = [pltpu.VMEM((DOT_ROWS, width), F32), pltpu.VMEM((3 * width, MP * width), BF16)]
-    return run(input_terms_kernel, "input_terms", 18, [], inputs, outputs, scratch)
+    return run(input_terms_kernel, "input_terms", 18, [place], inputs, outputs, scratch)
 
 
 def sum_terms(own, received, at):
@@ -841,12 +860,14 @@
     return [turned_by(term, step) for step, term in zip((1, 2, 3), terms)]
 
 
-def exchange(to_left, to_right):
+def exchange(to_core, to_other):
     count = lax.axis_size("seq")
-    ends = count - 1
-    from_left = lax.ppermute(to_right, "seq", [(i, i + 1) for i in range(ends)])
-    from_right = lax.ppermute(to_left, "seq", [(i + 1, i) for i in range(ends)])
-    return from_left, from_right
+    pairs = []
+    for i in range(1, count - 1, 2):
+        pairs += [(i, i + 1), (i + 1, i)]
+    from_other = lax.ppermute(to_other, "seq", pairs)
+    from_core = lax.ppermute(to_core, "seq", [(i, i ^ 1) for i in range(count)])
+    return from_core, from_other
 
 
 def tied(values, *others):
@@ -871,27 +892,25 @@
     far_grad = tied(grad_out, *token_shares)
     far = turned_by(far_grad, 2)
     grad_shares = [grad_out, to_previous(near_grad), far, to_next(near_grad)]
-    inverse, q, kv, to_left, to_right, normed, w = project(
+    inverse, q, kv, to_core, to_other, normed, w = project(
         me, token_shares, w_query, w_key, w_value
     )
-    from_left, from_right = exchange(to_left, to_right)
+    halo = exchange(to_core, to_other)
     near_q = tied(q, grad_shares[1], grad_shares[3])
     inner_out, inner_stats = forward_inner(bias, near_q, kv)
-    attended, stats = forward_edge(bias, q, kv, from_left, from_right, inner_out)
+    attended, stats = forward_edge(me, bias, q, kv, halo, inner_out)
     out_own, *terms = out_terms(me, attended, w_out)
     out_received = sum_over_mp(terms)
     grad_shares = tied(grad_shares, out_own)
     d_att = cotangent(me, grad_shares, w_out)
-    dq_f, d_kv, to_left, to_right = edge_backward(
-        bias, stats, q, kv, from_left, from_right, d_att
-    )
-    from_left, from_right = exchange(to_left, to_right)
+    dq_f, d_kv, to_core, to_other = edge_backward(me, bias, stats, q, kv, halo, d_att)
+    halo = exchange(to_core, to_other)
     d_query, d_kv = inner_backward(bias, inner_stats, q, kv, d_att, dq_f, d_kv)
     attended = tied(attended, *out_received)
     outer, inner = early_terms(grad_shares, attended, normed, d_query)
     d_query = tied(d_query, outer)
     d_proj, dots, own, keep_right, keep_left, right, left = input_terms(
-        d_query, d_kv, from_left, from_right, normed, w
+        me, d_query, d_kv, halo, normed, w
     )
     attn_out = finish_out(out_own, out_received)
     mine, *others = inner_terms(me, normed, d_proj, inner, outer)

time: 128 us -> 126 us (0.984)
  starting transfers between devices: 59.3 us -> 55.7 us
    ppermute x2, starting transfers between devices: 3.79 us -> 1 us  [sum_over_core(): lax.ppermute(other, 'seq', [(i, i ^ 1) for i in range(32)])]
    ppermute x4, starting transfers between devices: 14.8 us -> 12.6 us  [the longest x2 11.2 us: exchange(): from_core = lax.ppermute(to_core, 'seq', [(i, i ^ 1) for i in range(count)])]
    ppermute x6, starting transfers between devices: 14.1 us -> 15.8 us  [sent(): return lax.ppermute(value, 'seq', pairs)]
  transfers between devices with their start and end apart: 28 -> 28, of which waited for: 6 -> 7; matrix products, arithmetic and copies ran while one was open for 0% -> 0% of each run, Pallas kernels for 37% -> 38%
where the time goes in v7:
time: 126 us; the launch traced here: 125 us
  starting transfers between devices  55.7 us (44%)
  Pallas kernels  51.7 us (41%)
  waiting for transfers between devices  15 us (12%)
  local copies, waits for them, and re-layouts  1.8 us (1%)
    pallas_call x15, Pallas kernels, run(): pl.pallas_call(kernel, in_specs=[SCALAR] * len(scalars) + [RESIDENT] * le...  44.4 us
    ppermute x6, starting transfers between devices, sent(): return lax.ppermute(value, 'seq', pairs)  15.8 us
    ppermute x6, starting transfers between devices, to_previous(): return lax.ppermute(value, 'mp', [((i + 1) % MP, i) for i in range(MP)])  14.8 us
    ppermute x2, starting transfers between devices, exchange(): from_core = lax.ppermute(to_core, 'seq', [(i, i ^ 1) for i in range(count)])  11.2 us
    pallas_call x1, Pallas kernels, project(): pl.pallas_call(project_kernel, in_specs=[SCALAR] + [anywhere] * 10, out_s...  7.28 us
    ppermute x6, waiting for transfers between devices, to_next(): return lax.ppermute(value, 'mp', [(i, (i + 1) % MP) for i in range(MP)])  7.1 us
    ppermute x4, starting transfers between devices, turned_by(): return lax.ppermute(value, 'mp', [(i, (i + step) % MP) for i in range(MP)])  6.61 us
    ppermute x6, starting transfers between devices, to_next(): return lax.ppermute(value, 'mp', [(i, (i + 1) % MP) for i in range(MP)])  4.92 us
  transfers between devices with their start and end apart: 28, of which 7 were waited for; matrix products, arithmetic and copies ran while one was open for 0% of the time, Pallas kernels for 38%

profile of v7, /device:TPU:0, one launch (start us, length us, event | category | flops | bytes accessed | tf_op | source)
XLA Modules:
  0.0 125.4 jit_solution(1435542183647542278)
XLA Ops:
  1.7 2.1 %collective-permute-start.3 = (bf16[512,256]{1,0:T(8,128)(2,1)S(1)}, bf16[512,256]{1,0:T(8,128)(2,1)S(1)}, u32[]{:S(2)}, u32[]{:S(2)}) collective-permute-start(bf16[512,256]{1,0:T(8,128)(2,1)S(1)} %get-tuple-element.126), channel_id=1, source_target_pairs={{0,1},{1,2},{2,3},{3,0},{4,5},{5,6},{6,7},{7,4},{8,9},{9,10},{10,1... | collective-permute-start | bytes 786440 | tf_op jit(solution)/shard_map/ppermute | solution.py:839
  3.8 2.2 %collective-permute-start = (bf16[512,256]{1,0:T(8,128)(2,1)S(1)}, bf16[512,256]{1,0:T(8,128)(2,1)S(1)}, u32[]{:S(2)}, u32[]{:S(2)}) collective-permute-start(bf16[512,256]{1,0:T(8,128)(2,1)S(1)} %get-tuple-element.127), channel_id=1, source_target_pairs={{1,0},{2,1},{3,2},{0,3},{5,4},{6,5},{7,6},{4,7},{9,8},{10,9},{11,1... | collective-permute-start | bytes 786440 | tf_op jit(solution)/shard_map/ppermute | solution.py:843
  8.0 5.0 %collective-permute-done.3.t3b_any = bf16[512,256]{1,0:T(8,128)(2,1)S(1)} collective-permute-done((bf16[512,256]{1,0:T(8,128)(2,1)S(1)}, bf16[512,256]{1,0:T(8,128)(2,1)S(1)}, u32[]{:S(2)}, u32[]{:S(2)}) %collective-permute-start.3) | collective-permute-done | bytes 262176 | tf_op jit(solution)/shard_map/ppermute | solution.py:839
  13.0 3.3 %collective-permute-start.2 = (bf16[512,256]{1,0:T(8,128)(2,1)S(1)}, bf16[512,256]{1,0:T(8,128)(2,1)}, u32[]{:S(2)}, u32[]{:S(2)}) collective-permute-start(bf16[512,256]{1,0:T(8,128)(2,1)S(1)} %collective-permute-done.t1a_any), channel_id=1, source_target_pairs={{1,0},{2,1},{3,2},{0,3},{5,4},{6,5},{7,6},{4,7},{9,8},{10,9},{11,1... | collective-permute-start | bytes 786440 | tf_op jit(solution)/shard_map/ppermute | solution.py:843
  16.4 2.2 %collective-permute-done.1.t1b_any = bf16[512,256]{1,0:T(8,128)(2,1)S(1)} collective-permute-done((bf16[512,256]{1,0:T(8,128)(2,1)S(1)}, bf16[512,256]{1,0:T(8,128)(2,1)S(1)}, u32[]{:S(2)}, u32[]{:S(2)}) %collective-permute-start.1) | collective-permute-done | bytes 262176 | tf_op jit(solution)/shard_map/ppermute | solution.py:843
  25.0 7.3 %project.1 = (f32[8,256]{1,0:T(8,128)S(1)}, bf16[1792,256]{1,0:T(8,128)(2,1)S(1)}, bf16[2,1792,256]{2,1,0:T(8,128)(2,1)S(1)}, bf16[2,768,256]{2,1,0:T(8,128)(2,1...) custom-call(s32[4]{0:T(128)S(1)} %pad_add_fusion.place, ...), custom_call_target="tpu_custom_call" | custom-call | flops 1000000 | bytes 10000 | tf_op jit(solution)/shard_map/project/pallas_call | solution.py:217
  33.0 2.9 %collective-permute-start.7 = (bf16[2,768,256]{2,1,0:T(8,128)(2,1)}, bf16[2,768,256]{2,1,0:T(8,128)(2,1)}, u32[]{:S(2)}, u32[]{:S(2)}) collective-permute-start(bf16[2,768,256]{2,1,0:T(8,128)(2,1)} %get-tuple-element.69), channel_id=1, source_target_pairs={{0,4},{4,0},{8,12},{12,8},{16,20},{20,16},{24,28},{28,24},{32,36},... | collective-permute-start | bytes 2359304 | tf_op jit(solution)/shard_map/ppermute | solution.py:869
  35.9 3.0 %collective-permute-start.13 = (bf16[1024,256]{1,0:T(8,128)(2,1)}, bf16[1024,256]{1,0:T(8,128)(2,1)S(1)}, u32[]{:S(2)}, u32[]{:S(2)}) collective-permute-start(bf16[1024,256]{1,0:T(8,128)(2,1)} %g0.1), channel_id=1, source_target_pairs={{0,2},{1,3},{2,0},{3,1},{4,6},{5,7},{6,4},{7,5},{8,10},{9,11},{10,... | collective-permute-start | bytes 1572872 | tf_op jit(solution)/shard_map/ppermute | solution.py:856
  38.9 3.6 %forward_inner.1 = (f32[512,256]{1,0:T(8,128)S(1)}, f32[2,8,256]{2,1,0:T(8,128)S(1)}) custom-call(f32[2]{0:T(128)S(1)} %pad_maximum_fusion.bias_ref, bf16[1792,256]{1,0:T(8,128)(2,1)S(1)} %get-tuple-element.71.q, bf16[2,1792,256]{2,1,0:T(8,128)(2,1)S(1)} %get-tuple-element.67.kv), custom_call_target="tpu_custom_call" | custom-call | flops 4000000000 | bytes 10000 | tf_op jit(solution)/shard_map/forward_inner/pallas_call | solution.py:75
  42.6 6.8 %forward_edge.1 = (bf16[1024,256]{1,0:T(8,128)(2,1)S(1)}, f32[2,24,256]{2,1,0:T(8,128)S(1)}) custom-call(s32[4]{0:T(128)S(1)} %pad_add_fusion.place, f32[2]{0:T(128)S(1)} %pad_maximum_fusion.bias_ref, bf16[1792,256]{1,0:T(8,128)(2,1)S(1)} %get-tuple-element.71.q, bf16[2,1792,256]{2,1,0:T(8,128)(2,1)S(1)} %get-tuple-element.67.kv, ...), custom_call_target="tpu_custom_call" | custom-call | flops 1000000 | bytes 10000 | tf_op jit(solution)/shard_map/forward_edge/pallas_call | solution.py:75
  54.3 3.2 %cotangent.1.grads = bf16[1792,256]{1,0:T(8,128)(2,1)S(1)} custom-call(s32[4]{0:T(128)S(1)} %pad_add_fusion.place, bf16[1024,256]{1,0:T(8,128)(2,1)S(1)} %copy-done.4, bf16[1024,256]{1,0:T(8,128)(2,1)} %collective-permute-done.8.g1, bf16[1024,256]{1,0:T(8,128)(2,1)S(1)} %collective-permute-done.13.g2, bf16[1024,256]{1,0:T(8,128)(2,1)} %collective-permute-done.9.g3, ...), custom_call_target="tpu_custom_call" | custom-call | flops 1000000 | bytes 10000 | tf_op jit(solution)/shard_map/cotangent/pallas_call | solution.py:75
  57.5 10.9 %edge_backward.1 = (f32[1024,256]{1,0:T(8,128)S(1)}, f32[2,1024,256]{2,1,0:T(8,128)S(1)}, bf16[2,768,256]{2,1,0:T(8,128)(2,1)S(1)}, bf16[2,768,256]{2,1,0:T(8,128)(2,1)S(1)}) custom-call(s32[4]{0:T(128)S(1)} %pad_add_fusion.place, f32[2]{0:T(128)S(1)} %pad_maximum_fusion.bias_ref, f32[2,24,256]{2,1,0:T(8,128)S(1)} %get-tuple-element.84.stats, ...), custom_call_target="tpu_custom_call" | custom-call | flops 1000000 | bytes 10000 | tf_op jit(solution)/shard_map/edge_backward/pallas_call | solution.py:75
  69.1 8.3 %collective-permute-start.15 = (bf16[2,768,256]{2,1,0:T(8,128)(2,1)S(1)}, bf16[2,768,256]{2,1,0:T(8,128)(2,1)S(1)}, u32[]{:S(2)}, u32[]{:S(2)}) collective-permute-start(bf16[2,768,256]{2,1,0:T(8,128)(2,1)S(1)} %get-tuple-element.94), channel_id=1, source_target_pairs={{0,4},{4,0},{8,12},{12,8},{16,20},{20,16},{24,28},{28,24},{32,36},... | collective-permute-start | bytes 2359304 | tf_op jit(solution)/shard_map/ppermute | solution.py:869
  77.4 5.5 %inner_backward.1 = (bf16[1024,256]{1,0:T(8,128)(2,1)S(1)}, f32[2,1024,256]{2,1,0:T(8,128)S(1)}) custom-call(f32[2]{0:T(128)S(1)} %pad_maximum_fusion.bias_ref, f32[2,8,256]{2,1,0:T(8,128)S(1)} %get-tuple-element.78.stats, bf16[1792,256]{1,0:T(8,128)(2,1)S(1)} %get-tuple-element.71.q, bf16[2,1792,256]{2,1,0:T(8,128)(2,1)S(1)} %get-tuple-element.67.kv, ...), custom_call_target="tpu_custom_call" | custom-call | flops 1000000 | bytes 10000 | tf_op jit(solution)/shard_map/inner_backward/pallas_call | solution.py:75
  82.9 2.6 %early_terms.1 = (bf16[1024,256]{1,0:T(8,128)(2,1)S(1)}, bf16[1024,256]{1,0:T(8,128)(2,1)S(1)}) custom-call(bf16[1024,256]{1,0:T(8,128)(2,1)S(1)} %copy-done.4, bf16[1024,256]{1,0:T(8,128)(2,1)} %collective-permute-done.8.g1, bf16[1024,256]{1,0:T(8,128)(2,1)S(1)} %collective-permute-done.13.g2, bf16[1024,256]{1,0:T(8,128)(2,1)} %collective-permute-done.9.g3, ...), custom_call_target="tpu_custom_call" | custom-call | flops 4000000000 | bytes 10000 | tf_op jit(solution)/shard_map/early_terms/pallas_call | solution.py:75
  85.6 3.4 %input_terms.1 = (bf16[1024,512]{1,0:T(8,128)(2,1)S(1)}, bf16[16,256]{1,0:T(8,128)(2,1)S(1)}, bf16[1024,256]{1,0:T(8,128)(2,1)S(1)}, bf16[512,256]{1,0:T(8,128)(...) custom-call(s32[4]{0:T(128)S(1)} %pad_add_fusion.place, ...), custom_call_target="tpu_custom_call" | custom-call | flops 1000000 | bytes 10000 | tf_op jit(solution)/shard_map/input_terms/pallas_call | solution.py:75
  89.7 2.6 %collective-permute-start.17 = (bf16[1040,256]{1,0:T(8,128)(2,1)S(1)}, bf16[1040,256]{1,0:T(8,128)(2,1)S(1)}, u32[]{:S(2)}, u32[]{:S(2)}) collective-permute-start(bf16[1040,256]{1,0:T(8,128)(2,1)S(1)} %get-tuple-element.98), channel_id=1, source_target_pairs={{1,0},{2,1},{3,2},{0,3},{5,4},{6,5},{7,6},{4,7},{9,8},{10,9},{11,1... | collective-permute-start | bytes 1597448 | tf_op jit(solution)/shard_map/ppermute | solution.py:843
  92.3 2.1 %inner_terms.1 = (bf16[512,1024]{1,0:T(8,128)(2,1)S(1)}, bf16[256,1024]{1,0:T(8,128)(2,1)S(1)}, bf16[256,1024]{1,0:T(8,128)(2,1)S(1)}) custom-call(s32[4]{0:T(128)S(1)} %pad_add_fusion.place, bf16[1024,1024]{1,0:T(8,128)(2,1)S(1)} %copy-done, bf16[1024,512]{1,0:T(8,128)(2,1)S(1)} %get-tuple-element.105.d_proj, ...), custom_call_target="tpu_custom_call" | custom-call | flops 1000000 | bytes 10000 | tf_op jit(solution)/shard_map/inner_terms/pallas_call | solution.py:75
  98.4 2.6 %collective-permute-start.22 = (bf16[128,1024]{1,0:T(8,128)(2,1)S(1)}, bf16[128,1024]{1,0:T(8,128)(2,1)S(1)}, u32[]{:S(2)}, u32[]{:S(2)}) collective-permute-start(bf16[128,1024]{1,0:T(8,128)(2,1)S(1)} %get-tuple-element.111), channel_id=1, source_target_pairs={{0,8},{4,36},{8,16},{12,44},{16,24},{20,52},{24,0},{28,60},{32,40}... | collective-permute-start | bytes 786440 | tf_op jit(solution)/shard_map/ppermute | solution.py:826
  101.1 3.8 %collective-permute-start.23 = (bf16[128,1024]{1,0:T(8,128)(2,1)S(1)}, bf16[128,1024]{1,0:T(8,128)(2,1)S(1)}, u32[]{:S(2)}, u32[]{:S(2)}) collective-permute-start(bf16[128,1024]{1,0:T(8,128)(2,1)S(1)} %get-tuple-element.112), channel_id=1, source_target_pairs={{0,16},{4,68},{8,24},{12,76},{16,0},{20,84},{24,8},{28,92},{32,48}... | collective-permute-start | bytes 786440 | tf_op jit(solution)/shard_map/ppermute | solution.py:826
  105.5 3.2 %collective-permute-start.19 = (bf16[512,256]{1,0:T(8,128)(2,1)S(1)}, bf16[512,256]{1,0:T(8,128)(2,1)S(1)}, u32[]{:S(2)}, u32[]{:S(2)}) collective-permute-start(bf16[512,256]{1,0:T(8,128)(2,1)S(1)} %get-tuple-element.102), channel_id=1, source_target_pairs={{1,0},{2,1},{3,2},{0,3},{5,4},{6,5},{7,6},{4,7},{9,8},{10,9},{11,1... | collective-permute-start | bytes 786440 | tf_op jit(solution)/shard_map/ppermute | solution.py:843
  108.7 3.3 %collective-permute-done.23.c = bf16[128,1024]{1,0:T(8,128)(2,1)S(1)} collective-permute-done((bf16[128,1024]{1,0:T(8,128)(2,1)S(1)}, bf16[128,1024]{1,0:T(8,128)(2,1)S(1)}, u32[]{:S(2)}, u32[]{:S(2)}) %collective-permute-start.23) | collective-permute-done | bytes 262176 | tf_op jit(solution)/shard_map/ppermute | solution.py:826
  112.8 4.7 %collective-permute-start.25 = (bf16[32,1024]{1,0:T(8,128)(2,1)S(1)}, bf16[32,1024]{1,0:T(8,128)(2,1)S(1)}, u32[]{:S(2)}, u32[]{:S(2)}) collective-permute-start(bf16[32,1024]{1,0:T(8,128)(2,1)S(1)} %get-tuple-element.119), channel_id=1, source_target_pairs={{0,32},{4,12},{8,40},{12,20},{16,48},{20,28},{24,56},{28,4},{32,64... | collective-permute-start | bytes 196616 | tf_op jit(solution)/shard_map/ppermute | solution.py:826
  117.5 2.9 %collective-permute-start.26 = (bf16[32,1024]{1,0:T(8,128)(2,1)S(1)}, bf16[32,1024]{1,0:T(8,128)(2,1)S(1)}, u32[]{:S(2)}, u32[]{:S(2)}) collective-permute-start(bf16[32,1024]{1,0:T(8,128)(2,1)S(1)} %get-tuple-element.120), channel_id=1, source_target_pairs={{0,64},{4,20},{8,72},{12,28},{16,80},{20,4},{24,88},{28,12},{32,96... | collective-permute-start | bytes 196616 | tf_op jit(solution)/shard_map/ppermute | solution.py:826
  (71 shorter events, 27.0 us)
Async XLA Ops:
  1.7 11.3 %collective-permute-start.3 = (bf16[512,256]{1,0:T(8,128)(2,1)S(1)}, bf16[512,256]{1,0:T(8,128)(2,1)S(1)}, u32[]{:S(2)}, u32[]{:S(2)}) collective-permute-start(bf16[512,256]{1,0:T(8,128)(2,1)S(1)} %get-tuple-element.126), channel_id=1, source_target_pairs={{0,1},{1,2},{2,3},{3,0},{4,5},{5,6},{6,7},{7,4},{8,9},{9,10},{10,1... | collective-permute-start | bytes 786440 | tf_op jit(solution)/shard_map/ppermute | solution.py:839
  3.8 9.3 %collective-permute-start = (bf16[512,256]{1,0:T(8,128)(2,1)S(1)}, bf16[512,256]{1,0:T(8,128)(2,1)S(1)}, u32[]{:S(2)}, u32[]{:S(2)}) collective-permute-start(bf16[512,256]{1,0:T(8,128)(2,1)S(1)} %get-tuple-element.127), channel_id=1, source_target_pairs={{1,0},{2,1},{3,2},{0,3},{5,4},{6,5},{7,6},{4,7},{9,8},{10,9},{11,1... | collective-permute-start | bytes 786440 | tf_op jit(solution)/shard_map/ppermute | solution.py:843
  6.0 12.6 %collective-permute-start.1 = (bf16[512,256]{1,0:T(8,128)(2,1)S(1)}, bf16[512,256]{1,0:T(8,128)(2,1)S(1)}, u32[]{:S(2)}, u32[]{:S(2)}) collective-permute-start(bf16[512,256]{1,0:T(8,128)(2,1)S(1)} %get-tuple-element.126), channel_id=1, source_target_pairs={{1,0},{2,1},{3,2},{0,3},{5,4},{6,5},{7,6},{4,7},{9,8},{10,9},{11,1... | collective-permute-start | bytes 786440 | tf_op jit(solution)/shard_map/ppermute | solution.py:843
  7.9 10.7 %collective-permute-start.5 = (bf16[512,256]{1,0:T(8,128)(2,1)S(1)}, bf16[512,256]{1,0:T(8,128)(2,1)S(1)}, u32[]{:S(2)}, u32[]{:S(2)}) collective-permute-start(bf16[512,256]{1,0:T(8,128)(2,1)S(1)} %get-tuple-element.127), channel_id=1, source_target_pairs={{0,1},{1,2},{2,3},{3,0},{4,5},{5,6},{6,7},{7,4},{8,9},{9,10},{10,1... | collective-permute-start | bytes 786440 | tf_op jit(solution)/shard_map/ppermute | solution.py:839
  13.0 11.2 %collective-permute-start.4 = (bf16[512,256]{1,0:T(8,128)(2,1)S(1)}, bf16[512,256]{1,0:T(8,128)(2,1)S(1)}, u32[]{:S(2)}, u32[]{:S(2)}) collective-permute-start(bf16[512,256]{1,0:T(8,128)(2,1)S(1)} %collective-permute-done.3.t3b_any), channel_id=1, source_target_pairs={{0,1},{1,2},{2,3},{3,0},{4,5},{5,6},{6,7},{7,4},{8,9},{9,10},{10,1... | collective-permute-start | bytes 786440 | tf_op jit(solution)/shard_map/ppermute | solution.py:839
  13.0 11.9 %collective-permute-start.2 = (bf16[512,256]{1,0:T(8,128)(2,1)S(1)}, bf16[512,256]{1,0:T(8,128)(2,1)}, u32[]{:S(2)}, u32[]{:S(2)}) collective-permute-start(bf16[512,256]{1,0:T(8,128)(2,1)S(1)} %collective-permute-done.t1a_any), channel_id=1, source_target_pairs={{1,0},{2,1},{3,2},{0,3},{5,4},{6,5},{7,6},{4,7},{9,8},{10,9},{11,1... | collective-permute-start | bytes 786440 | tf_op jit(solution)/shard_map/ppermute | solution.py:843
  18.6 20.3 %collective-permute-start.9 = (bf16[1024,256]{1,0:T(8,128)(2,1)}, bf16[1024,256]{1,0:T(8,128)(2,1)}, u32[]{:S(2)}, u32[]{:S(2)}) collective-permute-start(bf16[1024,256]{1,0:T(8,128)(2,1)} %g0.1), channel_id=1, source_target_pairs={{0,1},{1,2},{2,3},{3,0},{4,5},{5,6},{6,7},{7,4},{8,9},{9,10},{10,1... | collective-permute-start | bytes 1572872 | tf_op jit(solution)/shard_map/ppermute | solution.py:839
  20.6 18.3 %collective-permute-start.8 = (bf16[1024,256]{1,0:T(8,128)(2,1)}, bf16[1024,256]{1,0:T(8,128)(2,1)}, u32[]{:S(2)}, u32[]{:S(2)}) collective-permute-start(bf16[1024,256]{1,0:T(8,128)(2,1)} %g0.1), channel_id=1, source_target_pairs={{1,0},{2,1},{3,2},{0,3},{5,4},{6,5},{7,6},{4,7},{9,8},{10,9},{11,1... | collective-permute-start | bytes 1572872 | tf_op jit(solution)/shard_map/ppermute | solution.py:843
  32.3 10.3 %collective-permute-start.6 = (bf16[2,768,256]{2,1,0:T(8,128)(2,1)}, bf16[2,768,256]{2,1,0:T(8,128)(2,1)S(1)}, u32[]{:S(2)}, u32[]{:S(2)}) collective-permute-start(bf16[2,768,256]{2,1,0:T(8,128)(2,1)} %get-tuple-element.68), channel_id=1, source_target_pairs={{4,8},{8,4},{12,16},{16,12},{20,24},{24,20},{28,32},{32,28},{36,40... | collective-permute-start | bytes 2359304 | tf_op jit(solution)/shard_map/ppermute | solution.py:868
  33.0 9.5 %collective-permute-start.7 = (bf16[2,768,256]{2,1,0:T(8,128)(2,1)}, bf16[2,768,256]{2,1,0:T(8,128)(2,1)}, u32[]{:S(2)}, u32[]{:S(2)}) collective-permute-start(bf16[2,768,256]{2,1,0:T(8,128)(2,1)} %get-tuple-element.69), channel_id=1, source_target_pairs={{0,4},{4,0},{8,12},{12,8},{16,20},{20,16},{24,28},{28,24},{32,36},... | collective-permute-start | bytes 2359304 | tf_op jit(solution)/shard_map/ppermute | solution.py:869
  35.9 18.5 %collective-permute-start.13 = (bf16[1024,256]{1,0:T(8,128)(2,1)}, bf16[1024,256]{1,0:T(8,128)(2,1)S(1)}, u32[]{:S(2)}, u32[]{:S(2)}) collective-permute-start(bf16[1024,256]{1,0:T(8,128)(2,1)} %g0.1), channel_id=1, source_target_pairs={{0,2},{1,3},{2,0},{3,1},{4,6},{5,7},{6,4},{7,5},{8,10},{9,11},{10,... | collective-permute-start | bytes 1572872 | tf_op jit(solution)/shard_map/ppermute | solution.py:856
  50.7 32.2 %collective-permute-start.10 = (bf16[1024,256]{1,0:T(8,128)(2,1)S(1)}, bf16[1024,256]{1,0:T(8,128)(2,1)S(1)}, u32[]{:S(2)}, u32[]{:S(2)}) collective-permute-start(bf16[1024,256]{1,0:T(8,128)(2,1)S(1)} %get-tuple-element.75), channel_id=1, source_target_pairs={{0,1},{1,2},{2,3},{3,0},{4,5},{5,6},{6,7},{7,4},{8,9},{9,10},{10,1... | collective-permute-start | bytes 1572872 | tf_op jit(solution)/shard_map/ppermute | solution.py:856
  51.6 31.3 %collective-permute-start.11 = (bf16[1024,256]{1,0:T(8,128)(2,1)S(1)}, bf16[1024,256]{1,0:T(8,128)(2,1)S(1)}, u32[]{:S(2)}, u32[]{:S(2)}) collective-permute-start(bf16[1024,256]{1,0:T(8,128)(2,1)S(1)} %get-tuple-element.76), channel_id=1, source_target_pairs={{0,2},{1,3},{2,0},{3,1},{4,6},{5,7},{6,4},{7,5},{8,10},{9,11},{10,... | collective-permute-start | bytes 1572872 | tf_op jit(solution)/shard_map/ppermute | solution.py:856
  53.4 29.5 %collective-permute-start.12 = (bf16[1024,256]{1,0:T(8,128)(2,1)S(1)}, bf16[1024,256]{1,0:T(8,128)(2,1)S(1)}, u32[]{:S(2)}, u32[]{:S(2)}) collective-permute-start(bf16[1024,256]{1,0:T(8,128)(2,1)S(1)} %get-tuple-element.77), channel_id=1, source_target_pairs={{0,3},{1,0},{2,1},{3,2},{4,7},{5,4},{6,5},{7,6},{8,11},{9,8},{10,9... | collective-permute-start | bytes 1572872 | tf_op jit(solution)/shard_map/ppermute | solution.py:856
  68.4 17.2 %collective-permute-start.14 = (bf16[2,768,256]{2,1,0:T(8,128)(2,1)S(1)}, bf16[2,768,256]{2,1,0:T(8,128)(2,1)S(1)}, u32[]{:S(2)}, u32[]{:S(2)}) collective-permute-start(bf16[2,768,256]{2,1,0:T(8,128)(2,1)S(1)} %get-tuple-element.93), channel_id=1, source_target_pairs={{4,8},{8,4},{12,16},{16,12},{20,24},{24,20},{28,32},{32,28},{36,40... | collective-permute-start | bytes 2359304 | tf_op jit(solution)/shard_map/ppermute | solution.py:868
  69.1 16.5 %collective-permute-start.15 = (bf16[2,768,256]{2,1,0:T(8,128)(2,1)S(1)}, bf16[2,768,256]{2,1,0:T(8,128)(2,1)S(1)}, u32[]{:S(2)}, u32[]{:S(2)}) collective-permute-start(bf16[2,768,256]{2,1,0:T(8,128)(2,1)S(1)} %get-tuple-element.94), channel_id=1, source_target_pairs={{0,4},{4,0},{8,12},{12,8},{16,20},{20,16},{24,28},{28,24},{32,36},... | collective-permute-start | bytes 2359304 | tf_op jit(solution)/shard_map/ppermute | solution.py:869
  89.0 16.2 %collective-permute-start.16 = (bf16[1040,256]{1,0:T(8,128)(2,1)S(1)}, bf16[1040,256]{1,0:T(8,128)(2,1)S(1)}, u32[]{:S(2)}, u32[]{:S(2)}) collective-permute-start(bf16[1040,256]{1,0:T(8,128)(2,1)S(1)} %get-tuple-element.97), channel_id=1, source_target_pairs={{0,1},{1,2},{2,3},{3,0},{4,5},{5,6},{6,7},{7,4},{8,9},{9,10},{10,1... | collective-permute-start | bytes 1597448 | tf_op jit(solution)/shard_map/ppermute | solution.py:839
  89.7 15.5 %collective-permute-start.17 = (bf16[1040,256]{1,0:T(8,128)(2,1)S(1)}, bf16[1040,256]{1,0:T(8,128)(2,1)S(1)}, u32[]{:S(2)}, u32[]{:S(2)}) collective-permute-start(bf16[1040,256]{1,0:T(8,128)(2,1)S(1)} %get-tuple-element.98), channel_id=1, source_target_pairs={{1,0},{2,1},{3,2},{0,3},{5,4},{6,5},{7,6},{4,7},{9,8},{10,9},{11,1... | collective-permute-start | bytes 1597448 | tf_op jit(solution)/shard_map/ppermute | solution.py:843
  98.4 10.2 %collective-permute-start.22 = (bf16[128,1024]{1,0:T(8,128)(2,1)S(1)}, bf16[128,1024]{1,0:T(8,128)(2,1)S(1)}, u32[]{:S(2)}, u32[]{:S(2)}) collective-permute-start(bf16[128,1024]{1,0:T(8,128)(2,1)S(1)} %get-tuple-element.111), channel_id=1, source_target_pairs={{0,8},{4,36},{8,16},{12,44},{16,24},{20,52},{24,0},{28,60},{32,40}... | collective-permute-start | bytes 786440 | tf_op jit(solution)/shard_map/ppermute | solution.py:826
  101.1 10.9 %collective-permute-start.23 = (bf16[128,1024]{1,0:T(8,128)(2,1)S(1)}, bf16[128,1024]{1,0:T(8,128)(2,1)S(1)}, u32[]{:S(2)}, u32[]{:S(2)}) collective-permute-start(bf16[128,1024]{1,0:T(8,128)(2,1)S(1)} %get-tuple-element.112), channel_id=1, source_target_pairs={{0,16},{4,68},{8,24},{12,76},{16,0},{20,84},{24,8},{28,92},{32,48}... | collective-permute-start | bytes 786440 | tf_op jit(solution)/shard_map/ppermute | solution.py:826
  104.8 7.2 %collective-permute-start.24 = (bf16[128,1024]{1,0:T(8,128)(2,1)S(1)}, bf16[128,1024]{1,0:T(8,128)(2,1)S(1)}, u32[]{:S(2)}, u32[]{:S(2)}) collective-permute-start(bf16[128,1024]{1,0:T(8,128)(2,1)S(1)} %get-tuple-element.113), channel_id=1, source_target_pairs={{0,24},{4,100},{8,0},{12,108},{16,8},{20,116},{24,16},{28,124},{32... | collective-permute-start | bytes 786440 | tf_op jit(solution)/shard_map/ppermute | solution.py:826
  105.4 17.5 %collective-permute-start.18 = (bf16[528,256]{1,0:T(8,128)(2,1)S(1)}, bf16[528,256]{1,0:T(8,128)(2,1)S(1)}, u32[]{:S(2)}, u32[]{:S(2)}) collective-permute-start(bf16[528,256]{1,0:T(8,128)(2,1)S(1)} %get-tuple-element.101), channel_id=1, source_target_pairs={{0,1},{1,2},{2,3},{3,0},{4,5},{5,6},{6,7},{7,4},{8,9},{9,10},{10,1... | collective-permute-start | bytes 811016 | tf_op jit(solution)/shard_map/ppermute | solution.py:839
  105.5 17.4 %collective-permute-start.19 = (bf16[512,256]{1,0:T(8,128)(2,1)S(1)}, bf16[512,256]{1,0:T(8,128)(2,1)S(1)}, u32[]{:S(2)}, u32[]{:S(2)}) collective-permute-start(bf16[512,256]{1,0:T(8,128)(2,1)S(1)} %get-tuple-element.102), channel_id=1, source_target_pairs={{1,0},{2,1},{3,2},{0,3},{5,4},{6,5},{7,6},{4,7},{9,8},{10,9},{11,1... | collective-permute-start | bytes 786440 | tf_op jit(solution)/shard_map/ppermute | solution.py:843
  112.8 11.8 %collective-permute-start.25 = (bf16[32,1024]{1,0:T(8,128)(2,1)S(1)}, bf16[32,1024]{1,0:T(8,128)(2,1)S(1)}, u32[]{:S(2)}, u32[]{:S(2)}) collective-permute-start(bf16[32,1024]{1,0:T(8,128)(2,1)S(1)} %get-tuple-element.119), channel_id=1, source_target_pairs={{0,32},{4,12},{8,40},{12,20},{16,48},{20,28},{24,56},{28,4},{32,64... | collective-permute-start | bytes 196616 | tf_op jit(solution)/shard_map/ppermute | solution.py:826
  (14 other events, 96.9 us)

commit v8 on v7

--- a/solution.py
+++ b/solution.py
@@ -62,6 +62,7 @@
 
 SMALL = pl.CostEstimate(flops=10**6, bytes_accessed=10**4, transcendentals=0)
 LARGE = pl.CostEstimate(flops=4 * 10**9, bytes_accessed=10**4, transcendentals=0)
+MIDDLE = pl.CostEstimate(flops=25 * 10**8, bytes_accessed=10**4, transcendentals=0)
 RELAY = pl.CostEstimate(flops=10**9, bytes_accessed=10**4, transcendentals=0)
 SCALAR = pl.BlockSpec(memory_space=pltpu.SMEM)
 RESIDENT = pl.BlockSpec(memory_space=pltpu.VMEM)
@@ -89,6 +90,7 @@
 
 
 ALL_ROWS = 7 * BLOCK
+EDGE_ROWS = 256 + 128 + 192
 LEVEL_BLOCK = (0, 4, 6)
 
 
@@ -181,18 +183,18 @@
         q[rows, :] = fine[0]
         q[mid_rows, :] = mid[0]
         q[low_rows, :] = low[0]
-        edge_mid = slice(256 + (step % 2) * 128, 384 + (step % 2) * 128)
-        edge_low = slice(512 + step * 64, 576 + step * 64)
         for n in range(2):
             kv[n, rows, :] = fine[1 + n]
             kv[n, mid_rows, :] = mid[1 + n]
             kv[n, low_rows, :] = low[1 + n]
-            edges[0, n, edge_low, :] = low[1 + n]
-            edges[1, n, edge_low, :] = low[1 + n]
-            side = 0 if step < 2 else 1
-            edges[side, n, edge_mid, :] = mid[1 + n]
             if step in (0, 3):
-                edges[side, n, 0:BLOCK, :] = fine[1 + n]
+                edges[step // 3, n, 0:BLOCK, :] = fine[1 + n]
+            if step in (1, 2):
+                edges[step - 1, n, 256:384, :] = mid[1 + n]
+            if step > 0:
+                edges[0, n, 320 + step * 64 : 384 + step * 64, :] = low[1 + n]
+            if step < 3:
+                edges[1, n, 384 + step * 64 : 448 + step * 64, :] = low[1 + n]
 
     parts = normalise(0)
     for step in range(4):
@@ -207,7 +209,7 @@
 def project(place, shares, wq, wk, wv):
     rows, width = shares[0].shape
     out = jax.ShapeDtypeStruct
-    edge = out((2, 3 * BLOCK, width), BF16)
+    edge = out((2, EDGE_ROWS, width), BF16)
     anywhere = pl.BlockSpec(memory_space=pl.ANY)
     share = pltpu.VMEM((rows, width), BF16)
     fixed = [
@@ -280,7 +282,7 @@
 
 def ext_rows(kv, halo, n, level, at, lanes):
     if at in (0, EXT_BLOCKS[level] - 1):
-        return halo_rows(halo, at == 0, (n, block_rows(level), lanes))
+        return halo[0 if at == 0 else 1][n, block_rows(level), lanes]
     return kv[n, block_rows(LEVEL_BLOCK[level] + at - 1), lanes]
 
 
@@ -403,9 +405,26 @@
 
 
 def forward_edge_kernel(
-    place, bias_ref, q, kv, from_other, from_core, inner, attended, stats, vt, out_f
+    place, bias_ref, q, kv, from_other, from_core, inner,
+    attended, stats, left, right, vt, out_f,
 ):
-    halo = (place, from_core, from_other)
+    received = (place, from_core, from_other)
+    pools = pool_both(0.5, 0.25)
+    every = slice(None)
+    for n in range(2):
+        for out, is_left in ((left, True), (right, False)):
+            fine = halo_rows(received, is_left, (n, slice(0, 256), every))
+            mid = halo_rows(received, is_left, (n, slice(256, 384), every))
+            low = halo_rows(received, is_left, (n, slice(384, 576), every))
+            coarse = nn(pools, fine).astype(BF16)
+            out[n, 0:256, :] = fine
+            if is_left:
+                out[n, 256:384, :], out[n, 384:512, :] = mid, coarse[0:128]
+                out[n, 512:704, :], out[n, 704:768, :] = low, coarse[128:192]
+            else:
+                out[n, 256:384, :], out[n, 384:512, :] = coarse[0:128], mid
+                out[n, 512:576, :], out[n, 576:768, :] = coarse[128:192], low
+    halo = (left, right)
 
     def one(pair, lanes):
         out_f[0:BLOCK, :] = jnp.zeros((BLOCK, PAIR), F32)
@@ -489,10 +508,15 @@
 
 
 def edge_kernel(
-    place, bias_ref, stats, q, kv, from_other, from_core, grads,
+    place, bias_ref, stats, q, kv, left, right, grads,
     dq_f, d_kv, to_core, to_other, kt, ext, dq_s, sums, edges,
 ):
-    halo = (place, from_core, from_other)
+    halo = (left, right)
+
+    def add_rows(factor, rows):
+        for s in range(factor):
+            spread = pl.ds(s, rows.shape[0], factor)
+            sums[spread, :] = sums[spread, :] + rows * (1.0 / factor)
 
     def one(pair, lanes):
         dq_s[...] = jnp.zeros_like(dq_s)
@@ -511,10 +535,21 @@
         )
         dq_f[:, lanes] = dq_s[...]
         for n in range(2):
-            for level in range(LEVELS):
-                first, last = FIRST_EXT[level], FIRST_EXT[level] + EXT_BLOCKS[level] - 1
-                edges[0, n, block_rows(level), lanes] = ext[n, first].astype(BF16)
-                edges[1, n, block_rows(level), lanes] = ext[n, last].astype(BF16)
+            for side in range(2):
+                fine, mid, low = (
+                    ext[n, FIRST_EXT[level] + side * (EXT_BLOCKS[level] - 1)]
+                    for level in range(LEVELS)
+                )
+                if side == 0:
+                    (mid, mid_near), (low, low_near) = (mid[0:128], mid[128:]), (low[0:192], low[192:])
+                else:
+                    (mid_near, mid), (low_near, low) = (mid[0:128], mid[128:]), (low[0:64], low[64:])
+                sums[0:BLOCK, :] = fine
+                add_rows(2, mid_near)
+                add_rows(4, low_near)
+                edges[side, n, 0:256, lanes] = sums[0:BLOCK, :].astype(BF16)
+                edges[side, n, 256:384, lanes] = mid.astype(BF16)
+                edges[side, n, 384:576, lanes] = low.astype(BF16)
             for b in range(4):
                 sums[block_rows(b), :] = ext[n, 1 + b]
             for b in range(2):
@@ -550,21 +585,22 @@
     width = q.shape[1]
     outputs = [held((2 * BLOCK, width), F32), held((width // PAIR, 8, BLOCK), F32)]
     scratch = [turned(EXT_BLOCKS[0]), pltpu.VMEM((4 * BLOCK, PAIR), F32)]
-    return run(forward_inner_kernel, "forward_inner", 12, [bias], [q, kv], outputs, scratch, LARGE)
+    return run(forward_inner_kernel, "forward_inner", 12, [bias], [q, kv], outputs, scratch, MIDDLE)
 
 
 def forward_edge(place, bias, q, kv, halo, inner):
     width = q.shape[1]
     inputs = [q, kv, *halo[::-1], inner]
     outputs = [held((4 * BLOCK, width), BF16), held((width // PAIR, 24, BLOCK), F32)]
+    outputs += [held((2, 3 * BLOCK, width), BF16)] * 2
     scratch = [turned(EXT_TOTAL), pltpu.VMEM((4 * BLOCK, PAIR), F32)]
     return run(forward_edge_kernel, "forward_edge", 12, [place, bias], inputs, outputs, scratch)
 
 
 def edge_backward(place, bias, stats, q, kv, halo, d_att):
     rows, width = 4 * BLOCK, q.shape[1]
-    edge = held((2, 3 * BLOCK, width), BF16)
-    inputs = [stats, q, kv, *halo[::-1], d_att]
+    edge = held((2, EDGE_ROWS, width), BF16)
+    inputs = [stats, q, kv, *halo, d_att]
     outputs = [held((rows, width), F32), held((2, rows, width), F32), edge, edge]
     scratch = [
         turned(EXT_TOTAL),
@@ -632,17 +668,19 @@
     for step in range(4):
         rows = block_rows(step)
         grads = [d_query[rows, :]]
-        mid_rows = slice(256 + (step % 2) * 128, 384 + (step % 2) * 128)
-        low_rows = slice(512 + step * 64, 576 + step * 64)
-        first = step < 2
+        every = slice(None)
         for n in range(2):
             total = d_kv[n, rows, :]
             if step in (0, 3):
-                fine = halo_rows(halo, first, (n, slice(0, BLOCK), slice(None)))
-                total = total + fine.astype(F32)
-            total = total + nn(half, halo_rows(halo, first, (n, mid_rows, slice(None))))
-            total = total + nn(quarter, from_core[n, low_rows, :])
-            total = total + nn(quarter, from_other[n, low_rows, :])
+                total = total + halo_rows(halo, step == 0, (n, slice(0, 256), every)).astype(F32)
+            else:
+                total = total + nn(half, halo_rows(halo, step == 1, (n, slice(256, 384), every)))
+            if step > 0:
+                low = slice(320 + step * 64, 384 + step * 64)
+                total = total + nn(quarter, halo_rows(halo, True, (n, low, every)))
+            if step < 3:
+                low = slice(384 + step * 64, 448 + step * 64)
+                total = total + nn(quarter, halo_rows(halo, False, (n, low, every)))
             grads.append(total.astype(BF16))
         for n, grad in enumerate(grads[1:]):
             d_proj[rows, n * width : (n + 1) * width] = grad
@@ -898,7 +936,7 @@
     halo = exchange(to_core, to_other)
     near_q = tied(q, grad_shares[1], grad_shares[3])
     inner_out, inner_stats = forward_inner(bias, near_q, kv)
-    attended, stats = forward_edge(me, bias, q, kv, halo, inner_out)
+    attended, stats, *halo = forward_edge(me, bias, q, kv, halo, inner_out)
     out_own, *terms = out_terms(me, attended, w_out)
     out_received = sum_over_mp(terms)
     grad_shares = tied(grad_shares, out_own)

time: 126 us -> 122 us (0.968)
  starting transfers between devices: 55.7 us -> 51.6 us
    ppermute x6, starting transfers between devices: 15.8 us -> 13.6 us  [sent(): return lax.ppermute(value, 'seq', pairs)]
    ppermute x2, starting transfers between devices: 11.2 us -> 9.11 us  [exchange(): from_core = lax.ppermute(to_core, 'seq', [(i, i ^ 1) for i in range(count)])]
    ppermute x6, waiting for transfers between devices: 7.1 us -> 5.83 us  [to_next(): return lax.ppermute(value, 'mp', [(i, (i + 1) % MP) for i in range(MP)])]
  transfers between devices with their start and end apart: 28 -> 28, of which waited for: 7 -> 7; matrix products, arithmetic and copies ran while one was open for 0% -> 0% of each run, Pallas kernels for 38% -> 40%
where the time goes in v8:
time: 122 us; the launch traced here: 121 us
  Pallas kernels  52 us (43%)
  starting transfers between devices  51.6 us (42%)
  waiting for transfers between devices  14.1 us (12%)
  local copies, waits for them, and re-layouts  2.51 us (2%)
    pallas_call x15, Pallas kernels, run(): pl.pallas_call(kernel, in_specs=[SCALAR] * len(scalars) + [RESIDENT] * le...  44.4 us
    ppermute x6, starting transfers between devices, to_previous(): return lax.ppermute(value, 'mp', [((i + 1) % MP, i) for i in range(MP)])  15.5 us
    ppermute x6, starting transfers between devices, sent(): return lax.ppermute(value, 'seq', pairs)  13.6 us
    ppermute x2, starting transfers between devices, exchange(): from_core = lax.ppermute(to_core, 'seq', [(i, i ^ 1) for i in range(count)])  9.11 us
    pallas_call x1, Pallas kernels, project(): pl.pallas_call(project_kernel, in_specs=[SCALAR] + [anywhere] * 10, out_s...  7.65 us
    ppermute x4, starting transfers between devices, turned_by(): return lax.ppermute(value, 'mp', [(i, (i + step) % MP) for i in range(MP)])  6.61 us
    ppermute x6, waiting for transfers between devices, to_next(): return lax.ppermute(value, 'mp', [(i, (i + 1) % MP) for i in range(MP)])  5.83 us
    ppermute x6, starting transfers between devices, to_next(): return lax.ppermute(value, 'mp', [(i, (i + 1) % MP) for i in range(MP)])  4.85 us
  transfers between devices with their start and end apart: 28, of which 7 were waited for; matrix products, arithmetic and copies ran while one was open for 0% of the time, Pallas kernels for 40%

profile of v8, /device:TPU:0, one launch (start us, length us, event | category | flops | bytes accessed | tf_op | source)
XLA Modules:
  0.0 121.3 jit_solution(4516108100622413723)
XLA Ops:
  1.7 2.1 %collective-permute-start.3 = (bf16[512,256]{1,0:T(8,128)(2,1)S(1)}, bf16[512,256]{1,0:T(8,128)(2,1)S(1)}, u32[]{:S(2)}, u32[]{:S(2)}) collective-permute-start(bf16[512,256]{1,0:T(8,128)(2,1)S(1)} %get-tuple-element.130), channel_id=1, source_target_pairs={{0,1},{1,2},{2,3},{3,0},{4,5},{5,6},{6,7},{7,4},{8,9},{9,10},{10,1... | collective-permute-start | bytes 786440 | tf_op jit(solution)/shard_map/ppermute | solution.py:877
  3.8 2.2 %collective-permute-start = (bf16[512,256]{1,0:T(8,128)(2,1)S(1)}, bf16[512,256]{1,0:T(8,128)(2,1)S(1)}, u32[]{:S(2)}, u32[]{:S(2)}) collective-permute-start(bf16[512,256]{1,0:T(8,128)(2,1)S(1)} %get-tuple-element.131), channel_id=1, source_target_pairs={{1,0},{2,1},{3,2},{0,3},{5,4},{6,5},{7,6},{4,7},{9,8},{10,9},{11,1... | collective-permute-start | bytes 786440 | tf_op jit(solution)/shard_map/ppermute | solution.py:881
  8.0 5.0 %collective-permute-done.3.t3b_any = bf16[512,256]{1,0:T(8,128)(2,1)S(1)} collective-permute-done((bf16[512,256]{1,0:T(8,128)(2,1)S(1)}, bf16[512,256]{1,0:T(8,128)(2,1)S(1)}, u32[]{:S(2)}, u32[]{:S(2)}) %collective-permute-start.3) | collective-permute-done | bytes 262176 | tf_op jit(solution)/shard_map/ppermute | solution.py:877
  13.0 3.3 %collective-permute-start.2 = (bf16[512,256]{1,0:T(8,128)(2,1)S(1)}, bf16[512,256]{1,0:T(8,128)(2,1)}, u32[]{:S(2)}, u32[]{:S(2)}) collective-permute-start(bf16[512,256]{1,0:T(8,128)(2,1)S(1)} %collective-permute-done.t1a_any), channel_id=1, source_target_pairs={{1,0},{2,1},{3,2},{0,3},{5,4},{6,5},{7,6},{4,7},{9,8},{10,9},{11,1... | collective-permute-start | bytes 786440 | tf_op jit(solution)/shard_map/ppermute | solution.py:881
  16.4 2.2 %collective-permute-done.1.t1b_any = bf16[512,256]{1,0:T(8,128)(2,1)S(1)} collective-permute-done((bf16[512,256]{1,0:T(8,128)(2,1)S(1)}, bf16[512,256]{1,0:T(8,128)(2,1)S(1)}, u32[]{:S(2)}, u32[]{:S(2)}) %collective-permute-start.1) | collective-permute-done | bytes 262176 | tf_op jit(solution)/shard_map/ppermute | solution.py:881
  21.3 2.1 %collective-permute-start.8 = (bf16[1024,256]{1,0:T(8,128)(2,1)}, bf16[1024,256]{1,0:T(8,128)(2,1)}, u32[]{:S(2)}, u32[]{:S(2)}) collective-permute-start(bf16[1024,256]{1,0:T(8,128)(2,1)} %g0.1), channel_id=1, source_target_pairs={{1,0},{2,1},{3,2},{0,3},{5,4},{6,5},{7,6},{4,7},{9,8},{10,9},{11,1... | collective-permute-start | bytes 1572872 | tf_op jit(solution)/shard_map/ppermute | solution.py:881
  25.0 7.6 %project.1 = (f32[8,256]{1,0:T(8,128)S(1)}, bf16[1792,256]{1,0:T(8,128)(2,1)S(1)}, bf16[2,1792,256]{2,1,0:T(8,128)(2,1)S(1)}, bf16[2,576,256]{2,1,0:T(8,128)(2,1...) custom-call(s32[4]{0:T(128)S(1)} %pad_add_fusion.place, ...), custom_call_target="tpu_custom_call" | custom-call | flops 1000000 | bytes 10000 | tf_op jit(solution)/shard_map/project/pallas_call | solution.py:219
  33.3 2.9 %collective-permute-start.7 = (bf16[2,576,256]{2,1,0:T(8,128)(2,1)}, bf16[2,576,256]{2,1,0:T(8,128)(2,1)}, u32[]{:S(2)}, u32[]{:S(2)}) collective-permute-start(bf16[2,576,256]{2,1,0:T(8,128)(2,1)} %get-tuple-element.71), channel_id=1, source_target_pairs={{0,4},{4,0},{8,12},{12,8},{16,20},{20,16},{24,28},{28,24},{32,36},... | collective-permute-start | bytes 1769480 | tf_op jit(solution)/shard_map/ppermute | solution.py:907
  36.3 3.0 %collective-permute-start.13 = (bf16[1024,256]{1,0:T(8,128)(2,1)}, bf16[1024,256]{1,0:T(8,128)(2,1)S(1)}, u32[]{:S(2)}, u32[]{:S(2)}) collective-permute-start(bf16[1024,256]{1,0:T(8,128)(2,1)} %g0.1), channel_id=1, source_target_pairs={{0,2},{1,3},{2,0},{3,1},{4,6},{5,7},{6,4},{7,5},{8,10},{9,11},{10,... | collective-permute-start | bytes 1572872 | tf_op jit(solution)/shard_map/ppermute | solution.py:894
  39.3 3.6 %forward_inner.1 = (f32[512,256]{1,0:T(8,128)S(1)}, f32[2,8,256]{2,1,0:T(8,128)S(1)}) custom-call(f32[2]{0:T(128)S(1)} %pad_maximum_fusion.bias_ref, bf16[1792,256]{1,0:T(8,128)(2,1)S(1)} %get-tuple-element.73.q, bf16[2,1792,256]{2,1,0:T(8,128)(2,1)S(1)} %get-tuple-element.69.kv), custom_call_target="tpu_custom_call" | custom-call | flops 2500000000 | bytes 10000 | tf_op jit(solution)/shard_map/forward_inner/pallas_call | solution.py:76
  42.9 6.9 %forward_edge.1 = (bf16[1024,256]{1,0:T(8,128)(2,1)S(1)}, f32[2,24,256]{2,1,0:T(8,128)S(1)}, bf16[2,768,256]{2,1,0:T(8,128)(2,1)S(1)}, bf16[2,768,256]{2,1,0:T(8,128)(2,1)S(1)}) custom-call(s32[4]{0:T(128)S(1)} %pad_add_fusion.place, f32[2]{0:T(128)S(1)} %pad_maximum_fusion.bias_ref, bf16[1792,256]{1,0:T(8,128)(2,1)S(1)} %get-tuple-element.73.q, ...), custom_call_target="tpu_custom_call" | custom-call | flops 1000000 | bytes 10000 | tf_op jit(solution)/shard_map/forward_edge/pallas_call | solution.py:76
  54.8 3.2 %cotangent.1.grads = bf16[1792,256]{1,0:T(8,128)(2,1)S(1)} custom-call(s32[4]{0:T(128)S(1)} %pad_add_fusion.place, bf16[1024,256]{1,0:T(8,128)(2,1)S(1)} %copy-done.4, bf16[1024,256]{1,0:T(8,128)(2,1)} %collective-permute-done.8.g1, bf16[1024,256]{1,0:T(8,128)(2,1)S(1)} %collective-permute-done.13.g2, bf16[1024,256]{1,0:T(8,128)(2,1)} %collective-permute-done.9.g3, ...), custom_call_target="tpu_custom_call" | custom-call | flops 1000000 | bytes 10000 | tf_op jit(solution)/shard_map/cotangent/pallas_call | solution.py:76
  58.0 10.7 %edge_backward.1 = (f32[1024,256]{1,0:T(8,128)S(1)}, f32[2,1024,256]{2,1,0:T(8,128)S(1)}, bf16[2,576,256]{2,1,0:T(8,128)(2,1)S(1)}, bf16[2,576,256]{2,1,0:T(8,128)(2,1)S(1)}) custom-call(s32[4]{0:T(128)S(1)} %pad_add_fusion.place, f32[2]{0:T(128)S(1)} %pad_maximum_fusion.bias_ref, f32[2,24,256]{2,1,0:T(8,128)S(1)} %get-tuple-element.86.stats, ...), custom_call_target="tpu_custom_call" | custom-call | flops 1000000 | bytes 10000 | tf_op jit(solution)/shard_map/edge_backward/pallas_call | solution.py:76
  69.4 6.2 %collective-permute-start.15 = (bf16[2,576,256]{2,1,0:T(8,128)(2,1)S(1)}, bf16[2,576,256]{2,1,0:T(8,128)(2,1)S(1)}, u32[]{:S(2)}, u32[]{:S(2)}) collective-permute-start(bf16[2,576,256]{2,1,0:T(8,128)(2,1)S(1)} %get-tuple-element.98), channel_id=1, source_target_pairs={{0,4},{4,0},{8,12},{12,8},{16,20},{20,16},{24,28},{28,24},{32,36},... | collective-permute-start | bytes 1769480 | tf_op jit(solution)/shard_map/ppermute | solution.py:907
  75.6 5.5 %inner_backward.1 = (bf16[1024,256]{1,0:T(8,128)(2,1)S(1)}, f32[2,1024,256]{2,1,0:T(8,128)S(1)}) custom-call(f32[2]{0:T(128)S(1)} %pad_maximum_fusion.bias_ref, f32[2,8,256]{2,1,0:T(8,128)S(1)} %get-tuple-element.80.stats, bf16[1792,256]{1,0:T(8,128)(2,1)S(1)} %get-tuple-element.73.q, bf16[2,1792,256]{2,1,0:T(8,128)(2,1)S(1)} %get-tuple-element.69.kv, ...), custom_call_target="tpu_custom_call" | custom-call | flops 1000000 | bytes 10000 | tf_op jit(solution)/shard_map/inner_backward/pallas_call | solution.py:76
  81.2 2.7 %early_terms.1 = (bf16[1024,256]{1,0:T(8,128)(2,1)S(1)}, bf16[1024,256]{1,0:T(8,128)(2,1)S(1)}) custom-call(bf16[1024,256]{1,0:T(8,128)(2,1)S(1)} %copy-done.4, bf16[1024,256]{1,0:T(8,128)(2,1)} %collective-permute-done.8.g1, bf16[1024,256]{1,0:T(8,128)(2,1)S(1)} %collective-permute-done.13.g2, bf16[1024,256]{1,0:T(8,128)(2,1)} %collective-permute-done.9.g3, ...), custom_call_target="tpu_custom_call" | custom-call | flops 4000000000 | bytes 10000 | tf_op jit(solution)/shard_map/early_terms/pallas_call | solution.py:76
  83.9 3.3 %input_terms.1 = (bf16[1024,512]{1,0:T(8,128)(2,1)S(1)}, bf16[16,256]{1,0:T(8,128)(2,1)S(1)}, bf16[1024,256]{1,0:T(8,128)(2,1)S(1)}, bf16[512,256]{1,0:T(8,128)(...) custom-call(s32[4]{0:T(128)S(1)} %pad_add_fusion.place, ...), custom_call_target="tpu_custom_call" | custom-call | flops 1000000 | bytes 10000 | tf_op jit(solution)/shard_map/input_terms/pallas_call | solution.py:76
  87.9 2.6 %collective-permute-start.17 = (bf16[1040,256]{1,0:T(8,128)(2,1)S(1)}, bf16[1040,256]{1,0:T(8,128)(2,1)S(1)}, u32[]{:S(2)}, u32[]{:S(2)}) collective-permute-start(bf16[1040,256]{1,0:T(8,128)(2,1)S(1)} %get-tuple-element.102), channel_id=1, source_target_pairs={{1,0},{2,1},{3,2},{0,3},{5,4},{6,5},{7,6},{4,7},{9,8},{10,9},{11,1... | collective-permute-start | bytes 1597448 | tf_op jit(solution)/shard_map/ppermute | solution.py:881
  90.5 2.1 %inner_terms.1 = (bf16[512,1024]{1,0:T(8,128)(2,1)S(1)}, bf16[256,1024]{1,0:T(8,128)(2,1)S(1)}, bf16[256,1024]{1,0:T(8,128)(2,1)S(1)}) custom-call(s32[4]{0:T(128)S(1)} %pad_add_fusion.place, bf16[1024,1024]{1,0:T(8,128)(2,1)S(1)} %copy-done, bf16[1024,512]{1,0:T(8,128)(2,1)S(1)} %get-tuple-element.109.d_proj, ...), custom_call_target="tpu_custom_call" | custom-call | flops 1000000 | bytes 10000 | tf_op jit(solution)/shard_map/inner_terms/pallas_call | solution.py:76
  97.7 4.8 %collective-permute-start.23 = (bf16[128,1024]{1,0:T(8,128)(2,1)S(1)}, bf16[128,1024]{1,0:T(8,128)(2,1)S(1)}, u32[]{:S(2)}, u32[]{:S(2)}) collective-permute-start(bf16[128,1024]{1,0:T(8,128)(2,1)S(1)} %get-tuple-element.116), channel_id=1, source_target_pairs={{0,16},{4,68},{8,24},{12,76},{16,0},{20,84},{24,8},{28,92},{32,48}... | collective-permute-start | bytes 786440 | tf_op jit(solution)/shard_map/ppermute | solution.py:864
  102.8 3.2 %collective-permute-start.19 = (bf16[512,256]{1,0:T(8,128)(2,1)S(1)}, bf16[512,256]{1,0:T(8,128)(2,1)S(1)}, u32[]{:S(2)}, u32[]{:S(2)}) collective-permute-start(bf16[512,256]{1,0:T(8,128)(2,1)S(1)} %get-tuple-element.106), channel_id=1, source_target_pairs={{1,0},{2,1},{3,2},{0,3},{5,4},{6,5},{7,6},{4,7},{9,8},{10,9},{11,1... | collective-permute-start | bytes 786440 | tf_op jit(solution)/shard_map/ppermute | solution.py:881
  106.0 3.7 %collective-permute-done.23.c = bf16[128,1024]{1,0:T(8,128)(2,1)S(1)} collective-permute-done((bf16[128,1024]{1,0:T(8,128)(2,1)S(1)}, bf16[128,1024]{1,0:T(8,128)(2,1)S(1)}, u32[]{:S(2)}, u32[]{:S(2)}) %collective-permute-start.23) | collective-permute-done | bytes 262176 | tf_op jit(solution)/shard_map/ppermute | solution.py:864
  110.5 3.0 %collective-permute-start.25 = (bf16[32,1024]{1,0:T(8,128)(2,1)S(1)}, bf16[32,1024]{1,0:T(8,128)(2,1)S(1)}, u32[]{:S(2)}, u32[]{:S(2)}) collective-permute-start(bf16[32,1024]{1,0:T(8,128)(2,1)S(1)} %get-tuple-element.123), channel_id=1, source_target_pairs={{0,32},{4,12},{8,40},{12,20},{16,48},{20,28},{24,56},{28,4},{32,64... | collective-permute-start | bytes 196616 | tf_op jit(solution)/shard_map/ppermute | solution.py:864
  113.5 2.9 %collective-permute-start.26 = (bf16[32,1024]{1,0:T(8,128)(2,1)S(1)}, bf16[32,1024]{1,0:T(8,128)(2,1)S(1)}, u32[]{:S(2)}, u32[]{:S(2)}) collective-permute-start(bf16[32,1024]{1,0:T(8,128)(2,1)S(1)} %get-tuple-element.124), channel_id=1, source_target_pairs={{0,64},{4,20},{8,72},{12,28},{16,80},{20,4},{24,88},{28,12},{32,96... | collective-permute-start | bytes 196616 | tf_op jit(solution)/shard_map/ppermute | solution.py:864
  (71 shorter events, 25.5 us)
Async XLA Ops:
  1.7 11.3 %collective-permute-start.3 = (bf16[512,256]{1,0:T(8,128)(2,1)S(1)}, bf16[512,256]{1,0:T(8,128)(2,1)S(1)}, u32[]{:S(2)}, u32[]{:S(2)}) collective-permute-start(bf16[512,256]{1,0:T(8,128)(2,1)S(1)} %get-tuple-element.130), channel_id=1, source_target_pairs={{0,1},{1,2},{2,3},{3,0},{4,5},{5,6},{6,7},{7,4},{8,9},{9,10},{10,1... | collective-permute-start | bytes 786440 | tf_op jit(solution)/shard_map/ppermute | solution.py:877
  3.8 9.3 %collective-permute-start = (bf16[512,256]{1,0:T(8,128)(2,1)S(1)}, bf16[512,256]{1,0:T(8,128)(2,1)S(1)}, u32[]{:S(2)}, u32[]{:S(2)}) collective-permute-start(bf16[512,256]{1,0:T(8,128)(2,1)S(1)} %get-tuple-element.131), channel_id=1, source_target_pairs={{1,0},{2,1},{3,2},{0,3},{5,4},{6,5},{7,6},{4,7},{9,8},{10,9},{11,1... | collective-permute-start | bytes 786440 | tf_op jit(solution)/shard_map/ppermute | solution.py:881
  6.0 12.6 %collective-permute-start.1 = (bf16[512,256]{1,0:T(8,128)(2,1)S(1)}, bf16[512,256]{1,0:T(8,128)(2,1)S(1)}, u32[]{:S(2)}, u32[]{:S(2)}) collective-permute-start(bf16[512,256]{1,0:T(8,128)(2,1)S(1)} %get-tuple-element.130), channel_id=1, source_target_pairs={{1,0},{2,1},{3,2},{0,3},{5,4},{6,5},{7,6},{4,7},{9,8},{10,9},{11,1... | collective-permute-start | bytes 786440 | tf_op jit(solution)/shard_map/ppermute | solution.py:881
  7.9 10.7 %collective-permute-start.5 = (bf16[512,256]{1,0:T(8,128)(2,1)S(1)}, bf16[512,256]{1,0:T(8,128)(2,1)S(1)}, u32[]{:S(2)}, u32[]{:S(2)}) collective-permute-start(bf16[512,256]{1,0:T(8,128)(2,1)S(1)} %get-tuple-element.131), channel_id=1, source_target_pairs={{0,1},{1,2},{2,3},{3,0},{4,5},{5,6},{6,7},{7,4},{8,9},{9,10},{10,1... | collective-permute-start | bytes 786440 | tf_op jit(solution)/shard_map/ppermute | solution.py:877
  13.0 11.2 %collective-permute-start.4 = (bf16[512,256]{1,0:T(8,128)(2,1)S(1)}, bf16[512,256]{1,0:T(8,128)(2,1)S(1)}, u32[]{:S(2)}, u32[]{:S(2)}) collective-permute-start(bf16[512,256]{1,0:T(8,128)(2,1)S(1)} %collective-permute-done.3.t3b_any), channel_id=1, source_target_pairs={{0,1},{1,2},{2,3},{3,0},{4,5},{5,6},{6,7},{7,4},{8,9},{9,10},{10,1... | collective-permute-start | bytes 786440 | tf_op jit(solution)/shard_map/ppermute | solution.py:877
  13.0 11.9 %collective-permute-start.2 = (bf16[512,256]{1,0:T(8,128)(2,1)S(1)}, bf16[512,256]{1,0:T(8,128)(2,1)}, u32[]{:S(2)}, u32[]{:S(2)}) collective-permute-start(bf16[512,256]{1,0:T(8,128)(2,1)S(1)} %collective-permute-done.t1a_any), channel_id=1, source_target_pairs={{1,0},{2,1},{3,2},{0,3},{5,4},{6,5},{7,6},{4,7},{9,8},{10,9},{11,1... | collective-permute-start | bytes 786440 | tf_op jit(solution)/shard_map/ppermute | solution.py:881
  19.3 19.9 %collective-permute-start.9 = (bf16[1024,256]{1,0:T(8,128)(2,1)}, bf16[1024,256]{1,0:T(8,128)(2,1)}, u32[]{:S(2)}, u32[]{:S(2)}) collective-permute-start(bf16[1024,256]{1,0:T(8,128)(2,1)} %g0.1), channel_id=1, source_target_pairs={{0,1},{1,2},{2,3},{3,0},{4,5},{5,6},{6,7},{7,4},{8,9},{9,10},{10,1... | collective-permute-start | bytes 1572872 | tf_op jit(solution)/shard_map/ppermute | solution.py:877
  21.3 18.0 %collective-permute-start.8 = (bf16[1024,256]{1,0:T(8,128)(2,1)}, bf16[1024,256]{1,0:T(8,128)(2,1)}, u32[]{:S(2)}, u32[]{:S(2)}) collective-permute-start(bf16[1024,256]{1,0:T(8,128)(2,1)} %g0.1), channel_id=1, source_target_pairs={{1,0},{2,1},{3,2},{0,3},{5,4},{6,5},{7,6},{4,7},{9,8},{10,9},{11,1... | collective-permute-start | bytes 1572872 | tf_op jit(solution)/shard_map/ppermute | solution.py:881
  32.6 10.2 %collective-permute-start.6 = (bf16[2,576,256]{2,1,0:T(8,128)(2,1)}, bf16[2,576,256]{2,1,0:T(8,128)(2,1)S(1)}, u32[]{:S(2)}, u32[]{:S(2)}) collective-permute-start(bf16[2,576,256]{2,1,0:T(8,128)(2,1)} %get-tuple-element.70), channel_id=1, source_target_pairs={{4,8},{8,4},{12,16},{16,12},{20,24},{24,20},{28,32},{32,28},{36,40... | collective-permute-start | bytes 1769480 | tf_op jit(solution)/shard_map/ppermute | solution.py:906
  33.3 9.5 %collective-permute-start.7 = (bf16[2,576,256]{2,1,0:T(8,128)(2,1)}, bf16[2,576,256]{2,1,0:T(8,128)(2,1)}, u32[]{:S(2)}, u32[]{:S(2)}) collective-permute-start(bf16[2,576,256]{2,1,0:T(8,128)(2,1)} %get-tuple-element.71), channel_id=1, source_target_pairs={{0,4},{4,0},{8,12},{12,8},{16,20},{20,16},{24,28},{28,24},{32,36},... | collective-permute-start | bytes 1769480 | tf_op jit(solution)/shard_map/ppermute | solution.py:907
  36.3 18.5 %collective-permute-start.13 = (bf16[1024,256]{1,0:T(8,128)(2,1)}, bf16[1024,256]{1,0:T(8,128)(2,1)S(1)}, u32[]{:S(2)}, u32[]{:S(2)}) collective-permute-start(bf16[1024,256]{1,0:T(8,128)(2,1)} %g0.1), channel_id=1, source_target_pairs={{0,2},{1,3},{2,0},{3,1},{4,6},{5,7},{6,4},{7,5},{8,10},{9,11},{10,... | collective-permute-start | bytes 1572872 | tf_op jit(solution)/shard_map/ppermute | solution.py:894
  51.2 30.0 %collective-permute-start.10 = (bf16[1024,256]{1,0:T(8,128)(2,1)S(1)}, bf16[1024,256]{1,0:T(8,128)(2,1)S(1)}, u32[]{:S(2)}, u32[]{:S(2)}) collective-permute-start(bf16[1024,256]{1,0:T(8,128)(2,1)S(1)} %get-tuple-element.77), channel_id=1, source_target_pairs={{0,1},{1,2},{2,3},{3,0},{4,5},{5,6},{6,7},{7,4},{8,9},{9,10},{10,1... | collective-permute-start | bytes 1572872 | tf_op jit(solution)/shard_map/ppermute | solution.py:894
  52.0 29.1 %collective-permute-start.11 = (bf16[1024,256]{1,0:T(8,128)(2,1)S(1)}, bf16[1024,256]{1,0:T(8,128)(2,1)S(1)}, u32[]{:S(2)}, u32[]{:S(2)}) collective-permute-start(bf16[1024,256]{1,0:T(8,128)(2,1)S(1)} %get-tuple-element.78), channel_id=1, source_target_pairs={{0,2},{1,3},{2,0},{3,1},{4,6},{5,7},{6,4},{7,5},{8,10},{9,11},{10,... | collective-permute-start | bytes 1572872 | tf_op jit(solution)/shard_map/ppermute | solution.py:894
  53.9 27.3 %collective-permute-start.12 = (bf16[1024,256]{1,0:T(8,128)(2,1)S(1)}, bf16[1024,256]{1,0:T(8,128)(2,1)S(1)}, u32[]{:S(2)}, u32[]{:S(2)}) collective-permute-start(bf16[1024,256]{1,0:T(8,128)(2,1)S(1)} %get-tuple-element.79), channel_id=1, source_target_pairs={{0,3},{1,0},{2,1},{3,2},{4,7},{5,4},{6,5},{7,6},{8,11},{9,8},{10,9... | collective-permute-start | bytes 1572872 | tf_op jit(solution)/shard_map/ppermute | solution.py:894
  68.7 15.2 %collective-permute-start.14 = (bf16[2,576,256]{2,1,0:T(8,128)(2,1)S(1)}, bf16[2,576,256]{2,1,0:T(8,128)(2,1)S(1)}, u32[]{:S(2)}, u32[]{:S(2)}) collective-permute-start(bf16[2,576,256]{2,1,0:T(8,128)(2,1)S(1)} %get-tuple-element.97), channel_id=1, source_target_pairs={{4,8},{8,4},{12,16},{16,12},{20,24},{24,20},{28,32},{32,28},{36,40... | collective-permute-start | bytes 1769480 | tf_op jit(solution)/shard_map/ppermute | solution.py:906
  69.4 14.5 %collective-permute-start.15 = (bf16[2,576,256]{2,1,0:T(8,128)(2,1)S(1)}, bf16[2,576,256]{2,1,0:T(8,128)(2,1)S(1)}, u32[]{:S(2)}, u32[]{:S(2)}) collective-permute-start(bf16[2,576,256]{2,1,0:T(8,128)(2,1)S(1)} %get-tuple-element.98), channel_id=1, source_target_pairs={{0,4},{4,0},{8,12},{12,8},{16,20},{20,16},{24,28},{28,24},{32,36},... | collective-permute-start | bytes 1769480 | tf_op jit(solution)/shard_map/ppermute | solution.py:907
  87.2 15.4 %collective-permute-start.16 = (bf16[1040,256]{1,0:T(8,128)(2,1)S(1)}, bf16[1040,256]{1,0:T(8,128)(2,1)S(1)}, u32[]{:S(2)}, u32[]{:S(2)}) collective-permute-start(bf16[1040,256]{1,0:T(8,128)(2,1)S(1)} %get-tuple-element.101), channel_id=1, source_target_pairs={{0,1},{1,2},{2,3},{3,0},{4,5},{5,6},{6,7},{7,4},{8,9},{9,10},{10,1... | collective-permute-start | bytes 1597448 | tf_op jit(solution)/shard_map/ppermute | solution.py:877
  87.9 14.7 %collective-permute-start.17 = (bf16[1040,256]{1,0:T(8,128)(2,1)S(1)}, bf16[1040,256]{1,0:T(8,128)(2,1)S(1)}, u32[]{:S(2)}, u32[]{:S(2)}) collective-permute-start(bf16[1040,256]{1,0:T(8,128)(2,1)S(1)} %get-tuple-element.102), channel_id=1, source_target_pairs={{1,0},{2,1},{3,2},{0,3},{5,4},{6,5},{7,6},{4,7},{9,8},{10,9},{11,1... | collective-permute-start | bytes 1597448 | tf_op jit(solution)/shard_map/ppermute | solution.py:881
  96.2 9.8 %collective-permute-start.22 = (bf16[128,1024]{1,0:T(8,128)(2,1)S(1)}, bf16[128,1024]{1,0:T(8,128)(2,1)S(1)}, u32[]{:S(2)}, u32[]{:S(2)}) collective-permute-start(bf16[128,1024]{1,0:T(8,128)(2,1)S(1)} %get-tuple-element.115), channel_id=1, source_target_pairs={{0,8},{4,36},{8,16},{12,44},{16,24},{20,52},{24,0},{28,60},{32,40}... | collective-permute-start | bytes 786440 | tf_op jit(solution)/shard_map/ppermute | solution.py:864
  97.7 12.0 %collective-permute-start.23 = (bf16[128,1024]{1,0:T(8,128)(2,1)S(1)}, bf16[128,1024]{1,0:T(8,128)(2,1)S(1)}, u32[]{:S(2)}, u32[]{:S(2)}) collective-permute-start(bf16[128,1024]{1,0:T(8,128)(2,1)S(1)} %get-tuple-element.116), channel_id=1, source_target_pairs={{0,16},{4,68},{8,24},{12,76},{16,0},{20,84},{24,8},{28,92},{32,48}... | collective-permute-start | bytes 786440 | tf_op jit(solution)/shard_map/ppermute | solution.py:864
  102.5 7.2 %collective-permute-start.24 = (bf16[128,1024]{1,0:T(8,128)(2,1)S(1)}, bf16[128,1024]{1,0:T(8,128)(2,1)S(1)}, u32[]{:S(2)}, u32[]{:S(2)}) collective-permute-start(bf16[128,1024]{1,0:T(8,128)(2,1)S(1)} %get-tuple-element.117), channel_id=1, source_target_pairs={{0,24},{4,100},{8,0},{12,108},{16,8},{20,116},{24,16},{28,124},{32... | collective-permute-start | bytes 786440 | tf_op jit(solution)/shard_map/ppermute | solution.py:864
  102.7 16.1 %collective-permute-start.18 = (bf16[528,256]{1,0:T(8,128)(2,1)S(1)}, bf16[528,256]{1,0:T(8,128)(2,1)S(1)}, u32[]{:S(2)}, u32[]{:S(2)}) collective-permute-start(bf16[528,256]{1,0:T(8,128)(2,1)S(1)} %get-tuple-element.105), channel_id=1, source_target_pairs={{0,1},{1,2},{2,3},{3,0},{4,5},{5,6},{6,7},{7,4},{8,9},{9,10},{10,1... | collective-permute-start | bytes 811016 | tf_op jit(solution)/shard_map/ppermute | solution.py:877
  102.8 16.0 %collective-permute-start.19 = (bf16[512,256]{1,0:T(8,128)(2,1)S(1)}, bf16[512,256]{1,0:T(8,128)(2,1)S(1)}, u32[]{:S(2)}, u32[]{:S(2)}) collective-permute-start(bf16[512,256]{1,0:T(8,128)(2,1)S(1)} %get-tuple-element.106), channel_id=1, source_target_pairs={{1,0},{2,1},{3,2},{0,3},{5,4},{6,5},{7,6},{4,7},{9,8},{10,9},{11,1... | collective-permute-start | bytes 786440 | tf_op jit(solution)/shard_map/ppermute | solution.py:881
  110.5 10.0 %collective-permute-start.25 = (bf16[32,1024]{1,0:T(8,128)(2,1)S(1)}, bf16[32,1024]{1,0:T(8,128)(2,1)S(1)}, u32[]{:S(2)}, u32[]{:S(2)}) collective-permute-start(bf16[32,1024]{1,0:T(8,128)(2,1)S(1)} %get-tuple-element.123), channel_id=1, source_target_pairs={{0,32},{4,12},{8,40},{12,20},{16,48},{20,28},{24,56},{28,4},{32,64... | collective-permute-start | bytes 196616 | tf_op jit(solution)/shard_map/ppermute | solution.py:864
  (14 other events, 86.5 us)

commit v9 on v8

--- a/solution.py
+++ b/solution.py
@@ -243,27 +243,43 @@
     )(place, *fixed)
 
 
-def cotangent_kernel(place, g0, g1, g2, g3, w_out, d_att, w_turned):
+def near_kernel(place, g0, g1, g3, w_out, total, w_turned):
     me = place[0]
     width = g0.shape[1]
-    pools = pool_both(1.0, 1.0)
-    for r in range(MP):
-        w_turned[block_rows(r), :] = w_out[:, share_rows(me, r, width)].T
+    for n, r in enumerate((0, 1, 3)):
+        w_turned[block_rows(n), :] = w_out[:, share_rows(me, r, width)].T
     for step in range(4):
         rows = block_rows(step)
-        shares = jnp.concatenate([share[rows, :] for share in (g0, g1, g2, g3)], axis=1)
-        fine = nn(shares, w_turned[...]).astype(BF16)
+        shares = jnp.concatenate([share[rows, :] for share in (g0, g1, g3)], axis=1)
+        total[rows, :] = nn(shares, w_turned[...])
+
+
+def near_cotangent(place, shares, w_out):
+    rows, width = shares[0].shape
+    inputs = [*shares, w_out]
+    scratch = [pltpu.VMEM((3 * width, width), BF16)]
+    outputs = [held((rows, width), F32)]
+    return run(near_kernel, "near_cotangent", 10, [place], inputs, outputs, scratch)[0]
+
+
+def cotangent_kernel(place, near, g2, w_out, d_att, w_turned):
+    width = g2.shape[1]
+    pools = pool_both(1.0, 1.0)
+    w_turned[...] = w_out[:, share_rows(place[0], 2, width)].T
+    for step in range(4):
+        rows = block_rows(step)
+        fine = (near[rows, :] + nn(g2[rows, :], w_turned[...])).astype(BF16)
         d_att[rows, :] = fine
         coarse = nn(pools, fine).astype(BF16)
         d_att[1024 + step * 128 : 1024 + (step + 1) * 128, :] = coarse[0:128]
         d_att[1536 + step * 64 : 1536 + (step + 1) * 64, :] = coarse[128:192]
 
 
-def cotangent(place, shares, w_out):
-    rows, width = shares[0].shape
+def cotangent(place, near, far, w_out):
+    width = far.shape[1]
+    scratch = [pltpu.VMEM((width, width), BF16)]
     outputs = [held((ALL_ROWS, width), BF16)]
-    scratch = [pltpu.VMEM((MP * width, width), BF16)]
-    return run(cotangent_kernel, "cotangent", 10, [place], [*shares, w_out], outputs, scratch)[0]
+    return run(cotangent_kernel, "cotangent", 10, [place], [near, far, w_out], outputs, scratch)[0]
 
 
 EDGE_UNITS = ((0, 0), (0, 3), (1, 0), (1, 1), (2, 0))
@@ -936,11 +952,13 @@
     halo = exchange(to_core, to_other)
     near_q = tied(q, grad_shares[1], grad_shares[3])
     inner_out, inner_stats = forward_inner(bias, near_q, kv)
+    near = near_cotangent(me, tied([grad_shares[n] for n in (0, 1, 3)], inner_out), w_out)
+    inner_out = tied(inner_out, near)
     attended, stats, *halo = forward_edge(me, bias, q, kv, halo, inner_out)
     out_own, *terms = out_terms(me, attended, w_out)
     out_received = sum_over_mp(terms)
     grad_shares = tied(grad_shares, out_own)
-    d_att = cotangent(me, grad_shares, w_out)
+    d_att = cotangent(me, near, grad_shares[2], w_out)
     dq_f, d_kv, to_core, to_other = edge_backward(me, bias, stats, q, kv, halo, d_att)
     halo = exchange(to_core, to_other)
     d_query, d_kv = inner_backward(bias, inner_stats, q, kv, d_att, dq_f, d_kv)
@@ -957,7 +975,7 @@
     onward_right, onward_left = relay(keep_right, keep_left, l1, r1)
     l2, r2 = to_next(onward_right), to_previous(onward_left)
     grad_tokens = finish_grad(own, l1, r1, l2, r2, tokens, inverse, dots)
-    *weight_grads, grad_w_out = sum_over_seq(me, core_sums, onward_right)
+    *weight_grads, grad_w_out = sum_over_seq(me, core_sums, onward_right, attn_out)
     return (attn_out, grad_tokens, *weight_grads, grad_w_out.T)
 
 

time: 122 us -> 120 us (0.984)
  starting transfers between devices: 51.6 us -> 49.4 us
    ppermute x2, starting transfers between devices: 9.11 us -> 7.26 us  [exchange(): from_core = lax.ppermute(to_core, 'seq', [(i, i ^ 1) for i in range(count)])]
    ppermute x6, starting transfers between devices: 4.85 us -> 6.62 us  [to_next(): return lax.ppermute(value, 'mp', [(i, (i + 1) % MP) for i in range(MP)])]
    ppermute x6, starting transfers between devices: 15.5 us -> 13.7 us  [to_previous(): return lax.ppermute(value, 'mp', [((i + 1) % MP, i) for i in range(MP)])]
    pallas_call x15 -> x16, Pallas kernels: 44.4 us -> 44.6 us  [run(): pl.pallas_call(kernel, in_specs=[SCALAR] * len(scalars) + [RESIDENT] * le...]
  transfers between devices with their start and end apart: 28 -> 28, of which waited for: 7 -> 9; matrix products, arithmetic and copies ran while one was open for 0% -> 0% of each run, Pallas kernels for 40% -> 40%
where the time goes in v9:
time: 120 us
  Pallas kernels  52.3 us (44%)
  starting transfers between devices  49.4 us (41%)
  waiting for transfers between devices  14.3 us (12%)
  local copies, waits for them, and re-layouts  2.5 us (2%)
    pallas_call x16, Pallas kernels, run(): pl.pallas_call(kernel, in_specs=[SCALAR] * len(scalars) + [RESIDENT] * le...  44.6 us
    ppermute x6, starting transfers between devices, to_previous(): return lax.ppermute(value, 'mp', [((i + 1) % MP, i) for i in range(MP)])  13.7 us
    ppermute x6, starting transfers between devices, sent(): return lax.ppermute(value, 'seq', pairs)  13.2 us
    pallas_call x1, Pallas kernels, project(): pl.pallas_call(project_kernel, in_specs=[SCALAR] + [anywhere] * 10, out_s...  7.65 us
    ppermute x2, starting transfers between devices, exchange(): from_core = lax.ppermute(to_core, 'seq', [(i, i ^ 1) for i in range(count)])  7.26 us
    ppermute x6, starting transfers between devices, to_next(): return lax.ppermute(value, 'mp', [(i, (i + 1) % MP) for i in range(MP)])  6.62 us
    ppermute x4, starting transfers between devices, turned_by(): return lax.ppermute(value, 'mp', [(i, (i + step) % MP) for i in range(MP)])  6.61 us
    ppermute x6, waiting for transfers between devices, to_next(): return lax.ppermute(value, 'mp', [(i, (i + 1) % MP) for i in range(MP)])  5.84 us
  transfers between devices with their start and end apart: 28, of which 9 were waited for; matrix products, arithmetic and copies ran while one was open for 0% of the time, Pallas kernels for 40%

profile of v9, /device:TPU:0, one launch (start us, length us, event | category | flops | bytes accessed | tf_op | source)
XLA Modules:
  0.0 119.5 jit_solution(2402858344792310815)
XLA Ops:
  1.7 2.1 %collective-permute-start.3 = (bf16[512,256]{1,0:T(8,128)(2,1)S(1)}, bf16[512,256]{1,0:T(8,128)(2,1)S(1)}, u32[]{:S(2)}, u32[]{:S(2)}) collective-permute-start(bf16[512,256]{1,0:T(8,128)(2,1)S(1)} %get-tuple-element.138), channel_id=1, source_target_pairs={{0,1},{1,2},{2,3},{3,0},{4,5},{5,6},{6,7},{7,4},{8,9},{9,10},{10,1... | collective-permute-start | bytes 786440 | tf_op jit(solution)/shard_map/ppermute | solution.py:893
  3.8 2.2 %collective-permute-start = (bf16[512,256]{1,0:T(8,128)(2,1)S(1)}, bf16[512,256]{1,0:T(8,128)(2,1)S(1)}, u32[]{:S(2)}, u32[]{:S(2)}) collective-permute-start(bf16[512,256]{1,0:T(8,128)(2,1)S(1)} %get-tuple-element.139), channel_id=1, source_target_pairs={{1,0},{2,1},{3,2},{0,3},{5,4},{6,5},{7,6},{4,7},{9,8},{10,9},{11,1... | collective-permute-start | bytes 786440 | tf_op jit(solution)/shard_map/ppermute | solution.py:897
  6.0 1.9 %collective-permute-start.1 = (bf16[512,256]{1,0:T(8,128)(2,1)S(1)}, bf16[512,256]{1,0:T(8,128)(2,1)S(1)}, u32[]{:S(2)}, u32[]{:S(2)}) collective-permute-start(bf16[512,256]{1,0:T(8,128)(2,1)S(1)} %get-tuple-element.138), channel_id=1, source_target_pairs={{1,0},{2,1},{3,2},{0,3},{5,4},{6,5},{7,6},{4,7},{9,8},{10,9},{11,1... | collective-permute-start | bytes 786440 | tf_op jit(solution)/shard_map/ppermute | solution.py:897
  8.0 5.0 %collective-permute-done.3.t3b_any = bf16[512,256]{1,0:T(8,128)(2,1)S(1)} collective-permute-done((bf16[512,256]{1,0:T(8,128)(2,1)S(1)}, bf16[512,256]{1,0:T(8,128)(2,1)S(1)}, u32[]{:S(2)}, u32[]{:S(2)}) %collective-permute-start.3) | collective-permute-done | bytes 262176 | tf_op jit(solution)/shard_map/ppermute | solution.py:893
  13.0 3.3 %collective-permute-start.2 = (bf16[512,256]{1,0:T(8,128)(2,1)S(1)}, bf16[512,256]{1,0:T(8,128)(2,1)}, u32[]{:S(2)}, u32[]{:S(2)}) collective-permute-start(bf16[512,256]{1,0:T(8,128)(2,1)S(1)} %collective-permute-done.t1a_any), channel_id=1, source_target_pairs={{1,0},{2,1},{3,2},{0,3},{5,4},{6,5},{7,6},{4,7},{9,8},{10,9},{11,1... | collective-permute-start | bytes 786440 | tf_op jit(solution)/shard_map/ppermute | solution.py:897
  16.4 2.2 %collective-permute-done.1.t1b_any = bf16[512,256]{1,0:T(8,128)(2,1)S(1)} collective-permute-done((bf16[512,256]{1,0:T(8,128)(2,1)S(1)}, bf16[512,256]{1,0:T(8,128)(2,1)S(1)}, u32[]{:S(2)}, u32[]{:S(2)}) %collective-permute-start.1) | collective-permute-done | bytes 262176 | tf_op jit(solution)/shard_map/ppermute | solution.py:897
  19.3 1.9 %collective-permute-start.9 = (bf16[1024,256]{1,0:T(8,128)(2,1)}, bf16[1024,256]{1,0:T(8,128)(2,1)}, u32[]{:S(2)}, u32[]{:S(2)}) collective-permute-start(bf16[1024,256]{1,0:T(8,128)(2,1)} %g0.1), channel_id=1, source_target_pairs={{0,1},{1,2},{2,3},{3,0},{4,5},{5,6},{6,7},{7,4},{8,9},{9,10},{10,1... | collective-permute-start | bytes 1572872 | tf_op jit(solution)/shard_map/ppermute | solution.py:893
  21.3 2.1 %collective-permute-start.8 = (bf16[1024,256]{1,0:T(8,128)(2,1)}, bf16[1024,256]{1,0:T(8,128)(2,1)}, u32[]{:S(2)}, u32[]{:S(2)}) collective-permute-start(bf16[1024,256]{1,0:T(8,128)(2,1)} %g0.1), channel_id=1, source_target_pairs={{1,0},{2,1},{3,2},{0,3},{5,4},{6,5},{7,6},{4,7},{9,8},{10,9},{11,1... | collective-permute-start | bytes 1572872 | tf_op jit(solution)/shard_map/ppermute | solution.py:897
  25.0 7.6 %project.1 = (f32[8,256]{1,0:T(8,128)S(1)}, bf16[1792,256]{1,0:T(8,128)(2,1)S(1)}, bf16[2,1792,256]{2,1,0:T(8,128)(2,1)S(1)}, bf16[2,576,256]{2,1,0:T(8,128)(2,1...) custom-call(s32[4]{0:T(128)S(1)} %pad_add_fusion.place, ...), custom_call_target="tpu_custom_call" | custom-call | flops 1000000 | bytes 10000 | tf_op jit(solution)/shard_map/project/pallas_call | solution.py:219
  33.3 2.9 %collective-permute-start.7 = (bf16[2,576,256]{2,1,0:T(8,128)(2,1)}, bf16[2,576,256]{2,1,0:T(8,128)(2,1)}, u32[]{:S(2)}, u32[]{:S(2)}) collective-permute-start(bf16[2,576,256]{2,1,0:T(8,128)(2,1)} %get-tuple-element.75), channel_id=1, source_target_pairs={{0,4},{4,0},{8,12},{12,8},{16,20},{20,16},{24,28},{28,24},{32,36},... | collective-permute-start | bytes 1769480 | tf_op jit(solution)/shard_map/ppermute | solution.py:923
  36.3 3.1 %collective-permute-start.13 = (bf16[1024,256]{1,0:T(8,128)(2,1)}, bf16[1024,256]{1,0:T(8,128)(2,1)S(1)}, u32[]{:S(2)}, u32[]{:S(2)}) collective-permute-start(bf16[1024,256]{1,0:T(8,128)(2,1)} %g0.1), channel_id=1, source_target_pairs={{0,2},{1,3},{2,0},{3,1},{4,6},{5,7},{6,4},{7,5},{8,10},{9,11},{10,... | collective-permute-start | bytes 1572872 | tf_op jit(solution)/shard_map/ppermute | solution.py:910
  39.5 3.6 %forward_inner.1 = (f32[512,256]{1,0:T(8,128)S(1)}, f32[2,8,256]{2,1,0:T(8,128)S(1)}) custom-call(f32[2]{0:T(128)S(1)} %pad_maximum_fusion.bias_ref, bf16[1792,256]{1,0:T(8,128)(2,1)S(1)} %get-tuple-element.77.q, bf16[2,1792,256]{2,1,0:T(8,128)(2,1)S(1)} %get-tuple-element.73.kv), custom_call_target="tpu_custom_call" | custom-call | flops 2500000000 | bytes 10000 | tf_op jit(solution)/shard_map/forward_inner/pallas_call | solution.py:76
  45.0 6.9 %forward_edge.1 = (bf16[1024,256]{1,0:T(8,128)(2,1)S(1)}, f32[2,24,256]{2,1,0:T(8,128)S(1)}, bf16[2,768,256]{2,1,0:T(8,128)(2,1)S(1)}, bf16[2,768,256]{2,1,0:T(8,128)(2,1)S(1)}) custom-call(s32[4]{0:T(128)S(1)} %pad_add_fusion.place, f32[2]{0:T(128)S(1)} %pad_maximum_fusion.bias_ref, bf16[1792,256]{1,0:T(8,128)(2,1)S(1)} %get-tuple-element.77.q, ...), custom_call_target="tpu_custom_call" | custom-call | flops 1000000 | bytes 10000 | tf_op jit(solution)/shard_map/forward_edge/pallas_call | solution.py:76
  58.3 10.7 %edge_backward.1 = (f32[1024,256]{1,0:T(8,128)S(1)}, f32[2,1024,256]{2,1,0:T(8,128)S(1)}, bf16[2,576,256]{2,1,0:T(8,128)(2,1)S(1)}, bf16[2,576,256]{2,1,0:T(8,128)(2,1)S(1)}) custom-call(s32[4]{0:T(128)S(1)} %pad_add_fusion.place, f32[2]{0:T(128)S(1)} %pad_maximum_fusion.bias_ref, f32[2,24,256]{2,1,0:T(8,128)S(1)} %get-tuple-element.91.stats, ...), custom_call_target="tpu_custom_call" | custom-call | flops 1000000 | bytes 10000 | tf_op jit(solution)/shard_map/edge_backward/pallas_call | solution.py:76
  69.7 4.4 %collective-permute-start.15 = (bf16[2,576,256]{2,1,0:T(8,128)(2,1)S(1)}, bf16[2,576,256]{2,1,0:T(8,128)(2,1)S(1)}, u32[]{:S(2)}, u32[]{:S(2)}) collective-permute-start(bf16[2,576,256]{2,1,0:T(8,128)(2,1)S(1)} %get-tuple-element.106), channel_id=1, source_target_pairs={{0,4},{4,0},{8,12},{12,8},{16,20},{20,16},{24,28},{28,24},{32,36},... | collective-permute-start | bytes 1769480 | tf_op jit(solution)/shard_map/ppermute | solution.py:923
  74.0 5.5 %inner_backward.1 = (bf16[1024,256]{1,0:T(8,128)(2,1)S(1)}, f32[2,1024,256]{2,1,0:T(8,128)S(1)}) custom-call(f32[2]{0:T(128)S(1)} %pad_maximum_fusion.bias_ref, f32[2,8,256]{2,1,0:T(8,128)S(1)} %get-tuple-element.88.stats, bf16[1792,256]{1,0:T(8,128)(2,1)S(1)} %get-tuple-element.77.q, bf16[2,1792,256]{2,1,0:T(8,128)(2,1)S(1)} %get-tuple-element.73.kv, ...), custom_call_target="tpu_custom_call" | custom-call | flops 1000000 | bytes 10000 | tf_op jit(solution)/shard_map/inner_backward/pallas_call | solution.py:76
  79.8 2.7 %early_terms.1 = (bf16[1024,256]{1,0:T(8,128)(2,1)S(1)}, bf16[1024,256]{1,0:T(8,128)(2,1)S(1)}) custom-call(bf16[1024,256]{1,0:T(8,128)(2,1)S(1)} %copy-done.4, bf16[1024,256]{1,0:T(8,128)(2,1)} %collective-permute-done.8.g1, bf16[1024,256]{1,0:T(8,128)(2,1)S(1)} %collective-permute-done.13.g2, bf16[1024,256]{1,0:T(8,128)(2,1)} %collective-permute-done.9.g3, ...), custom_call_target="tpu_custom_call" | custom-call | flops 4000000000 | bytes 10000 | tf_op jit(solution)/shard_map/early_terms/pallas_call | solution.py:76
  82.5 3.3 %input_terms.1 = (bf16[1024,512]{1,0:T(8,128)(2,1)S(1)}, bf16[16,256]{1,0:T(8,128)(2,1)S(1)}, bf16[1024,256]{1,0:T(8,128)(2,1)S(1)}, bf16[512,256]{1,0:T(8,128)(...) custom-call(s32[4]{0:T(128)S(1)} %pad_add_fusion.place, ...), custom_call_target="tpu_custom_call" | custom-call | flops 1000000 | bytes 10000 | tf_op jit(solution)/shard_map/input_terms/pallas_call | solution.py:76
  89.1 2.1 %inner_terms.1 = (bf16[512,1024]{1,0:T(8,128)(2,1)S(1)}, bf16[256,1024]{1,0:T(8,128)(2,1)S(1)}, bf16[256,1024]{1,0:T(8,128)(2,1)S(1)}) custom-call(s32[4]{0:T(128)S(1)} %pad_add_fusion.place, bf16[1024,1024]{1,0:T(8,128)(2,1)S(1)} %copy-done, bf16[1024,512]{1,0:T(8,128)(2,1)S(1)} %get-tuple-element.117.d_proj, ...), custom_call_target="tpu_custom_call" | custom-call | flops 1000000 | bytes 10000 | tf_op jit(solution)/shard_map/inner_terms/pallas_call | solution.py:76
  96.3 4.6 %collective-permute-start.23 = (bf16[128,1024]{1,0:T(8,128)(2,1)S(1)}, bf16[128,1024]{1,0:T(8,128)(2,1)S(1)}, u32[]{:S(2)}, u32[]{:S(2)}) collective-permute-start(bf16[128,1024]{1,0:T(8,128)(2,1)S(1)} %get-tuple-element.124), channel_id=1, source_target_pairs={{0,16},{4,68},{8,24},{12,76},{16,0},{20,84},{24,8},{28,92},{32,48}... | collective-permute-start | bytes 786440 | tf_op jit(solution)/shard_map/ppermute | solution.py:880
  102.2 2.5 %collective-permute-start.19 = (bf16[512,256]{1,0:T(8,128)(2,1)S(1)}, bf16[512,256]{1,0:T(8,128)(2,1)S(1)}, u32[]{:S(2)}, u32[]{:S(2)}) collective-permute-start(bf16[512,256]{1,0:T(8,128)(2,1)S(1)} %get-tuple-element.114), channel_id=1, source_target_pairs={{1,0},{2,1},{3,2},{0,3},{5,4},{6,5},{7,6},{4,7},{9,8},{10,9},{11,1... | collective-permute-start | bytes 786440 | tf_op jit(solution)/shard_map/ppermute | solution.py:897
  105.7 2.4 %collective-permute-done.23.c = bf16[128,1024]{1,0:T(8,128)(2,1)S(1)} collective-permute-done((bf16[128,1024]{1,0:T(8,128)(2,1)S(1)}, bf16[128,1024]{1,0:T(8,128)(2,1)S(1)}, u32[]{:S(2)}, u32[]{:S(2)}) %collective-permute-start.23) | collective-permute-done | bytes 262176 | tf_op jit(solution)/shard_map/ppermute | solution.py:880
  108.9 2.8 %collective-permute-start.25 = (bf16[32,1024]{1,0:T(8,128)(2,1)S(1)}, bf16[32,1024]{1,0:T(8,128)(2,1)S(1)}, u32[]{:S(2)}, u32[]{:S(2)}) collective-permute-start(bf16[32,1024]{1,0:T(8,128)(2,1)S(1)} %get-tuple-element.131), channel_id=1, source_target_pairs={{0,32},{4,12},{8,40},{12,20},{16,48},{20,28},{24,56},{28,4},{32,64... | collective-permute-start | bytes 196616 | tf_op jit(solution)/shard_map/ppermute | solution.py:880
  111.7 2.9 %collective-permute-start.26 = (bf16[32,1024]{1,0:T(8,128)(2,1)S(1)}, bf16[32,1024]{1,0:T(8,128)(2,1)S(1)}, u32[]{:S(2)}, u32[]{:S(2)}) collective-permute-start(bf16[32,1024]{1,0:T(8,128)(2,1)S(1)} %get-tuple-element.132), channel_id=1, source_target_pairs={{0,64},{4,20},{8,72},{12,28},{16,80},{20,4},{24,88},{28,12},{32,96... | collective-permute-start | bytes 196616 | tf_op jit(solution)/shard_map/ppermute | solution.py:880
  (72 shorter events, 29.9 us)
Async XLA Ops:
  1.7 11.3 %collective-permute-start.3 = (bf16[512,256]{1,0:T(8,128)(2,1)S(1)}, bf16[512,256]{1,0:T(8,128)(2,1)S(1)}, u32[]{:S(2)}, u32[]{:S(2)}) collective-permute-start(bf16[512,256]{1,0:T(8,128)(2,1)S(1)} %get-tuple-element.138), channel_id=1, source_target_pairs={{0,1},{1,2},{2,3},{3,0},{4,5},{5,6},{6,7},{7,4},{8,9},{9,10},{10,1... | collective-permute-start | bytes 786440 | tf_op jit(solution)/shard_map/ppermute | solution.py:893
  3.8 9.3 %collective-permute-start = (bf16[512,256]{1,0:T(8,128)(2,1)S(1)}, bf16[512,256]{1,0:T(8,128)(2,1)S(1)}, u32[]{:S(2)}, u32[]{:S(2)}) collective-permute-start(bf16[512,256]{1,0:T(8,128)(2,1)S(1)} %get-tuple-element.139), channel_id=1, source_target_pairs={{1,0},{2,1},{3,2},{0,3},{5,4},{6,5},{7,6},{4,7},{9,8},{10,9},{11,1... | collective-permute-start | bytes 786440 | tf_op jit(solution)/shard_map/ppermute | solution.py:897
  6.0 12.6 %collective-permute-start.1 = (bf16[512,256]{1,0:T(8,128)(2,1)S(1)}, bf16[512,256]{1,0:T(8,128)(2,1)S(1)}, u32[]{:S(2)}, u32[]{:S(2)}) collective-permute-start(bf16[512,256]{1,0:T(8,128)(2,1)S(1)} %get-tuple-element.138), channel_id=1, source_target_pairs={{1,0},{2,1},{3,2},{0,3},{5,4},{6,5},{7,6},{4,7},{9,8},{10,9},{11,1... | collective-permute-start | bytes 786440 | tf_op jit(solution)/shard_map/ppermute | solution.py:897
  7.9 10.7 %collective-permute-start.5 = (bf16[512,256]{1,0:T(8,128)(2,1)S(1)}, bf16[512,256]{1,0:T(8,128)(2,1)S(1)}, u32[]{:S(2)}, u32[]{:S(2)}) collective-permute-start(bf16[512,256]{1,0:T(8,128)(2,1)S(1)} %get-tuple-element.139), channel_id=1, source_target_pairs={{0,1},{1,2},{2,3},{3,0},{4,5},{5,6},{6,7},{7,4},{8,9},{9,10},{10,1... | collective-permute-start | bytes 786440 | tf_op jit(solution)/shard_map/ppermute | solution.py:893
  13.0 11.2 %collective-permute-start.4 = (bf16[512,256]{1,0:T(8,128)(2,1)S(1)}, bf16[512,256]{1,0:T(8,128)(2,1)S(1)}, u32[]{:S(2)}, u32[]{:S(2)}) collective-permute-start(bf16[512,256]{1,0:T(8,128)(2,1)S(1)} %collective-permute-done.3.t3b_any), channel_id=1, source_target_pairs={{0,1},{1,2},{2,3},{3,0},{4,5},{5,6},{6,7},{7,4},{8,9},{9,10},{10,1... | collective-permute-start | bytes 786440 | tf_op jit(solution)/shard_map/ppermute | solution.py:893
  13.0 11.9 %collective-permute-start.2 = (bf16[512,256]{1,0:T(8,128)(2,1)S(1)}, bf16[512,256]{1,0:T(8,128)(2,1)}, u32[]{:S(2)}, u32[]{:S(2)}) collective-permute-start(bf16[512,256]{1,0:T(8,128)(2,1)S(1)} %collective-permute-done.t1a_any), channel_id=1, source_target_pairs={{1,0},{2,1},{3,2},{0,3},{5,4},{6,5},{7,6},{4,7},{9,8},{10,9},{11,1... | collective-permute-start | bytes 786440 | tf_op jit(solution)/shard_map/ppermute | solution.py:897
  19.3 20.1 %collective-permute-start.9 = (bf16[1024,256]{1,0:T(8,128)(2,1)}, bf16[1024,256]{1,0:T(8,128)(2,1)}, u32[]{:S(2)}, u32[]{:S(2)}) collective-permute-start(bf16[1024,256]{1,0:T(8,128)(2,1)} %g0.1), channel_id=1, source_target_pairs={{0,1},{1,2},{2,3},{3,0},{4,5},{5,6},{6,7},{7,4},{8,9},{9,10},{10,1... | collective-permute-start | bytes 1572872 | tf_op jit(solution)/shard_map/ppermute | solution.py:893
  21.3 18.2 %collective-permute-start.8 = (bf16[1024,256]{1,0:T(8,128)(2,1)}, bf16[1024,256]{1,0:T(8,128)(2,1)}, u32[]{:S(2)}, u32[]{:S(2)}) collective-permute-start(bf16[1024,256]{1,0:T(8,128)(2,1)} %g0.1), channel_id=1, source_target_pairs={{1,0},{2,1},{3,2},{0,3},{5,4},{6,5},{7,6},{4,7},{9,8},{10,9},{11,1... | collective-permute-start | bytes 1572872 | tf_op jit(solution)/shard_map/ppermute | solution.py:897
  32.6 12.3 %collective-permute-start.6 = (bf16[2,576,256]{2,1,0:T(8,128)(2,1)}, bf16[2,576,256]{2,1,0:T(8,128)(2,1)S(1)}, u32[]{:S(2)}, u32[]{:S(2)}) collective-permute-start(bf16[2,576,256]{2,1,0:T(8,128)(2,1)} %get-tuple-element.74), channel_id=1, source_target_pairs={{4,8},{8,4},{12,16},{16,12},{20,24},{24,20},{28,32},{32,28},{36,40... | collective-permute-start | bytes 1769480 | tf_op jit(solution)/shard_map/ppermute | solution.py:922
  33.3 11.6 %collective-permute-start.7 = (bf16[2,576,256]{2,1,0:T(8,128)(2,1)}, bf16[2,576,256]{2,1,0:T(8,128)(2,1)}, u32[]{:S(2)}, u32[]{:S(2)}) collective-permute-start(bf16[2,576,256]{2,1,0:T(8,128)(2,1)} %get-tuple-element.75), channel_id=1, source_target_pairs={{0,4},{4,0},{8,12},{12,8},{16,20},{20,16},{24,28},{28,24},{32,36},... | collective-permute-start | bytes 1769480 | tf_op jit(solution)/shard_map/ppermute | solution.py:923
  36.3 20.3 %collective-permute-start.13 = (bf16[1024,256]{1,0:T(8,128)(2,1)}, bf16[1024,256]{1,0:T(8,128)(2,1)S(1)}, u32[]{:S(2)}, u32[]{:S(2)}) collective-permute-start(bf16[1024,256]{1,0:T(8,128)(2,1)} %g0.1), channel_id=1, source_target_pairs={{0,2},{1,3},{2,0},{3,1},{4,6},{5,7},{6,4},{7,5},{8,10},{9,11},{10,... | collective-permute-start | bytes 1572872 | tf_op jit(solution)/shard_map/ppermute | solution.py:910
  53.1 26.5 %collective-permute-start.10 = (bf16[1024,256]{1,0:T(8,128)(2,1)S(1)}, bf16[1024,256]{1,0:T(8,128)(2,1)S(1)}, u32[]{:S(2)}, u32[]{:S(2)}) collective-permute-start(bf16[1024,256]{1,0:T(8,128)(2,1)S(1)} %get-tuple-element.85), channel_id=1, source_target_pairs={{0,1},{1,2},{2,3},{3,0},{4,5},{5,6},{6,7},{7,4},{8,9},{9,10},{10,1... | collective-permute-start | bytes 1572872 | tf_op jit(solution)/shard_map/ppermute | solution.py:910
  53.8 25.8 %collective-permute-start.11 = (bf16[1024,256]{1,0:T(8,128)(2,1)S(1)}, bf16[1024,256]{1,0:T(8,128)(2,1)S(1)}, u32[]{:S(2)}, u32[]{:S(2)}) collective-permute-start(bf16[1024,256]{1,0:T(8,128)(2,1)S(1)} %get-tuple-element.86), channel_id=1, source_target_pairs={{0,2},{1,3},{2,0},{3,1},{4,6},{5,7},{6,4},{7,5},{8,10},{9,11},{10,... | collective-permute-start | bytes 1572872 | tf_op jit(solution)/shard_map/ppermute | solution.py:910
  55.6 24.2 %collective-permute-start.12 = (bf16[1024,256]{1,0:T(8,128)(2,1)S(1)}, bf16[1024,256]{1,0:T(8,128)(2,1)S(1)}, u32[]{:S(2)}, u32[]{:S(2)}) collective-permute-start(bf16[1024,256]{1,0:T(8,128)(2,1)S(1)} %get-tuple-element.87), channel_id=1, source_target_pairs={{0,3},{1,0},{2,1},{3,2},{4,7},{5,4},{6,5},{7,6},{8,11},{9,8},{10,9... | collective-permute-start | bytes 1572872 | tf_op jit(solution)/shard_map/ppermute | solution.py:910
  69.0 13.5 %collective-permute-start.14 = (bf16[2,576,256]{2,1,0:T(8,128)(2,1)S(1)}, bf16[2,576,256]{2,1,0:T(8,128)(2,1)S(1)}, u32[]{:S(2)}, u32[]{:S(2)}) collective-permute-start(bf16[2,576,256]{2,1,0:T(8,128)(2,1)S(1)} %get-tuple-element.105), channel_id=1, source_target_pairs={{4,8},{8,4},{12,16},{16,12},{20,24},{24,20},{28,32},{32,28},{36,40... | collective-permute-start | bytes 1769480 | tf_op jit(solution)/shard_map/ppermute | solution.py:922
  69.7 12.8 %collective-permute-start.15 = (bf16[2,576,256]{2,1,0:T(8,128)(2,1)S(1)}, bf16[2,576,256]{2,1,0:T(8,128)(2,1)S(1)}, u32[]{:S(2)}, u32[]{:S(2)}) collective-permute-start(bf16[2,576,256]{2,1,0:T(8,128)(2,1)S(1)} %get-tuple-element.106), channel_id=1, source_target_pairs={{0,4},{4,0},{8,12},{12,8},{16,20},{20,16},{24,28},{28,24},{32,36},... | collective-permute-start | bytes 1769480 | tf_op jit(solution)/shard_map/ppermute | solution.py:923
  85.8 15.2 %collective-permute-start.16 = (bf16[1040,256]{1,0:T(8,128)(2,1)S(1)}, bf16[1040,256]{1,0:T(8,128)(2,1)S(1)}, u32[]{:S(2)}, u32[]{:S(2)}) collective-permute-start(bf16[1040,256]{1,0:T(8,128)(2,1)S(1)} %get-tuple-element.109), channel_id=1, source_target_pairs={{0,1},{1,2},{2,3},{3,0},{4,5},{5,6},{6,7},{7,4},{8,9},{9,10},{10,1... | collective-permute-start | bytes 1597448 | tf_op jit(solution)/shard_map/ppermute | solution.py:893
  87.5 13.7 %collective-permute-start.17 = (bf16[1040,256]{1,0:T(8,128)(2,1)S(1)}, bf16[1040,256]{1,0:T(8,128)(2,1)S(1)}, u32[]{:S(2)}, u32[]{:S(2)}) collective-permute-start(bf16[1040,256]{1,0:T(8,128)(2,1)S(1)} %get-tuple-element.110), channel_id=1, source_target_pairs={{1,0},{2,1},{3,2},{0,3},{5,4},{6,5},{7,6},{4,7},{9,8},{10,9},{11,1... | collective-permute-start | bytes 1597448 | tf_op jit(solution)/shard_map/ppermute | solution.py:897
  94.8 10.9 %collective-permute-start.22 = (bf16[128,1024]{1,0:T(8,128)(2,1)S(1)}, bf16[128,1024]{1,0:T(8,128)(2,1)S(1)}, u32[]{:S(2)}, u32[]{:S(2)}) collective-permute-start(bf16[128,1024]{1,0:T(8,128)(2,1)S(1)} %get-tuple-element.123), channel_id=1, source_target_pairs={{0,8},{4,36},{8,16},{12,44},{16,24},{20,52},{24,0},{28,60},{32,40}... | collective-permute-start | bytes 786440 | tf_op jit(solution)/shard_map/ppermute | solution.py:880
  96.3 11.8 %collective-permute-start.23 = (bf16[128,1024]{1,0:T(8,128)(2,1)S(1)}, bf16[128,1024]{1,0:T(8,128)(2,1)S(1)}, u32[]{:S(2)}, u32[]{:S(2)}) collective-permute-start(bf16[128,1024]{1,0:T(8,128)(2,1)S(1)} %get-tuple-element.124), channel_id=1, source_target_pairs={{0,16},{4,68},{8,24},{12,76},{16,0},{20,84},{24,8},{28,92},{32,48}... | collective-permute-start | bytes 786440 | tf_op jit(solution)/shard_map/ppermute | solution.py:880
  101.0 7.2 %collective-permute-start.24 = (bf16[128,1024]{1,0:T(8,128)(2,1)S(1)}, bf16[128,1024]{1,0:T(8,128)(2,1)S(1)}, u32[]{:S(2)}, u32[]{:S(2)}) collective-permute-start(bf16[128,1024]{1,0:T(8,128)(2,1)S(1)} %get-tuple-element.125), channel_id=1, source_target_pairs={{0,24},{4,100},{8,0},{12,108},{16,8},{20,116},{24,16},{28,124},{32... | collective-permute-start | bytes 786440 | tf_op jit(solution)/shard_map/ppermute | solution.py:880
  101.4 14.6 %collective-permute-start.18 = (bf16[528,256]{1,0:T(8,128)(2,1)S(1)}, bf16[528,256]{1,0:T(8,128)(2,1)S(1)}, u32[]{:S(2)}, u32[]{:S(2)}) collective-permute-start(bf16[528,256]{1,0:T(8,128)(2,1)S(1)} %get-tuple-element.113), channel_id=1, source_target_pairs={{0,1},{1,2},{2,3},{3,0},{4,5},{5,6},{6,7},{7,4},{8,9},{9,10},{10,1... | collective-permute-start | bytes 811016 | tf_op jit(solution)/shard_map/ppermute | solution.py:893
  102.2 13.7 %collective-permute-start.19 = (bf16[512,256]{1,0:T(8,128)(2,1)S(1)}, bf16[512,256]{1,0:T(8,128)(2,1)S(1)}, u32[]{:S(2)}, u32[]{:S(2)}) collective-permute-start(bf16[512,256]{1,0:T(8,128)(2,1)S(1)} %get-tuple-element.114), channel_id=1, source_target_pairs={{1,0},{2,1},{3,2},{0,3},{5,4},{6,5},{7,6},{4,7},{9,8},{10,9},{11,1... | collective-permute-start | bytes 786440 | tf_op jit(solution)/shard_map/ppermute | solution.py:897
  108.9 8.7 %collective-permute-start.25 = (bf16[32,1024]{1,0:T(8,128)(2,1)S(1)}, bf16[32,1024]{1,0:T(8,128)(2,1)S(1)}, u32[]{:S(2)}, u32[]{:S(2)}) collective-permute-start(bf16[32,1024]{1,0:T(8,128)(2,1)S(1)} %get-tuple-element.131), channel_id=1, source_target_pairs={{0,32},{4,12},{8,40},{12,20},{16,48},{20,28},{24,56},{28,4},{32,64... | collective-permute-start | bytes 196616 | tf_op jit(solution)/shard_map/ppermute | solution.py:880
  (14 other events, 72.5 us)

commit v10 on v9

--- a/solution.py
+++ b/solution.py
@@ -669,18 +669,14 @@
 
 
 def input_terms_kernel(
-    place, d_query, d_kv, from_other, from_core, normed, w, d_proj,
-    dots, own, keep_right, keep_left, right, left, dot_rows, w_turned,
+    place, d_query, d_kv, from_other, from_core, normed, w_turned, d_proj,
+    dots, own, keep_right, keep_left, right, left, dot_rows,
 ):
     halo = (place, from_core, from_other)
     width = d_query.shape[1]
     half = spread_matrix(BLOCK // 2, 2, 0.5)
     quarter = spread_matrix(BLOCK // 4, 4, 0.25)
     dot_rows[12:16, :] = jnp.zeros((4, BLOCK), F32)
-    for r in range(MP):
-        for n in range(3):
-            at = slice(r * width, (r + 1) * width)
-            w_turned[block_rows(n), at] = w[at, n * width : (n + 1) * width].T
     for step in range(4):
         rows = block_rows(step)
         grads = [d_query[rows, :]]
@@ -726,7 +722,7 @@
     outputs = [held((rows, 2 * width), BF16), held((DOT_ROWS, width), BF16)]
     lengths = [rows, rows // 2, rows // 2, rows + DOT_ROWS, rows + DOT_ROWS]
     outputs += [held((n, width), BF16) for n in lengths]
-    scratch = [pltpu.VMEM((DOT_ROWS, width), F32), pltpu.VMEM((3 * width, MP * width), BF16)]
+    scratch = [pltpu.VMEM((DOT_ROWS, width), F32)]
     return run(input_terms_kernel, "input_terms", 18, [place], inputs, outputs, scratch)
 
 
@@ -787,23 +783,25 @@
     return run(finish_grad_kernel, "finish_grad", 8, [], inputs, outputs)[0]
 
 
-def early_kernel(g0, g1, g2, g3, attended, normed, d_query, outer, inner):
+def early_kernel(g0, g1, g2, g3, attended, normed, d_query, w, outer, inner, w_turned):
     width = g0.shape[1]
     rows = attended[...]
     for r, share in enumerate((g0, g1, g2, g3)):
         at = slice(r * width, (r + 1) * width)
         outer[at, :] = tn(share[...], rows).astype(BF16)
         inner[at, :] = tn(normed[:, at], d_query[...]).astype(BF16)
-
-
-def early_terms(shares, attended, normed, d_query):
+        for n in range(3):
+            w_turned[block_rows(n), at] = w[at, n * width : (n + 1) * width].T
+
+
+def early_terms(shares, attended, normed, d_query, w):
     width = attended.shape[1]
-    inputs = [*shares, attended, normed, d_query]
-    outputs = [held((MP * width, width), BF16)] * 2
+    inputs = [*shares, attended, normed, d_query, w]
+    outputs = [held((MP * width, width), BF16)] * 2 + [held((3 * width, MP * width), BF16)]
     return run(early_kernel, "early_terms", 14, [], inputs, outputs, (), LARGE)
 
 
-def inner_kernel(place, normed, d_proj, inner, outer, mine, other_low, other_high, rows_held):
+def inner_kernel(place, normed, d_proj, inner, outer, mine, other, rows_held):
     core = place[1]
     width = outer.shape[1]
     for block in range(MP):
@@ -815,27 +813,24 @@
             out = slice((4 * block + n) * 32, (4 * block + n + 1) * 32)
             first = block * width + n * 64
             mine[out, :] = rows_held[pl.ds(pl.multiple_of(first + core * 32, 32), 32), :]
-            other, start = (other_low, 0) if block < 2 else (other_high, 256)
-            other[out.start - start : out.stop - start, :] = rows_held[pl.ds(pl.multiple_of(first + 32 - core * 32, 32), 32), :]
+            other[out, :] = rows_held[pl.ds(pl.multiple_of(first + 32 - core * 32, 32), 32), :]
 
 
 def inner_terms(place, normed, d_proj, inner, outer):
     total = normed.shape[1]
     width = outer.shape[1]
-    outputs = [held((n, 4 * width), BF16) for n in (total // 2, total // 4, total // 4)]
+    outputs = [held((total // 2, 4 * width), BF16)] * 2
     scratch = [pltpu.VMEM((total, 4 * width), BF16)]
     return run(inner_kernel, "inner_terms", 16, [place], [normed, d_proj, inner, outer], outputs, scratch)
 
 
-def pair_sum_kernel(place, mine, got_low, got_high, *outs):
+def pair_sum_kernel(place, mine, got, *outs):
     z, core, x, y = place[0], place[1], place[2], place[3]
     for d, out in enumerate(outs):
         for n in range(4):
             chunk = jnp.where(core == 0, 4 * n + ((x + d) & 3), 4 * ((y + d - z + 4) & 3) + n)
             rows = pl.ds(pl.multiple_of(chunk * 32, 32), 32)
-            half = pl.ds(pl.multiple_of((chunk & 7) * 32, 32), 32)
-            got = jnp.where(chunk < 8, got_low[half, :], got_high[half, :])
-            total = mine[rows, :].astype(F32) + got.astype(F32)
+            total = mine[rows, :].astype(F32) + got[rows, :].astype(F32)
             out[32 * n : 32 * (n + 1), :] = total.astype(BF16)
 
 
@@ -963,7 +958,7 @@
     halo = exchange(to_core, to_other)
     d_query, d_kv = inner_backward(bias, inner_stats, q, kv, d_att, dq_f, d_kv)
     attended = tied(attended, *out_received)
-    outer, inner = early_terms(grad_shares, attended, normed, d_query)
+    outer, inner, w = early_terms(grad_shares, attended, normed, d_query, w)
     d_query = tied(d_query, outer)
     d_proj, dots, own, keep_right, keep_left, right, left = input_terms(
         me, d_query, d_kv, halo, normed, w

time: 120 us -> 121 us (level)
  waiting for transfers between devices: 14.3 us -> 15.8 us
    ppermute x6, waiting for transfers between devices: 5.84 us -> 11.6 us  [to_next(): return lax.ppermute(value, 'mp', [(i, (i + 1) % MP) for i in range(MP)])]
    ppermute x6, waiting for transfers between devices: 3.61 us -> 1.24 us  [sent(): return lax.ppermute(value, 'seq', pairs)]
    ppermute x2 -> x1, waiting for transfers between devices: 2.15 us -> 0.01 us  [sum_over_core(): lax.ppermute(other, 'seq', [(i, i ^ 1) for i in range(32)])]
  transfers between devices with their start and end apart: 28 -> 27, of which waited for: 9 -> 8; matrix products, arithmetic and copies ran while one was open for 0% -> 0% of each run, Pallas kernels for 40% -> 38%
where the time goes in v10:
time: 121 us
  Pallas kernels  51.9 us (43%)
  starting transfers between devices  50 us (41%)
  waiting for transfers between devices  15.8 us (13%)
  local copies, waits for them, and re-layouts  2.52 us (2%)
    pallas_call x16, Pallas kernels, run(): pl.pallas_call(kernel, in_specs=[SCALAR] * len(scalars) + [RESIDENT] * le...  44.2 us
    ppermute x6, starting transfers between devices, sent(): return lax.ppermute(value, 'seq', pairs)  14.3 us
    ppermute x6, starting transfers between devices, to_previous(): return lax.ppermute(value, 'mp', [((i + 1) % MP, i) for i in range(MP)])  13.8 us
    ppermute x6, waiting for transfers between devices, to_next(): return lax.ppermute(value, 'mp', [(i, (i + 1) % MP) for i in range(MP)])  11.6 us
    pallas_call x1, Pallas kernels, project(): pl.pallas_call(project_kernel, in_specs=[SCALAR] + [anywhere] * 10, out_s...  7.65 us
    ppermute x2, starting transfers between devices, exchange(): from_core = lax.ppermute(to_core, 'seq', [(i, i ^ 1) for i in range(count)])  7.25 us
    ppermute x4, starting transfers between devices, turned_by(): return lax.ppermute(value, 'mp', [(i, (i + step) % MP) for i in range(MP)])  6.61 us
    ppermute x6, starting transfers between devices, to_next(): return lax.ppermute(value, 'mp', [(i, (i + 1) % MP) for i in range(MP)])  6.54 us
  transfers between devices with their start and end apart: 27, of which 8 were waited for; matrix products, arithmetic and copies ran while one was open for 0% of the time, Pallas kernels for 38%

profile of v10, /device:TPU:0, one launch (start us, length us, event | category | flops | bytes accessed | tf_op | source)
XLA Modules:
  0.0 121.1 jit_solution(15126645891946578629)
XLA Ops:
  1.7 2.1 %collective-permute-start.3 = (bf16[512,256]{1,0:T(8,128)(2,1)S(1)}, bf16[512,256]{1,0:T(8,128)(2,1)S(1)}, u32[]{:S(2)}, u32[]{:S(2)}) collective-permute-start(bf16[512,256]{1,0:T(8,128)(2,1)S(1)} %get-tuple-element.138), channel_id=1, source_target_pairs={{0,1},{1,2},{2,3},{3,0},{4,5},{5,6},{6,7},{7,4},{8,9},{9,10},{10,1... | collective-permute-start | bytes 786440 | tf_op jit(solution)/shard_map/ppermute | solution.py:888
  3.8 2.2 %collective-permute-start = (bf16[512,256]{1,0:T(8,128)(2,1)S(1)}, bf16[512,256]{1,0:T(8,128)(2,1)S(1)}, u32[]{:S(2)}, u32[]{:S(2)}) collective-permute-start(bf16[512,256]{1,0:T(8,128)(2,1)S(1)} %get-tuple-element.139), channel_id=1, source_target_pairs={{1,0},{2,1},{3,2},{0,3},{5,4},{6,5},{7,6},{4,7},{9,8},{10,9},{11,1... | collective-permute-start | bytes 786440 | tf_op jit(solution)/shard_map/ppermute | solution.py:892
  6.0 1.9 %collective-permute-start.1 = (bf16[512,256]{1,0:T(8,128)(2,1)S(1)}, bf16[512,256]{1,0:T(8,128)(2,1)S(1)}, u32[]{:S(2)}, u32[]{:S(2)}) collective-permute-start(bf16[512,256]{1,0:T(8,128)(2,1)S(1)} %get-tuple-element.138), channel_id=1, source_target_pairs={{1,0},{2,1},{3,2},{0,3},{5,4},{6,5},{7,6},{4,7},{9,8},{10,9},{11,1... | collective-permute-start | bytes 786440 | tf_op jit(solution)/shard_map/ppermute | solution.py:892
  8.0 5.0 %collective-permute-done.3.t3b_any = bf16[512,256]{1,0:T(8,128)(2,1)S(1)} collective-permute-done((bf16[512,256]{1,0:T(8,128)(2,1)S(1)}, bf16[512,256]{1,0:T(8,128)(2,1)S(1)}, u32[]{:S(2)}, u32[]{:S(2)}) %collective-permute-start.3) | collective-permute-done | bytes 262176 | tf_op jit(solution)/shard_map/ppermute | solution.py:888
  13.0 3.3 %collective-permute-start.2 = (bf16[512,256]{1,0:T(8,128)(2,1)S(1)}, bf16[512,256]{1,0:T(8,128)(2,1)}, u32[]{:S(2)}, u32[]{:S(2)}) collective-permute-start(bf16[512,256]{1,0:T(8,128)(2,1)S(1)} %collective-permute-done.t1a_any), channel_id=1, source_target_pairs={{1,0},{2,1},{3,2},{0,3},{5,4},{6,5},{7,6},{4,7},{9,8},{10,9},{11,1... | collective-permute-start | bytes 786440 | tf_op jit(solution)/shard_map/ppermute | solution.py:892
  16.4 2.2 %collective-permute-done.1.t1b_any = bf16[512,256]{1,0:T(8,128)(2,1)S(1)} collective-permute-done((bf16[512,256]{1,0:T(8,128)(2,1)S(1)}, bf16[512,256]{1,0:T(8,128)(2,1)S(1)}, u32[]{:S(2)}, u32[]{:S(2)}) %collective-permute-start.1) | collective-permute-done | bytes 262176 | tf_op jit(solution)/shard_map/ppermute | solution.py:892
  19.3 1.9 %collective-permute-start.9 = (bf16[1024,256]{1,0:T(8,128)(2,1)}, bf16[1024,256]{1,0:T(8,128)(2,1)}, u32[]{:S(2)}, u32[]{:S(2)}) collective-permute-start(bf16[1024,256]{1,0:T(8,128)(2,1)} %g0.1), channel_id=1, source_target_pairs={{0,1},{1,2},{2,3},{3,0},{4,5},{5,6},{6,7},{7,4},{8,9},{9,10},{10,1... | collective-permute-start | bytes 1572872 | tf_op jit(solution)/shard_map/ppermute | solution.py:888
  21.3 2.2 %collective-permute-start.8 = (bf16[1024,256]{1,0:T(8,128)(2,1)}, bf16[1024,256]{1,0:T(8,128)(2,1)}, u32[]{:S(2)}, u32[]{:S(2)}) collective-permute-start(bf16[1024,256]{1,0:T(8,128)(2,1)} %g0.1), channel_id=1, source_target_pairs={{1,0},{2,1},{3,2},{0,3},{5,4},{6,5},{7,6},{4,7},{9,8},{10,9},{11,1... | collective-permute-start | bytes 1572872 | tf_op jit(solution)/shard_map/ppermute | solution.py:892
  25.0 7.6 %project.1 = (f32[8,256]{1,0:T(8,128)S(1)}, bf16[1792,256]{1,0:T(8,128)(2,1)S(1)}, bf16[2,1792,256]{2,1,0:T(8,128)(2,1)S(1)}, bf16[2,576,256]{2,1,0:T(8,128)(2,1...) custom-call(s32[4]{0:T(128)S(1)} %pad_add_fusion.place, ...), custom_call_target="tpu_custom_call" | custom-call | flops 1000000 | bytes 10000 | tf_op jit(solution)/shard_map/project/pallas_call | solution.py:219
  33.4 2.9 %collective-permute-start.7 = (bf16[2,576,256]{2,1,0:T(8,128)(2,1)}, bf16[2,576,256]{2,1,0:T(8,128)(2,1)}, u32[]{:S(2)}, u32[]{:S(2)}) collective-permute-start(bf16[2,576,256]{2,1,0:T(8,128)(2,1)} %get-tuple-element.75), channel_id=1, source_target_pairs={{0,4},{4,0},{8,12},{12,8},{16,20},{20,16},{24,28},{28,24},{32,36},... | collective-permute-start | bytes 1769480 | tf_op jit(solution)/shard_map/ppermute | solution.py:918
  36.3 3.1 %collective-permute-start.13 = (bf16[1024,256]{1,0:T(8,128)(2,1)}, bf16[1024,256]{1,0:T(8,128)(2,1)S(1)}, u32[]{:S(2)}, u32[]{:S(2)}) collective-permute-start(bf16[1024,256]{1,0:T(8,128)(2,1)} %g0.1), channel_id=1, source_target_pairs={{0,2},{1,3},{2,0},{3,1},{4,6},{5,7},{6,4},{7,5},{8,10},{9,11},{10,... | collective-permute-start | bytes 1572872 | tf_op jit(solution)/shard_map/ppermute | solution.py:905
  39.5 3.6 %forward_inner.1 = (f32[512,256]{1,0:T(8,128)S(1)}, f32[2,8,256]{2,1,0:T(8,128)S(1)}) custom-call(f32[2]{0:T(128)S(1)} %pad_maximum_fusion.bias_ref, bf16[1792,256]{1,0:T(8,128)(2,1)S(1)} %get-tuple-element.77.q, bf16[2,1792,256]{2,1,0:T(8,128)(2,1)S(1)} %get-tuple-element.73.kv), custom_call_target="tpu_custom_call" | custom-call | flops 2500000000 | bytes 10000 | tf_op jit(solution)/shard_map/forward_inner/pallas_call | solution.py:76
  45.0 6.7 %forward_edge.1 = (bf16[1024,256]{1,0:T(8,128)(2,1)S(1)}, f32[2,24,256]{2,1,0:T(8,128)S(1)}, bf16[2,768,256]{2,1,0:T(8,128)(2,1)S(1)}, bf16[2,768,256]{2,1,0:T(8,128)(2,1)S(1)}) custom-call(s32[4]{0:T(128)S(1)} %pad_add_fusion.place, f32[2]{0:T(128)S(1)} %pad_maximum_fusion.bias_ref, bf16[1792,256]{1,0:T(8,128)(2,1)S(1)} %get-tuple-element.77.q, ...), custom_call_target="tpu_custom_call" | custom-call | flops 1000000 | bytes 10000 | tf_op jit(solution)/shard_map/forward_edge/pallas_call | solution.py:76
  58.2 10.4 %edge_backward.1 = (f32[1024,256]{1,0:T(8,128)S(1)}, f32[2,1024,256]{2,1,0:T(8,128)S(1)}, bf16[2,576,256]{2,1,0:T(8,128)(2,1)S(1)}, bf16[2,576,256]{2,1,0:T(8,128)(2,1)S(1)}) custom-call(s32[4]{0:T(128)S(1)} %pad_add_fusion.place, f32[2]{0:T(128)S(1)} %pad_maximum_fusion.bias_ref, f32[2,24,256]{2,1,0:T(8,128)S(1)} %get-tuple-element.91.stats, ...), custom_call_target="tpu_custom_call" | custom-call | flops 1000000 | bytes 10000 | tf_op jit(solution)/shard_map/edge_backward/pallas_call | solution.py:76
  69.3 4.4 %collective-permute-start.15 = (bf16[2,576,256]{2,1,0:T(8,128)(2,1)S(1)}, bf16[2,576,256]{2,1,0:T(8,128)(2,1)S(1)}, u32[]{:S(2)}, u32[]{:S(2)}) collective-permute-start(bf16[2,576,256]{2,1,0:T(8,128)(2,1)S(1)} %get-tuple-element.107), channel_id=1, source_target_pairs={{0,4},{4,0},{8,12},{12,8},{16,20},{20,16},{24,28},{28,24},{32,36},... | collective-permute-start | bytes 1769480 | tf_op jit(solution)/shard_map/ppermute | solution.py:918
  73.6 5.5 %inner_backward.1 = (bf16[1024,256]{1,0:T(8,128)(2,1)S(1)}, f32[2,1024,256]{2,1,0:T(8,128)S(1)}) custom-call(f32[2]{0:T(128)S(1)} %pad_maximum_fusion.bias_ref, f32[2,8,256]{2,1,0:T(8,128)S(1)} %get-tuple-element.88.stats, bf16[1792,256]{1,0:T(8,128)(2,1)S(1)} %get-tuple-element.77.q, bf16[2,1792,256]{2,1,0:T(8,128)(2,1)S(1)} %get-tuple-element.73.kv, ...), custom_call_target="tpu_custom_call" | custom-call | flops 1000000 | bytes 10000 | tf_op jit(solution)/shard_map/inner_backward/pallas_call | solution.py:76
  79.7 2.8 %early_terms.1 = (bf16[1024,256]{1,0:T(8,128)(2,1)S(1)}, bf16[1024,256]{1,0:T(8,128)(2,1)S(1)}, bf16[768,1024]{1,0:T(8,128)(2,1)S(1)}) custom-call(bf16[1024,256]{1,0:T(8,128)(2,1)S(1)} %copy-done.3, bf16[1024,256]{1,0:T(8,128)(2,1)} %collective-permute-done.8.g1, bf16[1024,256]{1,0:T(8,128)(2,1)S(1)} %collective-permute-done.13.g2, ...), custom_call_target="tpu_custom_call" | custom-call | flops 4000000000 | bytes 10000 | tf_op jit(solution)/shard_map/early_terms/pallas_call | solution.py:76
  82.5 3.2 %input_terms.1 = (bf16[1024,512]{1,0:T(8,128)(2,1)S(1)}, bf16[16,256]{1,0:T(8,128)(2,1)S(1)}, bf16[1024,256]{1,0:T(8,128)(2,1)S(1)}, bf16[512,256]{1,0:T(8,128)(...) custom-call(s32[4]{0:T(128)S(1)} %pad_add_fusion.place, ...), custom_call_target="tpu_custom_call" | custom-call | flops 1000000 | bytes 10000 | tf_op jit(solution)/shard_map/input_terms/pallas_call | solution.py:76
  85.8 2.1 %inner_terms.1 = (bf16[512,1024]{1,0:T(8,128)(2,1)S(1)}, bf16[512,1024]{1,0:T(8,128)(2,1)S(1)}) custom-call(s32[4]{0:T(128)S(1)} %pad_add_fusion.place, bf16[1024,1024]{1,0:T(8,128)(2,1)S(1)} %copy-done, bf16[1024,512]{1,0:T(8,128)(2,1)S(1)} %get-tuple-element.118.d_proj, bf16[1024,256]{1,0:T(8,128)(2,1)S(1)} %get-tuple-element.119.inner, ...), custom_call_target="tpu_custom_call" | custom-call | flops 1000000 | bytes 10000 | tf_op jit(solution)/shard_map/inner_terms/pallas_call | solution.py:76
  93.7 4.3 %collective-permute-start.22 = (bf16[128,1024]{1,0:T(8,128)(2,1)S(1)}, bf16[128,1024]{1,0:T(8,128)(2,1)S(1)}, u32[]{:S(2)}, u32[]{:S(2)}) collective-permute-start(bf16[128,1024]{1,0:T(8,128)(2,1)S(1)} %get-tuple-element.124), channel_id=1, source_target_pairs={{0,16},{4,68},{8,24},{12,76},{16,0},{20,84},{24,8},{28,92},{32,48}... | collective-permute-start | bytes 786440 | tf_op jit(solution)/shard_map/ppermute | solution.py:875
  97.9 5.8 %collective-permute-done.16.l1 = bf16[1040,256]{1,0:T(8,128)(2,1)S(1)} collective-permute-done((bf16[1040,256]{1,0:T(8,128)(2,1)S(1)}, bf16[1040,256]{1,0:T(8,128)(2,1)S(1)}, u32[]{:S(2)}, u32[]{:S(2)}) %collective-permute-start.16) | collective-permute-done | bytes 532512 | tf_op jit(solution)/shard_map/ppermute | solution.py:888
  104.7 2.5 %collective-permute-start.19 = (bf16[512,256]{1,0:T(8,128)(2,1)S(1)}, bf16[512,256]{1,0:T(8,128)(2,1)S(1)}, u32[]{:S(2)}, u32[]{:S(2)}) collective-permute-start(bf16[512,256]{1,0:T(8,128)(2,1)S(1)} %get-tuple-element.115), channel_id=1, source_target_pairs={{1,0},{2,1},{3,2},{0,3},{5,4},{6,5},{7,6},{4,7},{9,8},{10,9},{11,1... | collective-permute-start | bytes 786440 | tf_op jit(solution)/shard_map/ppermute | solution.py:892
  109.1 4.2 %collective-permute-start.24 = (bf16[32,1024]{1,0:T(8,128)(2,1)S(1)}, bf16[32,1024]{1,0:T(8,128)(2,1)S(1)}, u32[]{:S(2)}, u32[]{:S(2)}) collective-permute-start(bf16[32,1024]{1,0:T(8,128)(2,1)S(1)} %get-tuple-element.131), channel_id=1, source_target_pairs={{0,32},{4,12},{8,40},{12,20},{16,48},{20,28},{24,56},{28,4},{32,64... | collective-permute-start | bytes 196616 | tf_op jit(solution)/shard_map/ppermute | solution.py:875
  113.3 2.9 %collective-permute-start.25 = (bf16[32,1024]{1,0:T(8,128)(2,1)S(1)}, bf16[32,1024]{1,0:T(8,128)(2,1)S(1)}, u32[]{:S(2)}, u32[]{:S(2)}) collective-permute-start(bf16[32,1024]{1,0:T(8,128)(2,1)S(1)} %get-tuple-element.132), channel_id=1, source_target_pairs={{0,64},{4,20},{8,72},{12,28},{16,80},{20,4},{24,88},{28,12},{32,96... | collective-permute-start | bytes 196616 | tf_op jit(solution)/shard_map/ppermute | solution.py:875
  (70 shorter events, 27.4 us)
Async XLA Ops:
  1.7 11.3 %collective-permute-start.3 = (bf16[512,256]{1,0:T(8,128)(2,1)S(1)}, bf16[512,256]{1,0:T(8,128)(2,1)S(1)}, u32[]{:S(2)}, u32[]{:S(2)}) collective-permute-start(bf16[512,256]{1,0:T(8,128)(2,1)S(1)} %get-tuple-element.138), channel_id=1, source_target_pairs={{0,1},{1,2},{2,3},{3,0},{4,5},{5,6},{6,7},{7,4},{8,9},{9,10},{10,1... | collective-permute-start | bytes 786440 | tf_op jit(solution)/shard_map/ppermute | solution.py:888
  3.8 9.3 %collective-permute-start = (bf16[512,256]{1,0:T(8,128)(2,1)S(1)}, bf16[512,256]{1,0:T(8,128)(2,1)S(1)}, u32[]{:S(2)}, u32[]{:S(2)}) collective-permute-start(bf16[512,256]{1,0:T(8,128)(2,1)S(1)} %get-tuple-element.139), channel_id=1, source_target_pairs={{1,0},{2,1},{3,2},{0,3},{5,4},{6,5},{7,6},{4,7},{9,8},{10,9},{11,1... | collective-permute-start | bytes 786440 | tf_op jit(solution)/shard_map/ppermute | solution.py:892
  6.0 12.6 %collective-permute-start.1 = (bf16[512,256]{1,0:T(8,128)(2,1)S(1)}, bf16[512,256]{1,0:T(8,128)(2,1)S(1)}, u32[]{:S(2)}, u32[]{:S(2)}) collective-permute-start(bf16[512,256]{1,0:T(8,128)(2,1)S(1)} %get-tuple-element.138), channel_id=1, source_target_pairs={{1,0},{2,1},{3,2},{0,3},{5,4},{6,5},{7,6},{4,7},{9,8},{10,9},{11,1... | collective-permute-start | bytes 786440 | tf_op jit(solution)/shard_map/ppermute | solution.py:892
  7.9 10.7 %collective-permute-start.5 = (bf16[512,256]{1,0:T(8,128)(2,1)S(1)}, bf16[512,256]{1,0:T(8,128)(2,1)S(1)}, u32[]{:S(2)}, u32[]{:S(2)}) collective-permute-start(bf16[512,256]{1,0:T(8,128)(2,1)S(1)} %get-tuple-element.139), channel_id=1, source_target_pairs={{0,1},{1,2},{2,3},{3,0},{4,5},{5,6},{6,7},{7,4},{8,9},{9,10},{10,1... | collective-permute-start | bytes 786440 | tf_op jit(solution)/shard_map/ppermute | solution.py:888
  13.0 11.2 %collective-permute-start.4 = (bf16[512,256]{1,0:T(8,128)(2,1)S(1)}, bf16[512,256]{1,0:T(8,128)(2,1)S(1)}, u32[]{:S(2)}, u32[]{:S(2)}) collective-permute-start(bf16[512,256]{1,0:T(8,128)(2,1)S(1)} %collective-permute-done.3.t3b_any), channel_id=1, source_target_pairs={{0,1},{1,2},{2,3},{3,0},{4,5},{5,6},{6,7},{7,4},{8,9},{9,10},{10,1... | collective-permute-start | bytes 786440 | tf_op jit(solution)/shard_map/ppermute | solution.py:888
  13.0 11.9 %collective-permute-start.2 = (bf16[512,256]{1,0:T(8,128)(2,1)S(1)}, bf16[512,256]{1,0:T(8,128)(2,1)}, u32[]{:S(2)}, u32[]{:S(2)}) collective-permute-start(bf16[512,256]{1,0:T(8,128)(2,1)S(1)} %collective-permute-done.t1a_any), channel_id=1, source_target_pairs={{1,0},{2,1},{3,2},{0,3},{5,4},{6,5},{7,6},{4,7},{9,8},{10,9},{11,1... | collective-permute-start | bytes 786440 | tf_op jit(solution)/shard_map/ppermute | solution.py:892
  19.3 20.1 %collective-permute-start.9 = (bf16[1024,256]{1,0:T(8,128)(2,1)}, bf16[1024,256]{1,0:T(8,128)(2,1)}, u32[]{:S(2)}, u32[]{:S(2)}) collective-permute-start(bf16[1024,256]{1,0:T(8,128)(2,1)} %g0.1), channel_id=1, source_target_pairs={{0,1},{1,2},{2,3},{3,0},{4,5},{5,6},{6,7},{7,4},{8,9},{9,10},{10,1... | collective-permute-start | bytes 1572872 | tf_op jit(solution)/shard_map/ppermute | solution.py:888
  21.3 18.2 %collective-permute-start.8 = (bf16[1024,256]{1,0:T(8,128)(2,1)}, bf16[1024,256]{1,0:T(8,128)(2,1)}, u32[]{:S(2)}, u32[]{:S(2)}) collective-permute-start(bf16[1024,256]{1,0:T(8,128)(2,1)} %g0.1), channel_id=1, source_target_pairs={{1,0},{2,1},{3,2},{0,3},{5,4},{6,5},{7,6},{4,7},{9,8},{10,9},{11,1... | collective-permute-start | bytes 1572872 | tf_op jit(solution)/shard_map/ppermute | solution.py:892
  32.6 12.3 %collective-permute-start.6 = (bf16[2,576,256]{2,1,0:T(8,128)(2,1)}, bf16[2,576,256]{2,1,0:T(8,128)(2,1)S(1)}, u32[]{:S(2)}, u32[]{:S(2)}) collective-permute-start(bf16[2,576,256]{2,1,0:T(8,128)(2,1)} %get-tuple-element.74), channel_id=1, source_target_pairs={{4,8},{8,4},{12,16},{16,12},{20,24},{24,20},{28,32},{32,28},{36,40... | collective-permute-start | bytes 1769480 | tf_op jit(solution)/shard_map/ppermute | solution.py:917
  33.4 11.6 %collective-permute-start.7 = (bf16[2,576,256]{2,1,0:T(8,128)(2,1)}, bf16[2,576,256]{2,1,0:T(8,128)(2,1)}, u32[]{:S(2)}, u32[]{:S(2)}) collective-permute-start(bf16[2,576,256]{2,1,0:T(8,128)(2,1)} %get-tuple-element.75), channel_id=1, source_target_pairs={{0,4},{4,0},{8,12},{12,8},{16,20},{20,16},{24,28},{28,24},{32,36},... | collective-permute-start | bytes 1769480 | tf_op jit(solution)/shard_map/ppermute | solution.py:918
  36.3 20.2 %collective-permute-start.13 = (bf16[1024,256]{1,0:T(8,128)(2,1)}, bf16[1024,256]{1,0:T(8,128)(2,1)S(1)}, u32[]{:S(2)}, u32[]{:S(2)}) collective-permute-start(bf16[1024,256]{1,0:T(8,128)(2,1)} %g0.1), channel_id=1, source_target_pairs={{0,2},{1,3},{2,0},{3,1},{4,6},{5,7},{6,4},{7,5},{8,10},{9,11},{10,... | collective-permute-start | bytes 1572872 | tf_op jit(solution)/shard_map/ppermute | solution.py:905
  53.0 26.1 %collective-permute-start.10 = (bf16[1024,256]{1,0:T(8,128)(2,1)S(1)}, bf16[1024,256]{1,0:T(8,128)(2,1)S(1)}, u32[]{:S(2)}, u32[]{:S(2)}) collective-permute-start(bf16[1024,256]{1,0:T(8,128)(2,1)S(1)} %get-tuple-element.85), channel_id=1, source_target_pairs={{0,1},{1,2},{2,3},{3,0},{4,5},{5,6},{6,7},{7,4},{8,9},{9,10},{10,1... | collective-permute-start | bytes 1572872 | tf_op jit(solution)/shard_map/ppermute | solution.py:905
  53.7 25.8 %collective-permute-start.11 = (bf16[1024,256]{1,0:T(8,128)(2,1)S(1)}, bf16[1024,256]{1,0:T(8,128)(2,1)S(1)}, u32[]{:S(2)}, u32[]{:S(2)}) collective-permute-start(bf16[1024,256]{1,0:T(8,128)(2,1)S(1)} %get-tuple-element.86), channel_id=1, source_target_pairs={{0,2},{1,3},{2,0},{3,1},{4,6},{5,7},{6,4},{7,5},{8,10},{9,11},{10,... | collective-permute-start | bytes 1572872 | tf_op jit(solution)/shard_map/ppermute | solution.py:905
  55.5 24.2 %collective-permute-start.12 = (bf16[1024,256]{1,0:T(8,128)(2,1)S(1)}, bf16[1024,256]{1,0:T(8,128)(2,1)S(1)}, u32[]{:S(2)}, u32[]{:S(2)}) collective-permute-start(bf16[1024,256]{1,0:T(8,128)(2,1)S(1)} %get-tuple-element.87), channel_id=1, source_target_pairs={{0,3},{1,0},{2,1},{3,2},{4,7},{5,4},{6,5},{7,6},{8,11},{9,8},{10,9... | collective-permute-start | bytes 1572872 | tf_op jit(solution)/shard_map/ppermute | solution.py:905
  68.6 14.0 %collective-permute-start.14 = (bf16[2,576,256]{2,1,0:T(8,128)(2,1)S(1)}, bf16[2,576,256]{2,1,0:T(8,128)(2,1)S(1)}, u32[]{:S(2)}, u32[]{:S(2)}) collective-permute-start(bf16[2,576,256]{2,1,0:T(8,128)(2,1)S(1)} %get-tuple-element.106), channel_id=1, source_target_pairs={{4,8},{8,4},{12,16},{16,12},{20,24},{24,20},{28,32},{32,28},{36,40... | collective-permute-start | bytes 1769480 | tf_op jit(solution)/shard_map/ppermute | solution.py:917
  69.3 13.3 %collective-permute-start.15 = (bf16[2,576,256]{2,1,0:T(8,128)(2,1)S(1)}, bf16[2,576,256]{2,1,0:T(8,128)(2,1)S(1)}, u32[]{:S(2)}, u32[]{:S(2)}) collective-permute-start(bf16[2,576,256]{2,1,0:T(8,128)(2,1)S(1)} %get-tuple-element.107), channel_id=1, source_target_pairs={{0,4},{4,0},{8,12},{12,8},{16,20},{20,16},{24,28},{28,24},{32,36},... | collective-permute-start | bytes 1769480 | tf_op jit(solution)/shard_map/ppermute | solution.py:918
  88.0 15.7 %collective-permute-start.16 = (bf16[1040,256]{1,0:T(8,128)(2,1)S(1)}, bf16[1040,256]{1,0:T(8,128)(2,1)S(1)}, u32[]{:S(2)}, u32[]{:S(2)}) collective-permute-start(bf16[1040,256]{1,0:T(8,128)(2,1)S(1)} %get-tuple-element.110), channel_id=1, source_target_pairs={{0,1},{1,2},{2,3},{3,0},{4,5},{5,6},{6,7},{7,4},{8,9},{9,10},{10,1... | collective-permute-start | bytes 1597448 | tf_op jit(solution)/shard_map/ppermute | solution.py:888
  89.6 14.2 %collective-permute-start.17 = (bf16[1040,256]{1,0:T(8,128)(2,1)S(1)}, bf16[1040,256]{1,0:T(8,128)(2,1)S(1)}, u32[]{:S(2)}, u32[]{:S(2)}) collective-permute-start(bf16[1040,256]{1,0:T(8,128)(2,1)S(1)} %get-tuple-element.111), channel_id=1, source_target_pairs={{1,0},{2,1},{3,2},{0,3},{5,4},{6,5},{7,6},{4,7},{9,8},{10,9},{11,1... | collective-permute-start | bytes 1597448 | tf_op jit(solution)/shard_map/ppermute | solution.py:892
  92.1 16.2 %collective-permute-start.21 = (bf16[128,1024]{1,0:T(8,128)(2,1)S(1)}, bf16[128,1024]{1,0:T(8,128)(2,1)S(1)}, u32[]{:S(2)}, u32[]{:S(2)}) collective-permute-start(bf16[128,1024]{1,0:T(8,128)(2,1)S(1)} %get-tuple-element.123), channel_id=1, source_target_pairs={{0,8},{4,36},{8,16},{12,44},{16,24},{20,52},{24,0},{28,60},{32,40}... | collective-permute-start | bytes 786440 | tf_op jit(solution)/shard_map/ppermute | solution.py:875
  93.7 14.7 %collective-permute-start.22 = (bf16[128,1024]{1,0:T(8,128)(2,1)S(1)}, bf16[128,1024]{1,0:T(8,128)(2,1)S(1)}, u32[]{:S(2)}, u32[]{:S(2)}) collective-permute-start(bf16[128,1024]{1,0:T(8,128)(2,1)S(1)} %get-tuple-element.124), channel_id=1, source_target_pairs={{0,16},{4,68},{8,24},{12,76},{16,0},{20,84},{24,8},{28,92},{32,48}... | collective-permute-start | bytes 786440 | tf_op jit(solution)/shard_map/ppermute | solution.py:875
  97.9 10.4 %collective-permute-start.23 = (bf16[128,1024]{1,0:T(8,128)(2,1)S(1)}, bf16[128,1024]{1,0:T(8,128)(2,1)S(1)}, u32[]{:S(2)}, u32[]{:S(2)}) collective-permute-start(bf16[128,1024]{1,0:T(8,128)(2,1)S(1)} %get-tuple-element.125), channel_id=1, source_target_pairs={{0,24},{4,100},{8,0},{12,108},{16,8},{20,116},{24,16},{28,124},{32... | collective-permute-start | bytes 786440 | tf_op jit(solution)/shard_map/ppermute | solution.py:875
  104.0 13.6 %collective-permute-start.18 = (bf16[528,256]{1,0:T(8,128)(2,1)S(1)}, bf16[528,256]{1,0:T(8,128)(2,1)S(1)}, u32[]{:S(2)}, u32[]{:S(2)}) collective-permute-start(bf16[528,256]{1,0:T(8,128)(2,1)S(1)} %get-tuple-element.114), channel_id=1, source_target_pairs={{0,1},{1,2},{2,3},{3,0},{4,5},{5,6},{6,7},{7,4},{8,9},{9,10},{10,1... | collective-permute-start | bytes 811016 | tf_op jit(solution)/shard_map/ppermute | solution.py:888
  104.7 12.8 %collective-permute-start.19 = (bf16[512,256]{1,0:T(8,128)(2,1)S(1)}, bf16[512,256]{1,0:T(8,128)(2,1)S(1)}, u32[]{:S(2)}, u32[]{:S(2)}) collective-permute-start(bf16[512,256]{1,0:T(8,128)(2,1)S(1)} %get-tuple-element.115), channel_id=1, source_target_pairs={{1,0},{2,1},{3,2},{0,3},{5,4},{6,5},{7,6},{4,7},{9,8},{10,9},{11,1... | collective-permute-start | bytes 786440 | tf_op jit(solution)/shard_map/ppermute | solution.py:892
  109.1 10.1 %collective-permute-start.24 = (bf16[32,1024]{1,0:T(8,128)(2,1)S(1)}, bf16[32,1024]{1,0:T(8,128)(2,1)S(1)}, u32[]{:S(2)}, u32[]{:S(2)}) collective-permute-start(bf16[32,1024]{1,0:T(8,128)(2,1)S(1)} %get-tuple-element.131), channel_id=1, source_target_pairs={{0,32},{4,12},{8,40},{12,20},{16,48},{20,28},{24,56},{28,4},{32,64... | collective-permute-start | bytes 196616 | tf_op jit(solution)/shard_map/ppermute | solution.py:875
  (13 other events, 73.9 us)

commit v11 on v9

--- a/solution.py
+++ b/solution.py
@@ -668,9 +668,21 @@
     return run(out_terms_kernel, "out_terms", 8, [place], [attended, w_out], outputs)
 
 
+def by_partner(place, sent, to_a, to_b):
+    odd = place[0] & 1
+    to_a[...] = sent[odd]
+    to_b[...] = sent[1 - odd]
+
+
+def from_side(place, from_a, from_b, before, rows):
+    odd = place[0] & 1
+    one, other = from_a[rows, :], from_b[rows, :]
+    return jnp.where(odd == 1, one, other) if before else jnp.where(odd == 1, other, one)
+
+
 def input_terms_kernel(
     place, d_query, d_kv, from_other, from_core, normed, w, d_proj,
-    dots, own, keep_right, keep_left, right, left, dot_rows, w_turned,
+    dots, own, keep_right, keep_left, to_a, to_b, dot_rows, w_turned, sent,
 ):
     halo = (place, from_core, from_other)
     width = d_query.shape[1]
@@ -708,7 +720,7 @@
             terms.append(term)
             part = term.astype(F32) * normed[rows, r * width : (r + 1) * width].astype(F32)
             dot = part if dot is None else dot + part
-        store_terms(step, terms, own, keep_right, keep_left, right, left)
+        store_terms(step, terms, own, keep_right, keep_left, sent.at[0], sent.at[1])
         dot = as_row(jnp.sum(dot, axis=1, keepdims=True))
         first = dot.astype(BF16).astype(F32)
         second = (dot - first).astype(BF16).astype(F32)
@@ -716,8 +728,9 @@
             dot_rows[4 * n + step : 4 * n + step + 1, :] = piece
     pieces = dot_rows[...].astype(BF16)
     dots[...] = pieces
-    right[4 * BLOCK :, :] = pieces
-    left[4 * BLOCK :, :] = pieces
+    for side in range(2):
+        sent[side, 4 * BLOCK :, :] = pieces
+    by_partner(place, sent, to_a, to_b)
 
 
 def input_terms(place, d_query, d_kv, halo, normed, w):
@@ -727,6 +740,7 @@
     lengths = [rows, rows // 2, rows // 2, rows + DOT_ROWS, rows + DOT_ROWS]
     outputs += [held((n, width), BF16) for n in lengths]
     scratch = [pltpu.VMEM((DOT_ROWS, width), F32), pltpu.VMEM((3 * width, MP * width), BF16)]
+    scratch += [pltpu.VMEM((2, rows + DOT_ROWS, width), BF16)]
     return run(input_terms_kernel, "input_terms", 18, [place], inputs, outputs, scratch)
 
 
@@ -748,43 +762,45 @@
     return run(finish_out_kernel, "finish_out", 8, [], [own, *received], outputs)[0]
 
 
-def relay_kernel(keep_right, keep_left, l1, r1, onward_right, onward_left):
+def relay_kernel(place, keep_right, keep_left, from_a, from_b, to_a, to_b, sent):
     half = keep_right.shape[0]
-    passed = l1[half : 2 * half, :].astype(F32)
-    onward_right[0:half, :] = (keep_right[...].astype(F32) + passed).astype(BF16)
-    passed = r1[half : 2 * half, :].astype(F32)
-    onward_left[...] = (keep_left[...].astype(F32) + passed).astype(BF16)
-    if onward_right.shape[0] > half:
-        onward_right[half:, :] = l1[2 * half :, :]
-
-
-def relay(keep_right, keep_left, l1, r1):
+    terms, dots = slice(half, 2 * half), slice(2 * half, 2 * half + DOT_ROWS)
+    for side, keep in enumerate((keep_right, keep_left)):
+        passed = from_side(place, from_a, from_b, side == 0, terms).astype(F32)
+        sent[side, 0:half, :] = (keep[...].astype(F32) + passed).astype(BF16)
+        sent[side, half:, :] = from_side(place, from_a, from_b, side == 0, dots)
+    by_partner(place, sent, to_a, to_b)
+
+
+def relay(place, keep_right, keep_left, from_a, from_b):
     half, width = keep_right.shape
-    outputs = [held((half + DOT_ROWS, width), BF16), held((half, width), BF16)]
-    return run(relay_kernel, "relay", 4, [], [keep_right, keep_left, l1, r1], outputs, (), RELAY)
-
-
-def finish_grad_kernel(own, l1, r1, l2, r2, tokens, inverse, dots, result):
+    outputs = [held((half + DOT_ROWS, width), BF16)] * 2
+    scratch = [pltpu.VMEM((2, half + DOT_ROWS, width), BF16)]
+    inputs = [keep_right, keep_left, from_a, from_b]
+    return run(relay_kernel, "relay", 6, [place], inputs, outputs, scratch, RELAY)
+
+
+def finish_grad_kernel(place, own, a1, b1, a2, b2, tokens, inverse, dots, result):
     rows, width = own.shape
-    half = r2.shape[0]
-    pieces = dots[...].astype(F32)
-    for message, first in ((l1, rows), (r1, rows), (l2, half)):
-        pieces = pieces + message[first : first + DOT_ROWS, :].astype(F32)
+    half = rows // 2
+    whole, part = slice(rows, rows + DOT_ROWS), slice(half, half + DOT_ROWS)
+    pieces = dots[...].astype(F32) + a1[whole, :].astype(F32) + b1[whole, :].astype(F32)
+    pieces = pieces + from_side(place, a2, b2, True, part).astype(F32)
     means = (pieces[0:4] + pieces[4:8] + pieces[8:12]) / (MP * width)
     for b in range(rows // BLOCK):
         at, near = block_rows(b), block_rows(b % 2)
         mean = as_column(means[b : b + 1, :])
         inv = as_column(inverse[b : b + 1, :])
         total = own[at, :].astype(F32)
-        for part in (r1, l2) if b < 2 else (l1, r2):
-            total = total + part[near, :].astype(F32)
+        total = total + from_side(place, a1, b1, b >= 2, near).astype(F32)
+        total = total + from_side(place, a2, b2, b < 2, near).astype(F32)
         result[at, :] = inv * (total - tokens[at, :].astype(F32) * inv * mean)
 
 
-def finish_grad(own, l1, r1, l2, r2, tokens, inverse, dots):
-    inputs = [own, l1, r1, l2, r2, tokens, inverse, dots]
+def finish_grad(place, own, a1, b1, a2, b2, tokens, inverse, dots):
+    inputs = [own, a1, b1, a2, b2, tokens, inverse, dots]
     outputs = [held(own.shape, F32)]
-    return run(finish_grad_kernel, "finish_grad", 8, [], inputs, outputs)[0]
+    return run(finish_grad_kernel, "finish_grad", 8, [place], inputs, outputs)[0]
 
 
 def early_kernel(g0, g1, g2, g3, attended, normed, d_query, outer, inner):
@@ -895,6 +911,14 @@
 
 def to_previous(value):
     return lax.ppermute(value, "mp", [((i + 1) % MP, i) for i in range(MP)])
+
+
+def swap_a(value):
+    return lax.ppermute(value, "mp", [(0, 1), (1, 0), (2, 3), (3, 2)])
+
+
+def swap_b(value):
+    return lax.ppermute(value, "mp", [(1, 2), (2, 1), (3, 0), (0, 3)])
 
 
 def gather_shares(share):
@@ -965,17 +989,17 @@
     attended = tied(attended, *out_received)
     outer, inner = early_terms(grad_shares, attended, normed, d_query)
     d_query = tied(d_query, outer)
-    d_proj, dots, own, keep_right, keep_left, right, left = input_terms(
+    d_proj, dots, own, keep_right, keep_left, to_a, to_b = input_terms(
         me, d_query, d_kv, halo, normed, w
     )
     attn_out = finish_out(out_own, out_received)
     mine, *others = inner_terms(me, normed, d_proj, inner, outer)
     core_sums = sum_over_core(me, mine, *others)
-    l1, r1 = to_next(right), to_previous(left)
-    onward_right, onward_left = relay(keep_right, keep_left, l1, r1)
-    l2, r2 = to_next(onward_right), to_previous(onward_left)
-    grad_tokens = finish_grad(own, l1, r1, l2, r2, tokens, inverse, dots)
-    *weight_grads, grad_w_out = sum_over_seq(me, core_sums, onward_right, attn_out)
+    a1, b1 = swap_a(to_a), swap_b(to_b)
+    to_a, to_b = relay(me, keep_right, keep_left, a1, b1)
+    a2, b2 = swap_a(to_a), swap_b(to_b)
+    grad_tokens = finish_grad(me, own, a1, b1, a2, b2, tokens, inverse, dots)
+    *weight_grads, grad_w_out = sum_over_seq(me, core_sums, to_a, attn_out)
     return (attn_out, grad_tokens, *weight_grads, grad_w_out.T)
 
 

time: 120 us -> 118 us (0.983)
  starting transfers between devices: 49.4 us -> 46.6 us
  Pallas kernels: 52.3 us -> 53.8 us
    ppermute x0 -> x4, starting transfers between devices: none -> 4.35 us  [the longest x2 2.64 us: swap_b(): return lax.ppermute(value, 'mp', [(1, 2), (2, 1), (3, 0), (0, 3)])]
    ppermute x6 -> x4, starting transfers between devices: 13.7 us -> 9.62 us  [to_previous(): return lax.ppermute(value, 'mp', [((i + 1) % MP, i) for i in range(MP)])]
    ppermute x6, waiting for transfers between devices: 3.61 us -> 0.74 us  [sent(): return lax.ppermute(value, 'seq', pairs)]
    ppermute x6 -> x4, starting transfers between devices: 6.62 us -> 4.09 us  [to_next(): return lax.ppermute(value, 'mp', [(i, (i + 1) % MP) for i in range(MP)])]
    ppermute x0 -> x4, waiting for transfers between devices: none -> 2.5 us  [the longest x2 2.49 us: swap_b(): return lax.ppermute(value, 'mp', [(1, 2), (2, 1), (3, 0), (0, 3)])]
    pallas_call x16, Pallas kernels: 44.6 us -> 46.2 us  [run(): pl.pallas_call(kernel, in_specs=[SCALAR] * len(scalars) + [RESIDENT] * le...]
    ppermute x6 -> x4, waiting for transfers between devices: 2.47 us -> 2.23 us  [to_previous(): return lax.ppermute(value, 'mp', [((i + 1) % MP, i) for i in range(MP)])]
    ppermute x6 -> x4, waiting for transfers between devices: 5.84 us -> 5.83 us  [to_next(): return lax.ppermute(value, 'mp', [(i, (i + 1) % MP) for i in range(MP)])]
  transfers between devices with their start and end apart: 28 -> 28, of which waited for: 9 -> 9; matrix products, arithmetic and copies ran while one was open for 0% -> 0% of each run, Pallas kernels for 40% -> 42%
where the time goes in v11:
time: 118 us
  Pallas kernels  53.8 us (46%)
  starting transfers between devices  46.6 us (39%)
  waiting for transfers between devices  13.7 us (12%)
  local copies, waits for them, and re-layouts  2.5 us (2%)
    pallas_call x16, Pallas kernels, run(): pl.pallas_call(kernel, in_specs=[SCALAR] * len(scalars) + [RESIDENT] * le...  46.2 us
    ppermute x6, starting transfers between devices, sent(): return lax.ppermute(value, 'seq', pairs)  12.7 us
    ppermute x4, starting transfers between devices, to_previous(): return lax.ppermute(value, 'mp', [((i + 1) % MP, i) for i in range(MP)])  9.62 us
    pallas_call x1, Pallas kernels, project(): pl.pallas_call(project_kernel, in_specs=[SCALAR] + [anywhere] * 10, out_s...  7.65 us
    ppermute x2, starting transfers between devices, exchange(): from_core = lax.ppermute(to_core, 'seq', [(i, i ^ 1) for i in range(count)])  7.26 us
    ppermute x4, starting transfers between devices, turned_by(): return lax.ppermute(value, 'mp', [(i, (i + step) % MP) for i in range(MP)])  6.61 us
    ppermute x4, waiting for transfers between devices, to_next(): return lax.ppermute(value, 'mp', [(i, (i + 1) % MP) for i in range(MP)])  5.83 us
    ppermute x4, starting transfers between devices, to_next(): return lax.ppermute(value, 'mp', [(i, (i + 1) % MP) for i in range(MP)])  4.09 us
  transfers between devices with their start and end apart: 28, of which 9 were waited for; matrix products, arithmetic and copies ran while one was open for 0% of the time, Pallas kernels for 42%

profile of v11, /device:TPU:0, one launch (start us, length us, event | category | flops | bytes accessed | tf_op | source)
XLA Modules:
  0.0 117.7 jit_solution(10935732290540635281)
XLA Ops:
  1.7 2.1 %collective-permute-start.3 = (bf16[512,256]{1,0:T(8,128)(2,1)S(1)}, bf16[512,256]{1,0:T(8,128)(2,1)S(1)}, u32[]{:S(2)}, u32[]{:S(2)}) collective-permute-start(bf16[512,256]{1,0:T(8,128)(2,1)S(1)} %get-tuple-element.138), channel_id=1, source_target_pairs={{0,1},{1,2},{2,3},{3,0},{4,5},{5,6},{6,7},{7,4},{8,9},{9,10},{10,1... | collective-permute-start | bytes 786440 | tf_op jit(solution)/shard_map/ppermute | solution.py:909
  3.8 2.2 %collective-permute-start = (bf16[512,256]{1,0:T(8,128)(2,1)S(1)}, bf16[512,256]{1,0:T(8,128)(2,1)S(1)}, u32[]{:S(2)}, u32[]{:S(2)}) collective-permute-start(bf16[512,256]{1,0:T(8,128)(2,1)S(1)} %get-tuple-element.139), channel_id=1, source_target_pairs={{1,0},{2,1},{3,2},{0,3},{5,4},{6,5},{7,6},{4,7},{9,8},{10,9},{11,1... | collective-permute-start | bytes 786440 | tf_op jit(solution)/shard_map/ppermute | solution.py:913
  6.0 1.9 %collective-permute-start.1 = (bf16[512,256]{1,0:T(8,128)(2,1)S(1)}, bf16[512,256]{1,0:T(8,128)(2,1)S(1)}, u32[]{:S(2)}, u32[]{:S(2)}) collective-permute-start(bf16[512,256]{1,0:T(8,128)(2,1)S(1)} %get-tuple-element.138), channel_id=1, source_target_pairs={{1,0},{2,1},{3,2},{0,3},{5,4},{6,5},{7,6},{4,7},{9,8},{10,9},{11,1... | collective-permute-start | bytes 786440 | tf_op jit(solution)/shard_map/ppermute | solution.py:913
  8.0 5.0 %collective-permute-done.3.t3b_any = bf16[512,256]{1,0:T(8,128)(2,1)S(1)} collective-permute-done((bf16[512,256]{1,0:T(8,128)(2,1)S(1)}, bf16[512,256]{1,0:T(8,128)(2,1)S(1)}, u32[]{:S(2)}, u32[]{:S(2)}) %collective-permute-start.3) | collective-permute-done | bytes 262176 | tf_op jit(solution)/shard_map/ppermute | solution.py:909
  13.0 3.3 %collective-permute-start.2 = (bf16[512,256]{1,0:T(8,128)(2,1)S(1)}, bf16[512,256]{1,0:T(8,128)(2,1)}, u32[]{:S(2)}, u32[]{:S(2)}) collective-permute-start(bf16[512,256]{1,0:T(8,128)(2,1)S(1)} %collective-permute-done.t1a_any), channel_id=1, source_target_pairs={{1,0},{2,1},{3,2},{0,3},{5,4},{6,5},{7,6},{4,7},{9,8},{10,9},{11,1... | collective-permute-start | bytes 786440 | tf_op jit(solution)/shard_map/ppermute | solution.py:913
  16.4 2.2 %collective-permute-done.1.t1b_any = bf16[512,256]{1,0:T(8,128)(2,1)S(1)} collective-permute-done((bf16[512,256]{1,0:T(8,128)(2,1)S(1)}, bf16[512,256]{1,0:T(8,128)(2,1)S(1)}, u32[]{:S(2)}, u32[]{:S(2)}) %collective-permute-start.1) | collective-permute-done | bytes 262176 | tf_op jit(solution)/shard_map/ppermute | solution.py:913
  19.3 1.9 %collective-permute-start.9 = (bf16[1024,256]{1,0:T(8,128)(2,1)}, bf16[1024,256]{1,0:T(8,128)(2,1)}, u32[]{:S(2)}, u32[]{:S(2)}) collective-permute-start(bf16[1024,256]{1,0:T(8,128)(2,1)} %g0.1), channel_id=1, source_target_pairs={{0,1},{1,2},{2,3},{3,0},{4,5},{5,6},{6,7},{7,4},{8,9},{9,10},{10,1... | collective-permute-start | bytes 1572872 | tf_op jit(solution)/shard_map/ppermute | solution.py:909
  21.3 2.1 %collective-permute-start.8 = (bf16[1024,256]{1,0:T(8,128)(2,1)}, bf16[1024,256]{1,0:T(8,128)(2,1)}, u32[]{:S(2)}, u32[]{:S(2)}) collective-permute-start(bf16[1024,256]{1,0:T(8,128)(2,1)} %g0.1), channel_id=1, source_target_pairs={{1,0},{2,1},{3,2},{0,3},{5,4},{6,5},{7,6},{4,7},{9,8},{10,9},{11,1... | collective-permute-start | bytes 1572872 | tf_op jit(solution)/shard_map/ppermute | solution.py:913
  25.0 7.6 %project.1 = (f32[8,256]{1,0:T(8,128)S(1)}, bf16[1792,256]{1,0:T(8,128)(2,1)S(1)}, bf16[2,1792,256]{2,1,0:T(8,128)(2,1)S(1)}, bf16[2,576,256]{2,1,0:T(8,128)(2,1...) custom-call(s32[4]{0:T(128)S(1)} %pad_add_fusion.place, ...), custom_call_target="tpu_custom_call" | custom-call | flops 1000000 | bytes 10000 | tf_op jit(solution)/shard_map/project/pallas_call | solution.py:219
  33.3 2.9 %collective-permute-start.7 = (bf16[2,576,256]{2,1,0:T(8,128)(2,1)}, bf16[2,576,256]{2,1,0:T(8,128)(2,1)}, u32[]{:S(2)}, u32[]{:S(2)}) collective-permute-start(bf16[2,576,256]{2,1,0:T(8,128)(2,1)} %get-tuple-element.75), channel_id=1, source_target_pairs={{0,4},{4,0},{8,12},{12,8},{16,20},{20,16},{24,28},{28,24},{32,36},... | collective-permute-start | bytes 1769480 | tf_op jit(solution)/shard_map/ppermute | solution.py:947
  36.3 3.1 %collective-permute-start.13 = (bf16[1024,256]{1,0:T(8,128)(2,1)}, bf16[1024,256]{1,0:T(8,128)(2,1)S(1)}, u32[]{:S(2)}, u32[]{:S(2)}) collective-permute-start(bf16[1024,256]{1,0:T(8,128)(2,1)} %g0.1), channel_id=1, source_target_pairs={{0,2},{1,3},{2,0},{3,1},{4,6},{5,7},{6,4},{7,5},{8,10},{9,11},{10,... | collective-permute-start | bytes 1572872 | tf_op jit(solution)/shard_map/ppermute | solution.py:934
  39.5 3.6 %forward_inner.1 = (f32[512,256]{1,0:T(8,128)S(1)}, f32[2,8,256]{2,1,0:T(8,128)S(1)}) custom-call(f32[2]{0:T(128)S(1)} %pad_maximum_fusion.bias_ref, bf16[1792,256]{1,0:T(8,128)(2,1)S(1)} %get-tuple-element.77.q, bf16[2,1792,256]{2,1,0:T(8,128)(2,1)S(1)} %get-tuple-element.73.kv), custom_call_target="tpu_custom_call" | custom-call | flops 2500000000 | bytes 10000 | tf_op jit(solution)/shard_map/forward_inner/pallas_call | solution.py:76
  45.0 6.9 %forward_edge.1 = (bf16[1024,256]{1,0:T(8,128)(2,1)S(1)}, f32[2,24,256]{2,1,0:T(8,128)S(1)}, bf16[2,768,256]{2,1,0:T(8,128)(2,1)S(1)}, bf16[2,768,256]{2,1,0:T(8,128)(2,1)S(1)}) custom-call(s32[4]{0:T(128)S(1)} %pad_add_fusion.place, f32[2]{0:T(128)S(1)} %pad_maximum_fusion.bias_ref, bf16[1792,256]{1,0:T(8,128)(2,1)S(1)} %get-tuple-element.77.q, ...), custom_call_target="tpu_custom_call" | custom-call | flops 1000000 | bytes 10000 | tf_op jit(solution)/shard_map/forward_edge/pallas_call | solution.py:76
  58.3 10.7 %edge_backward.1 = (f32[1024,256]{1,0:T(8,128)S(1)}, f32[2,1024,256]{2,1,0:T(8,128)S(1)}, bf16[2,576,256]{2,1,0:T(8,128)(2,1)S(1)}, bf16[2,576,256]{2,1,0:T(8,128)(2,1)S(1)}) custom-call(s32[4]{0:T(128)S(1)} %pad_add_fusion.place, f32[2]{0:T(128)S(1)} %pad_maximum_fusion.bias_ref, f32[2,24,256]{2,1,0:T(8,128)S(1)} %get-tuple-element.91.stats, ...), custom_call_target="tpu_custom_call" | custom-call | flops 1000000 | bytes 10000 | tf_op jit(solution)/shard_map/edge_backward/pallas_call | solution.py:76
  69.7 4.4 %collective-permute-start.15 = (bf16[2,576,256]{2,1,0:T(8,128)(2,1)S(1)}, bf16[2,576,256]{2,1,0:T(8,128)(2,1)S(1)}, u32[]{:S(2)}, u32[]{:S(2)}) collective-permute-start(bf16[2,576,256]{2,1,0:T(8,128)(2,1)S(1)} %get-tuple-element.106), channel_id=1, source_target_pairs={{0,4},{4,0},{8,12},{12,8},{16,20},{20,16},{24,28},{28,24},{32,36},... | collective-permute-start | bytes 1769480 | tf_op jit(solution)/shard_map/ppermute | solution.py:947
  74.0 5.5 %inner_backward.1 = (bf16[1024,256]{1,0:T(8,128)(2,1)S(1)}, f32[2,1024,256]{2,1,0:T(8,128)S(1)}) custom-call(f32[2]{0:T(128)S(1)} %pad_maximum_fusion.bias_ref, f32[2,8,256]{2,1,0:T(8,128)S(1)} %get-tuple-element.88.stats, bf16[1792,256]{1,0:T(8,128)(2,1)S(1)} %get-tuple-element.77.q, bf16[2,1792,256]{2,1,0:T(8,128)(2,1)S(1)} %get-tuple-element.73.kv, ...), custom_call_target="tpu_custom_call" | custom-call | flops 1000000 | bytes 10000 | tf_op jit(solution)/shard_map/inner_backward/pallas_call | solution.py:76
  79.8 2.7 %early_terms.1 = (bf16[1024,256]{1,0:T(8,128)(2,1)S(1)}, bf16[1024,256]{1,0:T(8,128)(2,1)S(1)}) custom-call(bf16[1024,256]{1,0:T(8,128)(2,1)S(1)} %copy-done.4, bf16[1024,256]{1,0:T(8,128)(2,1)} %collective-permute-done.8.g1, bf16[1024,256]{1,0:T(8,128)(2,1)S(1)} %collective-permute-done.13.g2, bf16[1024,256]{1,0:T(8,128)(2,1)} %collective-permute-done.9.g3, ...), custom_call_target="tpu_custom_call" | custom-call | flops 4000000000 | bytes 10000 | tf_op jit(solution)/shard_map/early_terms/pallas_call | solution.py:76
  82.5 3.5 %input_terms.1 = (bf16[1024,512]{1,0:T(8,128)(2,1)S(1)}, bf16[16,256]{1,0:T(8,128)(2,1)S(1)}, bf16[1024,256]{1,0:T(8,128)(2,1)S(1)}, bf16[512,256]{1,0:T(8,128)(...) custom-call(s32[4]{0:T(128)S(1)} %pad_add_fusion.place, ...), custom_call_target="tpu_custom_call" | custom-call | flops 1000000 | bytes 10000 | tf_op jit(solution)/shard_map/input_terms/pallas_call | solution.py:76
  88.8 2.1 %inner_terms.1 = (bf16[512,1024]{1,0:T(8,128)(2,1)S(1)}, bf16[256,1024]{1,0:T(8,128)(2,1)S(1)}, bf16[256,1024]{1,0:T(8,128)(2,1)S(1)}) custom-call(s32[4]{0:T(128)S(1)} %pad_add_fusion.place, bf16[1024,1024]{1,0:T(8,128)(2,1)S(1)} %copy-done, bf16[1024,512]{1,0:T(8,128)(2,1)S(1)} %get-tuple-element.117.d_proj, ...), custom_call_target="tpu_custom_call" | custom-call | flops 1000000 | bytes 10000 | tf_op jit(solution)/shard_map/inner_terms/pallas_call | solution.py:76
  96.4 2.8 %collective-permute-start.23 = (bf16[128,1024]{1,0:T(8,128)(2,1)S(1)}, bf16[128,1024]{1,0:T(8,128)(2,1)S(1)}, u32[]{:S(2)}, u32[]{:S(2)}) collective-permute-start(bf16[128,1024]{1,0:T(8,128)(2,1)S(1)} %get-tuple-element.124), channel_id=1, source_target_pairs={{0,16},{4,68},{8,24},{12,76},{16,0},{20,84},{24,8},{28,92},{32,48}... | collective-permute-start | bytes 786440 | tf_op jit(solution)/shard_map/ppermute | solution.py:896
  100.2 2.5 %collective-permute-done.17.from_b.b1 = bf16[1040,256]{1,0:T(8,128)(2,1)S(1)} collective-permute-done((bf16[1040,256]{1,0:T(8,128)(2,1)S(1)}, bf16[1040,256]{1,0:T(8,128)(2,1)S(1)}, u32[]{:S(2)}, u32[]{:S(2)}) %collective-permute-start.17) | collective-permute-done | bytes 532512 | tf_op jit(solution)/shard_map/ppermute | solution.py:921
  107.1 2.8 %collective-permute-start.25 = (bf16[32,1024]{1,0:T(8,128)(2,1)S(1)}, bf16[32,1024]{1,0:T(8,128)(2,1)S(1)}, u32[]{:S(2)}, u32[]{:S(2)}) collective-permute-start(bf16[32,1024]{1,0:T(8,128)(2,1)S(1)} %get-tuple-element.131), channel_id=1, source_target_pairs={{0,32},{4,12},{8,40},{12,20},{16,48},{20,28},{24,56},{28,4},{32,64... | collective-permute-start | bytes 196616 | tf_op jit(solution)/shard_map/ppermute | solution.py:896
  109.8 2.9 %collective-permute-start.26 = (bf16[32,1024]{1,0:T(8,128)(2,1)S(1)}, bf16[32,1024]{1,0:T(8,128)(2,1)S(1)}, u32[]{:S(2)}, u32[]{:S(2)}) collective-permute-start(bf16[32,1024]{1,0:T(8,128)(2,1)S(1)} %get-tuple-element.132), channel_id=1, source_target_pairs={{0,64},{4,20},{8,72},{12,28},{16,80},{20,4},{24,88},{28,12},{32,96... | collective-permute-start | bytes 196616 | tf_op jit(solution)/shard_map/ppermute | solution.py:896
  114.1 2.3 %finish_grad.1 = f32[1024,256]{1,0:T(8,128)} custom-call(s32[4]{0:T(128)S(1)} %pad_add_fusion.place, bf16[1024,256]{1,0:T(8,128)(2,1)S(1)} %get-tuple-element.108.own, bf16[1040,256]{1,0:T(8,128)(2,1)S(1)} %collective-permute-done.16.from_a.a1, bf16[1040,256]{1,0:T(8,128)(2,1)S(1)} %collective-permute-done.17.from_b.b1, ...), custom_call_target="tpu_custom_call" | custom-call | flops 1000000 | bytes 10000 | tf_op jit(solution)/shard_map/finish_grad/pallas_call | solution.py:76
  (72 shorter events, 29.8 us)
Async XLA Ops:
  1.7 11.3 %collective-permute-start.3 = (bf16[512,256]{1,0:T(8,128)(2,1)S(1)}, bf16[512,256]{1,0:T(8,128)(2,1)S(1)}, u32[]{:S(2)}, u32[]{:S(2)}) collective-permute-start(bf16[512,256]{1,0:T(8,128)(2,1)S(1)} %get-tuple-element.138), channel_id=1, source_target_pairs={{0,1},{1,2},{2,3},{3,0},{4,5},{5,6},{6,7},{7,4},{8,9},{9,10},{10,1... | collective-permute-start | bytes 786440 | tf_op jit(solution)/shard_map/ppermute | solution.py:909
  3.8 9.3 %collective-permute-start = (bf16[512,256]{1,0:T(8,128)(2,1)S(1)}, bf16[512,256]{1,0:T(8,128)(2,1)S(1)}, u32[]{:S(2)}, u32[]{:S(2)}) collective-permute-start(bf16[512,256]{1,0:T(8,128)(2,1)S(1)} %get-tuple-element.139), channel_id=1, source_target_pairs={{1,0},{2,1},{3,2},{0,3},{5,4},{6,5},{7,6},{4,7},{9,8},{10,9},{11,1... | collective-permute-start | bytes 786440 | tf_op jit(solution)/shard_map/ppermute | solution.py:913
  6.0 12.6 %collective-permute-start.1 = (bf16[512,256]{1,0:T(8,128)(2,1)S(1)}, bf16[512,256]{1,0:T(8,128)(2,1)S(1)}, u32[]{:S(2)}, u32[]{:S(2)}) collective-permute-start(bf16[512,256]{1,0:T(8,128)(2,1)S(1)} %get-tuple-element.138), channel_id=1, source_target_pairs={{1,0},{2,1},{3,2},{0,3},{5,4},{6,5},{7,6},{4,7},{9,8},{10,9},{11,1... | collective-permute-start | bytes 786440 | tf_op jit(solution)/shard_map/ppermute | solution.py:913
  7.9 10.7 %collective-permute-start.5 = (bf16[512,256]{1,0:T(8,128)(2,1)S(1)}, bf16[512,256]{1,0:T(8,128)(2,1)S(1)}, u32[]{:S(2)}, u32[]{:S(2)}) collective-permute-start(bf16[512,256]{1,0:T(8,128)(2,1)S(1)} %get-tuple-element.139), channel_id=1, source_target_pairs={{0,1},{1,2},{2,3},{3,0},{4,5},{5,6},{6,7},{7,4},{8,9},{9,10},{10,1... | collective-permute-start | bytes 786440 | tf_op jit(solution)/shard_map/ppermute | solution.py:909
  13.0 11.2 %collective-permute-start.4 = (bf16[512,256]{1,0:T(8,128)(2,1)S(1)}, bf16[512,256]{1,0:T(8,128)(2,1)S(1)}, u32[]{:S(2)}, u32[]{:S(2)}) collective-permute-start(bf16[512,256]{1,0:T(8,128)(2,1)S(1)} %collective-permute-done.3.t3b_any), channel_id=1, source_target_pairs={{0,1},{1,2},{2,3},{3,0},{4,5},{5,6},{6,7},{7,4},{8,9},{9,10},{10,1... | collective-permute-start | bytes 786440 | tf_op jit(solution)/shard_map/ppermute | solution.py:909
  13.0 11.9 %collective-permute-start.2 = (bf16[512,256]{1,0:T(8,128)(2,1)S(1)}, bf16[512,256]{1,0:T(8,128)(2,1)}, u32[]{:S(2)}, u32[]{:S(2)}) collective-permute-start(bf16[512,256]{1,0:T(8,128)(2,1)S(1)} %collective-permute-done.t1a_any), channel_id=1, source_target_pairs={{1,0},{2,1},{3,2},{0,3},{5,4},{6,5},{7,6},{4,7},{9,8},{10,9},{11,1... | collective-permute-start | bytes 786440 | tf_op jit(solution)/shard_map/ppermute | solution.py:913
  19.3 20.1 %collective-permute-start.9 = (bf16[1024,256]{1,0:T(8,128)(2,1)}, bf16[1024,256]{1,0:T(8,128)(2,1)}, u32[]{:S(2)}, u32[]{:S(2)}) collective-permute-start(bf16[1024,256]{1,0:T(8,128)(2,1)} %g0.1), channel_id=1, source_target_pairs={{0,1},{1,2},{2,3},{3,0},{4,5},{5,6},{6,7},{7,4},{8,9},{9,10},{10,1... | collective-permute-start | bytes 1572872 | tf_op jit(solution)/shard_map/ppermute | solution.py:909
  21.3 18.2 %collective-permute-start.8 = (bf16[1024,256]{1,0:T(8,128)(2,1)}, bf16[1024,256]{1,0:T(8,128)(2,1)}, u32[]{:S(2)}, u32[]{:S(2)}) collective-permute-start(bf16[1024,256]{1,0:T(8,128)(2,1)} %g0.1), channel_id=1, source_target_pairs={{1,0},{2,1},{3,2},{0,3},{5,4},{6,5},{7,6},{4,7},{9,8},{10,9},{11,1... | collective-permute-start | bytes 1572872 | tf_op jit(solution)/shard_map/ppermute | solution.py:913
  32.6 12.3 %collective-permute-start.6 = (bf16[2,576,256]{2,1,0:T(8,128)(2,1)}, bf16[2,576,256]{2,1,0:T(8,128)(2,1)S(1)}, u32[]{:S(2)}, u32[]{:S(2)}) collective-permute-start(bf16[2,576,256]{2,1,0:T(8,128)(2,1)} %get-tuple-element.74), channel_id=1, source_target_pairs={{4,8},{8,4},{12,16},{16,12},{20,24},{24,20},{28,32},{32,28},{36,40... | collective-permute-start | bytes 1769480 | tf_op jit(solution)/shard_map/ppermute | solution.py:946
  33.3 11.6 %collective-permute-start.7 = (bf16[2,576,256]{2,1,0:T(8,128)(2,1)}, bf16[2,576,256]{2,1,0:T(8,128)(2,1)}, u32[]{:S(2)}, u32[]{:S(2)}) collective-permute-start(bf16[2,576,256]{2,1,0:T(8,128)(2,1)} %get-tuple-element.75), channel_id=1, source_target_pairs={{0,4},{4,0},{8,12},{12,8},{16,20},{20,16},{24,28},{28,24},{32,36},... | collective-permute-start | bytes 1769480 | tf_op jit(solution)/shard_map/ppermute | solution.py:947
  36.3 20.3 %collective-permute-start.13 = (bf16[1024,256]{1,0:T(8,128)(2,1)}, bf16[1024,256]{1,0:T(8,128)(2,1)S(1)}, u32[]{:S(2)}, u32[]{:S(2)}) collective-permute-start(bf16[1024,256]{1,0:T(8,128)(2,1)} %g0.1), channel_id=1, source_target_pairs={{0,2},{1,3},{2,0},{3,1},{4,6},{5,7},{6,4},{7,5},{8,10},{9,11},{10,... | collective-permute-start | bytes 1572872 | tf_op jit(solution)/shard_map/ppermute | solution.py:934
  53.1 26.5 %collective-permute-start.10 = (bf16[1024,256]{1,0:T(8,128)(2,1)S(1)}, bf16[1024,256]{1,0:T(8,128)(2,1)S(1)}, u32[]{:S(2)}, u32[]{:S(2)}) collective-permute-start(bf16[1024,256]{1,0:T(8,128)(2,1)S(1)} %get-tuple-element.85), channel_id=1, source_target_pairs={{0,1},{1,2},{2,3},{3,0},{4,5},{5,6},{6,7},{7,4},{8,9},{9,10},{10,1... | collective-permute-start | bytes 1572872 | tf_op jit(solution)/shard_map/ppermute | solution.py:934
  53.8 25.8 %collective-permute-start.11 = (bf16[1024,256]{1,0:T(8,128)(2,1)S(1)}, bf16[1024,256]{1,0:T(8,128)(2,1)S(1)}, u32[]{:S(2)}, u32[]{:S(2)}) collective-permute-start(bf16[1024,256]{1,0:T(8,128)(2,1)S(1)} %get-tuple-element.86), channel_id=1, source_target_pairs={{0,2},{1,3},{2,0},{3,1},{4,6},{5,7},{6,4},{7,5},{8,10},{9,11},{10,... | collective-permute-start | bytes 1572872 | tf_op jit(solution)/shard_map/ppermute | solution.py:934
  55.6 24.2 %collective-permute-start.12 = (bf16[1024,256]{1,0:T(8,128)(2,1)S(1)}, bf16[1024,256]{1,0:T(8,128)(2,1)S(1)}, u32[]{:S(2)}, u32[]{:S(2)}) collective-permute-start(bf16[1024,256]{1,0:T(8,128)(2,1)S(1)} %get-tuple-element.87), channel_id=1, source_target_pairs={{0,3},{1,0},{2,1},{3,2},{4,7},{5,4},{6,5},{7,6},{8,11},{9,8},{10,9... | collective-permute-start | bytes 1572872 | tf_op jit(solution)/shard_map/ppermute | solution.py:934
  69.0 13.5 %collective-permute-start.14 = (bf16[2,576,256]{2,1,0:T(8,128)(2,1)S(1)}, bf16[2,576,256]{2,1,0:T(8,128)(2,1)S(1)}, u32[]{:S(2)}, u32[]{:S(2)}) collective-permute-start(bf16[2,576,256]{2,1,0:T(8,128)(2,1)S(1)} %get-tuple-element.105), channel_id=1, source_target_pairs={{4,8},{8,4},{12,16},{16,12},{20,24},{24,20},{28,32},{32,28},{36,40... | collective-permute-start | bytes 1769480 | tf_op jit(solution)/shard_map/ppermute | solution.py:946
  69.7 12.8 %collective-permute-start.15 = (bf16[2,576,256]{2,1,0:T(8,128)(2,1)S(1)}, bf16[2,576,256]{2,1,0:T(8,128)(2,1)S(1)}, u32[]{:S(2)}, u32[]{:S(2)}) collective-permute-start(bf16[2,576,256]{2,1,0:T(8,128)(2,1)S(1)} %get-tuple-element.106), channel_id=1, source_target_pairs={{0,4},{4,0},{8,12},{12,8},{16,20},{20,16},{24,28},{28,24},{32,36},... | collective-permute-start | bytes 1769480 | tf_op jit(solution)/shard_map/ppermute | solution.py:947
  86.0 14.2 %collective-permute-start.16 = (bf16[1040,256]{1,0:T(8,128)(2,1)S(1)}, bf16[1040,256]{1,0:T(8,128)(2,1)S(1)}, u32[]{:S(2)}, u32[]{:S(2)}) collective-permute-start(bf16[1040,256]{1,0:T(8,128)(2,1)S(1)} %get-tuple-element.109), channel_id=1, source_target_pairs={{0,1},{1,0},{2,3},{3,2},{4,5},{5,4},{6,7},{7,6},{8,9},{9,8},{10,11... | collective-permute-start | bytes 1597448 | tf_op jit(solution)/shard_map/ppermute | solution.py:917
  87.7 14.9 %collective-permute-start.17 = (bf16[1040,256]{1,0:T(8,128)(2,1)S(1)}, bf16[1040,256]{1,0:T(8,128)(2,1)S(1)}, u32[]{:S(2)}, u32[]{:S(2)}) collective-permute-start(bf16[1040,256]{1,0:T(8,128)(2,1)S(1)} %get-tuple-element.110), channel_id=1, source_target_pairs={{1,2},{2,1},{3,0},{0,3},{5,6},{6,5},{7,4},{4,7},{9,10},{10,9},{11,... | collective-permute-start | bytes 1597448 | tf_op jit(solution)/shard_map/ppermute | solution.py:921
  94.5 11.7 %collective-permute-start.22 = (bf16[128,1024]{1,0:T(8,128)(2,1)S(1)}, bf16[128,1024]{1,0:T(8,128)(2,1)S(1)}, u32[]{:S(2)}, u32[]{:S(2)}) collective-permute-start(bf16[128,1024]{1,0:T(8,128)(2,1)S(1)} %get-tuple-element.123), channel_id=1, source_target_pairs={{0,8},{4,36},{8,16},{12,44},{16,24},{20,52},{24,0},{28,60},{32,40}... | collective-permute-start | bytes 786440 | tf_op jit(solution)/shard_map/ppermute | solution.py:896
  96.4 9.9 %collective-permute-start.23 = (bf16[128,1024]{1,0:T(8,128)(2,1)S(1)}, bf16[128,1024]{1,0:T(8,128)(2,1)S(1)}, u32[]{:S(2)}, u32[]{:S(2)}) collective-permute-start(bf16[128,1024]{1,0:T(8,128)(2,1)S(1)} %get-tuple-element.124), channel_id=1, source_target_pairs={{0,16},{4,68},{8,24},{12,76},{16,0},{20,84},{24,8},{28,92},{32,48}... | collective-permute-start | bytes 786440 | tf_op jit(solution)/shard_map/ppermute | solution.py:896
  99.1 7.2 %collective-permute-start.24 = (bf16[128,1024]{1,0:T(8,128)(2,1)S(1)}, bf16[128,1024]{1,0:T(8,128)(2,1)S(1)}, u32[]{:S(2)}, u32[]{:S(2)}) collective-permute-start(bf16[128,1024]{1,0:T(8,128)(2,1)S(1)} %get-tuple-element.125), channel_id=1, source_target_pairs={{0,24},{4,100},{8,0},{12,108},{16,8},{20,116},{24,16},{28,124},{32... | collective-permute-start | bytes 786440 | tf_op jit(solution)/shard_map/ppermute | solution.py:896
  103.6 10.5 %collective-permute-start.19 = (bf16[528,256]{1,0:T(8,128)(2,1)S(1)}, bf16[528,256]{1,0:T(8,128)(2,1)S(1)}, u32[]{:S(2)}, u32[]{:S(2)}) collective-permute-start(bf16[528,256]{1,0:T(8,128)(2,1)S(1)} %get-tuple-element.114), channel_id=1, source_target_pairs={{1,2},{2,1},{3,0},{0,3},{5,6},{6,5},{7,4},{4,7},{9,10},{10,9},{11,... | collective-permute-start | bytes 811016 | tf_op jit(solution)/shard_map/ppermute | solution.py:921
  105.1 9.0 %collective-permute-start.18 = (bf16[528,256]{1,0:T(8,128)(2,1)S(1)}, bf16[528,256]{1,0:T(8,128)(2,1)S(1)}, u32[]{:S(2)}, u32[]{:S(2)}) collective-permute-start(bf16[528,256]{1,0:T(8,128)(2,1)S(1)} %get-tuple-element.113), channel_id=1, source_target_pairs={{0,1},{1,0},{2,3},{3,2},{4,5},{5,4},{6,7},{7,6},{8,9},{9,8},{10,11... | collective-permute-start | bytes 811016 | tf_op jit(solution)/shard_map/ppermute | solution.py:917
  107.1 9.3 %collective-permute-start.25 = (bf16[32,1024]{1,0:T(8,128)(2,1)S(1)}, bf16[32,1024]{1,0:T(8,128)(2,1)S(1)}, u32[]{:S(2)}, u32[]{:S(2)}) collective-permute-start(bf16[32,1024]{1,0:T(8,128)(2,1)S(1)} %get-tuple-element.131), channel_id=1, source_target_pairs={{0,32},{4,12},{8,40},{12,20},{16,48},{20,28},{24,56},{28,4},{32,64... | collective-permute-start | bytes 196616 | tf_op jit(solution)/shard_map/ppermute | solution.py:896
  (14 other events, 69.0 us)

commit v12 on v11

--- a/solution.py
+++ b/solution.py
@@ -656,9 +656,10 @@
 def out_terms_kernel(place, attended, w_out, *outs):
     me = place[0]
     width = attended.shape[1]
+    near = 1 + 2 * (me & 1)
     for step in range(4):
         rows = attended[block_rows(step), :]
-        for r, out in enumerate(outs):
+        for r, out in zip((0, near, 2, 4 - near), outs):
             term = nn(rows, w_out[:, share_rows(me, r, width)])
             out[block_rows(step), :] = term.astype(BF16)
 
@@ -935,7 +936,8 @@
 
 
 def sum_over_mp(terms):
-    return [turned_by(term, step) for step, term in zip((1, 2, 3), terms)]
+    to_a, far, to_b = terms
+    return [swap_a(to_a), turned_by(far, 2), swap_b(to_b)]
 
 
 def exchange(to_core, to_other):

time: 118 us -> 119 us (level)
  waiting for transfers between devices: 13.7 us -> 17.1 us
  starting transfers between devices: 46.6 us -> 44 us
    ppermute x4 -> x2, starting transfers between devices: 6.61 us -> 4.96 us  [turned_by(): return lax.ppermute(value, 'mp', [(i, (i + step) % MP) for i in range(MP)])]
    ppermute x2 -> x3, waiting for transfers between devices: 0.01 us -> 1.45 us  [swap_a(): return lax.ppermute(value, 'mp', [(0, 1), (1, 0), (2, 3), (3, 2)])]
    ppermute x2 -> x3, waiting for transfers between devices: 2.49 us -> 3.92 us  [swap_b(): return lax.ppermute(value, 'mp', [(1, 2), (2, 1), (3, 0), (0, 3)])]
    ppermute x2, starting transfers between devices: 7.26 us -> 5.99 us  [exchange(): from_core = lax.ppermute(to_core, 'seq', [(i, i ^ 1) for i in range(count)])]
    ppermute x2 -> x3, starting transfers between devices: 2.64 us -> 3.69 us  [swap_b(): return lax.ppermute(value, 'mp', [(1, 2), (2, 1), (3, 0), (0, 3)])]
  transfers between devices with their start and end apart: 28 -> 28, of which waited for: 9 -> 11; matrix products, arithmetic and copies ran while one was open for 0% -> 0% of each run, Pallas kernels for 42% -> 42%
where the time goes in v12:
time: 119 us; the launch traced here: 118 us
  Pallas kernels  53.8 us (45%)
  starting transfers between devices  44 us (37%)
  waiting for transfers between devices  17.1 us (14%)
  local copies, waits for them, and re-layouts  2.5 us (2%)
    pallas_call x16, Pallas kernels, run(): pl.pallas_call(kernel, in_specs=[SCALAR] * len(scalars) + [RESIDENT] * le...  46.2 us
    ppermute x6, starting transfers between devices, sent(): return lax.ppermute(value, 'seq', pairs)  12.4 us
    ppermute x4, starting transfers between devices, to_previous(): return lax.ppermute(value, 'mp', [((i + 1) % MP, i) for i in range(MP)])  9.62 us
    pallas_call x1, Pallas kernels, project(): pl.pallas_call(project_kernel, in_specs=[SCALAR] + [anywhere] * 10, out_s...  7.65 us
    ppermute x2, starting transfers between devices, exchange(): from_core = lax.ppermute(to_core, 'seq', [(i, i ^ 1) for i in range(count)])  5.99 us
    ppermute x4, waiting for transfers between devices, to_next(): return lax.ppermute(value, 'mp', [(i, (i + 1) % MP) for i in range(MP)])  5.83 us
    ppermute x2, starting transfers between devices, turned_by(): return lax.ppermute(value, 'mp', [(i, (i + step) % MP) for i in range(MP)])  4.96 us
    ppermute x4, starting transfers between devices, to_next(): return lax.ppermute(value, 'mp', [(i, (i + 1) % MP) for i in range(MP)])  4.09 us
  transfers between devices with their start and end apart: 28, of which 11 were waited for; matrix products, arithmetic and copies ran while one was open for 0% of the time, Pallas kernels for 42%

profile of v12, /device:TPU:0, one launch (start us, length us, event | category | flops | bytes accessed | tf_op | source)
XLA Modules:
  0.0 118.5 jit_solution(16585482581773320592)
XLA Ops:
  1.7 2.1 %collective-permute-start.3 = (bf16[512,256]{1,0:T(8,128)(2,1)S(1)}, bf16[512,256]{1,0:T(8,128)(2,1)S(1)}, u32[]{:S(2)}, u32[]{:S(2)}) collective-permute-start(bf16[512,256]{1,0:T(8,128)(2,1)S(1)} %get-tuple-element.138), channel_id=1, source_target_pairs={{0,1},{1,2},{2,3},{3,0},{4,5},{5,6},{6,7},{7,4},{8,9},{9,10},{10,1... | collective-permute-start | bytes 786440 | tf_op jit(solution)/shard_map/ppermute | solution.py:910
  3.8 2.2 %collective-permute-start = (bf16[512,256]{1,0:T(8,128)(2,1)S(1)}, bf16[512,256]{1,0:T(8,128)(2,1)S(1)}, u32[]{:S(2)}, u32[]{:S(2)}) collective-permute-start(bf16[512,256]{1,0:T(8,128)(2,1)S(1)} %get-tuple-element.139), channel_id=1, source_target_pairs={{1,0},{2,1},{3,2},{0,3},{5,4},{6,5},{7,6},{4,7},{9,8},{10,9},{11,1... | collective-permute-start | bytes 786440 | tf_op jit(solution)/shard_map/ppermute | solution.py:914
  6.0 1.9 %collective-permute-start.1 = (bf16[512,256]{1,0:T(8,128)(2,1)S(1)}, bf16[512,256]{1,0:T(8,128)(2,1)S(1)}, u32[]{:S(2)}, u32[]{:S(2)}) collective-permute-start(bf16[512,256]{1,0:T(8,128)(2,1)S(1)} %get-tuple-element.138), channel_id=1, source_target_pairs={{1,0},{2,1},{3,2},{0,3},{5,4},{6,5},{7,6},{4,7},{9,8},{10,9},{11,1... | collective-permute-start | bytes 786440 | tf_op jit(solution)/shard_map/ppermute | solution.py:914
  8.0 5.0 %collective-permute-done.3.t3b_any = bf16[512,256]{1,0:T(8,128)(2,1)S(1)} collective-permute-done((bf16[512,256]{1,0:T(8,128)(2,1)S(1)}, bf16[512,256]{1,0:T(8,128)(2,1)S(1)}, u32[]{:S(2)}, u32[]{:S(2)}) %collective-permute-start.3) | collective-permute-done | bytes 262176 | tf_op jit(solution)/shard_map/ppermute | solution.py:910
  13.0 3.3 %collective-permute-start.2 = (bf16[512,256]{1,0:T(8,128)(2,1)S(1)}, bf16[512,256]{1,0:T(8,128)(2,1)}, u32[]{:S(2)}, u32[]{:S(2)}) collective-permute-start(bf16[512,256]{1,0:T(8,128)(2,1)S(1)} %collective-permute-done.t1a_any), channel_id=1, source_target_pairs={{1,0},{2,1},{3,2},{0,3},{5,4},{6,5},{7,6},{4,7},{9,8},{10,9},{11,1... | collective-permute-start | bytes 786440 | tf_op jit(solution)/shard_map/ppermute | solution.py:914
  16.4 2.2 %collective-permute-done.1.t1b_any = bf16[512,256]{1,0:T(8,128)(2,1)S(1)} collective-permute-done((bf16[512,256]{1,0:T(8,128)(2,1)S(1)}, bf16[512,256]{1,0:T(8,128)(2,1)S(1)}, u32[]{:S(2)}, u32[]{:S(2)}) %collective-permute-start.1) | collective-permute-done | bytes 262176 | tf_op jit(solution)/shard_map/ppermute | solution.py:914
  21.3 2.1 %collective-permute-start.8 = (bf16[1024,256]{1,0:T(8,128)(2,1)}, bf16[1024,256]{1,0:T(8,128)(2,1)}, u32[]{:S(2)}, u32[]{:S(2)}) collective-permute-start(bf16[1024,256]{1,0:T(8,128)(2,1)} %g0.1), channel_id=1, source_target_pairs={{1,0},{2,1},{3,2},{0,3},{5,4},{6,5},{7,6},{4,7},{9,8},{10,9},{11,1... | collective-permute-start | bytes 1572872 | tf_op jit(solution)/shard_map/ppermute | solution.py:914
  25.0 7.6 %project.1 = (f32[8,256]{1,0:T(8,128)S(1)}, bf16[1792,256]{1,0:T(8,128)(2,1)S(1)}, bf16[2,1792,256]{2,1,0:T(8,128)(2,1)S(1)}, bf16[2,576,256]{2,1,0:T(8,128)(2,1...) custom-call(s32[4]{0:T(128)S(1)} %pad_add_fusion.place, ...), custom_call_target="tpu_custom_call" | custom-call | flops 1000000 | bytes 10000 | tf_op jit(solution)/shard_map/project/pallas_call | solution.py:219
  33.3 2.9 %collective-permute-start.7 = (bf16[2,576,256]{2,1,0:T(8,128)(2,1)}, bf16[2,576,256]{2,1,0:T(8,128)(2,1)}, u32[]{:S(2)}, u32[]{:S(2)}) collective-permute-start(bf16[2,576,256]{2,1,0:T(8,128)(2,1)} %get-tuple-element.75), channel_id=1, source_target_pairs={{0,4},{4,0},{8,12},{12,8},{16,20},{20,16},{24,28},{28,24},{32,36},... | collective-permute-start | bytes 1769480 | tf_op jit(solution)/shard_map/ppermute | solution.py:949
  36.3 3.1 %collective-permute-start.13 = (bf16[1024,256]{1,0:T(8,128)(2,1)}, bf16[1024,256]{1,0:T(8,128)(2,1)S(1)}, u32[]{:S(2)}, u32[]{:S(2)}) collective-permute-start(bf16[1024,256]{1,0:T(8,128)(2,1)} %g0.1), channel_id=1, source_target_pairs={{0,2},{1,3},{2,0},{3,1},{4,6},{5,7},{6,4},{7,5},{8,10},{9,11},{10,... | collective-permute-start | bytes 1572872 | tf_op jit(solution)/shard_map/ppermute | solution.py:935
  39.5 3.6 %forward_inner.1 = (f32[512,256]{1,0:T(8,128)S(1)}, f32[2,8,256]{2,1,0:T(8,128)S(1)}) custom-call(f32[2]{0:T(128)S(1)} %pad_maximum_fusion.bias_ref, bf16[1792,256]{1,0:T(8,128)(2,1)S(1)} %get-tuple-element.77.q, bf16[2,1792,256]{2,1,0:T(8,128)(2,1)S(1)} %get-tuple-element.73.kv), custom_call_target="tpu_custom_call" | custom-call | flops 2500000000 | bytes 10000 | tf_op jit(solution)/shard_map/forward_inner/pallas_call | solution.py:76
  45.0 6.9 %forward_edge.1 = (bf16[1024,256]{1,0:T(8,128)(2,1)S(1)}, f32[2,24,256]{2,1,0:T(8,128)S(1)}, bf16[2,768,256]{2,1,0:T(8,128)(2,1)S(1)}, bf16[2,768,256]{2,1,0:T(8,128)(2,1)S(1)}) custom-call(s32[4]{0:T(128)S(1)} %pad_add_fusion.place, f32[2]{0:T(128)S(1)} %pad_maximum_fusion.bias_ref, bf16[1792,256]{1,0:T(8,128)(2,1)S(1)} %get-tuple-element.77.q, ...), custom_call_target="tpu_custom_call" | custom-call | flops 1000000 | bytes 10000 | tf_op jit(solution)/shard_map/forward_edge/pallas_call | solution.py:76
  55.6 2.2 %collective-permute-start.12 = (bf16[1024,256]{1,0:T(8,128)(2,1)S(1)}, bf16[1024,256]{1,0:T(8,128)(2,1)S(1)}, u32[]{:S(2)}, u32[]{:S(2)}) collective-permute-start(bf16[1024,256]{1,0:T(8,128)(2,1)S(1)} %get-tuple-element.87), channel_id=1, source_target_pairs={{1,2},{2,1},{3,0},{0,3},{5,6},{6,5},{7,4},{4,7},{9,10},{10,9},{11,... | collective-permute-start | bytes 1572872 | tf_op jit(solution)/shard_map/ppermute | solution.py:922
  59.6 10.7 %edge_backward.1 = (f32[1024,256]{1,0:T(8,128)S(1)}, f32[2,1024,256]{2,1,0:T(8,128)S(1)}, bf16[2,576,256]{2,1,0:T(8,128)(2,1)S(1)}, bf16[2,576,256]{2,1,0:T(8,128)(2,1)S(1)}) custom-call(s32[4]{0:T(128)S(1)} %pad_add_fusion.place, f32[2]{0:T(128)S(1)} %pad_maximum_fusion.bias_ref, f32[2,24,256]{2,1,0:T(8,128)S(1)} %get-tuple-element.91.stats, ...), custom_call_target="tpu_custom_call" | custom-call | flops 1000000 | bytes 10000 | tf_op jit(solution)/shard_map/edge_backward/pallas_call | solution.py:76
  71.0 3.1 %collective-permute-start.15 = (bf16[2,576,256]{2,1,0:T(8,128)(2,1)S(1)}, bf16[2,576,256]{2,1,0:T(8,128)(2,1)S(1)}, u32[]{:S(2)}, u32[]{:S(2)}) collective-permute-start(bf16[2,576,256]{2,1,0:T(8,128)(2,1)S(1)} %get-tuple-element.106), channel_id=1, source_target_pairs={{0,4},{4,0},{8,12},{12,8},{16,20},{20,16},{24,28},{28,24},{32,36},... | collective-permute-start | bytes 1769480 | tf_op jit(solution)/shard_map/ppermute | solution.py:949
  74.1 5.5 %inner_backward.1 = (bf16[1024,256]{1,0:T(8,128)(2,1)S(1)}, f32[2,1024,256]{2,1,0:T(8,128)S(1)}) custom-call(f32[2]{0:T(128)S(1)} %pad_maximum_fusion.bias_ref, f32[2,8,256]{2,1,0:T(8,128)S(1)} %get-tuple-element.88.stats, bf16[1792,256]{1,0:T(8,128)(2,1)S(1)} %get-tuple-element.77.q, bf16[2,1792,256]{2,1,0:T(8,128)(2,1)S(1)} %get-tuple-element.73.kv, ...), custom_call_target="tpu_custom_call" | custom-call | flops 1000000 | bytes 10000 | tf_op jit(solution)/shard_map/inner_backward/pallas_call | solution.py:76
  79.7 2.6 %collective-permute-done.12.three = bf16[1024,256]{1,0:T(8,128)(2,1)S(1)} collective-permute-done((bf16[1024,256]{1,0:T(8,128)(2,1)S(1)}, bf16[1024,256]{1,0:T(8,128)(2,1)S(1)}, u32[]{:S(2)}, u32[]{:S(2)}) %collective-permute-start.12) | collective-permute-done | bytes 524320 | tf_op jit(solution)/shard_map/ppermute | solution.py:922
  82.4 2.7 %early_terms.1 = (bf16[1024,256]{1,0:T(8,128)(2,1)S(1)}, bf16[1024,256]{1,0:T(8,128)(2,1)S(1)}) custom-call(bf16[1024,256]{1,0:T(8,128)(2,1)S(1)} %copy-done.4, bf16[1024,256]{1,0:T(8,128)(2,1)} %collective-permute-done.8.g1, bf16[1024,256]{1,0:T(8,128)(2,1)S(1)} %collective-permute-done.13.g2, bf16[1024,256]{1,0:T(8,128)(2,1)} %collective-permute-done.9.g3, ...), custom_call_target="tpu_custom_call" | custom-call | flops 4000000000 | bytes 10000 | tf_op jit(solution)/shard_map/early_terms/pallas_call | solution.py:76
  85.1 3.5 %input_terms.1 = (bf16[1024,512]{1,0:T(8,128)(2,1)S(1)}, bf16[16,256]{1,0:T(8,128)(2,1)S(1)}, bf16[1024,256]{1,0:T(8,128)(2,1)S(1)}, bf16[512,256]{1,0:T(8,128)(...) custom-call(s32[4]{0:T(128)S(1)} %pad_add_fusion.place, ...), custom_call_target="tpu_custom_call" | custom-call | flops 1000000 | bytes 10000 | tf_op jit(solution)/shard_map/input_terms/pallas_call | solution.py:76
  89.7 2.1 %inner_terms.1 = (bf16[512,1024]{1,0:T(8,128)(2,1)S(1)}, bf16[256,1024]{1,0:T(8,128)(2,1)S(1)}, bf16[256,1024]{1,0:T(8,128)(2,1)S(1)}) custom-call(s32[4]{0:T(128)S(1)} %pad_add_fusion.place, bf16[1024,1024]{1,0:T(8,128)(2,1)S(1)} %copy-done, bf16[1024,512]{1,0:T(8,128)(2,1)S(1)} %get-tuple-element.117.d_proj, ...), custom_call_target="tpu_custom_call" | custom-call | flops 1000000 | bytes 10000 | tf_op jit(solution)/shard_map/inner_terms/pallas_call | solution.py:76
  97.0 3.0 %collective-permute-start.23 = (bf16[128,1024]{1,0:T(8,128)(2,1)S(1)}, bf16[128,1024]{1,0:T(8,128)(2,1)S(1)}, u32[]{:S(2)}, u32[]{:S(2)}) collective-permute-start(bf16[128,1024]{1,0:T(8,128)(2,1)S(1)} %get-tuple-element.124), channel_id=1, source_target_pairs={{0,16},{4,68},{8,24},{12,76},{16,0},{20,84},{24,8},{28,92},{32,48}... | collective-permute-start | bytes 786440 | tf_op jit(solution)/shard_map/ppermute | solution.py:897
  107.9 2.7 %collective-permute-start.25 = (bf16[32,1024]{1,0:T(8,128)(2,1)S(1)}, bf16[32,1024]{1,0:T(8,128)(2,1)S(1)}, u32[]{:S(2)}, u32[]{:S(2)}) collective-permute-start(bf16[32,1024]{1,0:T(8,128)(2,1)S(1)} %get-tuple-element.131), channel_id=1, source_target_pairs={{0,32},{4,12},{8,40},{12,20},{16,48},{20,28},{24,56},{28,4},{32,64... | collective-permute-start | bytes 196616 | tf_op jit(solution)/shard_map/ppermute | solution.py:897
  110.7 2.9 %collective-permute-start.26 = (bf16[32,1024]{1,0:T(8,128)(2,1)S(1)}, bf16[32,1024]{1,0:T(8,128)(2,1)S(1)}, u32[]{:S(2)}, u32[]{:S(2)}) collective-permute-start(bf16[32,1024]{1,0:T(8,128)(2,1)S(1)} %get-tuple-element.132), channel_id=1, source_target_pairs={{0,64},{4,20},{8,72},{12,28},{16,80},{20,4},{24,88},{28,12},{32,96... | collective-permute-start | bytes 196616 | tf_op jit(solution)/shard_map/ppermute | solution.py:897
  114.9 2.3 %finish_grad.1 = f32[1024,256]{1,0:T(8,128)} custom-call(s32[4]{0:T(128)S(1)} %pad_add_fusion.place, bf16[1024,256]{1,0:T(8,128)(2,1)S(1)} %get-tuple-element.108.own, bf16[1040,256]{1,0:T(8,128)(2,1)S(1)} %collective-permute-done.16.from_a.a1, bf16[1040,256]{1,0:T(8,128)(2,1)S(1)} %collective-permute-done.17.from_b.b1, ...), custom_call_target="tpu_custom_call" | custom-call | flops 1000000 | bytes 10000 | tf_op jit(solution)/shard_map/finish_grad/pallas_call | solution.py:76
  (72 shorter events, 31.2 us)
Async XLA Ops:
  1.7 11.3 %collective-permute-start.3 = (bf16[512,256]{1,0:T(8,128)(2,1)S(1)}, bf16[512,256]{1,0:T(8,128)(2,1)S(1)}, u32[]{:S(2)}, u32[]{:S(2)}) collective-permute-start(bf16[512,256]{1,0:T(8,128)(2,1)S(1)} %get-tuple-element.138), channel_id=1, source_target_pairs={{0,1},{1,2},{2,3},{3,0},{4,5},{5,6},{6,7},{7,4},{8,9},{9,10},{10,1... | collective-permute-start | bytes 786440 | tf_op jit(solution)/shard_map/ppermute | solution.py:910
  3.8 9.3 %collective-permute-start = (bf16[512,256]{1,0:T(8,128)(2,1)S(1)}, bf16[512,256]{1,0:T(8,128)(2,1)S(1)}, u32[]{:S(2)}, u32[]{:S(2)}) collective-permute-start(bf16[512,256]{1,0:T(8,128)(2,1)S(1)} %get-tuple-element.139), channel_id=1, source_target_pairs={{1,0},{2,1},{3,2},{0,3},{5,4},{6,5},{7,6},{4,7},{9,8},{10,9},{11,1... | collective-permute-start | bytes 786440 | tf_op jit(solution)/shard_map/ppermute | solution.py:914
  6.0 12.6 %collective-permute-start.1 = (bf16[512,256]{1,0:T(8,128)(2,1)S(1)}, bf16[512,256]{1,0:T(8,128)(2,1)S(1)}, u32[]{:S(2)}, u32[]{:S(2)}) collective-permute-start(bf16[512,256]{1,0:T(8,128)(2,1)S(1)} %get-tuple-element.138), channel_id=1, source_target_pairs={{1,0},{2,1},{3,2},{0,3},{5,4},{6,5},{7,6},{4,7},{9,8},{10,9},{11,1... | collective-permute-start | bytes 786440 | tf_op jit(solution)/shard_map/ppermute | solution.py:914
  7.9 10.7 %collective-permute-start.5 = (bf16[512,256]{1,0:T(8,128)(2,1)S(1)}, bf16[512,256]{1,0:T(8,128)(2,1)S(1)}, u32[]{:S(2)}, u32[]{:S(2)}) collective-permute-start(bf16[512,256]{1,0:T(8,128)(2,1)S(1)} %get-tuple-element.139), channel_id=1, source_target_pairs={{0,1},{1,2},{2,3},{3,0},{4,5},{5,6},{6,7},{7,4},{8,9},{9,10},{10,1... | collective-permute-start | bytes 786440 | tf_op jit(solution)/shard_map/ppermute | solution.py:910
  13.0 11.2 %collective-permute-start.4 = (bf16[512,256]{1,0:T(8,128)(2,1)S(1)}, bf16[512,256]{1,0:T(8,128)(2,1)S(1)}, u32[]{:S(2)}, u32[]{:S(2)}) collective-permute-start(bf16[512,256]{1,0:T(8,128)(2,1)S(1)} %collective-permute-done.3.t3b_any), channel_id=1, source_target_pairs={{0,1},{1,2},{2,3},{3,0},{4,5},{5,6},{6,7},{7,4},{8,9},{9,10},{10,1... | collective-permute-start | bytes 786440 | tf_op jit(solution)/shard_map/ppermute | solution.py:910
  13.0 11.9 %collective-permute-start.2 = (bf16[512,256]{1,0:T(8,128)(2,1)S(1)}, bf16[512,256]{1,0:T(8,128)(2,1)}, u32[]{:S(2)}, u32[]{:S(2)}) collective-permute-start(bf16[512,256]{1,0:T(8,128)(2,1)S(1)} %collective-permute-done.t1a_any), channel_id=1, source_target_pairs={{1,0},{2,1},{3,2},{0,3},{5,4},{6,5},{7,6},{4,7},{9,8},{10,9},{11,1... | collective-permute-start | bytes 786440 | tf_op jit(solution)/shard_map/ppermute | solution.py:914
  19.3 20.1 %collective-permute-start.9 = (bf16[1024,256]{1,0:T(8,128)(2,1)}, bf16[1024,256]{1,0:T(8,128)(2,1)}, u32[]{:S(2)}, u32[]{:S(2)}) collective-permute-start(bf16[1024,256]{1,0:T(8,128)(2,1)} %g0.1), channel_id=1, source_target_pairs={{0,1},{1,2},{2,3},{3,0},{4,5},{5,6},{6,7},{7,4},{8,9},{9,10},{10,1... | collective-permute-start | bytes 1572872 | tf_op jit(solution)/shard_map/ppermute | solution.py:910
  21.3 18.2 %collective-permute-start.8 = (bf16[1024,256]{1,0:T(8,128)(2,1)}, bf16[1024,256]{1,0:T(8,128)(2,1)}, u32[]{:S(2)}, u32[]{:S(2)}) collective-permute-start(bf16[1024,256]{1,0:T(8,128)(2,1)} %g0.1), channel_id=1, source_target_pairs={{1,0},{2,1},{3,2},{0,3},{5,4},{6,5},{7,6},{4,7},{9,8},{10,9},{11,1... | collective-permute-start | bytes 1572872 | tf_op jit(solution)/shard_map/ppermute | solution.py:914
  32.6 12.3 %collective-permute-start.6 = (bf16[2,576,256]{2,1,0:T(8,128)(2,1)}, bf16[2,576,256]{2,1,0:T(8,128)(2,1)S(1)}, u32[]{:S(2)}, u32[]{:S(2)}) collective-permute-start(bf16[2,576,256]{2,1,0:T(8,128)(2,1)} %get-tuple-element.74), channel_id=1, source_target_pairs={{4,8},{8,4},{12,16},{16,12},{20,24},{24,20},{28,32},{32,28},{36,40... | collective-permute-start | bytes 1769480 | tf_op jit(solution)/shard_map/ppermute | solution.py:948
  33.3 11.6 %collective-permute-start.7 = (bf16[2,576,256]{2,1,0:T(8,128)(2,1)}, bf16[2,576,256]{2,1,0:T(8,128)(2,1)}, u32[]{:S(2)}, u32[]{:S(2)}) collective-permute-start(bf16[2,576,256]{2,1,0:T(8,128)(2,1)} %get-tuple-element.75), channel_id=1, source_target_pairs={{0,4},{4,0},{8,12},{12,8},{16,20},{20,16},{24,28},{28,24},{32,36},... | collective-permute-start | bytes 1769480 | tf_op jit(solution)/shard_map/ppermute | solution.py:949
  36.3 21.6 %collective-permute-start.13 = (bf16[1024,256]{1,0:T(8,128)(2,1)}, bf16[1024,256]{1,0:T(8,128)(2,1)S(1)}, u32[]{:S(2)}, u32[]{:S(2)}) collective-permute-start(bf16[1024,256]{1,0:T(8,128)(2,1)} %g0.1), channel_id=1, source_target_pairs={{0,2},{1,3},{2,0},{3,1},{4,6},{5,7},{6,4},{7,5},{8,10},{9,11},{10,... | collective-permute-start | bytes 1572872 | tf_op jit(solution)/shard_map/ppermute | solution.py:935
  53.1 26.5 %collective-permute-start.10 = (bf16[1024,256]{1,0:T(8,128)(2,1)S(1)}, bf16[1024,256]{1,0:T(8,128)(2,1)S(1)}, u32[]{:S(2)}, u32[]{:S(2)}) collective-permute-start(bf16[1024,256]{1,0:T(8,128)(2,1)S(1)} %get-tuple-element.85), channel_id=1, source_target_pairs={{0,1},{1,0},{2,3},{3,2},{4,5},{5,4},{6,7},{7,6},{8,9},{9,8},{10,11... | collective-permute-start | bytes 1572872 | tf_op jit(solution)/shard_map/ppermute | solution.py:918
  53.8 25.9 %collective-permute-start.11 = (bf16[1024,256]{1,0:T(8,128)(2,1)S(1)}, bf16[1024,256]{1,0:T(8,128)(2,1)S(1)}, u32[]{:S(2)}, u32[]{:S(2)}) collective-permute-start(bf16[1024,256]{1,0:T(8,128)(2,1)S(1)} %get-tuple-element.86), channel_id=1, source_target_pairs={{0,2},{1,3},{2,0},{3,1},{4,6},{5,7},{6,4},{7,5},{8,10},{9,11},{10,... | collective-permute-start | bytes 1572872 | tf_op jit(solution)/shard_map/ppermute | solution.py:935
  55.6 26.7 %collective-permute-start.12 = (bf16[1024,256]{1,0:T(8,128)(2,1)S(1)}, bf16[1024,256]{1,0:T(8,128)(2,1)S(1)}, u32[]{:S(2)}, u32[]{:S(2)}) collective-permute-start(bf16[1024,256]{1,0:T(8,128)(2,1)S(1)} %get-tuple-element.87), channel_id=1, source_target_pairs={{1,2},{2,1},{3,0},{0,3},{5,6},{6,5},{7,4},{4,7},{9,10},{10,9},{11,... | collective-permute-start | bytes 1572872 | tf_op jit(solution)/shard_map/ppermute | solution.py:922
  70.3 14.8 %collective-permute-start.14 = (bf16[2,576,256]{2,1,0:T(8,128)(2,1)S(1)}, bf16[2,576,256]{2,1,0:T(8,128)(2,1)S(1)}, u32[]{:S(2)}, u32[]{:S(2)}) collective-permute-start(bf16[2,576,256]{2,1,0:T(8,128)(2,1)S(1)} %get-tuple-element.105), channel_id=1, source_target_pairs={{4,8},{8,4},{12,16},{16,12},{20,24},{24,20},{28,32},{32,28},{36,40... | collective-permute-start | bytes 1769480 | tf_op jit(solution)/shard_map/ppermute | solution.py:948
  71.0 14.1 %collective-permute-start.15 = (bf16[2,576,256]{2,1,0:T(8,128)(2,1)S(1)}, bf16[2,576,256]{2,1,0:T(8,128)(2,1)S(1)}, u32[]{:S(2)}, u32[]{:S(2)}) collective-permute-start(bf16[2,576,256]{2,1,0:T(8,128)(2,1)S(1)} %get-tuple-element.106), channel_id=1, source_target_pairs={{0,4},{4,0},{8,12},{12,8},{16,20},{20,16},{24,28},{28,24},{32,36},... | collective-permute-start | bytes 1769480 | tf_op jit(solution)/shard_map/ppermute | solution.py:949
  88.6 13.7 %collective-permute-start.16 = (bf16[1040,256]{1,0:T(8,128)(2,1)S(1)}, bf16[1040,256]{1,0:T(8,128)(2,1)S(1)}, u32[]{:S(2)}, u32[]{:S(2)}) collective-permute-start(bf16[1040,256]{1,0:T(8,128)(2,1)S(1)} %get-tuple-element.109), channel_id=1, source_target_pairs={{0,1},{1,0},{2,3},{3,2},{4,5},{5,4},{6,7},{7,6},{8,9},{9,8},{10,11... | collective-permute-start | bytes 1597448 | tf_op jit(solution)/shard_map/ppermute | solution.py:918
  88.6 14.9 %collective-permute-start.17 = (bf16[1040,256]{1,0:T(8,128)(2,1)S(1)}, bf16[1040,256]{1,0:T(8,128)(2,1)S(1)}, u32[]{:S(2)}, u32[]{:S(2)}) collective-permute-start(bf16[1040,256]{1,0:T(8,128)(2,1)S(1)} %get-tuple-element.110), channel_id=1, source_target_pairs={{1,2},{2,1},{3,0},{0,3},{5,6},{6,5},{7,4},{4,7},{9,10},{10,9},{11,... | collective-permute-start | bytes 1597448 | tf_op jit(solution)/shard_map/ppermute | solution.py:922
  95.4 10.9 %collective-permute-start.22 = (bf16[128,1024]{1,0:T(8,128)(2,1)S(1)}, bf16[128,1024]{1,0:T(8,128)(2,1)S(1)}, u32[]{:S(2)}, u32[]{:S(2)}) collective-permute-start(bf16[128,1024]{1,0:T(8,128)(2,1)S(1)} %get-tuple-element.123), channel_id=1, source_target_pairs={{0,8},{4,36},{8,16},{12,44},{16,24},{20,52},{24,0},{28,60},{32,40}... | collective-permute-start | bytes 786440 | tf_op jit(solution)/shard_map/ppermute | solution.py:897
  97.0 10.1 %collective-permute-start.23 = (bf16[128,1024]{1,0:T(8,128)(2,1)S(1)}, bf16[128,1024]{1,0:T(8,128)(2,1)S(1)}, u32[]{:S(2)}, u32[]{:S(2)}) collective-permute-start(bf16[128,1024]{1,0:T(8,128)(2,1)S(1)} %get-tuple-element.124), channel_id=1, source_target_pairs={{0,16},{4,68},{8,24},{12,76},{16,0},{20,84},{24,8},{28,92},{32,48}... | collective-permute-start | bytes 786440 | tf_op jit(solution)/shard_map/ppermute | solution.py:897
  100.0 7.2 %collective-permute-start.24 = (bf16[128,1024]{1,0:T(8,128)(2,1)S(1)}, bf16[128,1024]{1,0:T(8,128)(2,1)S(1)}, u32[]{:S(2)}, u32[]{:S(2)}) collective-permute-start(bf16[128,1024]{1,0:T(8,128)(2,1)S(1)} %get-tuple-element.125), channel_id=1, source_target_pairs={{0,24},{4,100},{8,0},{12,108},{16,8},{20,116},{24,16},{28,124},{32... | collective-permute-start | bytes 786440 | tf_op jit(solution)/shard_map/ppermute | solution.py:897
  104.5 10.5 %collective-permute-start.19 = (bf16[528,256]{1,0:T(8,128)(2,1)S(1)}, bf16[528,256]{1,0:T(8,128)(2,1)S(1)}, u32[]{:S(2)}, u32[]{:S(2)}) collective-permute-start(bf16[528,256]{1,0:T(8,128)(2,1)S(1)} %get-tuple-element.114), channel_id=1, source_target_pairs={{1,2},{2,1},{3,0},{0,3},{5,6},{6,5},{7,4},{4,7},{9,10},{10,9},{11,... | collective-permute-start | bytes 811016 | tf_op jit(solution)/shard_map/ppermute | solution.py:922
  104.8 10.1 %collective-permute-start.18 = (bf16[528,256]{1,0:T(8,128)(2,1)S(1)}, bf16[528,256]{1,0:T(8,128)(2,1)S(1)}, u32[]{:S(2)}, u32[]{:S(2)}) collective-permute-start(bf16[528,256]{1,0:T(8,128)(2,1)S(1)} %get-tuple-element.113), channel_id=1, source_target_pairs={{0,1},{1,0},{2,3},{3,2},{4,5},{5,4},{6,7},{7,6},{8,9},{9,8},{10,11... | collective-permute-start | bytes 811016 | tf_op jit(solution)/shard_map/ppermute | solution.py:918
  107.9 9.3 %collective-permute-start.25 = (bf16[32,1024]{1,0:T(8,128)(2,1)S(1)}, bf16[32,1024]{1,0:T(8,128)(2,1)S(1)}, u32[]{:S(2)}, u32[]{:S(2)}) collective-permute-start(bf16[32,1024]{1,0:T(8,128)(2,1)S(1)} %get-tuple-element.131), channel_id=1, source_target_pairs={{0,32},{4,12},{8,40},{12,20},{16,48},{20,28},{24,56},{28,4},{32,64... | collective-permute-start | bytes 196616 | tf_op jit(solution)/shard_map/ppermute | solution.py:897
  (14 other events, 71.4 us)
